TPU v7x, 32 devices: a whole 2x2x4 slice. The times are simulated.
32 devices in a mesh: freq: 4 (over z), dom: 8 (over y, x, core).
Axes of the slice: x: 2, y: 2, z: 4, core: 2. Of those that a mesh axis runs over, the one named last changes fastest.
Arguments:
- angular: float32 [8], P('freq'), may hold values from 0.5 to 4
- stiffness: float32 [8, 36, 1024], P('dom'), as said below
- mass_matrix: float32 [8, 36, 1024], P('dom'), as said below
- conductivity: float32 [8, 1024], P('dom'), may hold values from 0.3 to 3
- element_edges: int32 [8, 6, 1024], P('dom'), may hold values from 0 to 1279
- live_slots: int32 [8, 1024], P('dom'), may hold values from 0 to 1, as said below
- adjoint_source: float32 [8, 2, 8, 1280], P('freq', None, 'dom'), may hold values from -6 to 6
- forward_field: float32 [8, 2, 8, 1280], P('freq', None, 'dom'), may hold values from -6 to 6
- neighbour_map: int32 [8, 256], P('dom'), may hold values from 0 to 255, each once within a row
Outputs:
- gradient: float32 [8, 1024], P('dom')
- updated_conductivity: float32 [8, 1024], P('dom')
Inputs may be any that keep to these rules, and one draw needn't show every extreme that they name: `live_slots`: in each partition the live slots come first; at least half of the 1024 slots are live, and some partition has all slots live. `neighbour_map`: each row is a permutation of the rim slots; row 0 is not used. `stiffness`: each element matrix is symmetric with a strictly dominant positive diagonal. `mass_matrix`: each element matrix is symmetric with a strictly dominant positive diagonal.
All inputs are finite; a program needn't handle non-finite values.
Results may differ from a plain program's by a relative error of at most 0.0003.
Values sent between devices are 32-bit elements; how exact they have to be, the bound alone decides.
No kernel may reach another device: no remote copies, remote signals or barrier semaphores. Data moves between devices by JAX's collectives and lax.ppermute only.
A program may use at most 64 MiB of HBM per device.

v0:
```python
import functools

import jax
import jax.numpy as jnp
from jax import lax
from jax.experimental import pallas as pl
from jax.experimental.pallas import tpu as pltpu
from jax.sharding import PartitionSpec as P

LANES = 128
SIDE = 6
VMEM = pl.BlockSpec(memory_space=pltpu.VMEM)
SMEM = pl.BlockSpec(memory_space=pltpu.SMEM)

PICK_LANES = lax.GatherDimensionNumbers(
    offset_dims=(),
    collapsed_slice_dims=(1,),
    start_index_map=(1,),
    operand_batching_dims=(0,),
    start_indices_batching_dims=(0,),
)


def pick_lanes(block, lanes):
    return lax.gather(
        block,
        lanes[..., None],
        PICK_LANES,
        (1, 1),
        mode=lax.GatherScatterMode.PROMISE_IN_BOUNDS,
    )


def pick_wide(chunks, index):
    lanes = index & (LANES - 1)
    high = index >> 7
    level = [pick_lanes(chunk, lanes) for chunk in chunks]
    bit = 0
    while len(level) > 1:
        odd = (high >> bit) & 1 == 1
        level = [
            jnp.where(odd, level[t + 1], level[t]) if t + 1 < len(level) else level[t]
            for t in range(0, len(level), 2)
        ]
        bit += 1
    return level[0]


def row_ids(rows):
    return lax.broadcasted_iota(jnp.int32, (rows, LANES), 0)


def lane_ids(rows):
    return lax.broadcasted_iota(jnp.int32, (rows, LANES), 1)


def spread(row, rows):
    return jnp.broadcast_to(row, (rows, row.shape[-1]))


def cut(ref, start=0):
    return [ref[:, c : c + LANES] for c in range(start, ref.shape[-1], LANES)]


def swap_halves(block):
    return pltpu.roll(block, block.shape[0] // 2, 0)


def doubled(block):
    half = block.shape[0] // 2
    return jnp.where(row_ids(2 * half) < half, block, swap_halves(block))


def row_weights(angular_ref, rows, polars):
    ids = row_ids(rows)
    out = jnp.zeros((rows, LANES), jnp.float32)
    for f in range(angular_ref.shape[0]):
        for base in (0, rows // 2):
            here = (ids >= base + f * polars) & (ids < base + (f + 1) * polars)
            out = jnp.where(here, angular_ref[f], out)
    return out


def lane_sum(block):
    return jnp.broadcast_to(jnp.sum(block, axis=1, keepdims=True), block.shape)


def product(chunks, rate, inverse_scale, weights, edges, stiffness, mass, sigma, live, tables):
    rows = chunks[0].shape[0]
    half = rows // 2
    count = len(chunks)
    lower_half = row_ids(rows) < half
    slots = stiffness.shape[-1]

    def body(s, quad):
        here = pl.ds(pl.multiple_of(s * LANES, LANES), LANES)
        index = [spread(edges[pl.ds(j, 1), here], rows) for j in range(SIDE)]
        picked = [pick_wide(chunks, index[j]) for j in range(SIDE)]
        shift = weights * spread(sigma[:, here], rows)
        alive = spread(live[:, here], rows).astype(jnp.float32) * inverse_scale
        for i in range(SIDE):
            stiff = None
            heavy = None
            for j in range(SIDE):
                entry = pl.ds(SIDE * i + j, 1)
                one = spread(stiffness[entry, here], rows) * picked[j]
                two = spread(mass[entry, here], rows) * picked[j]
                stiff = one if stiff is None else stiff + one
                heavy = two if heavy is None else heavy + two
            value = (stiff + shift * heavy) * alive
            quad = quad + picked[i] * value
            if tables is None:
                continue
            values, places = tables
            coarse = value.astype(jnp.bfloat16).astype(jnp.float32)
            both = jnp.where(lower_half, coarse, value - coarse)
            high = index[i] >> 7
            column = pl.ds(pl.multiple_of(i * slots + s * LANES, LANES), LANES)
            for h in range(0, count, 2):
                block = [jnp.where(high == h + t, both, 0.0) for t in range(2)]
                values[rows * h : rows * (h + 2), column] = jnp.concatenate(
                    block, axis=0
                ).astype(jnp.bfloat16)
            lanes = spread(index[i][:1] & (LANES - 1), LANES)
            places[:, column] = jnp.where(lanes == row_ids(LANES), 1.0, 0.0).astype(
                jnp.bfloat16
            )
        return quad

    quad = lax.fori_loop(0, slots // LANES, body, jnp.zeros((rows, LANES), jnp.float32))
    if tables is None:
        return None, quad
    values, places = tables
    total = lax.dot_general(
        values[...],
        places[...],
        (((1,), (1,)), ((), ())),
        preferred_element_type=jnp.float32,
    )
    out = []
    for h in range(count):
        piece = total[rows * h : rows * (h + 1)]
        out.append(piece + swap_halves(piece))
    return out, quad


def joined(own, from_prior, from_above, order, inverse):
    rim = len(from_prior)
    lower = [own[c] + pick_wide(from_prior, order[c]) for c in range(rim)]
    upper = [own[len(own) - rim + c] + pick_wide(from_above, inverse[c]) for c in range(rim)]
    return lower + own[rim : len(own) - rim] + upper


def squares(chunks, rim, has_prior):
    total = None
    for c, chunk in enumerate(chunks):
        term = chunk * chunk
        if c < rim:
            term = term * (1.0 - has_prior)
        total = term if total is None else total + term
    return total


def put_lane(block, lane, value):
    return jnp.where(lane_ids(block.shape[0]) == lane, value, block)


def put_chunks(ref, chunks):
    for c, chunk in enumerate(chunks):
        ref[:, c * LANES : (c + 1) * LANES] = chunk


def first_stage(
    polars,
    angular,
    source,
    order_ref,
    prior_ref,
    above_ref,
    stiffness,
    mass,
    sigma,
    edges,
    live,
    field_ref,
    image_ref,
    lower_ref,
    upper_ref,
    inverse_ref,
    sums_ref,
    values,
    places,
):
    groups = source.shape[0]
    rows = 2 * groups
    ids = row_ids(rows)
    weights = row_weights(angular, rows, polars)

    peak = None
    for i in range(SIDE):
        entry = pl.ds((SIDE + 1) * i, 1)
        for f in range(angular.shape[0]):
            size = stiffness[entry, :] + angular[f] * sigma[...] * mass[entry, :]
            peak = size if peak is None else jnp.maximum(peak, size)
    peak = spread(peak * live[...].astype(jnp.float32), rows)
    scale = peak[:, :LANES]
    for c in range(LANES, peak.shape[-1], LANES):
        scale = jnp.maximum(scale, peak[:, c : c + LANES])
    scale = jnp.broadcast_to(jnp.max(scale, axis=1, keepdims=True), (rows, LANES))

    rim = order_ref.shape[-1]
    order = [spread(piece, rows) for piece in cut(order_ref)]
    above_order = spread(above_ref[groups : groups + 1, :], rim)
    slot = lax.broadcasted_iota(jnp.int32, (rim, rim), 0).astype(jnp.float32)
    match = jnp.where(above_order == slot, 1.0, 0.0).astype(jnp.bfloat16)
    numbers = lax.broadcasted_iota(jnp.int32, (2 * rows, rim), 1).astype(jnp.bfloat16)
    inverse = lax.dot_general(
        numbers, match, (((1,), (1,)), ((), ())), preferred_element_type=jnp.float32
    )[:rows].astype(jnp.int32)
    inverse_ref[...] = inverse
    inverse = [inverse[:, c : c + LANES] for c in range(0, rim, LANES)]

    own = [jnp.concatenate([piece, piece], axis=0) for piece in cut(source)]
    prior = cut(prior_ref)
    has_prior = spread(prior[0][groups : groups + 1], rows)
    field = joined(
        own, [doubled(x) for x in prior], [doubled(x) for x in cut(above_ref)], order, inverse
    )
    put_chunks(field_ref, field)
    image, quad = product(
        field,
        None,
        1.0 / scale,
        weights,
        edges,
        stiffness,
        mass,
        sigma,
        live,
        (values, places),
    )
    put_chunks(image_ref, image)
    count = rim // LANES
    first = ids < groups
    put_chunks(lower_ref, [jnp.where(first, x, scale) for x in image[:count]])
    put_chunks(upper_ref, [jnp.where(first, x, scale) for x in image[len(image) - count :]])
    sums = jnp.zeros((rows, LANES), jnp.float32)
    sums = put_lane(sums, 0, lane_sum(squares(field, count, has_prior)))
    sums = put_lane(sums, 1, lane_sum(quad))
    sums_ref[...] = jnp.where(first, sums, scale)


def later_stage(
    polars,
    step,
    last,
    angular,
    image_in,
    order_ref,
    inverse_ref,
    prior_ref,
    above_ref,
    sums_in,
    stiffness,
    mass,
    sigma,
    edges,
    live,
    field_ref,
    sums_ref,
    *rest,
):
    rows = image_in.shape[0]
    groups = rows // 2
    first = row_ids(rows) < groups
    weights = row_weights(angular, rows, polars)
    sums = sums_in[...]
    scale = jnp.where(first, swap_halves(sums), sums)
    inverse_scale = 1.0 / scale
    rim = order_ref.shape[-1]
    count = rim // LANES
    order = [spread(piece, rows) for piece in cut(order_ref)]
    inverse = cut(inverse_ref)

    def rescaled(block):
        ratio = swap_halves(block) * inverse_scale
        for _ in range(step):
            block = block * ratio
        return doubled(block)

    prior = cut(prior_ref)
    has_prior = jnp.where(first, swap_halves(prior[0]), prior[0])
    has_prior = jnp.where(has_prior > 0.0, 1.0, 0.0)
    field = joined(
        cut(image_in),
        [rescaled(x) for x in prior],
        [rescaled(x) for x in cut(above_ref)],
        order,
        inverse,
    )
    put_chunks(field_ref, field)
    image, quad = product(
        field,
        None,
        inverse_scale,
        weights,
        edges,
        stiffness,
        mass,
        sigma,
        live,
        None if last else (rest[4 - 1], rest[4]),
    )
    fresh = put_lane(sums, 2 * step, lane_sum(squares(field, count, has_prior)))
    fresh = put_lane(fresh, 2 * step + 1, lane_sum(quad))
    sums_ref[...] = jnp.where(first, fresh, scale)
    if not last:
        image_ref, lower_ref, upper_ref = rest[:3]
        put_chunks(image_ref, image)
        put_chunks(lower_ref, [jnp.where(first, x, scale) for x in image[:count]])
        put_chunks(upper_ref, [jnp.where(first, x, scale) for x in image[len(image) - count :]])


def gradient_stage(
    polars,
    angular,
    everyone,
    sums_in,
    field0,
    field1,
    field2,
    forward,
    mass,
    edges,
    live,
    term_ref,
):
    rows = field0.shape[0]
    groups = rows // 2
    first = row_ids(rows) < groups
    weights = jnp.where(first, row_weights(angular, rows, polars), 0.0)

    def scale_of(block):
        return jnp.where(first, swap_halves(block), block)

    parts = [everyone[q] for q in range(everyone.shape[0])]
    scales = [scale_of(block) for block in parts]
    top = functools.reduce(jnp.maximum, scales)
    lanes = lane_ids(rows)
    total = None
    for block, scale in zip(parts, scales):
        ratio = scale / top
        power = jnp.ones_like(ratio)
        factor = jnp.ones_like(ratio)
        for k in range(1, 6):
            power = power * ratio
            factor = jnp.where(lanes == k, power, factor)
        term = block * factor
        total = term if total is None else total + term
    m = [jnp.broadcast_to(total[:, k : k + 1], (rows, LANES)) for k in range(6)]
    l1 = m[2] / m[1]
    l2 = m[3] / m[1]
    d2 = m[3] - l1 * m[2]
    cross = m[4] - l2 * m[2]
    l3 = cross / d2
    d3 = m[5] - l2 * m[3] - l3 * cross
    y1 = m[1] - l1 * m[0]
    y2 = m[2] - l2 * m[0] - l3 * y1
    c2 = y2 / d3
    c1 = y1 / d2 - l3 * c2
    c0 = m[0] / m[1] - l1 * c1 - l2 * c2
    mine = scale_of(sums_in[...]) / top
    c0 = c0 / top
    c1 = c1 * mine / top
    c2 = c2 * mine * mine / top

    stacked = []
    for a, b, c, u in zip(cut(field0), cut(field1), cut(field2), cut(forward)):
        adjoint = c0 * a + c1 * b + c2 * c
        stacked.append(jnp.where(first, adjoint, jnp.concatenate([u, u], axis=0)))

    def body(s, carry):
        here = pl.ds(pl.multiple_of(s * LANES, LANES), LANES)
        picked = [
            pick_wide(stacked, spread(edges[pl.ds(j, 1), here], rows)) for j in range(SIDE)
        ]
        total = jnp.zeros((rows, LANES), jnp.float32)
        for i in range(SIDE):
            heavy = None
            for j in range(SIDE):
                one = spread(mass[pl.ds(SIDE * i + j, 1), here], rows) * picked[j]
                heavy = one if heavy is None else heavy + one
            total = total + picked[i] * swap_halves(heavy)
        term = jnp.sum(total * weights, axis=0, keepdims=True)
        term_ref[:, here] = -term * live[:, here].astype(jnp.float32)
        return carry

    lax.fori_loop(0, edges.shape[-1] // LANES, body, 0)


def call(kernel, arguments, outs, scratch=()):
    specs = [SMEM] + [VMEM] * (len(arguments) - 1)
    return pl.pallas_call(
        kernel,
        out_shape=outs,
        in_specs=specs,
        out_specs=jax.tree.map(lambda _: VMEM, outs),
        scratch_shapes=list(scratch),
        compiler_params=pltpu.CompilerParams(vmem_limit_bytes=24 * 1024 * 1024),
    )(*arguments)


def pass_along(block, distance):
    devices = range(lax.axis_size("dom"))
    route = [(i - distance, i) for i in devices if i - distance in devices]
    return lax.ppermute(block, "dom", route)


def gather_all(block, axis):
    size = lax.axis_size(axis)
    copies = jnp.broadcast_to(block[None], (size, *block.shape))
    return lax.all_to_all(copies, axis, 0, 0)


def local(
    angular,
    stiffness,
    mass_matrix,
    conductivity,
    element_edges,
    live_slots,
    adjoint_source,
    forward_field,
    neighbour_map,
):
    polars = adjoint_source.shape[1]
    groups = adjoint_source.shape[0] * polars
    rows = 2 * groups
    edge_count = adjoint_source.shape[-1]
    rim = neighbour_map.shape[-1]
    slots = element_edges.shape[-1]
    stiff, mass, edges = stiffness[0], mass_matrix[0], element_edges[0]
    source = adjoint_source.reshape(groups, edge_count)
    forward = forward_field.reshape(groups, edge_count)

    def shape(*dims, kind=jnp.float32):
        return jax.ShapeDtypeStruct(dims, kind)

    tables = (
        pltpu.VMEM((rows * edge_count // LANES, SIDE * slots), jnp.bfloat16),
        pltpu.VMEM((LANES, SIDE * slots), jnp.bfloat16),
    )
    elements = (stiff, mass, conductivity, edges, live_slots)
    field_shape, rim_shape = shape(rows, edge_count), shape(rows, rim)
    sums_shape = shape(rows, LANES)

    filler = jnp.ones((rows - groups - 1, rim), jnp.float32)
    down = jnp.concatenate([source[:, :rim], neighbour_map.astype(jnp.float32), filler], axis=0)
    up = jnp.concatenate(
        [source[:, edge_count - rim :], jnp.ones((rows - groups, rim), jnp.float32)], axis=0
    )
    above, prior = pass_along(down, -1), pass_along(up, 1)
    field0, image, lower, upper, inverse, sums = call(
        functools.partial(first_stage, polars),
        (angular, source, neighbour_map, prior, above, *elements),
        [
            field_shape,
            field_shape,
            rim_shape,
            rim_shape,
            shape(rows, rim, kind=jnp.int32),
            sums_shape,
        ],
        tables,
    )
    above, prior = pass_along(lower, -1), pass_along(upper, 1)
    field1, sums, image, lower, upper = call(
        functools.partial(later_stage, polars, 1, False),
        (angular, image, neighbour_map, inverse, prior, above, sums, *elements),
        [field_shape, sums_shape, field_shape, rim_shape, rim_shape],
        tables,
    )
    above, prior = pass_along(lower, -1), pass_along(upper, 1)
    field2, sums = call(
        functools.partial(later_stage, polars, 2, True),
        (angular, image, neighbour_map, inverse, prior, above, sums, *elements),
        [field_shape, sums_shape],
    )
    term = call(
        functools.partial(gradient_stage, polars),
        (
            angular,
            gather_all(sums, "dom"),
            sums,
            field0,
            field1,
            field2,
            forward,
            mass,
            edges,
            live_slots,
        ),
        shape(1, slots),
    )
    gradient = jnp.sum(gather_all(term, "freq"), axis=0)
    updated = conductivity * jnp.exp(-0.5 * jnp.tanh(gradient))
    return gradient, updated


def solution(mesh):
    return jax.shard_map(
        local,
        mesh=mesh,
        in_specs=(
            P("freq"),
            P("dom", None, None),
            P("dom", None, None),
            P("dom", None),
            P("dom", None, None),
            P("dom", None),
            P("freq", None, "dom", None),
            P("freq", None, "dom", None),
            P("dom", None),
        ),
        out_specs=(P("dom", None), P("dom", None)),
        check_vma=False,
    )
```

profile of v0, /device:TPU:0, one launch (start us, length us, event | category | flops | bytes accessed | tf_op | source)
XLA Modules:
  0.0 59.8 jit_solution(18327923565434896085)
XLA Ops:
  0.6 0.8 %reduce.1 = f32[2,2,1280]{2,1,0:T(2,128)S(1)} reduce(f32[2,2,1,1280]{3,2,1,0:T(1,128)} %param.15, f32[]{:T(128)} %constant.18), dimensions={2}, to_apply=%param.15.reduce_sub_computation | reduce | bytes 40964 | tf_op args[6]
  1.5 0.7 %copy-done.2 = s32[1,256]{1,0:T(1,128)S(1)} copy-done((s32[1,256]{1,0:T(1,128)S(1)}, s32[1,256]{1,0:T(1,128)}, u32[]{:S(2)}) %copy-start.2) | copy-done | bytes 1048
  2.1 0.1 pad.3.clone
  2.2 0.1 maximum_maximum_fusion
  2.3 1.3 %collective-permute-start.1 = (f32[8,256]{1,0:T(8,128)S(1)}, f32[8,256]{1,0:T(8,128)S(1)}, u32[]{:S(2)}, u32[]{:S(2)}) collective-permute-start(f32[8,256]{1,0:T(8,128)S(1)} %maximum_maximum_fusion), channel_id=1, source_target_pairs={{1,0},{2,1},{3,2},{4,3},{5,4},{6,5},{7,6},{9,8},{10,9},{11,10},{12... | collective-permute-start | bytes 24584 | tf_op jit(solution)/shard_map/ppermute | solution.py:416
  3.6 3.0 %collective-permute-start = (f32[8,256]{1,0:T(8,128)S(1)}, f32[8,256]{1,0:T(8,128)S(1)}, u32[]{:S(2)}, u32[]{:S(2)}) collective-permute-start(f32[8,256]{1,0:T(8,128)S(1)} %concatenate.6), channel_id=1, source_target_pairs={{0,1},{1,2},{2,3},{3,4},{4,5},{5,6},{6,7},{8,9},{9,10},{10,11},{11... | collective-permute-start | bytes 24584 | tf_op jit(solution)/shard_map/ppermute | solution.py:416
  6.6 1.0 %copy_bitcast_fusion = (f32[36,1024]{1,0:T(8,128)S(1)}, f32[36,1024]{1,0:T(8,128)S(1)}) fusion(f32[1,36,1024]{2,0,1:T(1,128)} %param.11, f32[1,36,1024]{2,0,1:T(1,128)} %param.10), kind=kLoop, calls=%fused_computation | loop fusion | bytes 589824
  7.8 0.6 %copy-done.1 = f32[1,1024]{1,0:T(1,128)S(1)} copy-done((f32[1,1024]{1,0:T(1,128)S(1)}, f32[1,1024]{1,0:T(1,128)}, u32[]{:S(2)}) %copy-start.1) | copy-done | bytes 4120
  8.4 3.3 %shard_map.104 = (f32[8,1280]{1,0:T(8,128)S(1)}, f32[8,1280]{1,0:T(8,128)S(1)}, f32[8,256]{1,0:T(8,128)S(1)}, f32[8,256]{1,0:T(8,128)S(1)}, s32[8,256]{1,0:T(8,128)S(1)}, /*index=5*/f32[8,128]{1,0:T(8,128)S(1)}) custom-call(f32[2]{0:T(128)S(1)} %copy-done.3, f32[4,1280]{1,0:T(4,128)S(1)} %reshape.31.source, s32[1,256]{1,0:T(1,128)S(1)} %copy-done.2, ...), custom_call_target="tpu_custom_call" | custom-call | tf_op jit(solution)/shard_map/pallas_call | solution.py:403
  11.8 4.5 %collective-permute-start.2 = (f32[8,256]{1,0:T(8,128)S(1)}, f32[8,256]{1,0:T(8,128)S(1)}, u32[]{:S(2)}, u32[]{:S(2)}) collective-permute-start(f32[8,256]{1,0:T(8,128)S(1)} %get-tuple-element.17), channel_id=1, source_target_pairs={{0,1},{1,2},{2,3},{3,4},{4,5},{5,6},{6,7},{8,9},{9,10},{10,11},{11... | collective-permute-start | bytes 24584 | tf_op jit(solution)/shard_map/ppermute | solution.py:416
  16.2 1.3 %collective-permute-start.3 = (f32[8,256]{1,0:T(8,128)S(1)}, f32[8,256]{1,0:T(8,128)S(1)}, u32[]{:S(2)}, u32[]{:S(2)}) collective-permute-start(f32[8,256]{1,0:T(8,128)S(1)} %get-tuple-element.18), channel_id=1, source_target_pairs={{1,0},{2,1},{3,2},{4,3},{5,4},{6,5},{7,6},{9,8},{10,9},{11,10},{12... | collective-permute-start | bytes 24584 | tf_op jit(solution)/shard_map/ppermute | solution.py:416
  17.5 3.2 %collective-permute-done.3.above_ref = f32[8,256]{1,0:T(8,128)S(1)} collective-permute-done((f32[8,256]{1,0:T(8,128)S(1)}, f32[8,256]{1,0:T(8,128)S(1)}, u32[]{:S(2)}, u32[]{:S(2)}) %collective-permute-start.3) | collective-permute-done | bytes 8224 | tf_op jit(solution)/shard_map/ppermute | solution.py:416
  20.7 3.3 %shard_map.105 = (f32[8,1280]{1,0:T(8,128)S(1)}, f32[8,128]{1,0:T(8,128)S(1)}, f32[8,1280]{1,0:T(8,128)S(1)}, f32[8,256]{1,0:T(8,128)S(1)}, f32[8,256]{1,0:T(8,128)S(1)}) custom-call(f32[2]{0:T(128)S(1)} %copy-done.3, f32[8,1280]{1,0:T(8,128)S(1)} %get-tuple-element.15.image_in, s32[1,256]{1,0:T(1,128)S(1)} %copy-done.2, ...), custom_call_target="tpu_custom_call" | custom-call | tf_op jit(solution)/shard_map/pallas_call | solution.py:403
  24.0 4.3 %collective-permute-start.4 = (f32[8,256]{1,0:T(8,128)S(1)}, f32[8,256]{1,0:T(8,128)S(1)}, u32[]{:S(2)}, u32[]{:S(2)}) collective-permute-start(f32[8,256]{1,0:T(8,128)S(1)} %get-tuple-element.21), channel_id=1, source_target_pairs={{0,1},{1,2},{2,3},{3,4},{4,5},{5,6},{6,7},{8,9},{9,10},{10,11},{11... | collective-permute-start | bytes 24584 | tf_op jit(solution)/shard_map/ppermute | solution.py:416
  28.3 1.3 %collective-permute-start.5 = (f32[8,256]{1,0:T(8,128)S(1)}, f32[8,256]{1,0:T(8,128)S(1)}, u32[]{:S(2)}, u32[]{:S(2)}) collective-permute-start(f32[8,256]{1,0:T(8,128)S(1)} %get-tuple-element.22), channel_id=1, source_target_pairs={{1,0},{2,1},{3,2},{4,3},{5,4},{6,5},{7,6},{9,8},{10,9},{11,10},{12... | collective-permute-start | bytes 24584 | tf_op jit(solution)/shard_map/ppermute | solution.py:416
  29.6 2.2 %collective-permute-done.5.above_ref = f32[8,256]{1,0:T(8,128)S(1)} collective-permute-done((f32[8,256]{1,0:T(8,128)S(1)}, f32[8,256]{1,0:T(8,128)S(1)}, u32[]{:S(2)}, u32[]{:S(2)}) %collective-permute-start.5) | collective-permute-done | bytes 8224 | tf_op jit(solution)/shard_map/ppermute | solution.py:416
  31.9 2.0 %shard_map.106 = (f32[8,1280]{1,0:T(8,128)S(1)}, f32[8,128]{1,0:T(8,128)S(1)}) custom-call(f32[2]{0:T(128)S(1)} %copy-done.3, f32[8,1280]{1,0:T(8,128)S(1)} %get-tuple-element.20.image_in, s32[1,256]{1,0:T(1,128)S(1)} %copy-done.2, s32[8,256]{1,0:T(8,128)S(1)} %get-tuple-element.16.inverse_ref, f32[8,256]{1,0:T(8,128)S(1)} %collective-permute-done.4.prior_ref, ...), custom_call_target="tpu_custom_call" | custom-call | tf_op jit(solution)/shard_map/pallas_call | solution.py:403
  33.9 0.6 %broadcast_in_dim.9 = f32[8,8,128]{2,1,0:T(8,128)} broadcast(f32[8,128]{1,0:T(8,128)S(1)} %get-tuple-element.24.sums_in), dimensions={1,2} | broadcast | bytes 36864 | tf_op jit(solution)/shard_map/broadcast_in_dim | solution.py:421
  34.5 7.5 %all-to-all-start = ((f32[8,8,128]{2,1,0:T(8,128)}), f32[8,8,128]{2,1,0:T(8,128)S(1)}, u32[]{:S(2)}, u32[]{:S(2)}) async-start(f32[8,8,128]{2,1,0:T(8,128)} %broadcast_in_dim.9), calls=%async_computation | async-start | bytes 65536 | tf_op jit(solution)/shard_map/all_to_all | solution.py:422
  42.0 0.1 reduce.2
  42.1 4.7 %all-to-all-done.everyone = f32[8,8,128]{2,1,0:T(8,128)S(1)} async-done(((f32[8,8,128]{2,1,0:T(8,128)}), f32[8,8,128]{2,1,0:T(8,128)S(1)}, u32[]{:S(2)}, u32[]{:S(2)}) %all-to-all-start) | async-done | bytes 32800 | tf_op jit(solution)/shard_map/all_to_all | solution.py:422
  46.9 2.0 %shard_map.107 = f32[1,1024]{1,0:T(1,128)S(1)} custom-call(f32[2]{0:T(128)S(1)} %copy-done.3, f32[8,8,128]{2,1,0:T(8,128)S(1)} %all-to-all-done.everyone, f32[8,128]{1,0:T(8,128)S(1)} %get-tuple-element.24.sums_in, f32[8,1280]{1,0:T(8,128)S(1)} %get-tuple-element.25.field0, f32[8,1280]{1,0:T(8,128)S(1)} %get-tuple-element.26.field1, ...), custom_call_target="tpu_custom_call" | custom-call | tf_op jit(solution)/shard_map/pallas_call | solution.py:403
  48.9 10.3 %all_to_all.10 = f32[4,1,1024]{2,1,0:T(1,128)S(1)} all-to-all(f32[4,1,1024]{2,1,0:T(1,128)S(1)} %broadcast_in_dim.21), channel_id=1, replica_groups=mesh['freq'=4,'dom'=8] {'freq'}, dimensions={0} | all-to-all | bytes 32768 | tf_op jit(solution)/shard_map/all_to_all | solution.py:422
  59.2 0.6 %exponential_multiply_fusion = f32[1,1024]{1,0:T(1,128)} fusion(f32[1,1024]{1,0:T(1,128)S(1)} %copy-done.1, f32[1,1024]{1,0:T(1,128)S(1)} %bitcast.14), kind=kLoop, calls=%fused_computation.4 | loop fusion | flops 2048 | bytes 12288 | tf_op jit(solution)/shard_map/mul | solution.py:506
  (25 shorter events, 0.2 us)
Async XLA Ops:
  1.4 0.7 %copy-start.2 = (s32[1,256]{1,0:T(1,128)S(1)}, s32[1,256]{1,0:T(1,128)}, u32[]{:S(2)}) copy-start(s32[1,256]{1,0:T(1,128)} %order_ref.5) | copy-start | bytes 3076
  2.3 5.4 %collective-permute-start.1 = (f32[8,256]{1,0:T(8,128)S(1)}, f32[8,256]{1,0:T(8,128)S(1)}, u32[]{:S(2)}, u32[]{:S(2)}) collective-permute-start(f32[8,256]{1,0:T(8,128)S(1)} %maximum_maximum_fusion), channel_id=1, source_target_pairs={{1,0},{2,1},{3,2},{4,3},{5,4},{6,5},{7,6},{9,8},{10,9},{11,10},{12... | collective-permute-start | bytes 24584 | tf_op jit(solution)/shard_map/ppermute | solution.py:416
  3.6 4.1 %copy-start.4 = (s32[1,6,1024]{2,0,1:T(1,128)S(1)}, s32[1,6,1024]{2,0,1:T(1,128)}, u32[]{:S(2)}) copy-start(s32[1,6,1024]{2,0,1:T(1,128)} %param.13) | copy-start | bytes 73732
  3.6 4.1 %collective-permute-start = (f32[8,256]{1,0:T(8,128)S(1)}, f32[8,256]{1,0:T(8,128)S(1)}, u32[]{:S(2)}, u32[]{:S(2)}) collective-permute-start(f32[8,256]{1,0:T(8,128)S(1)} %concatenate.6), channel_id=1, source_target_pairs={{0,1},{1,2},{2,3},{3,4},{4,5},{5,6},{6,7},{8,9},{9,10},{10,11},{11... | collective-permute-start | bytes 24584 | tf_op jit(solution)/shard_map/ppermute | solution.py:416
  7.7 0.7 %copy-start.1 = (f32[1,1024]{1,0:T(1,128)S(1)}, f32[1,1024]{1,0:T(1,128)}, u32[]{:S(2)}) copy-start(f32[1,1024]{1,0:T(1,128)} %sigma.5) | copy-start | bytes 12292
  7.7 0.7 %copy-start = (s32[1,1024]{1,0:T(1,128)S(1)}, s32[1,1024]{1,0:T(1,128)}, u32[]{:S(2)}) copy-start(s32[1,1024]{1,0:T(1,128)} %live.7) | copy-start | bytes 12292
  7.8 0.7 %copy-start.3 = (f32[2]{0:T(128)S(1)}, f32[2]{0:T(128)}, u32[]{:S(2)}) copy-start(f32[2]{0:T(128)} %angular.7) | copy-start | bytes 28
  11.8 5.8 %collective-permute-start.2 = (f32[8,256]{1,0:T(8,128)S(1)}, f32[8,256]{1,0:T(8,128)S(1)}, u32[]{:S(2)}, u32[]{:S(2)}) collective-permute-start(f32[8,256]{1,0:T(8,128)S(1)} %get-tuple-element.17), channel_id=1, source_target_pairs={{0,1},{1,2},{2,3},{3,4},{4,5},{5,6},{6,7},{8,9},{9,10},{10,11},{11... | collective-permute-start | bytes 24584 | tf_op jit(solution)/shard_map/ppermute | solution.py:416
  16.2 4.5 %collective-permute-start.3 = (f32[8,256]{1,0:T(8,128)S(1)}, f32[8,256]{1,0:T(8,128)S(1)}, u32[]{:S(2)}, u32[]{:S(2)}) collective-permute-start(f32[8,256]{1,0:T(8,128)S(1)} %get-tuple-element.18), channel_id=1, source_target_pairs={{1,0},{2,1},{3,2},{4,3},{5,4},{6,5},{7,6},{9,8},{10,9},{11,10},{12... | collective-permute-start | bytes 24584 | tf_op jit(solution)/shard_map/ppermute | solution.py:416
  24.0 5.6 %collective-permute-start.4 = (f32[8,256]{1,0:T(8,128)S(1)}, f32[8,256]{1,0:T(8,128)S(1)}, u32[]{:S(2)}, u32[]{:S(2)}) collective-permute-start(f32[8,256]{1,0:T(8,128)S(1)} %get-tuple-element.21), channel_id=1, source_target_pairs={{0,1},{1,2},{2,3},{3,4},{4,5},{5,6},{6,7},{8,9},{9,10},{10,11},{11... | collective-permute-start | bytes 24584 | tf_op jit(solution)/shard_map/ppermute | solution.py:416
  28.3 3.5 %collective-permute-start.5 = (f32[8,256]{1,0:T(8,128)S(1)}, f32[8,256]{1,0:T(8,128)S(1)}, u32[]{:S(2)}, u32[]{:S(2)}) collective-permute-start(f32[8,256]{1,0:T(8,128)S(1)} %get-tuple-element.22), channel_id=1, source_target_pairs={{1,0},{2,1},{3,2},{4,3},{5,4},{6,5},{7,6},{9,8},{10,9},{11,10},{12... | collective-permute-start | bytes 24584 | tf_op jit(solution)/shard_map/ppermute | solution.py:416
  34.5 7.5 %copy-start.5 = (f32[2,2,1,1280]{3,2,1,0:T(1,128)S(1)}, f32[2,2,1,1280]{3,2,1,0:T(1,128)}, u32[]{:S(2)}) copy-start(f32[2,2,1,1280]{3,2,1,0:T(1,128)} %param.16) | copy-start | bytes 61444
  34.5 12.4 %all-to-all-start = ((f32[8,8,128]{2,1,0:T(8,128)}), f32[8,8,128]{2,1,0:T(8,128)S(1)}, u32[]{:S(2)}, u32[]{:S(2)}) async-start(f32[8,8,128]{2,1,0:T(8,128)} %broadcast_in_dim.9), calls=%async_computation | async-start | bytes 65536 | tf_op jit(solution)/shard_map/all_to_all | solution.py:422
  59.2 0.6 %copy-start.6 = (f32[1024]{0:T(1024)}, f32[1024]{0:T(1024)S(1)}, u32[]{:S(2)}) copy-start(f32[1024]{0:T(1024)S(1)} %reduce_sum.11) | copy-start | bytes 12292
where the time goes:
time: 60.4 us; the launch traced here: 59.8 us
  starting transfers between devices  23.2 us (38%)
  Pallas kernels  10.6 us (18%)
  blocking collectives  10.3 us (17%)
  waiting for transfers between devices  10.2 us (17%)
  local copies, waits for them, and re-layouts  3.14 us (5%)
  other arithmetic  1.56 us (3%)
  between operations  0.84 us (1%)
    ppermute x6, starting transfers between devices, pass_along(): return lax.ppermute(block, 'dom', route)  15.7 us
    pallas_call x4, Pallas kernels, call(): pl.pallas_call(kernel, out_shape=outs, in_specs=specs, out_specs=jax.tree...  10.6 us
    all_to_all x1, blocking collectives, gather_all(): return lax.all_to_all(copies, axis, 0, 0)  10.3 us
    all_to_all x1, starting transfers between devices, gather_all(): return lax.all_to_all(copies, axis, 0, 0)  7.54 us
    ppermute x6, waiting for transfers between devices, pass_along(): return lax.ppermute(block, 'dom', route)  5.43 us
    all_to_all x1, waiting for transfers between devices, gather_all(): return lax.all_to_all(copies, axis, 0, 0)  4.75 us
    unnamed x16, local copies, waits for them, and re-layouts  2.39 us
  transfers between devices with their start and end apart: 7, of which 3 were waited for; matrix products, arithmetic and copies ran while one was open for 2% of the time, Pallas kernels for 0%

commit v1 on v0

v1 whole, which is shorter than its diff:
```python
import functools

import jax
import jax.numpy as jnp
from jax import lax
from jax.experimental import pallas as pl
from jax.experimental.pallas import tpu as pltpu
from jax.sharding import PartitionSpec as P

LANES = 128
SUBLANES = 8
SIDE = 6
VMEM = pl.BlockSpec(memory_space=pltpu.VMEM)
SMEM = pl.BlockSpec(memory_space=pltpu.SMEM)

PICK_LANES = lax.GatherDimensionNumbers(
    offset_dims=(),
    collapsed_slice_dims=(1,),
    start_index_map=(1,),
    operand_batching_dims=(0,),
    start_indices_batching_dims=(0,),
)


def pick_lanes(block, lanes):
    return lax.gather(
        block,
        lanes[..., None],
        PICK_LANES,
        (1, 1),
        mode=lax.GatherScatterMode.PROMISE_IN_BOUNDS,
    )


def pick_wide(chunks, index):
    lanes = index & (LANES - 1)
    high = index >> 7
    level = [pick_lanes(chunk, lanes) for chunk in chunks]
    bit = 0
    while len(level) > 1:
        odd = (high >> bit) & 1 == 1
        level = [
            jnp.where(odd, level[t + 1], level[t]) if t + 1 < len(level) else level[t]
            for t in range(0, len(level), 2)
        ]
        bit += 1
    return level[0]


def row_ids(rows):
    return lax.broadcasted_iota(jnp.int32, (rows, LANES), 0)


def lane_ids(rows):
    return lax.broadcasted_iota(jnp.int32, (rows, LANES), 1)


def spread(row, rows):
    return jnp.broadcast_to(row, (rows, row.shape[-1]))


def cut(ref):
    return [ref[:, c : c + LANES] for c in range(0, ref.shape[-1], LANES)]


def swap_halves(block):
    return pltpu.roll(block, block.shape[0] // 2, 0)


def doubled(block):
    half = block.shape[0] // 2
    return jnp.where(row_ids(2 * half) < half, block, swap_halves(block))


def lane_sum(block):
    return jnp.broadcast_to(jnp.sum(block, axis=1, keepdims=True), block.shape)


def put_lane(block, lane, value):
    return jnp.where(lane_ids(block.shape[0]) == lane, value, block)


def put_chunks(ref, chunks):
    for c, chunk in enumerate(chunks):
        ref[:, c * LANES : (c + 1) * LANES] = chunk


def is_even():
    return lax.rem(lax.axis_index("dom"), 2) == 0


def put_rims(across_ref, beside_ref, lower, upper):
    even = is_even()
    for c, (low, high) in enumerate(zip(lower, upper)):
        here = slice(c * LANES, (c + 1) * LANES)
        across_ref[:, here] = jnp.where(even, low, high)
        beside_ref[:, here] = jnp.where(even, high, low)


def take_rims(across_ref, beside_ref):
    even = is_even()
    pairs = list(zip(cut(across_ref), cut(beside_ref)))
    prior = [jnp.where(even, a, b) for a, b in pairs]
    above = [jnp.where(even, b, a) for a, b in pairs]
    return prior, above


def picks_of(rows_of_group, edges):
    chunks = [spread(row, edges.shape[1]) for row in rows_of_group]
    return [pick_wide(chunks, edges[j]) for j in range(SIDE)]


def group_rows(ref, g):
    return [ref[g : g + 1, c : c + LANES] for c in range(0, ref.shape[-1], LANES)]


def times_block(entries, base, picked):
    out = []
    for i in range(SIDE):
        total = None
        for j in range(SIDE):
            one = entries[base + SIDE * i + j] * picked[j]
            total = one if total is None else total + one
        out.append(total)
    return out


def weighted_sum(left, right):
    total = None
    for a, b in zip(left, right):
        total = a * b if total is None else total + a * b
    return total


def scatter(pieces, edges, places, count):
    depth = SIDE * edges.shape[1]
    rows = pieces.shape[0] // depth
    slots = edges.shape[1] * LANES
    total = None
    for i in range(SIDE):
        columns = []
        for s in range(edges.shape[1]):
            both = pieces[pl.ds(i * edges.shape[1] + s, rows, stride=depth), :]
            high = spread(edges[i, s : s + 1, :] >> 7, rows)
            stacked = [jnp.where(high == h, both, 0.0) for h in range(count)]
            columns.append(jnp.concatenate(stacked, axis=0).astype(jnp.bfloat16))
        part = lax.dot_general(
            jnp.concatenate(columns, axis=1),
            places[:, i * slots : (i + 1) * slots],
            (((1,), (1,)), ((), ())),
            preferred_element_type=jnp.float32,
        )
        total = part if total is None else total + part
    out = []
    for h in range(count):
        piece = total[rows * h : rows * (h + 1)]
        out.append(piece + swap_halves(piece))
    return out


def joined(own, from_prior, from_above, order, inverse):
    rim = len(from_prior)
    lower = [own[c] + pick_wide(from_prior, order[c]) for c in range(rim)]
    upper = [own[len(own) - rim + c] + pick_wide(from_above, inverse[c]) for c in range(rim)]
    return lower + own[rim : len(own) - rim] + upper


def squares(chunks, rim, has_prior):
    total = None
    for c, chunk in enumerate(chunks):
        term = chunk * chunk
        if c < rim:
            term = term * (1.0 - has_prior)
        total = term if total is None else total + term
    return total


def rims_stage(source, order_ref, across_ref, beside_ref, stacked_ref):
    groups = source.shape[0]
    rows = stacked_ref.shape[0]
    first = row_ids(rows) < groups
    chunks = []
    for c in range(0, source.shape[-1], LANES):
        piece = [source[g, :, c : c + LANES] for g in range(groups)]
        chunks.append(jnp.concatenate(piece + piece, axis=0))
    put_chunks(stacked_ref, chunks)
    order = [spread(piece.astype(jnp.float32), rows) for piece in cut(order_ref)]
    count = len(order)
    lower = [jnp.where(first, x, o) for x, o in zip(chunks[:count], order)]
    upper = [jnp.where(first, x, 1.0) for x in chunks[len(chunks) - count :]]
    put_rims(across_ref, beside_ref, lower, upper)


def table_stage(
    angular, stiffness, mass, sigma, live, edges, places_ref, blocks_ref, scale_ref
):
    rows = edges.shape[1]
    alive = live[...].astype(jnp.float32)
    weight = sigma[...]
    freqs = angular.shape[0]
    peak = None
    for i in range(SIDE):
        for f in range(freqs):
            entry = (SIDE + 1) * i
            size = stiffness[entry] + angular[f] * weight * mass[entry]
            peak = size if peak is None else jnp.maximum(peak, size)
    peak = jnp.max(peak * alive, axis=1, keepdims=True)
    scale = jnp.broadcast_to(jnp.max(peak, axis=0, keepdims=True), scale_ref.shape)
    scale_ref[...] = scale
    alive = alive / scale[:1, :1]
    for entry in range(SIDE * SIDE):
        stiff = stiffness[entry] * alive
        heavy = mass[entry] * (weight * alive)
        for f in range(freqs):
            blocks_ref[f * SIDE * SIDE + entry] = stiff + angular[f] * heavy
    numbers = row_ids(LANES)

    def body(i, carry):
        for s in range(rows):
            lanes = spread(edges[i, s : s + 1, :] & (LANES - 1), LANES)
            column = pl.ds(pl.multiple_of((i * rows + s) * LANES, LANES), LANES)
            places_ref[:, column] = jnp.where(lanes == numbers, 1.0, 0.0).astype(jnp.bfloat16)
        return carry

    lax.fori_loop(0, SIDE, body, 0)


def apply_all(field_ref, blocks, edges, polars, groups, pieces, visit):
    rows = field_ref.shape[0]
    depth = SIDE * edges.shape[1]
    forms = jnp.zeros((rows, LANES), jnp.float32)
    for g in range(groups):
        picked = picks_of(group_rows(field_ref, g), edges)
        visit(g, picked)
        values = times_block(blocks, (g // polars) * SIDE * SIDE, picked)
        form = jnp.sum(weighted_sum(picked, values), axis=0, keepdims=True)
        forms = jnp.where(row_ids(rows) == g, spread(form, rows), forms)
        if pieces is None:
            continue
        for i, value in enumerate(values):
            coarse = value.astype(jnp.bfloat16).astype(jnp.float32)
            for part, piece in enumerate((coarse, value - coarse)):
                at = (part * groups + g) * depth + i * edges.shape[1]
                pieces[at : at + edges.shape[1], :] = piece
    return lane_sum(forms)


def first_stage(
    polars,
    source,
    order_ref,
    across_in,
    beside_in,
    scale_in,
    blocks,
    edges,
    places,
    picks_ref,
    image_ref,
    across_ref,
    beside_ref,
    inverse_ref,
    sums_ref,
    field_ref,
    pieces,
):
    rows = source.shape[0]
    groups = rows // 2
    first = row_ids(rows) < groups
    scale = scale_in[...]
    prior, above = take_rims(across_in, beside_in)

    rim = order_ref.shape[-1]
    order = [spread(piece, rows) for piece in cut(order_ref)]
    above_order = spread(
        jnp.concatenate([x[groups : groups + 1] for x in above], axis=1), rim
    )
    slot = lax.broadcasted_iota(jnp.int32, (rim, rim), 0).astype(jnp.float32)
    match = jnp.where(above_order == slot, 1.0, 0.0).astype(jnp.bfloat16)
    numbers = lax.broadcasted_iota(jnp.int32, (2 * rows, rim), 1).astype(jnp.bfloat16)
    inverse = lax.dot_general(
        numbers, match, (((1,), (1,)), ((), ())), preferred_element_type=jnp.float32
    )[:rows].astype(jnp.int32)
    inverse_ref[...] = inverse
    inverse = [inverse[:, c : c + LANES] for c in range(0, rim, LANES)]

    has_prior = spread(prior[0][groups : groups + 1], rows)
    field = joined(
        cut(source), [doubled(x) for x in prior], [doubled(x) for x in above], order, inverse
    )
    put_chunks(field_ref, field)

    def visit(g, picked):
        for j in range(SIDE):
            picks_ref[g * SIDE + j] = picked[j]

    forms = apply_all(field_ref, blocks, edges, polars, groups, pieces, visit)
    image = scatter(pieces, edges, places, len(field))
    put_chunks(image_ref, image)
    count = rim // LANES
    put_rims(
        across_ref,
        beside_ref,
        [jnp.where(first, x, scale) for x in image[:count]],
        [jnp.where(first, x, scale) for x in image[len(image) - count :]],
    )
    sums = jnp.zeros((rows, LANES), jnp.float32)
    sums = put_lane(sums, 0, lane_sum(squares(field, count, has_prior)))
    sums = put_lane(sums, 1, forms)
    sums_ref[...] = jnp.where(first, sums, scale)


def later_stage(
    polars,
    step,
    last,
    image_in,
    order_ref,
    inverse_ref,
    across_in,
    beside_in,
    sums_in,
    blocks,
    edges,
    heavy,
    *rest,
):
    if last:
        terms_ref, sums_ref, field_ref = rest
        pieces = None
    else:
        places, terms_ref, sums_ref, image_ref, across_ref, beside_ref, field_ref, pieces = rest
    rows = image_in.shape[0]
    groups = rows // 2
    first = row_ids(rows) < groups
    sums = sums_in[...]
    scale = jnp.where(first, swap_halves(sums), sums)
    inverse_scale = 1.0 / scale
    rim = order_ref.shape[-1]
    count = rim // LANES
    order = [spread(piece, rows) for piece in cut(order_ref)]
    inverse = cut(inverse_ref)

    def rescaled(block):
        ratio = swap_halves(block) * inverse_scale
        for _ in range(step):
            block = block * ratio
        return doubled(block)

    prior, above = take_rims(across_in, beside_in)
    has_prior = jnp.where(first, swap_halves(prior[0]), prior[0])
    has_prior = jnp.where(has_prior > 0.0, 1.0, 0.0)
    field = joined(
        cut(image_in),
        [rescaled(x) for x in prior],
        [rescaled(x) for x in above],
        order,
        inverse,
    )
    put_chunks(field_ref, field)

    def visit(g, picked):
        terms_ref[g] = weighted_sum(picked, [heavy[g * SIDE + i] for i in range(SIDE)])

    forms = apply_all(field_ref, blocks, edges, polars, groups, pieces, visit)
    fresh = put_lane(sums, 2 * step, lane_sum(squares(field, count, has_prior)))
    fresh = put_lane(fresh, 2 * step + 1, forms)
    sums_ref[...] = jnp.where(first, fresh, scale)
    if not last:
        image = scatter(pieces, edges, places, len(field))
        put_chunks(image_ref, image)
        put_rims(
            across_ref,
            beside_ref,
            [jnp.where(first, x, scale) for x in image[:count]],
            [jnp.where(first, x, scale) for x in image[len(image) - count :]],
        )


def forward_stage(polars, angular, forward, mass, live, edges, picks, heavy_ref, terms_ref):
    dead = -live[...].astype(jnp.float32)
    for g in range(forward.shape[0]):
        rows = [forward[g, :, c : c + LANES] for c in range(0, forward.shape[-1], LANES)]
        values = times_block(mass, 0, picks_of(rows, edges))
        factor = dead * angular[g // polars]
        values = [factor * value for value in values]
        for i in range(SIDE):
            heavy_ref[g * SIDE + i] = values[i]
        terms_ref[g] = weighted_sum(values, [picks[g * SIDE + i] for i in range(SIDE)])


def combine_stage(everyone, sums_in, terms0, terms1, terms2, out_ref):
    rows = sums_in.shape[0]
    groups = rows // 2
    first = row_ids(rows) < groups

    def scale_of(block):
        return jnp.where(first, swap_halves(block), block)

    parts = [everyone[q] for q in range(everyone.shape[0])]
    scales = [scale_of(block) for block in parts]
    top = functools.reduce(jnp.maximum, scales)
    lanes = lane_ids(rows)
    inverse_top = 1.0 / top
    total = None
    for block, scale in zip(parts, scales):
        ratio = scale * inverse_top
        power = jnp.ones_like(ratio)
        factor = jnp.ones_like(ratio)
        for k in range(1, 6):
            power = power * ratio
            factor = jnp.where(lanes == k, power, factor)
        term = block * factor
        total = term if total is None else total + term
    m = [jnp.broadcast_to(total[:, k : k + 1], (rows, LANES)) for k in range(6)]
    l1 = m[2] / m[1]
    l2 = m[3] / m[1]
    d2 = m[3] - l1 * m[2]
    cross = m[4] - l2 * m[2]
    l3 = cross / d2
    d3 = m[5] - l2 * m[3] - l3 * cross
    y1 = m[1] - l1 * m[0]
    y2 = m[2] - l2 * m[0] - l3 * y1
    c2 = y2 / d3
    c1 = y1 / d2 - l3 * c2
    c0 = m[0] / m[1] - l1 * c1 - l2 * c2
    mine = scale_of(sums_in[...]) * inverse_top
    c0 = c0 * inverse_top
    c1 = c1 * mine * inverse_top
    c2 = c2 * mine * mine * inverse_top
    out = None
    for terms, c in ((terms0, c0), (terms1, c1), (terms2, c2)):
        for g in range(groups):
            one = terms[g] * spread(c[g : g + 1], out_ref.shape[0])
            out = one if out is None else out + one
    out_ref[...] = out


def call(kernel, arguments, outs, scratch=(), scalars=0, cost=0):
    return pl.pallas_call(
        kernel,
        out_shape=outs,
        in_specs=[SMEM] * scalars + [VMEM] * (len(arguments) - scalars),
        out_specs=jax.tree.map(lambda _: VMEM, outs),
        scratch_shapes=list(scratch),
        cost_estimate=pl.CostEstimate(flops=cost, bytes_accessed=cost, transcendentals=0),
        compiler_params=pltpu.CompilerParams(vmem_limit_bytes=16 * 1024 * 1024),
    )(*arguments)


def swap(block, axis, offset):
    size = lax.axis_size(axis)
    route = []
    for low in range(offset, size - 1, 2):
        route += [(low, low + 1), (low + 1, low)]
    return lax.ppermute(block, axis, route)


def gather_all(block, axis):
    size = lax.axis_size(axis)
    copies = jnp.broadcast_to(block[None], (size, *block.shape))
    return lax.all_to_all(copies, axis, 0, 0)


def sum_over(block, axis):
    size = lax.axis_size(axis)
    if size & (size - 1):
        return jnp.sum(gather_all(block, axis), axis=0)
    step = 1
    while step < size:
        block = block + lax.ppermute(block, axis, [(i, i ^ step) for i in range(size)])
        step *= 2
    return block


def local(
    angular,
    stiffness,
    mass_matrix,
    conductivity,
    element_edges,
    live_slots,
    adjoint_source,
    forward_field,
    neighbour_map,
):
    freqs = angular.shape[0]
    polars = adjoint_source.shape[1]
    groups = freqs * polars
    rows = 2 * groups
    edge_count = adjoint_source.shape[-1]
    rim = neighbour_map.shape[-1]
    slots = element_edges.shape[-1]
    tall = slots // LANES
    stiff = stiffness.reshape(SIDE * SIDE, tall, LANES)
    mass = mass_matrix.reshape(SIDE * SIDE, tall, LANES)
    edges = element_edges.reshape(SIDE, tall, LANES)
    sigma = conductivity.reshape(tall, LANES)
    live = live_slots.reshape(tall, LANES)
    source = adjoint_source.reshape(groups, 1, edge_count)
    forward = forward_field.reshape(groups, 1, edge_count)

    def shape(*dims, kind=jnp.float32):
        return jax.ShapeDtypeStruct(dims, kind)

    field_shape, rim_shape = shape(rows, edge_count), shape(rows, rim)
    sums_shape, terms_shape = shape(rows, LANES), shape(groups, tall, LANES)
    picks_shape = shape(groups * SIDE, tall, LANES)
    field_room = pltpu.VMEM((rows, edge_count), jnp.float32)
    piece_room = pltpu.VMEM((rows * SIDE * tall, LANES), jnp.float32)

    across, beside, source = call(
        rims_stage, (source, neighbour_map), [rim_shape, rim_shape, field_shape]
    )
    across, beside = swap(across, "dom", 1), swap(beside, "dom", 0)
    places, blocks, scale = call(
        table_stage,
        (angular, stiff, mass, sigma, live, edges),
        [
            shape(LANES, SIDE * slots, kind=jnp.bfloat16),
            shape(freqs * SIDE * SIDE, tall, LANES),
            sums_shape,
        ],
        scalars=1,
        cost=4_000_000,
    )
    picks, image, across, beside, inverse, sums = call(
        functools.partial(first_stage, polars),
        (source, neighbour_map, across, beside, scale, blocks, edges, places),
        [
            picks_shape,
            field_shape,
            rim_shape,
            rim_shape,
            shape(rows, rim, kind=jnp.int32),
            sums_shape,
        ],
        (field_room, piece_room),
    )
    across, beside = swap(across, "dom", 1), swap(beside, "dom", 0)
    heavy, terms0 = call(
        functools.partial(forward_stage, polars),
        (angular, forward, mass, live, edges, picks),
        [picks_shape, terms_shape],
        scalars=1,
        cost=4_000_000,
    )
    terms1, sums, image, across, beside = call(
        functools.partial(later_stage, polars, 1, False),
        (image, neighbour_map, inverse, across, beside, sums, blocks, edges, heavy, places),
        [terms_shape, sums_shape, field_shape, rim_shape, rim_shape],
        (field_room, piece_room),
    )
    across, beside = swap(across, "dom", 1), swap(beside, "dom", 0)
    terms2, sums = call(
        functools.partial(later_stage, polars, 2, True),
        (image, neighbour_map, inverse, across, beside, sums, blocks, edges, heavy),
        [terms_shape, sums_shape],
        (field_room,),
    )
    term = call(
        combine_stage,
        (gather_all(sums, "dom"), sums, terms0, terms1, terms2),
        shape(tall, LANES),
    )
    gradient = sum_over(term, "freq").reshape(1, slots)
    updated = conductivity * jnp.exp(-0.5 * jnp.tanh(gradient))
    return gradient, updated


def solution(mesh):
    return jax.shard_map(
        local,
        mesh=mesh,
        in_specs=(
            P("freq"),
            P("dom", None, None),
            P("dom", None, None),
            P("dom", None),
            P("dom", None, None),
            P("dom", None),
            P("freq", None, "dom", None),
            P("freq", None, "dom", None),
            P("dom", None),
        ),
        out_specs=(P("dom", None), P("dom", None)),
        check_vma=False,
    )
```

time: 60.4 us -> 45.3 us (0.75)
  starting transfers between devices: 23.2 us -> 16.8 us
  waiting for transfers between devices: 10.2 us -> 4.78 us
  Pallas kernels: 10.6 us -> 5.31 us
  local copies, waits for them, and re-layouts: 3.14 us -> 6.7 us
  other arithmetic: 1.56 us -> 0.62 us
    all_to_all x1 -> x0, starting transfers between devices: 7.54 us -> none  [gather_all(): return lax.all_to_all(copies, axis, 0, 0)]
    pallas_call x4 -> x7, Pallas kernels: 10.6 us -> 5.31 us  [call(): pl.pallas_call(kernel, out_shape=outs, in_specs=[SMEM] * scalars + [VMEM]...]
    all_to_all x1 -> x0, waiting for transfers between devices: 4.75 us -> none  [gather_all(): return lax.all_to_all(copies, axis, 0, 0)]
    unnamed x16 -> x30, local copies, waits for them, and re-layouts: 2.39 us -> 6.69 us
    ppermute x6 -> x8, starting transfers between devices: 15.7 us -> 16.8 us  [the longest x6 12.6 us: swap(): return lax.ppermute(block, axis, route)]
    unnamed x2 -> x0, other arithmetic: 0.85 us -> none
    ppermute x6 -> x8, waiting for transfers between devices: 5.43 us -> 4.78 us  [the longest x2 3.94 us: sum_over(): lax.ppermute(block, axis, [(i, i ^ step) for i in range(size)])]
    broadcast_in_dim x2 -> x1, local copies, waits for them, and re-layouts: 0.62 us -> 0.01 us  [gather_all(): copies = jnp.broadcast_to(block[None], (size, *block.shape))]
  transfers between devices with their start and end apart: 7 -> 8, of which waited for: 3 -> 3; matrix products, arithmetic and copies ran while one was open for 2% -> 0% of each run, Pallas kernels for 0% -> 5%
where the time goes in v1:
time: 45.3 us; the launch traced here: 44.8 us
  starting transfers between devices  16.8 us (37%)
  blocking collectives  9.78 us (22%)
  local copies, waits for them, and re-layouts  6.7 us (15%)
  Pallas kernels  5.31 us (12%)
  waiting for transfers between devices  4.78 us (11%)
  between operations  0.78 us (2%)
  other arithmetic  0.62 us (1%)
    ppermute x6, starting transfers between devices, swap(): return lax.ppermute(block, axis, route)  12.6 us
    all_to_all x1, blocking collectives, gather_all(): return lax.all_to_all(copies, axis, 0, 0)  9.78 us
    unnamed x30, local copies, waits for them, and re-layouts  6.69 us
    pallas_call x7, Pallas kernels, call(): pl.pallas_call(kernel, out_shape=outs, in_specs=[SMEM] * scalars + [VMEM]...  5.31 us
    ppermute x2, starting transfers between devices, sum_over(): lax.ppermute(block, axis, [(i, i ^ step) for i in range(size)])  4.23 us
    ppermute x2, waiting for transfers between devices, sum_over(): lax.ppermute(block, axis, [(i, i ^ step) for i in range(size)])  3.94 us
  transfers between devices with their start and end apart: 8, of which 3 were waited for; matrix products, arithmetic and copies ran while one was open for 0% of the time, Pallas kernels for 5%

profile of v1, /device:TPU:0, one launch (start us, length us, event | category | flops | bytes accessed | tf_op | source)
XLA Modules:
  0.0 44.8 jit_solution(9731790127995769904)
XLA Ops:
  0.7 0.7 %copy-done.6 = f32[2,2,1,1280]{3,2,1,0:T(1,128)S(1)} copy-done((f32[2,2,1,1280]{3,2,1,0:T(1,128)S(1)}, f32[2,2,1,1280]{3,2,1,0:T(1,128)}, u32[]{:S(2)}) %copy-start.6) | copy-done | bytes 20504
  1.4 0.7 %copy-done.7 = s32[1,256]{1,0:T(1,128)S(1)} copy-done((s32[1,256]{1,0:T(1,128)S(1)}, s32[1,256]{1,0:T(1,128)}, u32[]{:S(2)}) %copy-start.7) | copy-done | bytes 1048
  2.1 0.7 %collective-permute-start = (f32[8,256]{1,0:T(8,128)S(1)}, f32[8,256]{1,0:T(8,128)S(1)}, u32[]{:S(2)}, u32[]{:S(2)}) collective-permute-start(f32[8,256]{1,0:T(8,128)S(1)} %get-tuple-element.24), channel_id=1, source_target_pairs={{1,2},{2,1},{3,4},{4,3},{5,6},{6,5},{9,10},{10,9},{11,12},{12,11},... | collective-permute-start | bytes 24584 | tf_op jit(solution)/shard_map/ppermute | solution.py:456
  2.8 4.4 %collective-permute-start.1 = (f32[8,256]{1,0:T(8,128)S(1)}, f32[8,256]{1,0:T(8,128)S(1)}, u32[]{:S(2)}, u32[]{:S(2)}) collective-permute-start(f32[8,256]{1,0:T(8,128)S(1)} %get-tuple-element.25), channel_id=1, source_target_pairs={{0,1},{1,0},{2,3},{3,2},{4,5},{5,4},{6,7},{7,6},{8,9},{9,8},{10,11... | collective-permute-start | bytes 24584 | tf_op jit(solution)/shard_map/ppermute | solution.py:456
  7.1 0.7 %copy-done = s32[1,6,1024]{2,0,1:T(1,128)S(1)} copy-done((s32[1,6,1024]{2,0,1:T(1,128)S(1)}, s32[1,6,1024]{2,0,1:T(1,128)}, u32[]{:S(2)}) %copy-start) | copy-done | bytes 24600
  7.9 0.9 %copy-done.2 = f32[1,36,1024]{2,0,1:T(1,128)S(1)} copy-done((f32[1,36,1024]{2,0,1:T(1,128)S(1)}, f32[1,36,1024]{2,0,1:T(1,128)}, u32[]{:S(2)}) %copy-start.2) | copy-done | bytes 147480
  8.8 0.9 %copy-done.4 = f32[1,36,1024]{2,0,1:T(1,128)S(1)} copy-done((f32[1,36,1024]{2,0,1:T(1,128)S(1)}, f32[1,36,1024]{2,0,1:T(1,128)}, u32[]{:S(2)}) %copy-start.4) | copy-done | bytes 147480
  9.7 0.7 %copy-done.9 = s32[1,1024]{1,0:T(1,128)S(1)} copy-done((s32[1,1024]{1,0:T(1,128)S(1)}, s32[1,1024]{1,0:T(1,128)}, u32[]{:S(2)}) %copy-start.9) | copy-done | bytes 4120
  10.4 0.7 %copy-done.11 = f32[1,1024]{1,0:T(1,128)S(1)} copy-done((f32[1,1024]{1,0:T(1,128)S(1)}, f32[1,1024]{1,0:T(1,128)}, u32[]{:S(2)}) %copy-start.11) | copy-done | bytes 4120
  11.7 1.2 %shard_map.105 = (bf16[128,6144]{1,0:T(8,128)(2,1)S(1)}, f32[72,8,128]{2,1,0:T(8,128)S(1)}, f32[8,128]{1,0:T(8,128)S(1)}) custom-call(f32[2]{0:T(128)S(1)} %copy-done.13, f32[36,8,128]{2,1,0:T(8,128)S(1)} %bitcast.15, f32[36,8,128]{2,1,0:T(8,128)S(1)} %bitcast.13, f32[8,128]{1,0:T(8,128)S(1)} %bitcast.20, s32[8,128]{1,0:T(8,128)S(1)} %bitcast.18, ...), custom_call_target="tpu_custom_call" | custom-call | flops 4000000 | bytes 4000000 | tf_op jit(solution)/shard_map/pallas_call | solution.py:440
  13.0 0.7 %copy-done.8 = s32[1,256]{1,0:T(1,128)S(1)} copy-done((s32[1,256]{1,0:T(1,128)S(1)}, s32[1,256]{1,0:T(1,128)}, u32[]{:S(2)}) %copy-start.8) | copy-done | bytes 1048
  13.7 1.2 %shard_map.106 = (f32[24,8,128]{2,1,0:T(8,128)S(1)}, f32[8,1280]{1,0:T(8,128)S(1)}, f32[8,256]{1,0:T(8,128)S(1)}, f32[8,256]{1,0:T(8,128)S(1)}, s32[8,256]{1,0:T(8,128)S(1)}, /*index=5*/f32[8,128]{1,0:T(8,128)S(1)}) custom-call(f32[8,1280]{1,0:T(8,128)S(1)} %get-tuple-element.23.source, s32[1,256]{1,0:T(1,128)S(1)} %copy-done.8, ...), custom_call_target="tpu_custom_call" | custom-call | tf_op jit(solution)/shard_map/pallas_call | solution.py:440
  14.9 0.7 %collective-permute-start.2 = (f32[8,256]{1,0:T(8,128)S(1)}, f32[8,256]{1,0:T(8,128)S(1)}, u32[]{:S(2)}, u32[]{:S(2)}) collective-permute-start(f32[8,256]{1,0:T(8,128)S(1)} %get-tuple-element.31), channel_id=1, source_target_pairs={{1,2},{2,1},{3,4},{4,3},{5,6},{6,5},{9,10},{10,9},{11,12},{12,11},... | collective-permute-start | bytes 24584 | tf_op jit(solution)/shard_map/ppermute | solution.py:456
  15.6 2.9 %collective-permute-start.3 = (f32[8,256]{1,0:T(8,128)S(1)}, f32[8,256]{1,0:T(8,128)S(1)}, u32[]{:S(2)}, u32[]{:S(2)}) collective-permute-start(f32[8,256]{1,0:T(8,128)S(1)} %get-tuple-element.32), channel_id=1, source_target_pairs={{0,1},{1,0},{2,3},{3,2},{4,5},{5,4},{6,7},{7,6},{8,9},{9,8},{10,11... | collective-permute-start | bytes 24584 | tf_op jit(solution)/shard_map/ppermute | solution.py:456
  18.5 0.9 %shard_map.107 = (f32[24,8,128]{2,1,0:T(8,128)S(1)}, f32[4,8,128]{2,1,0:T(8,128)S(1)}) custom-call(f32[2]{0:T(128)S(1)} %copy-done.13, f32[4,1,1280]{2,1,0:T(1,128)S(1)} %bitcast.16, f32[36,8,128]{2,1,0:T(8,128)S(1)} %bitcast.14, s32[8,128]{1,0:T(8,128)S(1)} %bitcast.19, s32[6,8,128]{2,1,0:T(8,128)S(1)} %bitcast.10, f32[24,8,128]{2,1,0:T(8,128)S(1)} %get-tuple-element.34.picks), custom_call_target="tpu_custom_call" | custom-call | flops 4000000 | bytes 4000000 | tf_op jit(solution)/shard_map/pallas_call | solution.py:440
  19.5 1.2 %shard_map.108 = (f32[4,8,128]{2,1,0:T(8,128)S(1)}, f32[8,128]{1,0:T(8,128)S(1)}, f32[8,1280]{1,0:T(8,128)S(1)}, f32[8,256]{1,0:T(8,128)S(1)}, f32[8,256]{1,0:T(8,128)S(1)}) custom-call(f32[8,1280]{1,0:T(8,128)S(1)} %get-tuple-element.29.image_in, s32[1,256]{1,0:T(1,128)S(1)} %copy-done.8, s32[8,256]{1,0:T(8,128)S(1)} %get-tuple-element.30.inverse_ref, ...), custom_call_target="tpu_custom_call" | custom-call | tf_op jit(solution)/shard_map/pallas_call | solution.py:440
  20.7 0.7 %collective-permute-start.4 = (f32[8,256]{1,0:T(8,128)S(1)}, f32[8,256]{1,0:T(8,128)S(1)}, u32[]{:S(2)}, u32[]{:S(2)}) collective-permute-start(f32[8,256]{1,0:T(8,128)S(1)} %get-tuple-element.37), channel_id=1, source_target_pairs={{1,2},{2,1},{3,4},{4,3},{5,6},{6,5},{9,10},{10,9},{11,12},{12,11},... | collective-permute-start | bytes 24584 | tf_op jit(solution)/shard_map/ppermute | solution.py:456
  21.3 3.3 %collective-permute-start.5 = (f32[8,256]{1,0:T(8,128)S(1)}, f32[8,256]{1,0:T(8,128)S(1)}, u32[]{:S(2)}, u32[]{:S(2)}) collective-permute-start(f32[8,256]{1,0:T(8,128)S(1)} %get-tuple-element.38), channel_id=1, source_target_pairs={{0,1},{1,0},{2,3},{3,2},{4,5},{5,4},{6,7},{7,6},{8,9},{9,8},{10,11... | collective-permute-start | bytes 24584 | tf_op jit(solution)/shard_map/ppermute | solution.py:456
  24.7 0.8 %collective-permute-done.5.beside_in = f32[8,256]{1,0:T(8,128)S(1)} collective-permute-done((f32[8,256]{1,0:T(8,128)S(1)}, f32[8,256]{1,0:T(8,128)S(1)}, u32[]{:S(2)}, u32[]{:S(2)}) %collective-permute-start.5) | collective-permute-done | bytes 8224 | tf_op jit(solution)/shard_map/ppermute | solution.py:456
  26.0 9.8 %all_to_all.5.everyone = f32[8,8,128]{2,1,0:T(8,128)S(1)} all-to-all(f32[8,8,128]{2,1,0:T(8,128)S(1)} %broadcast_in_dim.2), channel_id=1, replica_groups=mesh['freq'=4,'dom'=8] {'dom'}, dimensions={0} | all-to-all | bytes 65536 | tf_op jit(solution)/shard_map/all_to_all | solution.py:462
  36.0 1.6 %collective-permute-start.6 = (f32[8,128]{1,0:T(8,128)S(1)}, f32[8,128]{1,0:T(8,128)S(1)}, u32[]{:S(2)}, u32[]{:S(2)}) collective-permute-start(f32[8,128]{1,0:T(8,128)S(1)} %shard_map.110), channel_id=1, source_target_pairs={{0,8},{8,0},{16,24},{24,16},{1,9},{9,1},{17,25},{25,17},{2,10},{10... | collective-permute-start | bytes 12296 | tf_op jit(solution)/shard_map/ppermute | solution.py:471
  37.6 2.0 %collective-permute-done.6 = f32[8,128]{1,0:T(8,128)S(1)} collective-permute-done((f32[8,128]{1,0:T(8,128)S(1)}, f32[8,128]{1,0:T(8,128)S(1)}, u32[]{:S(2)}, u32[]{:S(2)}) %collective-permute-start.6) | collective-permute-done | bytes 4128 | tf_op jit(solution)/shard_map/ppermute | solution.py:471
  39.6 2.6 %collective-permute-start.7 = (f32[8,128]{1,0:T(8,128)S(1)}, f32[8,128]{1,0:T(8,128)S(1)}, u32[]{:S(2)}, u32[]{:S(2)}) collective-permute-start(f32[8,128]{1,0:T(8,128)S(1)} %add.6), channel_id=1, source_target_pairs={{0,16},{8,24},{16,0},{24,8},{1,17},{9,25},{17,1},{25,9},{2,18},{10... | collective-permute-start | bytes 12296 | tf_op jit(solution)/shard_map/ppermute | solution.py:471
  42.2 1.9 %collective-permute-done.7 = f32[8,128]{1,0:T(8,128)S(1)} collective-permute-done((f32[8,128]{1,0:T(8,128)S(1)}, f32[8,128]{1,0:T(8,128)S(1)}, u32[]{:S(2)}, u32[]{:S(2)}) %collective-permute-start.7) | collective-permute-done | bytes 4128 | tf_op jit(solution)/shard_map/ppermute | solution.py:471
  (34 shorter events, 2.0 us)
Async XLA Ops:
  0.6 17.9 %copy-start.1 = (s32[1,6,1024]{2,0,1:T(1,128)S(1)}, s32[1,6,1024]{2,0,1:T(1,128)}, u32[]{:S(2)}) copy-start(s32[1,6,1024]{2,0,1:T(1,128)} %param.13) | copy-start | bytes 73732
  0.6 0.7 %copy-start.6 = (f32[2,2,1,1280]{3,2,1,0:T(1,128)S(1)}, f32[2,2,1,1280]{3,2,1,0:T(1,128)}, u32[]{:S(2)}) copy-start(f32[2,2,1,1280]{3,2,1,0:T(1,128)} %param.15) | copy-start | bytes 61444
  1.4 0.7 %copy-start.7 = (s32[1,256]{1,0:T(1,128)S(1)}, s32[1,256]{1,0:T(1,128)}, u32[]{:S(2)}) copy-start(s32[1,256]{1,0:T(1,128)} %order_ref.7) | copy-start | bytes 3076
  2.1 16.5 %copy-start.10 = (s32[1,1024]{1,0:T(1,128)S(1)}, s32[1,1024]{1,0:T(1,128)}, u32[]{:S(2)}) copy-start(s32[1,1024]{1,0:T(1,128)} %param.14) | copy-start | bytes 12292
  2.1 10.9 %collective-permute-start = (f32[8,256]{1,0:T(8,128)S(1)}, f32[8,256]{1,0:T(8,128)S(1)}, u32[]{:S(2)}, u32[]{:S(2)}) collective-permute-start(f32[8,256]{1,0:T(8,128)S(1)} %get-tuple-element.24), channel_id=1, source_target_pairs={{1,2},{2,1},{3,4},{4,3},{5,6},{6,5},{9,10},{10,9},{11,12},{12,11},... | collective-permute-start | bytes 24584 | tf_op jit(solution)/shard_map/ppermute | solution.py:456
  2.8 10.2 %collective-permute-start.1 = (f32[8,256]{1,0:T(8,128)S(1)}, f32[8,256]{1,0:T(8,128)S(1)}, u32[]{:S(2)}, u32[]{:S(2)}) collective-permute-start(f32[8,256]{1,0:T(8,128)S(1)} %get-tuple-element.25), channel_id=1, source_target_pairs={{0,1},{1,0},{2,3},{3,2},{4,5},{5,4},{6,7},{7,6},{8,9},{9,8},{10,11... | collective-permute-start | bytes 24584 | tf_op jit(solution)/shard_map/ppermute | solution.py:456
  7.1 0.7 %copy-start = (s32[1,6,1024]{2,0,1:T(1,128)S(1)}, s32[1,6,1024]{2,0,1:T(1,128)}, u32[]{:S(2)}) copy-start(s32[1,6,1024]{2,0,1:T(1,128)} %param.13) | copy-start | bytes 73732
  7.9 0.9 %copy-start.2 = (f32[1,36,1024]{2,0,1:T(1,128)S(1)}, f32[1,36,1024]{2,0,1:T(1,128)}, u32[]{:S(2)}) copy-start(f32[1,36,1024]{2,0,1:T(1,128)} %param.11) | copy-start | bytes 442372
  8.8 0.9 %copy-start.4 = (f32[1,36,1024]{2,0,1:T(1,128)S(1)}, f32[1,36,1024]{2,0,1:T(1,128)}, u32[]{:S(2)}) copy-start(f32[1,36,1024]{2,0,1:T(1,128)} %param.10) | copy-start | bytes 442372
  9.7 0.7 %copy-start.9 = (s32[1,1024]{1,0:T(1,128)S(1)}, s32[1,1024]{1,0:T(1,128)}, u32[]{:S(2)}) copy-start(s32[1,1024]{1,0:T(1,128)} %param.14) | copy-start | bytes 12292
  10.4 0.7 %copy-start.11 = (f32[1,1024]{1,0:T(1,128)S(1)}, f32[1,1024]{1,0:T(1,128)}, u32[]{:S(2)}) copy-start(f32[1,1024]{1,0:T(1,128)} %param.12) | copy-start | bytes 12292
  11.1 0.7 %copy-start.13 = (f32[2]{0:T(128)S(1)}, f32[2]{0:T(128)}, u32[]{:S(2)}) copy-start(f32[2]{0:T(128)} %angular.3) | copy-start | bytes 28
  11.7 6.8 %copy-start.3 = (f32[1,36,1024]{2,0,1:T(1,128)S(1)}, f32[1,36,1024]{2,0,1:T(1,128)}, u32[]{:S(2)}) copy-start(f32[1,36,1024]{2,0,1:T(1,128)} %param.11) | copy-start | bytes 442372
  11.7 6.8 %copy-start.5 = (f32[2,2,1,1280]{3,2,1,0:T(1,128)S(1)}, f32[2,2,1,1280]{3,2,1,0:T(1,128)}, u32[]{:S(2)}) copy-start(f32[2,2,1,1280]{3,2,1,0:T(1,128)} %param.16) | copy-start | bytes 61444
  13.0 0.7 %copy-start.8 = (s32[1,256]{1,0:T(1,128)S(1)}, s32[1,256]{1,0:T(1,128)}, u32[]{:S(2)}) copy-start(s32[1,256]{1,0:T(1,128)} %order_ref.7) | copy-start | bytes 3076
  14.9 29.2 %copy-start.12 = (f32[1,1024]{1,0:T(1,128)S(1)}, f32[1,1024]{1,0:T(1,128)}, u32[]{:S(2)}) copy-start(f32[1,1024]{1,0:T(1,128)} %param.12) | copy-start | bytes 12292
  14.9 4.6 %collective-permute-start.2 = (f32[8,256]{1,0:T(8,128)S(1)}, f32[8,256]{1,0:T(8,128)S(1)}, u32[]{:S(2)}, u32[]{:S(2)}) collective-permute-start(f32[8,256]{1,0:T(8,128)S(1)} %get-tuple-element.31), channel_id=1, source_target_pairs={{1,2},{2,1},{3,4},{4,3},{5,6},{6,5},{9,10},{10,9},{11,12},{12,11},... | collective-permute-start | bytes 24584 | tf_op jit(solution)/shard_map/ppermute | solution.py:456
  15.6 3.9 %collective-permute-start.3 = (f32[8,256]{1,0:T(8,128)S(1)}, f32[8,256]{1,0:T(8,128)S(1)}, u32[]{:S(2)}, u32[]{:S(2)}) collective-permute-start(f32[8,256]{1,0:T(8,128)S(1)} %get-tuple-element.32), channel_id=1, source_target_pairs={{0,1},{1,0},{2,3},{3,2},{4,5},{5,4},{6,7},{7,6},{8,9},{9,8},{10,11... | collective-permute-start | bytes 24584 | tf_op jit(solution)/shard_map/ppermute | solution.py:456
  20.7 4.0 %collective-permute-start.4 = (f32[8,256]{1,0:T(8,128)S(1)}, f32[8,256]{1,0:T(8,128)S(1)}, u32[]{:S(2)}, u32[]{:S(2)}) collective-permute-start(f32[8,256]{1,0:T(8,128)S(1)} %get-tuple-element.37), channel_id=1, source_target_pairs={{1,2},{2,1},{3,4},{4,3},{5,6},{6,5},{9,10},{10,9},{11,12},{12,11},... | collective-permute-start | bytes 24584 | tf_op jit(solution)/shard_map/ppermute | solution.py:456
  21.3 4.1 %collective-permute-start.5 = (f32[8,256]{1,0:T(8,128)S(1)}, f32[8,256]{1,0:T(8,128)S(1)}, u32[]{:S(2)}, u32[]{:S(2)}) collective-permute-start(f32[8,256]{1,0:T(8,128)S(1)} %get-tuple-element.38), channel_id=1, source_target_pairs={{0,1},{1,0},{2,3},{3,2},{4,5},{5,4},{6,7},{7,6},{8,9},{9,8},{10,11... | collective-permute-start | bytes 24584 | tf_op jit(solution)/shard_map/ppermute | solution.py:456
  36.0 3.7 %collective-permute-start.6 = (f32[8,128]{1,0:T(8,128)S(1)}, f32[8,128]{1,0:T(8,128)S(1)}, u32[]{:S(2)}, u32[]{:S(2)}) collective-permute-start(f32[8,128]{1,0:T(8,128)S(1)} %shard_map.110), channel_id=1, source_target_pairs={{0,8},{8,0},{16,24},{24,16},{1,9},{9,1},{17,25},{25,17},{2,10},{10... | collective-permute-start | bytes 12296 | tf_op jit(solution)/shard_map/ppermute | solution.py:471
  39.6 4.5 %collective-permute-start.7 = (f32[8,128]{1,0:T(8,128)S(1)}, f32[8,128]{1,0:T(8,128)S(1)}, u32[]{:S(2)}, u32[]{:S(2)}) collective-permute-start(f32[8,128]{1,0:T(8,128)S(1)} %add.6), channel_id=1, source_target_pairs={{0,16},{8,24},{16,0},{24,8},{1,17},{9,25},{17,1},{25,9},{2,18},{10... | collective-permute-start | bytes 12296 | tf_op jit(solution)/shard_map/ppermute | solution.py:471
  44.2 0.6 %copy-start.14 = (f32[8,128]{1,0:T(8,128)}, f32[8,128]{1,0:T(8,128)S(1)}, u32[]{:S(2)}) copy-start(f32[8,128]{1,0:T(8,128)S(1)} %add.7) | copy-start | bytes 12292

commit v2 on v1

--- a/solution.py
+++ b/solution.py
@@ -11,7 +11,7 @@
 SUBLANES = 8
 SIDE = 6
 VMEM = pl.BlockSpec(memory_space=pltpu.VMEM)
-SMEM = pl.BlockSpec(memory_space=pltpu.SMEM)
+HBM = pl.BlockSpec(memory_space=pltpu.HBM)
 
 PICK_LANES = lax.GatherDimensionNumbers(
     offset_dims=(),
@@ -175,7 +175,51 @@
     return total
 
 
-def rims_stage(source, order_ref, across_ref, beside_ref, stacked_ref):
+def load_stage(
+    angular_in,
+    source_in,
+    order_in,
+    stiffness_in,
+    mass_in,
+    sigma_in,
+    live_in,
+    edges_in,
+    forward_in,
+    across_ref,
+    beside_ref,
+    stacked_ref,
+    order_ref,
+    rates_ref,
+    stiffness_ref,
+    mass_ref,
+    sigma_ref,
+    live_ref,
+    edges_ref,
+    forward_ref,
+    angular,
+    source,
+    order,
+    arrived,
+):
+    routes = (
+        (source_in, source),
+        (order_in, order),
+        (angular_in, angular),
+        (edges_in, edges_ref),
+        (stiffness_in, stiffness_ref),
+        (mass_in, mass_ref),
+        (sigma_in, sigma_ref),
+        (live_in, live_ref),
+        (forward_in, forward_ref),
+    )
+    copies = [
+        pltpu.make_async_copy(here, there, arrived.at[n])
+        for n, (here, there) in enumerate(routes)
+    ]
+    for copy in copies:
+        copy.start()
+    for copy in copies[:2]:
+        copy.wait()
     groups = source.shape[0]
     rows = stacked_ref.shape[0]
     first = row_ids(rows) < groups
@@ -184,25 +228,30 @@
         piece = [source[g, :, c : c + LANES] for g in range(groups)]
         chunks.append(jnp.concatenate(piece + piece, axis=0))
     put_chunks(stacked_ref, chunks)
-    order = [spread(piece.astype(jnp.float32), rows) for piece in cut(order_ref)]
-    count = len(order)
-    lower = [jnp.where(first, x, o) for x, o in zip(chunks[:count], order)]
+    order_ref[...] = spread(order[...], rows)
+    numbers = [x.astype(jnp.float32) for x in cut(order_ref)]
+    count = len(numbers)
+    lower = [jnp.where(first, x, o) for x, o in zip(chunks[:count], numbers)]
     upper = [jnp.where(first, x, 1.0) for x in chunks[len(chunks) - count :]]
     put_rims(across_ref, beside_ref, lower, upper)
+    for copy in copies[2:]:
+        copy.wait()
+    for f in range(angular.shape[0]):
+        rates_ref[f] = jnp.full(rates_ref.shape[1:], angular[f], jnp.float32)
 
 
 def table_stage(
-    angular, stiffness, mass, sigma, live, edges, places_ref, blocks_ref, scale_ref
+    rates, stiffness, mass, sigma, live, edges, places_ref, blocks_ref, scale_ref
 ):
     rows = edges.shape[1]
     alive = live[...].astype(jnp.float32)
     weight = sigma[...]
-    freqs = angular.shape[0]
+    freqs = rates.shape[0]
     peak = None
     for i in range(SIDE):
         for f in range(freqs):
             entry = (SIDE + 1) * i
-            size = stiffness[entry] + angular[f] * weight * mass[entry]
+            size = stiffness[entry] + rates[f] * weight * mass[entry]
             peak = size if peak is None else jnp.maximum(peak, size)
     peak = jnp.max(peak * alive, axis=1, keepdims=True)
     scale = jnp.broadcast_to(jnp.max(peak, axis=0, keepdims=True), scale_ref.shape)
@@ -212,7 +261,7 @@
         stiff = stiffness[entry] * alive
         heavy = mass[entry] * (weight * alive)
         for f in range(freqs):
-            blocks_ref[f * SIDE * SIDE + entry] = stiff + angular[f] * heavy
+            blocks_ref[f * SIDE * SIDE + entry] = stiff + rates[f] * heavy
     numbers = row_ids(LANES)
 
     def body(i, carry):
@@ -271,7 +320,7 @@
     prior, above = take_rims(across_in, beside_in)
 
     rim = order_ref.shape[-1]
-    order = [spread(piece, rows) for piece in cut(order_ref)]
+    order = cut(order_ref)
     above_order = spread(
         jnp.concatenate([x[groups : groups + 1] for x in above], axis=1), rim
     )
@@ -338,7 +387,7 @@
     inverse_scale = 1.0 / scale
     rim = order_ref.shape[-1]
     count = rim // LANES
-    order = [spread(piece, rows) for piece in cut(order_ref)]
+    order = cut(order_ref)
     inverse = cut(inverse_ref)
 
     def rescaled(block):
@@ -377,12 +426,12 @@
         )
 
 
-def forward_stage(polars, angular, forward, mass, live, edges, picks, heavy_ref, terms_ref):
+def forward_stage(polars, rates, forward, mass, live, edges, picks, heavy_ref, terms_ref):
     dead = -live[...].astype(jnp.float32)
     for g in range(forward.shape[0]):
         rows = [forward[g, :, c : c + LANES] for c in range(0, forward.shape[-1], LANES)]
         values = times_block(mass, 0, picks_of(rows, edges))
-        factor = dead * angular[g // polars]
+        factor = dead * rates[g // polars]
         values = [factor * value for value in values]
         for i in range(SIDE):
             heavy_ref[g * SIDE + i] = values[i]
@@ -436,11 +485,11 @@
     out_ref[...] = out
 
 
-def call(kernel, arguments, outs, scratch=(), scalars=0, cost=0):
+def call(kernel, arguments, outs, scratch=(), space=VMEM, cost=0):
     return pl.pallas_call(
         kernel,
         out_shape=outs,
-        in_specs=[SMEM] * scalars + [VMEM] * (len(arguments) - scalars),
+        in_specs=[space] * len(arguments),
         out_specs=jax.tree.map(lambda _: VMEM, outs),
         scratch_shapes=list(scratch),
         cost_estimate=pl.CostEstimate(flops=cost, bytes_accessed=cost, transcendentals=0),
@@ -509,24 +558,52 @@
     field_room = pltpu.VMEM((rows, edge_count), jnp.float32)
     piece_room = pltpu.VMEM((rows * SIDE * tall, LANES), jnp.float32)
 
-    across, beside, source = call(
-        rims_stage, (source, neighbour_map), [rim_shape, rim_shape, field_shape]
+    arguments = (
+        angular,
+        source,
+        neighbour_map,
+        stiff,
+        mass,
+        sigma,
+        live,
+        edges,
+        forward,
+    )
+    arguments = [pltpu.with_memory_space_constraint(x, pltpu.HBM) for x in arguments]
+    kept = [jax.ShapeDtypeStruct(x.shape, x.dtype) for x in arguments[3:]]
+    across, beside, source, order, rates, stiff, mass, sigma, live, edges, forward = call(
+        load_stage,
+        arguments,
+        [
+            rim_shape,
+            rim_shape,
+            field_shape,
+            shape(rows, rim, kind=jnp.int32),
+            shape(freqs, tall, LANES),
+            *kept,
+        ],
+        (
+            pltpu.SMEM(angular.shape, angular.dtype),
+            pltpu.VMEM(source.shape, source.dtype),
+            pltpu.VMEM(neighbour_map.shape, neighbour_map.dtype),
+            pltpu.SemaphoreType.DMA((len(arguments),)),
+        ),
+        space=HBM,
     )
     across, beside = swap(across, "dom", 1), swap(beside, "dom", 0)
     places, blocks, scale = call(
         table_stage,
-        (angular, stiff, mass, sigma, live, edges),
+        (rates, stiff, mass, sigma, live, edges),
         [
             shape(LANES, SIDE * slots, kind=jnp.bfloat16),
             shape(freqs * SIDE * SIDE, tall, LANES),
             sums_shape,
         ],
-        scalars=1,
         cost=4_000_000,
     )
     picks, image, across, beside, inverse, sums = call(
         functools.partial(first_stage, polars),
-        (source, neighbour_map, across, beside, scale, blocks, edges, places),
+        (source, order, across, beside, scale, blocks, edges, places),
         [
             picks_shape,
             field_shape,
@@ -540,21 +617,20 @@
     across, beside = swap(across, "dom", 1), swap(beside, "dom", 0)
     heavy, terms0 = call(
         functools.partial(forward_stage, polars),
-        (angular, forward, mass, live, edges, picks),
+        (rates, forward, mass, live, edges, picks),
         [picks_shape, terms_shape],
-        scalars=1,
         cost=4_000_000,
     )
     terms1, sums, image, across, beside = call(
         functools.partial(later_stage, polars, 1, False),
-        (image, neighbour_map, inverse, across, beside, sums, blocks, edges, heavy, places),
+        (image, order, inverse, across, beside, sums, blocks, edges, heavy, places),
         [terms_shape, sums_shape, field_shape, rim_shape, rim_shape],
         (field_room, piece_room),
     )
     across, beside = swap(across, "dom", 1), swap(beside, "dom", 0)
     terms2, sums = call(
         functools.partial(later_stage, polars, 2, True),
-        (image, neighbour_map, inverse, across, beside, sums, blocks, edges, heavy),
+        (image, order, inverse, across, beside, sums, blocks, edges, heavy),
         [terms_shape, sums_shape],
         (field_room,),
     )
@@ -564,7 +640,7 @@
         shape(tall, LANES),
     )
     gradient = sum_over(term, "freq").reshape(1, slots)
-    updated = conductivity * jnp.exp(-0.5 * jnp.tanh(gradient))
+    updated = sigma.reshape(1, slots) * jnp.exp(-0.5 * jnp.tanh(gradient))
     return gradient, updated
 
 

time: 45.3 us -> 40.4 us (0.89)
  local copies, waits for them, and re-layouts: 6.7 us -> 0.01 us
  starting transfers between devices: 16.8 us -> 17.9 us
  blocking collectives: 9.78 us -> 10.3 us
  waiting for transfers between devices: 4.78 us -> 5.3 us
    unnamed x30 -> x2, local copies, waits for them, and re-layouts: 6.69 us -> 0.01 us
    ppermute x6, starting transfers between devices: 12.6 us -> 13.6 us  [swap(): return lax.ppermute(block, axis, route)]
    all_to_all x1, blocking collectives: 9.78 us -> 10.3 us  [gather_all(): return lax.all_to_all(copies, axis, 0, 0)]
    ppermute x6, waiting for transfers between devices: 0.84 us -> 1.35 us  [swap(): return lax.ppermute(block, axis, route)]
  transfers between devices with their start and end apart: 8 -> 8, of which waited for: 3 -> 5; matrix products, arithmetic and copies ran while one was open for 0% -> 0% of each run, Pallas kernels for 5% -> 3%
where the time goes in v2:
time: 40.4 us; the launch traced here: 40.2 us
  starting transfers between devices  17.9 us (44%)
  blocking collectives  10.3 us (25%)
  Pallas kernels  5.34 us (13%)
  waiting for transfers between devices  5.3 us (13%)
  between operations  0.72 us (2%)
  other arithmetic  0.62 us (2%)
    ppermute x6, starting transfers between devices, swap(): return lax.ppermute(block, axis, route)  13.6 us
    all_to_all x1, blocking collectives, gather_all(): return lax.all_to_all(copies, axis, 0, 0)  10.3 us
    pallas_call x7, Pallas kernels, call(): pl.pallas_call(kernel, out_shape=outs, in_specs=[space] * len(arguments),...  5.34 us
    ppermute x2, starting transfers between devices, sum_over(): lax.ppermute(block, axis, [(i, i ^ step) for i in range(size)])  4.23 us
    ppermute x2, waiting for transfers between devices, sum_over(): lax.ppermute(block, axis, [(i, i ^ step) for i in range(size)])  3.95 us
    ppermute x6, waiting for transfers between devices, swap(): return lax.ppermute(block, axis, route)  1.35 us
  transfers between devices with their start and end apart: 8, of which 5 were waited for; matrix products, arithmetic and copies ran while one was open for 0% of the time, Pallas kernels for 3%

profile of v2, /device:TPU:0, one launch (start us, length us, event | category | flops | bytes accessed | tf_op | source)
XLA Modules:
  0.0 40.2 jit_solution(13828150310401159865)
XLA Ops:
  0.6 1.1 %shard_map.104 = (f32[8,256]{1,0:T(8,128)S(1)}, f32[8,256]{1,0:T(8,128)S(1)}, f32[8,1280]{1,0:T(8,128)S(1)}, s32[8,256]{1,0:T(8,128)S(1)}, f32[2,8,128]{2,1,0:T(...) custom-call(f32[2]{0:T(128)} %angular_in.1, ...), custom_call_target="tpu_custom_call" | custom-call | tf_op jit(solution)/shard_map/pallas_call | solution.py:489
  1.8 0.7 %collective-permute-start = (f32[8,256]{1,0:T(8,128)S(1)}, f32[8,256]{1,0:T(8,128)S(1)}, u32[]{:S(2)}, u32[]{:S(2)}) collective-permute-start(f32[8,256]{1,0:T(8,128)S(1)} %get-tuple-element.33), channel_id=1, source_target_pairs={{1,2},{2,1},{3,4},{4,3},{5,6},{6,5},{9,10},{10,9},{11,12},{12,11},... | collective-permute-start | bytes 24584 | tf_op jit(solution)/shard_map/ppermute | solution.py:505
  2.4 4.4 %collective-permute-start.1 = (f32[8,256]{1,0:T(8,128)S(1)}, f32[8,256]{1,0:T(8,128)S(1)}, u32[]{:S(2)}, u32[]{:S(2)}) collective-permute-start(f32[8,256]{1,0:T(8,128)S(1)} %get-tuple-element.34), channel_id=1, source_target_pairs={{0,1},{1,0},{2,3},{3,2},{4,5},{5,4},{6,7},{7,6},{8,9},{9,8},{10,11... | collective-permute-start | bytes 24584 | tf_op jit(solution)/shard_map/ppermute | solution.py:505
  6.8 0.7 %shard_map.105 = (bf16[128,6144]{1,0:T(8,128)(2,1)S(1)}, f32[72,8,128]{2,1,0:T(8,128)S(1)}, f32[8,128]{1,0:T(8,128)S(1)}) custom-call(f32[2,8,128]{2,1,0:T(8,128)S(1)} %get-tuple-element.35.rates, f32[36,8,128]{2,1,0:T(8,128)S(1)} %get-tuple-element.36.stiffness, f32[36,8,128]{2,1,0:T(8,128)S(1)} %get-tuple-element.37.mass, ...), custom_call_target="tpu_custom_call" | custom-call | flops 4000000 | bytes 4000000 | tf_op jit(solution)/shard_map/pallas_call | solution.py:489
  7.5 0.0 collective-permute-done.across_in
  7.5 0.1 collective-permute-done.1.beside_in
  7.6 1.2 %shard_map.106 = (f32[24,8,128]{2,1,0:T(8,128)S(1)}, f32[8,1280]{1,0:T(8,128)S(1)}, f32[8,256]{1,0:T(8,128)S(1)}, f32[8,256]{1,0:T(8,128)S(1)}, s32[8,256]{1,0:T(8,128)S(1)}, /*index=5*/f32[8,128]{1,0:T(8,128)S(1)}) custom-call(f32[8,1280]{1,0:T(8,128)S(1)} %get-tuple-element.31.source, s32[8,256]{1,0:T(8,128)S(1)} %get-tuple-element.32.order_ref, ...), custom_call_target="tpu_custom_call" | custom-call | tf_op jit(solution)/shard_map/pallas_call | solution.py:489
  8.9 0.7 %collective-permute-start.2 = (f32[8,256]{1,0:T(8,128)S(1)}, f32[8,256]{1,0:T(8,128)S(1)}, u32[]{:S(2)}, u32[]{:S(2)}) collective-permute-start(f32[8,256]{1,0:T(8,128)S(1)} %get-tuple-element.46), channel_id=1, source_target_pairs={{1,2},{2,1},{3,4},{4,3},{5,6},{6,5},{9,10},{10,9},{11,12},{12,11},... | collective-permute-start | bytes 24584 | tf_op jit(solution)/shard_map/ppermute | solution.py:505
  9.6 3.5 %collective-permute-start.3 = (f32[8,256]{1,0:T(8,128)S(1)}, f32[8,256]{1,0:T(8,128)S(1)}, u32[]{:S(2)}, u32[]{:S(2)}) collective-permute-start(f32[8,256]{1,0:T(8,128)S(1)} %get-tuple-element.47), channel_id=1, source_target_pairs={{0,1},{1,0},{2,3},{3,2},{4,5},{5,4},{6,7},{7,6},{8,9},{9,8},{10,11... | collective-permute-start | bytes 24584 | tf_op jit(solution)/shard_map/ppermute | solution.py:505
  13.0 0.4 shard_map.107
  13.4 0.0 collective-permute-done.2.across_in
  13.4 0.4 %collective-permute-done.3.beside_in = f32[8,256]{1,0:T(8,128)S(1)} collective-permute-done((f32[8,256]{1,0:T(8,128)S(1)}, f32[8,256]{1,0:T(8,128)S(1)}, u32[]{:S(2)}, u32[]{:S(2)}) %collective-permute-start.3) | collective-permute-done | bytes 8224 | tf_op jit(solution)/shard_map/ppermute | solution.py:505
  13.9 1.2 %shard_map.108 = (f32[4,8,128]{2,1,0:T(8,128)S(1)}, f32[8,128]{1,0:T(8,128)S(1)}, f32[8,1280]{1,0:T(8,128)S(1)}, f32[8,256]{1,0:T(8,128)S(1)}, f32[8,256]{1,0:T(8,128)S(1)}) custom-call(f32[8,1280]{1,0:T(8,128)S(1)} %get-tuple-element.44.image_in, s32[8,256]{1,0:T(8,128)S(1)} %get-tuple-element.32.order_ref, s32[8,256]{1,0:T(8,128)S(1)} %get-tuple-element.45.inverse_ref, ...), custom_call_target="tpu_custom_call" | custom-call | tf_op jit(solution)/shard_map/pallas_call | solution.py:489
  15.0 0.7 %collective-permute-start.4 = (f32[8,256]{1,0:T(8,128)S(1)}, f32[8,256]{1,0:T(8,128)S(1)}, u32[]{:S(2)}, u32[]{:S(2)}) collective-permute-start(f32[8,256]{1,0:T(8,128)S(1)} %get-tuple-element.53), channel_id=1, source_target_pairs={{1,2},{2,1},{3,4},{4,3},{5,6},{6,5},{9,10},{10,9},{11,12},{12,11},... | collective-permute-start | bytes 24584 | tf_op jit(solution)/shard_map/ppermute | solution.py:505
  15.7 3.8 %collective-permute-start.5 = (f32[8,256]{1,0:T(8,128)S(1)}, f32[8,256]{1,0:T(8,128)S(1)}, u32[]{:S(2)}, u32[]{:S(2)}) collective-permute-start(f32[8,256]{1,0:T(8,128)S(1)} %get-tuple-element.54), channel_id=1, source_target_pairs={{0,1},{1,0},{2,3},{3,2},{4,5},{5,4},{6,7},{7,6},{8,9},{9,8},{10,11... | collective-permute-start | bytes 24584 | tf_op jit(solution)/shard_map/ppermute | solution.py:505
  19.5 0.8 %collective-permute-done.5.beside_in = f32[8,256]{1,0:T(8,128)S(1)} collective-permute-done((f32[8,256]{1,0:T(8,128)S(1)}, f32[8,256]{1,0:T(8,128)S(1)}, u32[]{:S(2)}, u32[]{:S(2)}) %collective-permute-start.5) | collective-permute-done | bytes 8224 | tf_op jit(solution)/shard_map/ppermute | solution.py:505
  20.4 0.5 %shard_map.109 = (f32[4,8,128]{2,1,0:T(8,128)S(1)}, f32[8,128]{1,0:T(8,128)S(1)}) custom-call(f32[8,1280]{1,0:T(8,128)S(1)} %get-tuple-element.52.image_in, s32[8,256]{1,0:T(8,128)S(1)} %get-tuple-element.32.order_ref, s32[8,256]{1,0:T(8,128)S(1)} %get-tuple-element.45.inverse_ref, f32[8,256]{1,0:T(8,128)S(1)} %collective-permute-done.4.across_in, ...), custom_call_target="tpu_custom_call" | custom-call | tf_op jit(solution)/shard_map/pallas_call | solution.py:489
  20.9 10.3 %all_to_all.5.everyone = f32[8,8,128]{2,1,0:T(8,128)S(1)} all-to-all(f32[8,8,128]{2,1,0:T(8,128)S(1)} %broadcast_in_dim.2), channel_id=1, replica_groups=mesh['freq'=4,'dom'=8] {'dom'}, dimensions={0} | all-to-all | bytes 65536 | tf_op jit(solution)/shard_map/all_to_all | solution.py:511
  31.3 0.1 shard_map.110
  31.4 1.6 %collective-permute-start.6 = (f32[8,128]{1,0:T(8,128)S(1)}, f32[8,128]{1,0:T(8,128)S(1)}, u32[]{:S(2)}, u32[]{:S(2)}) collective-permute-start(f32[8,128]{1,0:T(8,128)S(1)} %shard_map.110), channel_id=1, source_target_pairs={{0,8},{8,0},{16,24},{24,16},{1,9},{9,1},{17,25},{25,17},{2,10},{10... | collective-permute-start | bytes 12296 | tf_op jit(solution)/shard_map/ppermute | solution.py:520
  33.0 2.0 %collective-permute-done.6 = f32[8,128]{1,0:T(8,128)S(1)} collective-permute-done((f32[8,128]{1,0:T(8,128)S(1)}, f32[8,128]{1,0:T(8,128)S(1)}, u32[]{:S(2)}, u32[]{:S(2)}) %collective-permute-start.6) | collective-permute-done | bytes 4128 | tf_op jit(solution)/shard_map/ppermute | solution.py:520
  35.1 2.6 %collective-permute-start.7 = (f32[8,128]{1,0:T(8,128)S(1)}, f32[8,128]{1,0:T(8,128)S(1)}, u32[]{:S(2)}, u32[]{:S(2)}) collective-permute-start(f32[8,128]{1,0:T(8,128)S(1)} %add.6), channel_id=1, source_target_pairs={{0,16},{8,24},{16,0},{24,8},{1,17},{9,25},{17,1},{25,9},{2,18},{10... | collective-permute-start | bytes 12296 | tf_op jit(solution)/shard_map/ppermute | solution.py:520
  37.7 1.9 %collective-permute-done.7 = f32[8,128]{1,0:T(8,128)S(1)} collective-permute-done((f32[8,128]{1,0:T(8,128)S(1)}, f32[8,128]{1,0:T(8,128)S(1)}, u32[]{:S(2)}, u32[]{:S(2)}) %collective-permute-start.7) | collective-permute-done | bytes 4128 | tf_op jit(solution)/shard_map/ppermute | solution.py:520
  39.6 0.6 %exponential_multiply_fusion = f32[1,1024]{1,0:T(1,128)} fusion(f32[1,1024]{1,0:T(1,128)S(1)} %bitcast.9, f32[1,1024]{1,0:T(1,128)S(1)} %bitcast.15), kind=kLoop, calls=%fused_computation | loop fusion | flops 2048 | bytes 12288 | tf_op jit(solution)/shard_map/mul | solution.py:643
  (6 shorter events, 0.0 us)
Async XLA Ops:
  1.8 5.8 %collective-permute-start = (f32[8,256]{1,0:T(8,128)S(1)}, f32[8,256]{1,0:T(8,128)S(1)}, u32[]{:S(2)}, u32[]{:S(2)}) collective-permute-start(f32[8,256]{1,0:T(8,128)S(1)} %get-tuple-element.33), channel_id=1, source_target_pairs={{1,2},{2,1},{3,4},{4,3},{5,6},{6,5},{9,10},{10,9},{11,12},{12,11},... | collective-permute-start | bytes 24584 | tf_op jit(solution)/shard_map/ppermute | solution.py:505
  2.4 5.2 %collective-permute-start.1 = (f32[8,256]{1,0:T(8,128)S(1)}, f32[8,256]{1,0:T(8,128)S(1)}, u32[]{:S(2)}, u32[]{:S(2)}) collective-permute-start(f32[8,256]{1,0:T(8,128)S(1)} %get-tuple-element.34), channel_id=1, source_target_pairs={{0,1},{1,0},{2,3},{3,2},{4,5},{5,4},{6,7},{7,6},{8,9},{9,8},{10,11... | collective-permute-start | bytes 24584 | tf_op jit(solution)/shard_map/ppermute | solution.py:505
  8.9 4.6 %collective-permute-start.2 = (f32[8,256]{1,0:T(8,128)S(1)}, f32[8,256]{1,0:T(8,128)S(1)}, u32[]{:S(2)}, u32[]{:S(2)}) collective-permute-start(f32[8,256]{1,0:T(8,128)S(1)} %get-tuple-element.46), channel_id=1, source_target_pairs={{1,2},{2,1},{3,4},{4,3},{5,6},{6,5},{9,10},{10,9},{11,12},{12,11},... | collective-permute-start | bytes 24584 | tf_op jit(solution)/shard_map/ppermute | solution.py:505
  9.6 4.3 %collective-permute-start.3 = (f32[8,256]{1,0:T(8,128)S(1)}, f32[8,256]{1,0:T(8,128)S(1)}, u32[]{:S(2)}, u32[]{:S(2)}) collective-permute-start(f32[8,256]{1,0:T(8,128)S(1)} %get-tuple-element.47), channel_id=1, source_target_pairs={{0,1},{1,0},{2,3},{3,2},{4,5},{5,4},{6,7},{7,6},{8,9},{9,8},{10,11... | collective-permute-start | bytes 24584 | tf_op jit(solution)/shard_map/ppermute | solution.py:505
  15.0 4.5 %collective-permute-start.4 = (f32[8,256]{1,0:T(8,128)S(1)}, f32[8,256]{1,0:T(8,128)S(1)}, u32[]{:S(2)}, u32[]{:S(2)}) collective-permute-start(f32[8,256]{1,0:T(8,128)S(1)} %get-tuple-element.53), channel_id=1, source_target_pairs={{1,2},{2,1},{3,4},{4,3},{5,6},{6,5},{9,10},{10,9},{11,12},{12,11},... | collective-permute-start | bytes 24584 | tf_op jit(solution)/shard_map/ppermute | solution.py:505
  15.7 4.6 %collective-permute-start.5 = (f32[8,256]{1,0:T(8,128)S(1)}, f32[8,256]{1,0:T(8,128)S(1)}, u32[]{:S(2)}, u32[]{:S(2)}) collective-permute-start(f32[8,256]{1,0:T(8,128)S(1)} %get-tuple-element.54), channel_id=1, source_target_pairs={{0,1},{1,0},{2,3},{3,2},{4,5},{5,4},{6,7},{7,6},{8,9},{9,8},{10,11... | collective-permute-start | bytes 24584 | tf_op jit(solution)/shard_map/ppermute | solution.py:505
  31.4 3.7 %collective-permute-start.6 = (f32[8,128]{1,0:T(8,128)S(1)}, f32[8,128]{1,0:T(8,128)S(1)}, u32[]{:S(2)}, u32[]{:S(2)}) collective-permute-start(f32[8,128]{1,0:T(8,128)S(1)} %shard_map.110), channel_id=1, source_target_pairs={{0,8},{8,0},{16,24},{24,16},{1,9},{9,1},{17,25},{25,17},{2,10},{10... | collective-permute-start | bytes 12296 | tf_op jit(solution)/shard_map/ppermute | solution.py:520
  35.1 4.5 %collective-permute-start.7 = (f32[8,128]{1,0:T(8,128)S(1)}, f32[8,128]{1,0:T(8,128)S(1)}, u32[]{:S(2)}, u32[]{:S(2)}) collective-permute-start(f32[8,128]{1,0:T(8,128)S(1)} %add.6), channel_id=1, source_target_pairs={{0,16},{8,24},{16,0},{24,8},{1,17},{9,25},{17,1},{25,9},{2,18},{10... | collective-permute-start | bytes 12296 | tf_op jit(solution)/shard_map/ppermute | solution.py:520
  39.6 0.6 %copy-start = (f32[8,128]{1,0:T(8,128)}, f32[8,128]{1,0:T(8,128)S(1)}, u32[]{:S(2)}) copy-start(f32[8,128]{1,0:T(8,128)S(1)} %add.7) | copy-start | bytes 12292

commit v3 on v2

--- a/solution.py
+++ b/solution.py
@@ -505,21 +505,8 @@
     return lax.ppermute(block, axis, route)
 
 
-def gather_all(block, axis):
-    size = lax.axis_size(axis)
-    copies = jnp.broadcast_to(block[None], (size, *block.shape))
-    return lax.all_to_all(copies, axis, 0, 0)
-
-
 def sum_over(block, axis):
-    size = lax.axis_size(axis)
-    if size & (size - 1):
-        return jnp.sum(gather_all(block, axis), axis=0)
-    step = 1
-    while step < size:
-        block = block + lax.ppermute(block, axis, [(i, i ^ step) for i in range(size)])
-        step *= 2
-    return block
+    return jnp.sum(lax.all_gather(block, axis), axis=0)
 
 
 def local(
@@ -636,7 +623,7 @@
     )
     term = call(
         combine_stage,
-        (gather_all(sums, "dom"), sums, terms0, terms1, terms2),
+        (lax.all_gather(sums, "dom"), sums, terms0, terms1, terms2),
         shape(tall, LANES),
     )
     gradient = sum_over(term, "freq").reshape(1, slots)

time: 40.4 us -> 47.2 us (1.17)
  blocking collectives: 10.3 us -> 25.3 us
  starting transfers between devices: 17.9 us -> 13.6 us
  waiting for transfers between devices: 5.3 us -> 1.35 us
    all_gather x0 -> x2, blocking collectives: none -> 25.3 us  [the longest x1 13.4 us: sum_over(): return jnp.sum(lax.all_gather(block, axis), axis=0)]
    all_to_all x1 -> x0, blocking collectives: 10.3 us -> none  [gather_all(): return lax.all_to_all(copies, axis, 0, 0)]
    ppermute x2 -> x0, starting transfers between devices: 4.23 us -> none  [sum_over(): lax.ppermute(block, axis, [(i, i ^ step) for i in range(size)])]
    ppermute x2 -> x0, waiting for transfers between devices: 3.95 us -> none  [sum_over(): lax.ppermute(block, axis, [(i, i ^ step) for i in range(size)])]
  transfers between devices with their start and end apart: 8 -> 6, of which waited for: 5 -> 3; matrix products, arithmetic and copies ran while one was open for 0% -> 0% of each run, Pallas kernels for 3% -> 2%
where the time goes in v3:
time: 47.2 us; the launch traced here: 47 us
  blocking collectives  25.3 us (54%)
  starting transfers between devices  13.6 us (29%)
  Pallas kernels  5.34 us (11%)
  waiting for transfers between devices  1.35 us (3%)
  between operations  0.71 us (2%)
  other arithmetic  0.62 us (1%)
    ppermute x6, starting transfers between devices, swap(): return lax.ppermute(block, axis, route)  13.6 us
    all_gather x1, blocking collectives, sum_over(): return jnp.sum(lax.all_gather(block, axis), axis=0)  13.4 us
    all_gather x1, blocking collectives, local(): lax.all_gather(sums, 'dom')  12 us
    pallas_call x7, Pallas kernels, call(): pl.pallas_call(kernel, out_shape=outs, in_specs=[space] * len(arguments),...  5.34 us
    ppermute x6, waiting for transfers between devices, swap(): return lax.ppermute(block, axis, route)  1.35 us
  transfers between devices with their start and end apart: 6, of which 3 were waited for; matrix products, arithmetic and copies ran while one was open for 0% of the time, Pallas kernels for 2%

profile of v3, /device:TPU:0, one launch (start us, length us, event | category | flops | bytes accessed | tf_op | source)
XLA Modules:
  0.0 47.0 jit_solution(13183787337580070834)
XLA Ops:
  0.6 1.1 %shard_map.104 = (f32[8,256]{1,0:T(8,128)S(1)}, f32[8,256]{1,0:T(8,128)S(1)}, f32[8,1280]{1,0:T(8,128)S(1)}, s32[8,256]{1,0:T(8,128)S(1)}, f32[2,8,128]{2,1,0:T(...) custom-call(f32[2]{0:T(128)} %angular_in.1, ...), custom_call_target="tpu_custom_call" | custom-call | tf_op jit(solution)/shard_map/pallas_call | solution.py:489
  1.8 0.7 %collective-permute-start = (f32[8,256]{1,0:T(8,128)S(1)}, f32[8,256]{1,0:T(8,128)S(1)}, u32[]{:S(2)}, u32[]{:S(2)}) collective-permute-start(f32[8,256]{1,0:T(8,128)S(1)} %get-tuple-element.33), channel_id=1, source_target_pairs={{1,2},{2,1},{3,4},{4,3},{5,6},{6,5},{9,10},{10,9},{11,12},{12,11},... | collective-permute-start | bytes 24584 | tf_op jit(solution)/shard_map/ppermute | solution.py:505
  2.4 4.4 %collective-permute-start.1 = (f32[8,256]{1,0:T(8,128)S(1)}, f32[8,256]{1,0:T(8,128)S(1)}, u32[]{:S(2)}, u32[]{:S(2)}) collective-permute-start(f32[8,256]{1,0:T(8,128)S(1)} %get-tuple-element.34), channel_id=1, source_target_pairs={{0,1},{1,0},{2,3},{3,2},{4,5},{5,4},{6,7},{7,6},{8,9},{9,8},{10,11... | collective-permute-start | bytes 24584 | tf_op jit(solution)/shard_map/ppermute | solution.py:505
  6.8 0.7 %shard_map.105 = (bf16[128,6144]{1,0:T(8,128)(2,1)S(1)}, f32[72,8,128]{2,1,0:T(8,128)S(1)}, f32[8,128]{1,0:T(8,128)S(1)}) custom-call(f32[2,8,128]{2,1,0:T(8,128)S(1)} %get-tuple-element.35.rates, f32[36,8,128]{2,1,0:T(8,128)S(1)} %get-tuple-element.36.stiffness, f32[36,8,128]{2,1,0:T(8,128)S(1)} %get-tuple-element.37.mass, ...), custom_call_target="tpu_custom_call" | custom-call | flops 4000000 | bytes 4000000 | tf_op jit(solution)/shard_map/pallas_call | solution.py:489
  7.5 0.0 collective-permute-done.across_in
  7.5 0.1 collective-permute-done.1.beside_in
  7.6 1.2 %shard_map.106 = (f32[24,8,128]{2,1,0:T(8,128)S(1)}, f32[8,1280]{1,0:T(8,128)S(1)}, f32[8,256]{1,0:T(8,128)S(1)}, f32[8,256]{1,0:T(8,128)S(1)}, s32[8,256]{1,0:T(8,128)S(1)}, /*index=5*/f32[8,128]{1,0:T(8,128)S(1)}) custom-call(f32[8,1280]{1,0:T(8,128)S(1)} %get-tuple-element.31.source, s32[8,256]{1,0:T(8,128)S(1)} %get-tuple-element.32.order_ref, ...), custom_call_target="tpu_custom_call" | custom-call | tf_op jit(solution)/shard_map/pallas_call | solution.py:489
  8.9 0.7 %collective-permute-start.2 = (f32[8,256]{1,0:T(8,128)S(1)}, f32[8,256]{1,0:T(8,128)S(1)}, u32[]{:S(2)}, u32[]{:S(2)}) collective-permute-start(f32[8,256]{1,0:T(8,128)S(1)} %get-tuple-element.46), channel_id=1, source_target_pairs={{1,2},{2,1},{3,4},{4,3},{5,6},{6,5},{9,10},{10,9},{11,12},{12,11},... | collective-permute-start | bytes 24584 | tf_op jit(solution)/shard_map/ppermute | solution.py:505
  9.6 3.5 %collective-permute-start.3 = (f32[8,256]{1,0:T(8,128)S(1)}, f32[8,256]{1,0:T(8,128)S(1)}, u32[]{:S(2)}, u32[]{:S(2)}) collective-permute-start(f32[8,256]{1,0:T(8,128)S(1)} %get-tuple-element.47), channel_id=1, source_target_pairs={{0,1},{1,0},{2,3},{3,2},{4,5},{5,4},{6,7},{7,6},{8,9},{9,8},{10,11... | collective-permute-start | bytes 24584 | tf_op jit(solution)/shard_map/ppermute | solution.py:505
  13.0 0.4 shard_map.107
  13.4 0.0 collective-permute-done.2.across_in
  13.4 0.4 collective-permute-done.3.beside_in
  13.9 1.2 %shard_map.108 = (f32[4,8,128]{2,1,0:T(8,128)S(1)}, f32[8,128]{1,0:T(8,128)S(1)}, f32[8,1280]{1,0:T(8,128)S(1)}, f32[8,256]{1,0:T(8,128)S(1)}, f32[8,256]{1,0:T(8,128)S(1)}) custom-call(f32[8,1280]{1,0:T(8,128)S(1)} %get-tuple-element.44.image_in, s32[8,256]{1,0:T(8,128)S(1)} %get-tuple-element.32.order_ref, s32[8,256]{1,0:T(8,128)S(1)} %get-tuple-element.45.inverse_ref, ...), custom_call_target="tpu_custom_call" | custom-call | tf_op jit(solution)/shard_map/pallas_call | solution.py:489
  15.0 0.7 %collective-permute-start.4 = (f32[8,256]{1,0:T(8,128)S(1)}, f32[8,256]{1,0:T(8,128)S(1)}, u32[]{:S(2)}, u32[]{:S(2)}) collective-permute-start(f32[8,256]{1,0:T(8,128)S(1)} %get-tuple-element.53), channel_id=1, source_target_pairs={{1,2},{2,1},{3,4},{4,3},{5,6},{6,5},{9,10},{10,9},{11,12},{12,11},... | collective-permute-start | bytes 24584 | tf_op jit(solution)/shard_map/ppermute | solution.py:505
  15.7 3.8 %collective-permute-start.5 = (f32[8,256]{1,0:T(8,128)S(1)}, f32[8,256]{1,0:T(8,128)S(1)}, u32[]{:S(2)}, u32[]{:S(2)}) collective-permute-start(f32[8,256]{1,0:T(8,128)S(1)} %get-tuple-element.54), channel_id=1, source_target_pairs={{0,1},{1,0},{2,3},{3,2},{4,5},{5,4},{6,7},{7,6},{8,9},{9,8},{10,11... | collective-permute-start | bytes 24584 | tf_op jit(solution)/shard_map/ppermute | solution.py:505
  19.5 0.0 collective-permute-done.4.across_in
  19.5 0.8 %collective-permute-done.5.beside_in = f32[8,256]{1,0:T(8,128)S(1)} collective-permute-done((f32[8,256]{1,0:T(8,128)S(1)}, f32[8,256]{1,0:T(8,128)S(1)}, u32[]{:S(2)}, u32[]{:S(2)}) %collective-permute-start.5) | collective-permute-done | bytes 8224 | tf_op jit(solution)/shard_map/ppermute | solution.py:505
  20.4 0.5 %shard_map.109 = (f32[4,8,128]{2,1,0:T(8,128)S(1)}, f32[8,128]{1,0:T(8,128)S(1)}) custom-call(f32[8,1280]{1,0:T(8,128)S(1)} %get-tuple-element.52.image_in, s32[8,256]{1,0:T(8,128)S(1)} %get-tuple-element.32.order_ref, s32[8,256]{1,0:T(8,128)S(1)} %get-tuple-element.45.inverse_ref, f32[8,256]{1,0:T(8,128)S(1)} %collective-permute-done.4.across_in, ...), custom_call_target="tpu_custom_call" | custom-call | tf_op jit(solution)/shard_map/pallas_call | solution.py:489
  20.9 12.0 %all-gather = f32[64,128]{1,0:T(8,128)S(1)} all-gather(f32[8,128]{1,0:T(8,128)S(1)} %get-tuple-element.56.sums_in), channel_id=2, replica_groups=mesh['freq'=4,'dom'=8] {'dom'}, dimensions={0}, use_global_device_ids=true | all-gather | bytes 36864 | tf_op jit(solution)/shard_map/all_gather | solution.py:626
  32.9 0.1 shard_map.110
  33.0 13.4 %all-gather.1 = f32[32,128]{1,0:T(8,128)S(1)} all-gather(f32[8,128]{1,0:T(8,128)S(1)} %shard_map.110), channel_id=3, replica_groups=mesh['freq'=4,'dom'=8] {'freq'}, dimensions={0}, use_global_device_ids=true | all-gather | bytes 20480 | tf_op jit(solution)/shard_map/all_gather | solution.py:509
  46.4 0.0 copy-start
  46.4 0.6 %exponential_multiply_fusion = f32[1,1024]{1,0:T(1,128)} fusion(f32[1,1024]{1,0:T(1,128)S(1)} %bitcast.13, f32[1,1024]{1,0:T(1,128)S(1)} %bitcast.19), kind=kLoop, calls=%fused_computation.1 | loop fusion | flops 2048 | bytes 12288 | tf_op jit(solution)/shard_map/mul | solution.py:630
  47.0 0.0 copy-done
  (1 shorter events, 0.0 us)
Async XLA Ops:
  1.8 5.8 %collective-permute-start = (f32[8,256]{1,0:T(8,128)S(1)}, f32[8,256]{1,0:T(8,128)S(1)}, u32[]{:S(2)}, u32[]{:S(2)}) collective-permute-start(f32[8,256]{1,0:T(8,128)S(1)} %get-tuple-element.33), channel_id=1, source_target_pairs={{1,2},{2,1},{3,4},{4,3},{5,6},{6,5},{9,10},{10,9},{11,12},{12,11},... | collective-permute-start | bytes 24584 | tf_op jit(solution)/shard_map/ppermute | solution.py:505
  2.4 5.2 %collective-permute-start.1 = (f32[8,256]{1,0:T(8,128)S(1)}, f32[8,256]{1,0:T(8,128)S(1)}, u32[]{:S(2)}, u32[]{:S(2)}) collective-permute-start(f32[8,256]{1,0:T(8,128)S(1)} %get-tuple-element.34), channel_id=1, source_target_pairs={{0,1},{1,0},{2,3},{3,2},{4,5},{5,4},{6,7},{7,6},{8,9},{9,8},{10,11... | collective-permute-start | bytes 24584 | tf_op jit(solution)/shard_map/ppermute | solution.py:505
  8.9 4.6 %collective-permute-start.2 = (f32[8,256]{1,0:T(8,128)S(1)}, f32[8,256]{1,0:T(8,128)S(1)}, u32[]{:S(2)}, u32[]{:S(2)}) collective-permute-start(f32[8,256]{1,0:T(8,128)S(1)} %get-tuple-element.46), channel_id=1, source_target_pairs={{1,2},{2,1},{3,4},{4,3},{5,6},{6,5},{9,10},{10,9},{11,12},{12,11},... | collective-permute-start | bytes 24584 | tf_op jit(solution)/shard_map/ppermute | solution.py:505
  9.6 4.3 %collective-permute-start.3 = (f32[8,256]{1,0:T(8,128)S(1)}, f32[8,256]{1,0:T(8,128)S(1)}, u32[]{:S(2)}, u32[]{:S(2)}) collective-permute-start(f32[8,256]{1,0:T(8,128)S(1)} %get-tuple-element.47), channel_id=1, source_target_pairs={{0,1},{1,0},{2,3},{3,2},{4,5},{5,4},{6,7},{7,6},{8,9},{9,8},{10,11... | collective-permute-start | bytes 24584 | tf_op jit(solution)/shard_map/ppermute | solution.py:505
  15.0 4.5 %collective-permute-start.4 = (f32[8,256]{1,0:T(8,128)S(1)}, f32[8,256]{1,0:T(8,128)S(1)}, u32[]{:S(2)}, u32[]{:S(2)}) collective-permute-start(f32[8,256]{1,0:T(8,128)S(1)} %get-tuple-element.53), channel_id=1, source_target_pairs={{1,2},{2,1},{3,4},{4,3},{5,6},{6,5},{9,10},{10,9},{11,12},{12,11},... | collective-permute-start | bytes 24584 | tf_op jit(solution)/shard_map/ppermute | solution.py:505
  15.7 4.6 %collective-permute-start.5 = (f32[8,256]{1,0:T(8,128)S(1)}, f32[8,256]{1,0:T(8,128)S(1)}, u32[]{:S(2)}, u32[]{:S(2)}) collective-permute-start(f32[8,256]{1,0:T(8,128)S(1)} %get-tuple-element.54), channel_id=1, source_target_pairs={{0,1},{1,0},{2,3},{3,2},{4,5},{5,4},{6,7},{7,6},{8,9},{9,8},{10,11... | collective-permute-start | bytes 24584 | tf_op jit(solution)/shard_map/ppermute | solution.py:505
  46.4 0.6 %copy-start = (f32[8,128]{1,0:T(8,128)}, f32[8,128]{1,0:T(8,128)S(1)}, u32[]{:S(2)}) copy-start(f32[8,128]{1,0:T(8,128)S(1)} %bitcast_reduce_fusion) | copy-start | bytes 12292

commit v4 on v1

--- a/solution.py
+++ b/solution.py
@@ -11,7 +11,7 @@
 SUBLANES = 8
 SIDE = 6
 VMEM = pl.BlockSpec(memory_space=pltpu.VMEM)
-SMEM = pl.BlockSpec(memory_space=pltpu.SMEM)
+HBM = pl.BlockSpec(memory_space=pltpu.HBM)
 
 PICK_LANES = lax.GatherDimensionNumbers(
     offset_dims=(),
@@ -86,7 +86,8 @@
 
 
 def is_even():
-    return lax.rem(lax.axis_index("dom"), 2) == 0
+    device = lax.axis_index("dom")
+    return lax.rem(device + 1 + device // 2, 2) == 0
 
 
 def put_rims(across_ref, beside_ref, lower, upper):
@@ -175,49 +176,142 @@
     return total
 
 
-def rims_stage(source, order_ref, across_ref, beside_ref, stacked_ref):
-    groups = source.shape[0]
-    rows = stacked_ref.shape[0]
+def start_copies(routes, arrived):
+    copies = [
+        pltpu.make_async_copy(here, there, arrived.at[n])
+        for n, (here, there) in enumerate(routes)
+    ]
+    for copy in copies:
+        copy.start()
+    return copies
+
+
+def load_stage(
+    source_in,
+    order_in,
+    angular_in,
+    stiffness_in,
+    mass_in,
+    edges_in,
+    sigma_in,
+    live_in,
+    forward_in,
+    source_ref,
+    parcel_ref,
+    sigma_ref,
+    rates_ref,
+    order,
+    angular,
+    edges,
+    live,
+    arrived,
+):
+    count = source_in.shape[0]
+    tall = sigma_ref.shape[0]
+    matrix = stiffness_in.shape[0]
+    base = 2 * matrix
+    copies = start_copies(
+        (
+            (source_in, source_ref.at[pl.ds(0, count)]),
+            (order_in, order),
+            (edges_in, edges),
+            (sigma_in, sigma_ref),
+            (live_in, live),
+            (angular_in, angular),
+            (stiffness_in, parcel_ref.at[pl.ds(0, matrix)]),
+            (mass_in, parcel_ref.at[pl.ds(matrix, matrix)]),
+            (forward_in, parcel_ref.at[pl.ds(base + (SIDE + 2) * tall, forward_in.shape[0])]),
+        ),
+        arrived,
+    )
+    for copy in copies:
+        copy.wait()
+    for c, piece in enumerate(cut(order)):
+        at = count + c * SUBLANES
+        source_ref[at : at + SUBLANES, :] = spread(piece.astype(jnp.float32), SUBLANES)
+    parcel_ref[base : base + SIDE * tall, :] = edges[...].astype(jnp.float32)
+    base += SIDE * tall
+    parcel_ref[base : base + tall, :] = sigma_ref[...]
+    parcel_ref[base + tall : base + 2 * tall, :] = live[...].astype(jnp.float32)
+    for f in range(angular.shape[0]):
+        rates_ref[f] = jnp.full(rates_ref.shape[1:], angular[f], jnp.float32)
+
+
+class Elements:
+    def __init__(self, parcel, tall):
+        self.parcel, self.tall = parcel, tall
+
+    def __getitem__(self, entry):
+        return self.parcel[entry * self.tall : (entry + 1) * self.tall, :]
+
+    def stiffness(self, entry):
+        return self[entry]
+
+    def mass(self, entry):
+        return self[SIDE * SIDE + entry]
+
+    def edges(self, j):
+        return self[2 * SIDE * SIDE + j].astype(jnp.int32)
+
+    def sigma(self):
+        return self[2 * SIDE * SIDE + SIDE]
+
+    def live(self):
+        return self[2 * SIDE * SIDE + SIDE + 1]
+
+    def forward(self, row):
+        at = (2 * SIDE * SIDE + SIDE + 2) * self.tall + row
+        return self.parcel[at : at + 1, :]
+
+
+def rims_stage(groups, parcel, across_ref, beside_ref, stacked_ref, order_ref):
+    rows = 2 * groups
+    count = stacked_ref.shape[-1] // LANES
     first = row_ids(rows) < groups
     chunks = []
-    for c in range(0, source.shape[-1], LANES):
-        piece = [source[g, :, c : c + LANES] for g in range(groups)]
+    for c in range(count):
+        piece = [parcel[g * count + c : g * count + c + 1, :] for g in range(groups)]
         chunks.append(jnp.concatenate(piece + piece, axis=0))
     put_chunks(stacked_ref, chunks)
-    order = [spread(piece.astype(jnp.float32), rows) for piece in cut(order_ref)]
-    count = len(order)
-    lower = [jnp.where(first, x, o) for x, o in zip(chunks[:count], order)]
-    upper = [jnp.where(first, x, 1.0) for x in chunks[len(chunks) - count :]]
+    rim = order_ref.shape[-1] // LANES
+    numbers = []
+    for c in range(rim):
+        at = groups * count + c * SUBLANES
+        numbers.append(spread(parcel[at : at + 1, :], rows))
+    put_chunks(order_ref, [x.astype(jnp.int32) for x in numbers])
+    lower = [jnp.where(first, x, o) for x, o in zip(chunks[:rim], numbers)]
+    upper = [jnp.where(first, x, 1.0) for x in chunks[count - rim :]]
     put_rims(across_ref, beside_ref, lower, upper)
 
 
-def table_stage(
-    angular, stiffness, mass, sigma, live, edges, places_ref, blocks_ref, scale_ref
-):
-    rows = edges.shape[1]
-    alive = live[...].astype(jnp.float32)
-    weight = sigma[...]
-    freqs = angular.shape[0]
+def table_stage(rates, parcel, places_ref, blocks_ref, scale_ref, edges_ref):
+    rows = edges_ref.shape[1]
+    elements = Elements(parcel, rows)
+    alive = elements.live()
+    weight = elements.sigma()
+    freqs = rates.shape[0]
     peak = None
     for i in range(SIDE):
+        entry = (SIDE + 1) * i
         for f in range(freqs):
-            entry = (SIDE + 1) * i
-            size = stiffness[entry] + angular[f] * weight * mass[entry]
+            size = elements.stiffness(entry) + rates[f] * weight * elements.mass(entry)
             peak = size if peak is None else jnp.maximum(peak, size)
     peak = jnp.max(peak * alive, axis=1, keepdims=True)
     scale = jnp.broadcast_to(jnp.max(peak, axis=0, keepdims=True), scale_ref.shape)
     scale_ref[...] = scale
     alive = alive / scale[:1, :1]
     for entry in range(SIDE * SIDE):
-        stiff = stiffness[entry] * alive
-        heavy = mass[entry] * (weight * alive)
+        stiff = elements.stiffness(entry) * alive
+        heavy = elements.mass(entry) * (weight * alive)
         for f in range(freqs):
-            blocks_ref[f * SIDE * SIDE + entry] = stiff + angular[f] * heavy
+            blocks_ref[f * SIDE * SIDE + entry] = stiff + rates[f] * heavy
+    for j in range(SIDE):
+        edges_ref[j] = elements.edges(j)
     numbers = row_ids(LANES)
 
     def body(i, carry):
         for s in range(rows):
-            lanes = spread(edges[i, s : s + 1, :] & (LANES - 1), LANES)
+            lanes = spread(edges_ref[i, s : s + 1, :] & (LANES - 1), LANES)
             column = pl.ds(pl.multiple_of((i * rows + s) * LANES, LANES), LANES)
             places_ref[:, column] = jnp.where(lanes == numbers, 1.0, 0.0).astype(jnp.bfloat16)
         return carry
@@ -271,7 +365,7 @@
     prior, above = take_rims(across_in, beside_in)
 
     rim = order_ref.shape[-1]
-    order = [spread(piece, rows) for piece in cut(order_ref)]
+    order = cut(order_ref)
     above_order = spread(
         jnp.concatenate([x[groups : groups + 1] for x in above], axis=1), rim
     )
@@ -326,8 +420,11 @@
     *rest,
 ):
     if last:
-        terms_ref, sums_ref, field_ref = rest
+        terms0, terms1, terms_ref, sums_ref, field_ref = rest
         pieces = None
+        groups = terms0.shape[0]
+        terms_ref[groups : 2 * groups] = terms0[...]
+        terms_ref[2 * groups : 3 * groups] = terms1[...]
     else:
         places, terms_ref, sums_ref, image_ref, across_ref, beside_ref, field_ref, pieces = rest
     rows = image_in.shape[0]
@@ -338,7 +435,7 @@
     inverse_scale = 1.0 / scale
     rim = order_ref.shape[-1]
     count = rim // LANES
-    order = [spread(piece, rows) for piece in cut(order_ref)]
+    order = cut(order_ref)
     inverse = cut(inverse_ref)
 
     def rescaled(block):
@@ -366,7 +463,9 @@
     fresh = put_lane(sums, 2 * step, lane_sum(squares(field, count, has_prior)))
     fresh = put_lane(fresh, 2 * step + 1, forms)
     sums_ref[...] = jnp.where(first, fresh, scale)
-    if not last:
+    if last:
+        terms_ref[3 * groups] = scale
+    else:
         image = scatter(pieces, edges, places, len(field))
         put_chunks(image_ref, image)
         put_rims(
@@ -377,20 +476,24 @@
         )
 
 
-def forward_stage(polars, angular, forward, mass, live, edges, picks, heavy_ref, terms_ref):
-    dead = -live[...].astype(jnp.float32)
-    for g in range(forward.shape[0]):
-        rows = [forward[g, :, c : c + LANES] for c in range(0, forward.shape[-1], LANES)]
+def forward_stage(polars, rates, parcel, edges, picks, heavy_ref, terms_ref):
+    groups = terms_ref.shape[0]
+    elements = Elements(parcel, edges.shape[1])
+    mass = [elements.mass(entry) for entry in range(SIDE * SIDE)]
+    dead = -elements.live()
+    count = (parcel.shape[0] - (2 * SIDE * SIDE + SIDE + 2) * edges.shape[1]) // groups
+    for g in range(groups):
+        rows = [elements.forward(g * count + c) for c in range(count)]
         values = times_block(mass, 0, picks_of(rows, edges))
-        factor = dead * angular[g // polars]
+        factor = dead * rates[g // polars]
         values = [factor * value for value in values]
         for i in range(SIDE):
             heavy_ref[g * SIDE + i] = values[i]
         terms_ref[g] = weighted_sum(values, [picks[g * SIDE + i] for i in range(SIDE)])
 
 
-def combine_stage(everyone, sums_in, terms0, terms1, terms2, out_ref):
-    rows = sums_in.shape[0]
+def combine_stage(everyone, terms, out_ref):
+    rows = everyone.shape[1]
     groups = rows // 2
     first = row_ids(rows) < groups
 
@@ -424,23 +527,23 @@
     c2 = y2 / d3
     c1 = y1 / d2 - l3 * c2
     c0 = m[0] / m[1] - l1 * c1 - l2 * c2
-    mine = scale_of(sums_in[...]) * inverse_top
+    mine = terms[3 * groups] * inverse_top
     c0 = c0 * inverse_top
     c1 = c1 * mine * inverse_top
     c2 = c2 * mine * mine * inverse_top
     out = None
-    for terms, c in ((terms0, c0), (terms1, c1), (terms2, c2)):
+    for place, c in enumerate((c2, c0, c1)):
         for g in range(groups):
-            one = terms[g] * spread(c[g : g + 1], out_ref.shape[0])
+            one = terms[place * groups + g] * spread(c[g : g + 1], out_ref.shape[0])
             out = one if out is None else out + one
     out_ref[...] = out
 
 
-def call(kernel, arguments, outs, scratch=(), scalars=0, cost=0):
+def call(kernel, arguments, outs, scratch=(), space=VMEM, cost=0):
     return pl.pallas_call(
         kernel,
         out_shape=outs,
-        in_specs=[SMEM] * scalars + [VMEM] * (len(arguments) - scalars),
+        in_specs=[space] * len(arguments),
         out_specs=jax.tree.map(lambda _: VMEM, outs),
         scratch_shapes=list(scratch),
         cost_estimate=pl.CostEstimate(flops=cost, bytes_accessed=cost, transcendentals=0),
@@ -448,12 +551,20 @@
     )(*arguments)
 
 
-def swap(block, axis, offset):
-    size = lax.axis_size(axis)
+def device_of(partition):
+    return partition ^ 1 if partition // 2 % 2 == 0 else partition
+
+
+def swap(block, offset):
     route = []
-    for low in range(offset, size - 1, 2):
-        route += [(low, low + 1), (low + 1, low)]
-    return lax.ppermute(block, axis, route)
+    for low in range(offset, lax.axis_size("dom") - 1, 2):
+        pair = device_of(low), device_of(low + 1)
+        route += [pair, pair[::-1]]
+    return lax.ppermute(block, "dom", route)
+
+
+def trade(block):
+    return lax.ppermute(block, "dom", [(i, device_of(i)) for i in range(lax.axis_size("dom"))])
 
 
 def gather_all(block, axis):
@@ -492,13 +603,14 @@
     rim = neighbour_map.shape[-1]
     slots = element_edges.shape[-1]
     tall = slots // LANES
-    stiff = stiffness.reshape(SIDE * SIDE, tall, LANES)
-    mass = mass_matrix.reshape(SIDE * SIDE, tall, LANES)
-    edges = element_edges.reshape(SIDE, tall, LANES)
+    matrix = SIDE * SIDE * tall
+    stiff = stiffness.reshape(matrix, LANES)
+    mass = mass_matrix.reshape(matrix, LANES)
+    edges = element_edges.reshape(SIDE * tall, LANES)
     sigma = conductivity.reshape(tall, LANES)
     live = live_slots.reshape(tall, LANES)
-    source = adjoint_source.reshape(groups, 1, edge_count)
-    forward = forward_field.reshape(groups, 1, edge_count)
+    source = adjoint_source.reshape(-1, LANES)
+    forward = forward_field.reshape(-1, LANES)
 
     def shape(*dims, kind=jnp.float32):
         return jax.ShapeDtypeStruct(dims, kind)
@@ -509,24 +621,47 @@
     field_room = pltpu.VMEM((rows, edge_count), jnp.float32)
     piece_room = pltpu.VMEM((rows * SIDE * tall, LANES), jnp.float32)
 
-    across, beside, source = call(
-        rims_stage, (source, neighbour_map), [rim_shape, rim_shape, field_shape]
-    )
-    across, beside = swap(across, "dom", 1), swap(beside, "dom", 0)
-    places, blocks, scale = call(
+    arguments = (source, neighbour_map, angular, stiff, mass, edges, sigma, live, forward)
+    parcel, elements, sigma, rates = call(
+        load_stage,
+        [pltpu.with_memory_space_constraint(x, pltpu.HBM) for x in arguments],
+        [
+            shape(source.shape[0] + rim // LANES * SUBLANES, LANES),
+            shape(2 * matrix + (SIDE + 2) * tall + forward.shape[0], LANES),
+            shape(tall, LANES),
+            shape(freqs, tall, LANES),
+        ],
+        (
+            pltpu.VMEM(neighbour_map.shape, neighbour_map.dtype),
+            pltpu.SMEM(angular.shape, angular.dtype),
+            pltpu.VMEM(edges.shape, edges.dtype),
+            pltpu.VMEM(live.shape, live.dtype),
+            pltpu.SemaphoreType.DMA((len(arguments),)),
+        ),
+        space=HBM,
+    )
+    parcel = trade(parcel)
+    elements = trade(elements)
+    across, beside, source, order = call(
+        functools.partial(rims_stage, groups),
+        (parcel,),
+        [rim_shape, rim_shape, field_shape, shape(rows, rim, kind=jnp.int32)],
+    )
+    across, beside = swap(across, 1), swap(beside, 0)
+    places, blocks, scale, edges = call(
         table_stage,
-        (angular, stiff, mass, sigma, live, edges),
+        (rates, elements),
         [
             shape(LANES, SIDE * slots, kind=jnp.bfloat16),
             shape(freqs * SIDE * SIDE, tall, LANES),
             sums_shape,
+            shape(SIDE, tall, LANES, kind=jnp.int32),
         ],
-        scalars=1,
         cost=4_000_000,
     )
     picks, image, across, beside, inverse, sums = call(
         functools.partial(first_stage, polars),
-        (source, neighbour_map, across, beside, scale, blocks, edges, places),
+        (source, order, across, beside, scale, blocks, edges, places),
         [
             picks_shape,
             field_shape,
@@ -537,34 +672,33 @@
         ],
         (field_room, piece_room),
     )
-    across, beside = swap(across, "dom", 1), swap(beside, "dom", 0)
+    across, beside = swap(across, 1), swap(beside, 0)
     heavy, terms0 = call(
         functools.partial(forward_stage, polars),
-        (angular, forward, mass, live, edges, picks),
+        (rates, elements, edges, picks),
         [picks_shape, terms_shape],
-        scalars=1,
         cost=4_000_000,
     )
     terms1, sums, image, across, beside = call(
         functools.partial(later_stage, polars, 1, False),
-        (image, neighbour_map, inverse, across, beside, sums, blocks, edges, heavy, places),
+        (image, order, inverse, across, beside, sums, blocks, edges, heavy, places),
         [terms_shape, sums_shape, field_shape, rim_shape, rim_shape],
         (field_room, piece_room),
     )
-    across, beside = swap(across, "dom", 1), swap(beside, "dom", 0)
-    terms2, sums = call(
+    across, beside = swap(across, 1), swap(beside, 0)
+    terms, sums = call(
         functools.partial(later_stage, polars, 2, True),
-        (image, neighbour_map, inverse, across, beside, sums, blocks, edges, heavy),
-        [terms_shape, sums_shape],
+        (image, order, inverse, across, beside, sums, blocks, edges, heavy, terms0, terms1),
+        [shape(3 * groups + 1, tall, LANES), sums_shape],
         (field_room,),
     )
     term = call(
         combine_stage,
-        (gather_all(sums, "dom"), sums, terms0, terms1, terms2),
+        (gather_all(sums, "dom"), trade(terms)),
         shape(tall, LANES),
     )
     gradient = sum_over(term, "freq").reshape(1, slots)
-    updated = conductivity * jnp.exp(-0.5 * jnp.tanh(gradient))
+    updated = sigma.reshape(1, slots) * jnp.exp(-0.5 * jnp.tanh(gradient))
     return gradient, updated
 
 

time: 45.3 us -> 46.8 us (1.033)
  waiting for transfers between devices: 4.78 us -> 11.6 us
  local copies, waits for them, and re-layouts: 6.7 us -> 0.01 us
  starting transfers between devices: 16.8 us -> 19.4 us
  blocking collectives: 9.78 us -> 8.7 us
    ppermute x6 -> x9, waiting for transfers between devices: 0.84 us -> 7.7 us  [the longest x6 6.57 us: swap(): return lax.ppermute(block, 'dom', route)]
    unnamed x30 -> x2, local copies, waits for them, and re-layouts: 6.69 us -> 0.01 us
    ppermute x6 -> x9, starting transfers between devices: 12.6 us -> 15.1 us  [the longest x6 8.88 us: swap(): return lax.ppermute(block, 'dom', route)]
    all_to_all x1, blocking collectives: 9.78 us -> 8.7 us  [gather_all(): return lax.all_to_all(copies, axis, 0, 0)]
    pallas_call x7 -> x8, Pallas kernels: 5.31 us -> 5.4 us  [call(): pl.pallas_call(kernel, out_shape=outs, in_specs=[space] * len(arguments),...]
  transfers between devices with their start and end apart: 8 -> 11, of which waited for: 3 -> 6; matrix products, arithmetic and copies ran while one was open for 0% -> 0% of each run, Pallas kernels for 5% -> 2%
where the time goes in v4:
time: 46.8 us; the launch traced here: 46.5 us
  starting transfers between devices  19.4 us (41%)
  waiting for transfers between devices  11.6 us (25%)
  blocking collectives  8.7 us (19%)
  Pallas kernels  5.4 us (12%)
  between operations  0.77 us (2%)
  other arithmetic  0.62 us (1%)
    ppermute x6, starting transfers between devices, swap(): return lax.ppermute(block, 'dom', route)  8.88 us
    all_to_all x1, blocking collectives, gather_all(): return lax.all_to_all(copies, axis, 0, 0)  8.7 us
    ppermute x6, waiting for transfers between devices, swap(): return lax.ppermute(block, 'dom', route)  6.57 us
    ppermute x3, starting transfers between devices, trade(): lax.ppermute(block, 'dom', [(i, device_of(i)) for i in range(lax.axis_siz...  6.24 us
    pallas_call x8, Pallas kernels, call(): pl.pallas_call(kernel, out_shape=outs, in_specs=[space] * len(arguments),...  5.4 us
    ppermute x2, starting transfers between devices, sum_over(): lax.ppermute(block, axis, [(i, i ^ step) for i in range(size)])  4.23 us
    ppermute x2, waiting for transfers between devices, sum_over(): lax.ppermute(block, axis, [(i, i ^ step) for i in range(size)])  3.95 us
    ppermute x3, waiting for transfers between devices, trade(): lax.ppermute(block, 'dom', [(i, device_of(i)) for i in range(lax.axis_siz...  1.13 us
  transfers between devices with their start and end apart: 11, of which 6 were waited for; matrix products, arithmetic and copies ran while one was open for 0% of the time, Pallas kernels for 2%

profile of v4, /device:TPU:0, one launch (start us, length us, event | category | flops | bytes accessed | tf_op | source)
XLA Modules:
  0.0 46.5 jit_solution(9669607402221488912)
XLA Ops:
  0.6 1.2 %shard_map.104 = (f32[56,128]{1,0:T(8,128)S(1)}, f32[680,128]{1,0:T(8,128)S(1)}, f32[8,128]{1,0:T(8,128)S(1)}, f32[2,8,128]{2,1,0:T(8,128)S(1)}) custom-call(f32[40,128]{1,0:T(8,128)} %bitcast.13, s32[1,256]{1,0:T(1,128)} %order_in.1, f32[2]{0:T(128)} %angular_in.1, f32[288,128]{1,0:T(8,128)} %bitcast.10, f32[288,128]{1,0:T(8,128)} %bitcast.11, ...), custom_call_target="tpu_custom_call" | custom-call | tf_op jit(solution)/shard_map/pallas_call | solution.py:543
  1.8 2.4 %collective-permute-start.3 = (f32[680,128]{1,0:T(8,128)S(1)}, f32[680,128]{1,0:T(8,128)S(1)}, u32[]{:S(2)}, u32[]{:S(2)}) collective-permute-start(f32[680,128]{1,0:T(8,128)S(1)} %get-tuple-element.35), channel_id=1, source_target_pairs={{0,1},{1,0},{2,2},{3,3},{4,5},{5,4},{6,6},{7,7},{8,9},{9,8},{10,10... | collective-permute-start | bytes 1044488 | tf_op jit(solution)/shard_map/ppermute | solution.py:567
  4.2 2.0 %collective-permute-start = (f32[56,128]{1,0:T(8,128)S(1)}, f32[56,128]{1,0:T(8,128)S(1)}, u32[]{:S(2)}, u32[]{:S(2)}) collective-permute-start(f32[56,128]{1,0:T(8,128)S(1)} %get-tuple-element.29), channel_id=1, source_target_pairs={{0,1},{1,0},{2,2},{3,3},{4,5},{5,4},{6,6},{7,7},{8,9},{9,8},{10,10... | collective-permute-start | bytes 86024 | tf_op jit(solution)/shard_map/ppermute | solution.py:567
  6.1 1.1 %collective-permute-done.parcel = f32[56,128]{1,0:T(8,128)S(1)} collective-permute-done((f32[56,128]{1,0:T(8,128)S(1)}, f32[56,128]{1,0:T(8,128)S(1)}, u32[]{:S(2)}, u32[]{:S(2)}) %collective-permute-start) | collective-permute-done | bytes 28704 | tf_op jit(solution)/shard_map/ppermute | solution.py:567
  7.3 1.9 %collective-permute-start.1 = (f32[8,256]{1,0:T(8,128)S(1)}, f32[8,256]{1,0:T(8,128)S(1)}, u32[]{:S(2)}, u32[]{:S(2)}) collective-permute-start(f32[8,256]{1,0:T(8,128)S(1)} %get-tuple-element.32), channel_id=1, source_target_pairs={{0,2},{2,0},{3,5},{5,3},{4,6},{6,4},{8,10},{10,8},{11,13},{13,11},... | collective-permute-start | bytes 24584 | tf_op jit(solution)/shard_map/ppermute | solution.py:563
  9.3 0.7 %shard_map.106 = (bf16[128,6144]{1,0:T(8,128)(2,1)S(1)}, f32[72,8,128]{2,1,0:T(8,128)S(1)}, f32[8,128]{1,0:T(8,128)S(1)}, s32[6,8,128]{2,1,0:T(8,128)S(1)}) custom-call(f32[2,8,128]{2,1,0:T(8,128)S(1)} %get-tuple-element.34.rates, f32[680,128]{1,0:T(8,128)S(1)} %collective-permute-done.3.parcel), custom_call_target="tpu_custom_call" | custom-call | flops 4000000 | bytes 4000000 | tf_op jit(solution)/shard_map/pallas_call | solution.py:543
  10.0 2.8 %collective-permute-done.1.across_in = f32[8,256]{1,0:T(8,128)S(1)} collective-permute-done((f32[8,256]{1,0:T(8,128)S(1)}, f32[8,256]{1,0:T(8,128)S(1)}, u32[]{:S(2)}, u32[]{:S(2)}) %collective-permute-start.1) | collective-permute-done | bytes 8224 | tf_op jit(solution)/shard_map/ppermute | solution.py:563
  12.8 1.3 %shard_map.107 = (f32[24,8,128]{2,1,0:T(8,128)S(1)}, f32[8,1280]{1,0:T(8,128)S(1)}, f32[8,256]{1,0:T(8,128)S(1)}, f32[8,256]{1,0:T(8,128)S(1)}, s32[8,256]{1,0:T(8,128)S(1)}, /*index=5*/f32[8,128]{1,0:T(8,128)S(1)}) custom-call(f32[8,1280]{1,0:T(8,128)S(1)} %get-tuple-element.30.source, s32[8,256]{1,0:T(8,128)S(1)} %get-tuple-element.31.order_ref, ...), custom_call_target="tpu_custom_call" | custom-call | tf_op jit(solution)/shard_map/pallas_call | solution.py:543
  14.1 3.4 %collective-permute-start.4 = (f32[8,256]{1,0:T(8,128)S(1)}, f32[8,256]{1,0:T(8,128)S(1)}, u32[]{:S(2)}, u32[]{:S(2)}) collective-permute-start(f32[8,256]{1,0:T(8,128)S(1)} %get-tuple-element.42), channel_id=1, source_target_pairs={{0,2},{2,0},{3,5},{5,3},{4,6},{6,4},{8,10},{10,8},{11,13},{13,11},... | collective-permute-start | bytes 24584 | tf_op jit(solution)/shard_map/ppermute | solution.py:563
  17.5 0.1 collective-permute-start.5
  17.6 0.4 shard_map.108
  18.0 1.7 %collective-permute-done.4.across_in = f32[8,256]{1,0:T(8,128)S(1)} collective-permute-done((f32[8,256]{1,0:T(8,128)S(1)}, f32[8,256]{1,0:T(8,128)S(1)}, u32[]{:S(2)}, u32[]{:S(2)}) %collective-permute-start.4) | collective-permute-done | bytes 8224 | tf_op jit(solution)/shard_map/ppermute | solution.py:563
  19.6 1.2 %shard_map.109 = (f32[4,8,128]{2,1,0:T(8,128)S(1)}, f32[8,128]{1,0:T(8,128)S(1)}, f32[8,1280]{1,0:T(8,128)S(1)}, f32[8,256]{1,0:T(8,128)S(1)}, f32[8,256]{1,0:T(8,128)S(1)}) custom-call(f32[8,1280]{1,0:T(8,128)S(1)} %get-tuple-element.40.image_in, s32[8,256]{1,0:T(8,128)S(1)} %get-tuple-element.31.order_ref, s32[8,256]{1,0:T(8,128)S(1)} %get-tuple-element.41.inverse_ref, ...), custom_call_target="tpu_custom_call" | custom-call | tf_op jit(solution)/shard_map/pallas_call | solution.py:543
  20.8 3.4 %collective-permute-start.6 = (f32[8,256]{1,0:T(8,128)S(1)}, f32[8,256]{1,0:T(8,128)S(1)}, u32[]{:S(2)}, u32[]{:S(2)}) collective-permute-start(f32[8,256]{1,0:T(8,128)S(1)} %get-tuple-element.48), channel_id=1, source_target_pairs={{0,2},{2,0},{3,5},{5,3},{4,6},{6,4},{8,10},{10,8},{11,13},{13,11},... | collective-permute-start | bytes 24584 | tf_op jit(solution)/shard_map/ppermute | solution.py:563
  24.3 2.1 %collective-permute-done.6.across_in = f32[8,256]{1,0:T(8,128)S(1)} collective-permute-done((f32[8,256]{1,0:T(8,128)S(1)}, f32[8,256]{1,0:T(8,128)S(1)}, u32[]{:S(2)}, u32[]{:S(2)}) %collective-permute-start.6) | collective-permute-done | bytes 8224 | tf_op jit(solution)/shard_map/ppermute | solution.py:563
  26.4 0.6 %shard_map.110 = (f32[13,8,128]{2,1,0:T(8,128)S(1)}, f32[8,128]{1,0:T(8,128)S(1)}) custom-call(f32[8,1280]{1,0:T(8,128)S(1)} %get-tuple-element.47.image_in, s32[8,256]{1,0:T(8,128)S(1)} %get-tuple-element.31.order_ref, s32[8,256]{1,0:T(8,128)S(1)} %get-tuple-element.41.inverse_ref, f32[8,256]{1,0:T(8,128)S(1)} %collective-permute-done.6.across_in, ...), custom_call_target="tpu_custom_call" | custom-call | tf_op jit(solution)/shard_map/pallas_call | solution.py:543
  26.9 1.9 %collective-permute-start.8 = (f32[13,8,128]{2,1,0:T(8,128)S(1)}, f32[13,8,128]{2,1,0:T(8,128)S(1)}, u32[]{:S(2)}, u32[]{:S(2)}) collective-permute-start(f32[13,8,128]{2,1,0:T(8,128)S(1)} %get-tuple-element.54), channel_id=1, source_target_pairs={{0,1},{1,0},{2,2},{3,3},{4,5},{5,4},{6,6},{7,7},{8,9},{9,8},{10,10... | collective-permute-start | bytes 159752 | tf_op jit(solution)/shard_map/ppermute | solution.py:567
  28.9 8.7 %all_to_all.5.everyone = f32[8,8,128]{2,1,0:T(8,128)S(1)} all-to-all(f32[8,8,128]{2,1,0:T(8,128)S(1)} %broadcast_in_dim.2), channel_id=1, replica_groups=mesh['freq'=4,'dom'=8] {'dom'}, dimensions={0} | all-to-all | bytes 65536 | tf_op jit(solution)/shard_map/all_to_all | solution.py:573
  37.6 0.1 shard_map.111
  37.7 1.6 %collective-permute-start.9 = (f32[8,128]{1,0:T(8,128)S(1)}, f32[8,128]{1,0:T(8,128)S(1)}, u32[]{:S(2)}, u32[]{:S(2)}) collective-permute-start(f32[8,128]{1,0:T(8,128)S(1)} %shard_map.111), channel_id=1, source_target_pairs={{0,8},{8,0},{16,24},{24,16},{1,9},{9,1},{17,25},{25,17},{2,10},{10... | collective-permute-start | bytes 12296 | tf_op jit(solution)/shard_map/ppermute | solution.py:582
  39.3 2.0 %collective-permute-done.9 = f32[8,128]{1,0:T(8,128)S(1)} collective-permute-done((f32[8,128]{1,0:T(8,128)S(1)}, f32[8,128]{1,0:T(8,128)S(1)}, u32[]{:S(2)}, u32[]{:S(2)}) %collective-permute-start.9) | collective-permute-done | bytes 4128 | tf_op jit(solution)/shard_map/ppermute | solution.py:582
  41.4 2.6 %collective-permute-start.10 = (f32[8,128]{1,0:T(8,128)S(1)}, f32[8,128]{1,0:T(8,128)S(1)}, u32[]{:S(2)}, u32[]{:S(2)}) collective-permute-start(f32[8,128]{1,0:T(8,128)S(1)} %add.6), channel_id=1, source_target_pairs={{0,16},{8,24},{16,0},{24,8},{1,17},{9,25},{17,1},{25,9},{2,18},{10... | collective-permute-start | bytes 12296 | tf_op jit(solution)/shard_map/ppermute | solution.py:582
  44.0 1.9 %collective-permute-done.10 = f32[8,128]{1,0:T(8,128)S(1)} collective-permute-done((f32[8,128]{1,0:T(8,128)S(1)}, f32[8,128]{1,0:T(8,128)S(1)}, u32[]{:S(2)}, u32[]{:S(2)}) %collective-permute-start.10) | collective-permute-done | bytes 4128 | tf_op jit(solution)/shard_map/ppermute | solution.py:582
  45.9 0.6 %exponential_multiply_fusion = f32[1,1024]{1,0:T(1,128)} fusion(f32[1,1024]{1,0:T(1,128)S(1)} %bitcast.9, f32[1,1024]{1,0:T(1,128)S(1)} %bitcast.15), kind=kLoop, calls=%fused_computation | loop fusion | flops 2048 | bytes 12288 | tf_op jit(solution)/shard_map/mul | solution.py:701
  (13 shorter events, 0.2 us)
Async XLA Ops:
  1.8 7.5 %collective-permute-start.3 = (f32[680,128]{1,0:T(8,128)S(1)}, f32[680,128]{1,0:T(8,128)S(1)}, u32[]{:S(2)}, u32[]{:S(2)}) collective-permute-start(f32[680,128]{1,0:T(8,128)S(1)} %get-tuple-element.35), channel_id=1, source_target_pairs={{0,1},{1,0},{2,2},{3,3},{4,5},{5,4},{6,6},{7,7},{8,9},{9,8},{10,10... | collective-permute-start | bytes 1044488 | tf_op jit(solution)/shard_map/ppermute | solution.py:567
  4.2 3.1 %collective-permute-start = (f32[56,128]{1,0:T(8,128)S(1)}, f32[56,128]{1,0:T(8,128)S(1)}, u32[]{:S(2)}, u32[]{:S(2)}) collective-permute-start(f32[56,128]{1,0:T(8,128)S(1)} %get-tuple-element.29), channel_id=1, source_target_pairs={{0,1},{1,0},{2,2},{3,3},{4,5},{5,4},{6,6},{7,7},{8,9},{9,8},{10,10... | collective-permute-start | bytes 86024 | tf_op jit(solution)/shard_map/ppermute | solution.py:567
  7.3 5.5 %collective-permute-start.1 = (f32[8,256]{1,0:T(8,128)S(1)}, f32[8,256]{1,0:T(8,128)S(1)}, u32[]{:S(2)}, u32[]{:S(2)}) collective-permute-start(f32[8,256]{1,0:T(8,128)S(1)} %get-tuple-element.32), channel_id=1, source_target_pairs={{0,2},{2,0},{3,5},{5,3},{4,6},{6,4},{8,10},{10,8},{11,13},{13,11},... | collective-permute-start | bytes 24584 | tf_op jit(solution)/shard_map/ppermute | solution.py:563
  9.2 3.6 %collective-permute-start.2 = (f32[8,256]{1,0:T(8,128)S(1)}, f32[8,256]{1,0:T(8,128)S(1)}, u32[]{:S(2)}, u32[]{:S(2)}) collective-permute-start(f32[8,256]{1,0:T(8,128)S(1)} %get-tuple-element.33), channel_id=1, source_target_pairs={{1,0},{0,1},{2,3},{3,2},{5,4},{4,5},{6,7},{7,6},{9,8},{8,9},{10,11... | collective-permute-start | bytes 24584 | tf_op jit(solution)/shard_map/ppermute | solution.py:563
  14.1 5.5 %collective-permute-start.4 = (f32[8,256]{1,0:T(8,128)S(1)}, f32[8,256]{1,0:T(8,128)S(1)}, u32[]{:S(2)}, u32[]{:S(2)}) collective-permute-start(f32[8,256]{1,0:T(8,128)S(1)} %get-tuple-element.42), channel_id=1, source_target_pairs={{0,2},{2,0},{3,5},{5,3},{4,6},{6,4},{8,10},{10,8},{11,13},{13,11},... | collective-permute-start | bytes 24584 | tf_op jit(solution)/shard_map/ppermute | solution.py:563
  17.5 2.2 %collective-permute-start.5 = (f32[8,256]{1,0:T(8,128)S(1)}, f32[8,256]{1,0:T(8,128)S(1)}, u32[]{:S(2)}, u32[]{:S(2)}) collective-permute-start(f32[8,256]{1,0:T(8,128)S(1)} %get-tuple-element.43), channel_id=1, source_target_pairs={{1,0},{0,1},{2,3},{3,2},{5,4},{4,5},{6,7},{7,6},{9,8},{8,9},{10,11... | collective-permute-start | bytes 24584 | tf_op jit(solution)/shard_map/ppermute | solution.py:563
  20.8 5.5 %collective-permute-start.6 = (f32[8,256]{1,0:T(8,128)S(1)}, f32[8,256]{1,0:T(8,128)S(1)}, u32[]{:S(2)}, u32[]{:S(2)}) collective-permute-start(f32[8,256]{1,0:T(8,128)S(1)} %get-tuple-element.48), channel_id=1, source_target_pairs={{0,2},{2,0},{3,5},{5,3},{4,6},{6,4},{8,10},{10,8},{11,13},{13,11},... | collective-permute-start | bytes 24584 | tf_op jit(solution)/shard_map/ppermute | solution.py:563
  24.2 2.2 %collective-permute-start.7 = (f32[8,256]{1,0:T(8,128)S(1)}, f32[8,256]{1,0:T(8,128)S(1)}, u32[]{:S(2)}, u32[]{:S(2)}) collective-permute-start(f32[8,256]{1,0:T(8,128)S(1)} %get-tuple-element.49), channel_id=1, source_target_pairs={{1,0},{0,1},{2,3},{3,2},{5,4},{4,5},{6,7},{7,6},{9,8},{8,9},{10,11... | collective-permute-start | bytes 24584 | tf_op jit(solution)/shard_map/ppermute | solution.py:563
  26.9 10.6 %collective-permute-start.8 = (f32[13,8,128]{2,1,0:T(8,128)S(1)}, f32[13,8,128]{2,1,0:T(8,128)S(1)}, u32[]{:S(2)}, u32[]{:S(2)}) collective-permute-start(f32[13,8,128]{2,1,0:T(8,128)S(1)} %get-tuple-element.54), channel_id=1, source_target_pairs={{0,1},{1,0},{2,2},{3,3},{4,5},{5,4},{6,6},{7,7},{8,9},{9,8},{10,10... | collective-permute-start | bytes 159752 | tf_op jit(solution)/shard_map/ppermute | solution.py:567
  37.7 3.7 %collective-permute-start.9 = (f32[8,128]{1,0:T(8,128)S(1)}, f32[8,128]{1,0:T(8,128)S(1)}, u32[]{:S(2)}, u32[]{:S(2)}) collective-permute-start(f32[8,128]{1,0:T(8,128)S(1)} %shard_map.111), channel_id=1, source_target_pairs={{0,8},{8,0},{16,24},{24,16},{1,9},{9,1},{17,25},{25,17},{2,10},{10... | collective-permute-start | bytes 12296 | tf_op jit(solution)/shard_map/ppermute | solution.py:582
  41.4 4.5 %collective-permute-start.10 = (f32[8,128]{1,0:T(8,128)S(1)}, f32[8,128]{1,0:T(8,128)S(1)}, u32[]{:S(2)}, u32[]{:S(2)}) collective-permute-start(f32[8,128]{1,0:T(8,128)S(1)} %add.6), channel_id=1, source_target_pairs={{0,16},{8,24},{16,0},{24,8},{1,17},{9,25},{17,1},{25,9},{2,18},{10... | collective-permute-start | bytes 12296 | tf_op jit(solution)/shard_map/ppermute | solution.py:582
  45.9 0.6 %copy-start = (f32[8,128]{1,0:T(8,128)}, f32[8,128]{1,0:T(8,128)S(1)}, u32[]{:S(2)}) copy-start(f32[8,128]{1,0:T(8,128)S(1)} %add.7) | copy-start | bytes 12292

commit v5 on v1

--- a/solution.py
+++ b/solution.py
@@ -11,7 +11,7 @@
 SUBLANES = 8
 SIDE = 6
 VMEM = pl.BlockSpec(memory_space=pltpu.VMEM)
-SMEM = pl.BlockSpec(memory_space=pltpu.SMEM)
+HBM = pl.BlockSpec(memory_space=pltpu.HBM)
 
 PICK_LANES = lax.GatherDimensionNumbers(
     offset_dims=(),
@@ -175,7 +175,21 @@
     return total
 
 
-def rims_stage(source, order_ref, across_ref, beside_ref, stacked_ref):
+def start_copies(routes, arrived):
+    copies = [
+        pltpu.make_async_copy(here, there, arrived.at[n])
+        for n, (here, there) in enumerate(routes)
+    ]
+    for copy in copies:
+        copy.start()
+    return copies
+
+
+def rims_stage(
+    source_in, order_in, across_ref, beside_ref, stacked_ref, order_ref, source, order, arrived
+):
+    for copy in start_copies(((source_in, source), (order_in, order)), arrived):
+        copy.wait()
     groups = source.shape[0]
     rows = stacked_ref.shape[0]
     first = row_ids(rows) < groups
@@ -184,25 +198,71 @@
         piece = [source[g, :, c : c + LANES] for g in range(groups)]
         chunks.append(jnp.concatenate(piece + piece, axis=0))
     put_chunks(stacked_ref, chunks)
-    order = [spread(piece.astype(jnp.float32), rows) for piece in cut(order_ref)]
-    count = len(order)
-    lower = [jnp.where(first, x, o) for x, o in zip(chunks[:count], order)]
+    order_ref[...] = spread(order[...], rows)
+    numbers = [x.astype(jnp.float32) for x in cut(order_ref)]
+    count = len(numbers)
+    lower = [jnp.where(first, x, o) for x, o in zip(chunks[:count], numbers)]
     upper = [jnp.where(first, x, 1.0) for x in chunks[len(chunks) - count :]]
     put_rims(across_ref, beside_ref, lower, upper)
 
 
 def table_stage(
-    angular, stiffness, mass, sigma, live, edges, places_ref, blocks_ref, scale_ref
+    angular_in,
+    stiffness_in,
+    mass_in,
+    sigma_in,
+    live_in,
+    edges_in,
+    forward_in,
+    places_ref,
+    blocks_ref,
+    scale_ref,
+    rates,
+    mass,
+    sigma,
+    live,
+    edges,
+    forward_ref,
+    angular,
+    stiffness,
+    arrived,
 ):
+    copies = start_copies(
+        (
+            (edges_in, edges),
+            (angular_in, angular),
+            (sigma_in, sigma),
+            (live_in, live),
+            (stiffness_in, stiffness),
+            (mass_in, mass),
+            (forward_in, forward_ref),
+        ),
+        arrived,
+    )
+    copies[0].wait()
+    numbers = row_ids(LANES)
     rows = edges.shape[1]
+
+    def body(i, carry):
+        for s in range(rows):
+            lanes = spread(edges[i, s : s + 1, :] & (LANES - 1), LANES)
+            column = pl.ds(pl.multiple_of((i * rows + s) * LANES, LANES), LANES)
+            places_ref[:, column] = jnp.where(lanes == numbers, 1.0, 0.0).astype(jnp.bfloat16)
+        return carry
+
+    lax.fori_loop(0, SIDE, body, 0)
+    for copy in copies[1:]:
+        copy.wait()
+    for f in range(angular.shape[0]):
+        rates[f] = jnp.full(rates.shape[1:], angular[f], jnp.float32)
     alive = live[...].astype(jnp.float32)
     weight = sigma[...]
-    freqs = angular.shape[0]
+    freqs = rates.shape[0]
     peak = None
     for i in range(SIDE):
         for f in range(freqs):
             entry = (SIDE + 1) * i
-            size = stiffness[entry] + angular[f] * weight * mass[entry]
+            size = stiffness[entry] + rates[f] * weight * mass[entry]
             peak = size if peak is None else jnp.maximum(peak, size)
     peak = jnp.max(peak * alive, axis=1, keepdims=True)
     scale = jnp.broadcast_to(jnp.max(peak, axis=0, keepdims=True), scale_ref.shape)
@@ -212,17 +272,7 @@
         stiff = stiffness[entry] * alive
         heavy = mass[entry] * (weight * alive)
         for f in range(freqs):
-            blocks_ref[f * SIDE * SIDE + entry] = stiff + angular[f] * heavy
-    numbers = row_ids(LANES)
-
-    def body(i, carry):
-        for s in range(rows):
-            lanes = spread(edges[i, s : s + 1, :] & (LANES - 1), LANES)
-            column = pl.ds(pl.multiple_of((i * rows + s) * LANES, LANES), LANES)
-            places_ref[:, column] = jnp.where(lanes == numbers, 1.0, 0.0).astype(jnp.bfloat16)
-        return carry
-
-    lax.fori_loop(0, SIDE, body, 0)
+            blocks_ref[f * SIDE * SIDE + entry] = stiff + rates[f] * heavy
 
 
 def apply_all(field_ref, blocks, edges, polars, groups, pieces, visit):
@@ -271,7 +321,7 @@
     prior, above = take_rims(across_in, beside_in)
 
     rim = order_ref.shape[-1]
-    order = [spread(piece, rows) for piece in cut(order_ref)]
+    order = cut(order_ref)
     above_order = spread(
         jnp.concatenate([x[groups : groups + 1] for x in above], axis=1), rim
     )
@@ -338,7 +388,7 @@
     inverse_scale = 1.0 / scale
     rim = order_ref.shape[-1]
     count = rim // LANES
-    order = [spread(piece, rows) for piece in cut(order_ref)]
+    order = cut(order_ref)
     inverse = cut(inverse_ref)
 
     def rescaled(block):
@@ -377,12 +427,12 @@
         )
 
 
-def forward_stage(polars, angular, forward, mass, live, edges, picks, heavy_ref, terms_ref):
+def forward_stage(polars, rates, forward, mass, live, edges, picks, heavy_ref, terms_ref):
     dead = -live[...].astype(jnp.float32)
     for g in range(forward.shape[0]):
         rows = [forward[g, :, c : c + LANES] for c in range(0, forward.shape[-1], LANES)]
         values = times_block(mass, 0, picks_of(rows, edges))
-        factor = dead * angular[g // polars]
+        factor = dead * rates[g // polars]
         values = [factor * value for value in values]
         for i in range(SIDE):
             heavy_ref[g * SIDE + i] = values[i]
@@ -436,11 +486,15 @@
     out_ref[...] = out
 
 
-def call(kernel, arguments, outs, scratch=(), scalars=0, cost=0):
+def pinned(*arguments):
+    return [pltpu.with_memory_space_constraint(x, pltpu.HBM) for x in arguments]
+
+
+def call(kernel, arguments, outs, scratch=(), space=VMEM, cost=0):
     return pl.pallas_call(
         kernel,
         out_shape=outs,
-        in_specs=[SMEM] * scalars + [VMEM] * (len(arguments) - scalars),
+        in_specs=[space] * len(arguments),
         out_specs=jax.tree.map(lambda _: VMEM, outs),
         scratch_shapes=list(scratch),
         cost_estimate=pl.CostEstimate(flops=cost, bytes_accessed=cost, transcendentals=0),
@@ -466,7 +520,14 @@
     size = lax.axis_size(axis)
     if size & (size - 1):
         return jnp.sum(gather_all(block, axis), axis=0)
-    step = 1
+    near = min(size, 4)
+    parts = [block] + [None] * (near - 1)
+    for step in reversed(range(1, near)):
+        parts[step] = lax.ppermute(block, axis, [(i, i ^ step) for i in range(size)])
+    while len(parts) > 1:
+        parts = [a + b for a, b in zip(parts[::2], parts[1::2])]
+    block = parts[0]
+    step = near
     while step < size:
         block = block + lax.ppermute(block, axis, [(i, i ^ step) for i in range(size)])
         step *= 2
@@ -509,24 +570,40 @@
     field_room = pltpu.VMEM((rows, edge_count), jnp.float32)
     piece_room = pltpu.VMEM((rows * SIDE * tall, LANES), jnp.float32)
 
-    across, beside, source = call(
-        rims_stage, (source, neighbour_map), [rim_shape, rim_shape, field_shape]
+    across, beside, source, order = call(
+        rims_stage,
+        pinned(source, neighbour_map),
+        [rim_shape, rim_shape, field_shape, shape(rows, rim, kind=jnp.int32)],
+        (
+            pltpu.VMEM(source.shape, source.dtype),
+            pltpu.VMEM(neighbour_map.shape, neighbour_map.dtype),
+            pltpu.SemaphoreType.DMA((2,)),
+        ),
+        space=HBM,
     )
     across, beside = swap(across, "dom", 1), swap(beside, "dom", 0)
-    places, blocks, scale = call(
+    kept = [jax.ShapeDtypeStruct(x.shape, x.dtype) for x in (mass, sigma, live, edges, forward)]
+    places, blocks, scale, rates, mass, sigma, live, edges, forward = call(
         table_stage,
-        (angular, stiff, mass, sigma, live, edges),
+        pinned(angular, stiff, mass, sigma, live, edges, forward),
         [
             shape(LANES, SIDE * slots, kind=jnp.bfloat16),
             shape(freqs * SIDE * SIDE, tall, LANES),
             sums_shape,
+            shape(freqs, tall, LANES),
+            *kept,
         ],
-        scalars=1,
+        (
+            pltpu.SMEM(angular.shape, angular.dtype),
+            pltpu.VMEM(stiff.shape, stiff.dtype),
+            pltpu.SemaphoreType.DMA((7,)),
+        ),
+        space=HBM,
         cost=4_000_000,
     )
     picks, image, across, beside, inverse, sums = call(
         functools.partial(first_stage, polars),
-        (source, neighbour_map, across, beside, scale, blocks, edges, places),
+        (source, order, across, beside, scale, blocks, edges, places),
         [
             picks_shape,
             field_shape,
@@ -540,21 +617,20 @@
     across, beside = swap(across, "dom", 1), swap(beside, "dom", 0)
     heavy, terms0 = call(
         functools.partial(forward_stage, polars),
-        (angular, forward, mass, live, edges, picks),
+        (rates, forward, mass, live, edges, picks),
         [picks_shape, terms_shape],
-        scalars=1,
         cost=4_000_000,
     )
     terms1, sums, image, across, beside = call(
         functools.partial(later_stage, polars, 1, False),
-        (image, neighbour_map, inverse, across, beside, sums, blocks, edges, heavy, places),
+        (image, order, inverse, across, beside, sums, blocks, edges, heavy, places),
         [terms_shape, sums_shape, field_shape, rim_shape, rim_shape],
         (field_room, piece_room),
     )
     across, beside = swap(across, "dom", 1), swap(beside, "dom", 0)
     terms2, sums = call(
         functools.partial(later_stage, polars, 2, True),
-        (image, neighbour_map, inverse, across, beside, sums, blocks, edges, heavy),
+        (image, order, inverse, across, beside, sums, blocks, edges, heavy),
         [terms_shape, sums_shape],
         (field_room,),
     )
@@ -564,7 +640,7 @@
         shape(tall, LANES),
     )
     gradient = sum_over(term, "freq").reshape(1, slots)
-    updated = conductivity * jnp.exp(-0.5 * jnp.tanh(gradient))
+    updated = sigma.reshape(1, slots) * jnp.exp(-0.5 * jnp.tanh(gradient))
     return gradient, updated
 
 

time: 45.3 us -> 40.1 us (0.89)
  local copies, waits for them, and re-layouts: 6.7 us -> 0.01 us
  starting transfers between devices: 16.8 us -> 17.4 us
  blocking collectives: 9.78 us -> 10.3 us
  Pallas kernels: 5.31 us -> 5.79 us
    unnamed x30 -> x2, local copies, waits for them, and re-layouts: 6.69 us -> 0.01 us
    all_to_all x1, blocking collectives: 9.78 us -> 10.3 us  [gather_all(): return lax.all_to_all(copies, axis, 0, 0)]
    pallas_call x7, Pallas kernels: 5.31 us -> 5.79 us  [call(): pl.pallas_call(kernel, out_shape=outs, in_specs=[space] * len(arguments),...]
    ppermute x2 -> x3, waiting for transfers between devices: 3.94 us -> 3.72 us  [sum_over(): lax.ppermute(block, axis, [(i, i ^ step) for i in range(size)])]
    ppermute x2 -> x3, starting transfers between devices: 4.23 us -> 4.45 us  [sum_over(): lax.ppermute(block, axis, [(i, i ^ step) for i in range(size)])]
  transfers between devices with their start and end apart: 8 -> 9, of which waited for: 3 -> 4; matrix products, arithmetic and copies ran while one was open for 0% -> 0% of each run, Pallas kernels for 5% -> 5%
where the time goes in v5:
time: 40.1 us; the launch traced here: 39.8 us
  starting transfers between devices  17.4 us (43%)
  blocking collectives  10.3 us (26%)
  Pallas kernels  5.79 us (14%)
  waiting for transfers between devices  4.97 us (12%)
  between operations  0.73 us (2%)
  other arithmetic  0.62 us (2%)
    ppermute x6, starting transfers between devices, swap(): return lax.ppermute(block, axis, route)  12.9 us
    all_to_all x1, blocking collectives, gather_all(): return lax.all_to_all(copies, axis, 0, 0)  10.3 us
    pallas_call x7, Pallas kernels, call(): pl.pallas_call(kernel, out_shape=outs, in_specs=[space] * len(arguments),...  5.79 us
    ppermute x3, starting transfers between devices, sum_over(): lax.ppermute(block, axis, [(i, i ^ step) for i in range(size)])  4.45 us
    ppermute x3, waiting for transfers between devices, sum_over(): lax.ppermute(block, axis, [(i, i ^ step) for i in range(size)])  3.72 us
    ppermute x6, waiting for transfers between devices, swap(): return lax.ppermute(block, axis, route)  1.25 us
  transfers between devices with their start and end apart: 9, of which 4 were waited for; matrix products, arithmetic and copies ran while one was open for 0% of the time, Pallas kernels for 5%

profile of v5, /device:TPU:0, one launch (start us, length us, event | category | flops | bytes accessed | tf_op | source)
XLA Modules:
  0.0 39.8 jit_solution(10629474163272771425)
XLA Ops:
  0.6 0.8 %shard_map.104 = (f32[8,256]{1,0:T(8,128)S(1)}, f32[8,256]{1,0:T(8,128)S(1)}, f32[8,1280]{1,0:T(8,128)S(1)}, s32[8,256]{1,0:T(8,128)S(1)}) custom-call(f32[4,1,1280]{2,1,0:T(1,128)} %bitcast.13, s32[1,256]{1,0:T(1,128)} %order_in.1), custom_call_target="tpu_custom_call" | custom-call | tf_op jit(solution)/shard_map/pallas_call | solution.py:494
  1.4 0.7 %collective-permute-start = (f32[8,256]{1,0:T(8,128)S(1)}, f32[8,256]{1,0:T(8,128)S(1)}, u32[]{:S(2)}, u32[]{:S(2)}) collective-permute-start(f32[8,256]{1,0:T(8,128)S(1)} %get-tuple-element.32), channel_id=1, source_target_pairs={{1,2},{2,1},{3,4},{4,3},{5,6},{6,5},{9,10},{10,9},{11,12},{12,11},... | collective-permute-start | bytes 24584 | tf_op jit(solution)/shard_map/ppermute | solution.py:510
  2.1 4.4 %collective-permute-start.1 = (f32[8,256]{1,0:T(8,128)S(1)}, f32[8,256]{1,0:T(8,128)S(1)}, u32[]{:S(2)}, u32[]{:S(2)}) collective-permute-start(f32[8,256]{1,0:T(8,128)S(1)} %get-tuple-element.33), channel_id=1, source_target_pairs={{0,1},{1,0},{2,3},{3,2},{4,5},{5,4},{6,7},{7,6},{8,9},{9,8},{10,11... | collective-permute-start | bytes 24584 | tf_op jit(solution)/shard_map/ppermute | solution.py:510
  6.4 1.5 %shard_map.105 = (bf16[128,6144]{1,0:T(8,128)(2,1)S(1)}, f32[72,8,128]{2,1,0:T(8,128)S(1)}, f32[8,128]{1,0:T(8,128)S(1)}, f32[2,8,128]{2,1,0:T(8,128)S(1)}, f32[...) custom-call(f32[2]{0:T(128)} %angular_in.1, ...), custom_call_target="tpu_custom_call" | custom-call | flops 4000000 | bytes 4000000 | tf_op jit(solution)/shard_map/pallas_call | solution.py:494
  8.0 0.0 collective-permute-done.1.beside_in
  8.0 1.2 %shard_map.106 = (f32[24,8,128]{2,1,0:T(8,128)S(1)}, f32[8,1280]{1,0:T(8,128)S(1)}, f32[8,256]{1,0:T(8,128)S(1)}, f32[8,256]{1,0:T(8,128)S(1)}, s32[8,256]{1,0:T(8,128)S(1)}, /*index=5*/f32[8,128]{1,0:T(8,128)S(1)}) custom-call(f32[8,1280]{1,0:T(8,128)S(1)} %get-tuple-element.30.source, s32[8,256]{1,0:T(8,128)S(1)} %get-tuple-element.31.order_ref, ...), custom_call_target="tpu_custom_call" | custom-call | tf_op jit(solution)/shard_map/pallas_call | solution.py:494
  9.2 0.7 %collective-permute-start.2 = (f32[8,256]{1,0:T(8,128)S(1)}, f32[8,256]{1,0:T(8,128)S(1)}, u32[]{:S(2)}, u32[]{:S(2)}) collective-permute-start(f32[8,256]{1,0:T(8,128)S(1)} %get-tuple-element.40), channel_id=1, source_target_pairs={{1,2},{2,1},{3,4},{4,3},{5,6},{6,5},{9,10},{10,9},{11,12},{12,11},... | collective-permute-start | bytes 24584 | tf_op jit(solution)/shard_map/ppermute | solution.py:510
  9.9 2.9 %collective-permute-start.3 = (f32[8,256]{1,0:T(8,128)S(1)}, f32[8,256]{1,0:T(8,128)S(1)}, u32[]{:S(2)}, u32[]{:S(2)}) collective-permute-start(f32[8,256]{1,0:T(8,128)S(1)} %get-tuple-element.41), channel_id=1, source_target_pairs={{0,1},{1,0},{2,3},{3,2},{4,5},{5,4},{6,7},{7,6},{8,9},{9,8},{10,11... | collective-permute-start | bytes 24584 | tf_op jit(solution)/shard_map/ppermute | solution.py:510
  12.8 0.4 %shard_map.107 = (f32[24,8,128]{2,1,0:T(8,128)S(1)}, f32[4,8,128]{2,1,0:T(8,128)S(1)}) custom-call(f32[2,8,128]{2,1,0:T(8,128)S(1)} %get-tuple-element.43.rates, f32[4,1,1280]{2,1,0:T(1,128)S(1)} %get-tuple-element.44.forward, f32[36,8,128]{2,1,0:T(8,128)S(1)} %get-tuple-element.45.mass, s32[8,128]{1,0:T(8,128)S(1)} %get-tuple-element.46.live, ...), custom_call_target="tpu_custom_call" | custom-call | flops 4000000 | bytes 4000000 | tf_op jit(solution)/shard_map/pallas_call | solution.py:494
  13.2 0.0 collective-permute-done.2.across_in
  13.3 0.4 %collective-permute-done.3.beside_in = f32[8,256]{1,0:T(8,128)S(1)} collective-permute-done((f32[8,256]{1,0:T(8,128)S(1)}, f32[8,256]{1,0:T(8,128)S(1)}, u32[]{:S(2)}, u32[]{:S(2)}) %collective-permute-start.3) | collective-permute-done | bytes 8224 | tf_op jit(solution)/shard_map/ppermute | solution.py:510
  13.7 1.2 %shard_map.108 = (f32[4,8,128]{2,1,0:T(8,128)S(1)}, f32[8,128]{1,0:T(8,128)S(1)}, f32[8,1280]{1,0:T(8,128)S(1)}, f32[8,256]{1,0:T(8,128)S(1)}, f32[8,256]{1,0:T(8,128)S(1)}) custom-call(f32[8,1280]{1,0:T(8,128)S(1)} %get-tuple-element.38.image_in, s32[8,256]{1,0:T(8,128)S(1)} %get-tuple-element.31.order_ref, s32[8,256]{1,0:T(8,128)S(1)} %get-tuple-element.39.inverse_ref, ...), custom_call_target="tpu_custom_call" | custom-call | tf_op jit(solution)/shard_map/pallas_call | solution.py:494
  14.8 0.7 %collective-permute-start.4 = (f32[8,256]{1,0:T(8,128)S(1)}, f32[8,256]{1,0:T(8,128)S(1)}, u32[]{:S(2)}, u32[]{:S(2)}) collective-permute-start(f32[8,256]{1,0:T(8,128)S(1)} %get-tuple-element.50), channel_id=1, source_target_pairs={{1,2},{2,1},{3,4},{4,3},{5,6},{6,5},{9,10},{10,9},{11,12},{12,11},... | collective-permute-start | bytes 24584 | tf_op jit(solution)/shard_map/ppermute | solution.py:510
  15.5 3.6 %collective-permute-start.5 = (f32[8,256]{1,0:T(8,128)S(1)}, f32[8,256]{1,0:T(8,128)S(1)}, u32[]{:S(2)}, u32[]{:S(2)}) collective-permute-start(f32[8,256]{1,0:T(8,128)S(1)} %get-tuple-element.51), channel_id=1, source_target_pairs={{0,1},{1,0},{2,3},{3,2},{4,5},{5,4},{6,7},{7,6},{8,9},{9,8},{10,11... | collective-permute-start | bytes 24584 | tf_op jit(solution)/shard_map/ppermute | solution.py:510
  19.1 0.8 %collective-permute-done.5.beside_in = f32[8,256]{1,0:T(8,128)S(1)} collective-permute-done((f32[8,256]{1,0:T(8,128)S(1)}, f32[8,256]{1,0:T(8,128)S(1)}, u32[]{:S(2)}, u32[]{:S(2)}) %collective-permute-start.5) | collective-permute-done | bytes 8224 | tf_op jit(solution)/shard_map/ppermute | solution.py:510
  20.0 0.5 %shard_map.109 = (f32[4,8,128]{2,1,0:T(8,128)S(1)}, f32[8,128]{1,0:T(8,128)S(1)}) custom-call(f32[8,1280]{1,0:T(8,128)S(1)} %get-tuple-element.49.image_in, s32[8,256]{1,0:T(8,128)S(1)} %get-tuple-element.31.order_ref, s32[8,256]{1,0:T(8,128)S(1)} %get-tuple-element.39.inverse_ref, f32[8,256]{1,0:T(8,128)S(1)} %collective-permute-done.4.across_in, ...), custom_call_target="tpu_custom_call" | custom-call | tf_op jit(solution)/shard_map/pallas_call | solution.py:494
  20.5 10.3 %all_to_all.5.everyone = f32[8,8,128]{2,1,0:T(8,128)S(1)} all-to-all(f32[8,8,128]{2,1,0:T(8,128)S(1)} %broadcast_in_dim.2), channel_id=1, replica_groups=mesh['freq'=4,'dom'=8] {'dom'}, dimensions={0} | all-to-all | bytes 65536 | tf_op jit(solution)/shard_map/all_to_all | solution.py:516
  30.9 0.1 shard_map.110
  31.0 3.7 %collective-permute-start.8 = (f32[8,128]{1,0:T(8,128)S(1)}, f32[8,128]{1,0:T(8,128)S(1)}, u32[]{:S(2)}, u32[]{:S(2)}) collective-permute-start(f32[8,128]{1,0:T(8,128)S(1)} %shard_map.110), channel_id=1, source_target_pairs={{0,24},{8,16},{16,8},{24,0},{1,25},{9,17},{17,9},{25,1},{2,26},{10... | collective-permute-start | bytes 12296 | tf_op jit(solution)/shard_map/ppermute | solution.py:526
  34.7 0.8 %collective-permute-start.6 = (f32[8,128]{1,0:T(8,128)S(1)}, f32[8,128]{1,0:T(8,128)S(1)}, u32[]{:S(2)}, u32[]{:S(2)}) collective-permute-start(f32[8,128]{1,0:T(8,128)S(1)} %shard_map.110), channel_id=1, source_target_pairs={{0,8},{8,0},{16,24},{24,16},{1,9},{9,1},{17,25},{25,17},{2,10},{10... | collective-permute-start | bytes 12296 | tf_op jit(solution)/shard_map/ppermute | solution.py:526
  35.5 1.0 %collective-permute-done.8 = f32[8,128]{1,0:T(8,128)S(1)} collective-permute-done((f32[8,128]{1,0:T(8,128)S(1)}, f32[8,128]{1,0:T(8,128)S(1)}, u32[]{:S(2)}, u32[]{:S(2)}) %collective-permute-start.8) | collective-permute-done | bytes 4128 | tf_op jit(solution)/shard_map/ppermute | solution.py:526
  36.5 2.7 %collective-permute-done.7 = f32[8,128]{1,0:T(8,128)S(1)} collective-permute-done((f32[8,128]{1,0:T(8,128)S(1)}, f32[8,128]{1,0:T(8,128)S(1)}, u32[]{:S(2)}, u32[]{:S(2)}) %collective-permute-start.7) | collective-permute-done | bytes 4128 | tf_op jit(solution)/shard_map/ppermute | solution.py:526
  39.2 0.0 copy-start
  39.2 0.6 %exponential_multiply_fusion = f32[1,1024]{1,0:T(1,128)} fusion(f32[1,1024]{1,0:T(1,128)S(1)} %bitcast.9, f32[1,1024]{1,0:T(1,128)S(1)} %bitcast.15), kind=kLoop, calls=%fused_computation | loop fusion | flops 2048 | bytes 12288 | tf_op jit(solution)/shard_map/mul | solution.py:643
  (7 shorter events, 0.0 us)
Async XLA Ops:
  1.4 6.6 %collective-permute-start = (f32[8,256]{1,0:T(8,128)S(1)}, f32[8,256]{1,0:T(8,128)S(1)}, u32[]{:S(2)}, u32[]{:S(2)}) collective-permute-start(f32[8,256]{1,0:T(8,128)S(1)} %get-tuple-element.32), channel_id=1, source_target_pairs={{1,2},{2,1},{3,4},{4,3},{5,6},{6,5},{9,10},{10,9},{11,12},{12,11},... | collective-permute-start | bytes 24584 | tf_op jit(solution)/shard_map/ppermute | solution.py:510
  2.1 5.9 %collective-permute-start.1 = (f32[8,256]{1,0:T(8,128)S(1)}, f32[8,256]{1,0:T(8,128)S(1)}, u32[]{:S(2)}, u32[]{:S(2)}) collective-permute-start(f32[8,256]{1,0:T(8,128)S(1)} %get-tuple-element.33), channel_id=1, source_target_pairs={{0,1},{1,0},{2,3},{3,2},{4,5},{5,4},{6,7},{7,6},{8,9},{9,8},{10,11... | collective-permute-start | bytes 24584 | tf_op jit(solution)/shard_map/ppermute | solution.py:510
  9.2 4.0 %collective-permute-start.2 = (f32[8,256]{1,0:T(8,128)S(1)}, f32[8,256]{1,0:T(8,128)S(1)}, u32[]{:S(2)}, u32[]{:S(2)}) collective-permute-start(f32[8,256]{1,0:T(8,128)S(1)} %get-tuple-element.40), channel_id=1, source_target_pairs={{1,2},{2,1},{3,4},{4,3},{5,6},{6,5},{9,10},{10,9},{11,12},{12,11},... | collective-permute-start | bytes 24584 | tf_op jit(solution)/shard_map/ppermute | solution.py:510
  9.9 3.7 %collective-permute-start.3 = (f32[8,256]{1,0:T(8,128)S(1)}, f32[8,256]{1,0:T(8,128)S(1)}, u32[]{:S(2)}, u32[]{:S(2)}) collective-permute-start(f32[8,256]{1,0:T(8,128)S(1)} %get-tuple-element.41), channel_id=1, source_target_pairs={{0,1},{1,0},{2,3},{3,2},{4,5},{5,4},{6,7},{7,6},{8,9},{9,8},{10,11... | collective-permute-start | bytes 24584 | tf_op jit(solution)/shard_map/ppermute | solution.py:510
  14.8 4.3 %collective-permute-start.4 = (f32[8,256]{1,0:T(8,128)S(1)}, f32[8,256]{1,0:T(8,128)S(1)}, u32[]{:S(2)}, u32[]{:S(2)}) collective-permute-start(f32[8,256]{1,0:T(8,128)S(1)} %get-tuple-element.50), channel_id=1, source_target_pairs={{1,2},{2,1},{3,4},{4,3},{5,6},{6,5},{9,10},{10,9},{11,12},{12,11},... | collective-permute-start | bytes 24584 | tf_op jit(solution)/shard_map/ppermute | solution.py:510
  15.5 4.5 %collective-permute-start.5 = (f32[8,256]{1,0:T(8,128)S(1)}, f32[8,256]{1,0:T(8,128)S(1)}, u32[]{:S(2)}, u32[]{:S(2)}) collective-permute-start(f32[8,256]{1,0:T(8,128)S(1)} %get-tuple-element.51), channel_id=1, source_target_pairs={{0,1},{1,0},{2,3},{3,2},{4,5},{5,4},{6,7},{7,6},{8,9},{9,8},{10,11... | collective-permute-start | bytes 24584 | tf_op jit(solution)/shard_map/ppermute | solution.py:510
  31.0 5.5 %collective-permute-start.8 = (f32[8,128]{1,0:T(8,128)S(1)}, f32[8,128]{1,0:T(8,128)S(1)}, u32[]{:S(2)}, u32[]{:S(2)}) collective-permute-start(f32[8,128]{1,0:T(8,128)S(1)} %shard_map.110), channel_id=1, source_target_pairs={{0,24},{8,16},{16,8},{24,0},{1,25},{9,17},{17,9},{25,1},{2,26},{10... | collective-permute-start | bytes 12296 | tf_op jit(solution)/shard_map/ppermute | solution.py:526
  34.7 4.5 %collective-permute-start.7 = (f32[8,128]{1,0:T(8,128)S(1)}, f32[8,128]{1,0:T(8,128)S(1)}, u32[]{:S(2)}, u32[]{:S(2)}) collective-permute-start(f32[8,128]{1,0:T(8,128)S(1)} %shard_map.110), channel_id=1, source_target_pairs={{0,16},{8,24},{16,0},{24,8},{1,17},{9,25},{17,1},{25,9},{2,18},{10... | collective-permute-start | bytes 12296 | tf_op jit(solution)/shard_map/ppermute | solution.py:526
  34.7 4.5 %collective-permute-start.6 = (f32[8,128]{1,0:T(8,128)S(1)}, f32[8,128]{1,0:T(8,128)S(1)}, u32[]{:S(2)}, u32[]{:S(2)}) collective-permute-start(f32[8,128]{1,0:T(8,128)S(1)} %shard_map.110), channel_id=1, source_target_pairs={{0,8},{8,0},{16,24},{24,16},{1,9},{9,1},{17,25},{25,17},{2,10},{10... | collective-permute-start | bytes 12296 | tf_op jit(solution)/shard_map/ppermute | solution.py:526
  39.2 0.6 %copy-start = (f32[8,128]{1,0:T(8,128)}, f32[8,128]{1,0:T(8,128)S(1)}, u32[]{:S(2)}) copy-start(f32[8,128]{1,0:T(8,128)S(1)} %add_add_fusion) | copy-start | bytes 12292

commit v6 on v5

--- a/solution.py
+++ b/solution.py
@@ -132,7 +132,7 @@
     return total
 
 
-def scatter(pieces, edges, places, count):
+def scatter(pieces, edges, places, heights):
     depth = SIDE * edges.shape[1]
     rows = pieces.shape[0] // depth
     slots = edges.shape[1] * LANES
@@ -142,7 +142,7 @@
         for s in range(edges.shape[1]):
             both = pieces[pl.ds(i * edges.shape[1] + s, rows, stride=depth), :]
             high = spread(edges[i, s : s + 1, :] >> 7, rows)
-            stacked = [jnp.where(high == h, both, 0.0) for h in range(count)]
+            stacked = [jnp.where(high == h, both, 0.0) for h in heights]
             columns.append(jnp.concatenate(stacked, axis=0).astype(jnp.bfloat16))
         part = lax.dot_general(
             jnp.concatenate(columns, axis=1),
@@ -152,16 +152,26 @@
         )
         total = part if total is None else total + part
     out = []
-    for h in range(count):
-        piece = total[rows * h : rows * (h + 1)]
+    for n in range(len(heights)):
+        piece = total[rows * n : rows * (n + 1)]
         out.append(piece + swap_halves(piece))
     return out
 
 
-def joined(own, from_prior, from_above, order, inverse):
-    rim = len(from_prior)
-    lower = [own[c] + pick_wide(from_prior, order[c]) for c in range(rim)]
-    upper = [own[len(own) - rim + c] + pick_wide(from_above, inverse[c]) for c in range(rim)]
+def rim_heights(edge_count, rim):
+    count = edge_count // LANES
+    return [*range(rim), *range(count - rim, count)], list(range(rim, count - rim))
+
+
+def corrections(from_prior, from_above, order, inverse):
+    lower = [pick_wide(from_prior, index) for index in order]
+    return lower + [pick_wide(from_above, index) for index in inverse]
+
+
+def corrected(own, delta):
+    rim = len(delta) // 2
+    lower = [a + b for a, b in zip(own[:rim], delta[:rim])]
+    upper = [a + b for a, b in zip(own[len(own) - rim :], delta[rim:])]
     return lower + own[rim : len(own) - rim] + upper
 
 
@@ -214,9 +224,11 @@
     live_in,
     edges_in,
     forward_in,
+    source,
     places_ref,
     blocks_ref,
     scale_ref,
+    picks_ref,
     rates,
     mass,
     sigma,
@@ -251,6 +263,7 @@
         return carry
 
     lax.fori_loop(0, SIDE, body, 0)
+    put_picks(picks_ref, source, edges, scale_ref.shape[0] // 2)
     for copy in copies[1:]:
         copy.wait()
     for f in range(angular.shape[0]):
@@ -275,12 +288,32 @@
             blocks_ref[f * SIDE * SIDE + entry] = stiff + rates[f] * heavy
 
 
-def apply_all(field_ref, blocks, edges, polars, groups, pieces, visit):
-    rows = field_ref.shape[0]
+def put_picks(picks_ref, field, edges, groups):
+    for g in range(groups):
+        for j, value in enumerate(picks_of(group_rows(field, g), edges)):
+            picks_ref[g * SIDE + j] = value
+
+
+def pick_rims(rows, index, edge_count):
+    rim = len(rows) // 2
+    start = edge_count - rim * LANES
+    lower = pick_wide([spread(row, index.shape[0]) for row in rows[:rim]], index)
+    upper = pick_wide([spread(row, index.shape[0]) for row in rows[rim:]], index - start)
+    lower = jnp.where(index < rim * LANES, lower, 0.0)
+    return lower + jnp.where(index >= start, upper, 0.0)
+
+
+def apply_all(delta_ref, own_picks, blocks, edges, polars, edge_count, pieces, visit):
+    rows = delta_ref.shape[0]
+    groups = rows // 2
     depth = SIDE * edges.shape[1]
     forms = jnp.zeros((rows, LANES), jnp.float32)
     for g in range(groups):
-        picked = picks_of(group_rows(field_ref, g), edges)
+        delta = group_rows(delta_ref, g)
+        picked = [
+            own_picks[g * SIDE + j] + pick_rims(delta, edges[j], edge_count)
+            for j in range(SIDE)
+        ]
         visit(g, picked)
         values = times_block(blocks, (g // polars) * SIDE * SIDE, picked)
         form = jnp.sum(weighted_sum(picked, values), axis=0, keepdims=True)
@@ -292,151 +325,170 @@
             for part, piece in enumerate((coarse, value - coarse)):
                 at = (part * groups + g) * depth + i * edges.shape[1]
                 pieces[at : at + edges.shape[1], :] = piece
-    return lane_sum(forms)
-
-
-def first_stage(
+    return forms
+
+
+def invert(above, groups, rows):
+    above_order = jnp.concatenate([x[groups : groups + 1] for x in above], axis=1)
+    rim = above_order.shape[1]
+    slot = lax.broadcasted_iota(jnp.int32, (rim, rim), 0).astype(jnp.float32)
+    match = jnp.where(spread(above_order, rim) == slot, 1.0, 0.0).astype(jnp.bfloat16)
+    numbers = lax.broadcasted_iota(jnp.int32, (2 * rows, rim), 1).astype(jnp.bfloat16)
+    inverse = lax.dot_general(
+        numbers, match, (((1,), (1,)), ((), ())), preferred_element_type=jnp.float32
+    )
+    return inverse[:rows].astype(jnp.int32)
+
+
+def rescaled(block, inverse_scale, step):
+    ratio = swap_halves(block) * inverse_scale
+    for _ in range(step):
+        block = block * ratio
+    return doubled(block)
+
+
+def front_stage(
     polars,
-    source,
+    step,
+    edge_count,
     order_ref,
     across_in,
     beside_in,
     scale_in,
+    own_picks,
     blocks,
     edges,
     places,
-    picks_ref,
-    image_ref,
-    across_ref,
-    beside_ref,
-    inverse_ref,
-    sums_ref,
-    field_ref,
-    pieces,
+    *rest,
 ):
-    rows = source.shape[0]
+    if step == 0:
+        inverse_ref, *rest = rest
+    else:
+        inverse_in, *rest = rest
+    delta_ref, picks_ref, pieces, forms_ref, rims_ref, across_ref, beside_ref = rest
+    rows = delta_ref.shape[0]
     groups = rows // 2
     first = row_ids(rows) < groups
     scale = scale_in[...]
     prior, above = take_rims(across_in, beside_in)
-
-    rim = order_ref.shape[-1]
-    order = cut(order_ref)
-    above_order = spread(
-        jnp.concatenate([x[groups : groups + 1] for x in above], axis=1), rim
-    )
-    slot = lax.broadcasted_iota(jnp.int32, (rim, rim), 0).astype(jnp.float32)
-    match = jnp.where(above_order == slot, 1.0, 0.0).astype(jnp.bfloat16)
-    numbers = lax.broadcasted_iota(jnp.int32, (2 * rows, rim), 1).astype(jnp.bfloat16)
-    inverse = lax.dot_general(
-        numbers, match, (((1,), (1,)), ((), ())), preferred_element_type=jnp.float32
-    )[:rows].astype(jnp.int32)
-    inverse_ref[...] = inverse
-    inverse = [inverse[:, c : c + LANES] for c in range(0, rim, LANES)]
-
-    has_prior = spread(prior[0][groups : groups + 1], rows)
-    field = joined(
-        cut(source), [doubled(x) for x in prior], [doubled(x) for x in above], order, inverse
-    )
-    put_chunks(field_ref, field)
+    if step == 0:
+        inverse_ref[...] = invert(above, groups, rows)
+        inverse = cut(inverse_ref)
+        prior, above = [doubled(x) for x in prior], [doubled(x) for x in above]
+    else:
+        inverse = cut(inverse_in)
+        inverse_scale = 1.0 / scale
+        prior = [rescaled(x, inverse_scale, step) for x in prior]
+        above = [rescaled(x, inverse_scale, step) for x in above]
+    put_chunks(delta_ref, corrections(prior, above, cut(order_ref), inverse))
 
     def visit(g, picked):
         for j in range(SIDE):
             picks_ref[g * SIDE + j] = picked[j]
 
-    forms = apply_all(field_ref, blocks, edges, polars, groups, pieces, visit)
-    image = scatter(pieces, edges, places, len(field))
-    put_chunks(image_ref, image)
-    count = rim // LANES
+    forms_ref[...] = apply_all(
+        delta_ref, own_picks, blocks, edges, polars, edge_count, pieces, visit
+    )
+    rim = len(prior)
+    chunks = scatter(pieces, edges, places, rim_heights(edge_count, rim)[0])
+    put_chunks(rims_ref, chunks)
     put_rims(
         across_ref,
         beside_ref,
-        [jnp.where(first, x, scale) for x in image[:count]],
-        [jnp.where(first, x, scale) for x in image[len(image) - count :]],
-    )
-    sums = jnp.zeros((rows, LANES), jnp.float32)
-    sums = put_lane(sums, 0, lane_sum(squares(field, count, has_prior)))
-    sums = put_lane(sums, 1, forms)
-    sums_ref[...] = jnp.where(first, sums, scale)
-
-
-def later_stage(
+        [jnp.where(first, x, scale) for x in chunks[:rim]],
+        [jnp.where(first, x, scale) for x in chunks[rim:]],
+    )
+
+
+def inner_products(step, sums, own, delta, forms, across_in, beside_in):
+    rows = sums.shape[0]
+    first = row_ids(rows) < rows // 2
+    prior, _ = take_rims(across_in, beside_in)
+    has_prior = jnp.where(first, swap_halves(prior[0]), prior[0])
+    has_prior = spread(jnp.where(has_prior[:1, :1] > 0.0, 1.0, 0.0), rows)
+    field = corrected(own, delta)
+    sums = put_lane(sums, 2 * step, lane_sum(squares(field, len(delta) // 2, has_prior)))
+    return put_lane(sums, 2 * step + 1, lane_sum(forms))
+
+
+def back_stage(
     polars,
     step,
-    last,
-    image_in,
-    order_ref,
-    inverse_ref,
+    own,
+    delta,
+    forms,
     across_in,
     beside_in,
     sums_in,
+    picks,
+    pieces,
+    rims,
+    edges,
+    places,
+    *rest,
+):
+    if step == 0:
+        rates, forward, mass, live, heavy, terms_ref, sums_ref, image_ref, picks_ref = rest
+    else:
+        heavy, terms_ref, sums_ref, image_ref, picks_ref = rest
+    rows, edge_count = own.shape
+    groups = rows // 2
+    rim = rims.shape[-1] // LANES // 2
+    outer = cut(rims)
+    inner = scatter(pieces, edges, places, rim_heights(edge_count, rim)[1])
+    put_chunks(image_ref, outer[:rim] + inner + outer[rim:])
+    put_picks(picks_ref, image_ref, edges, groups)
+    if step == 0:
+        dead = -live[...].astype(jnp.float32)
+        for g in range(groups):
+            row = [forward[g, :, c : c + LANES] for c in range(0, edge_count, LANES)]
+            values = times_block(mass, 0, picks_of(row, edges))
+            factor = dead * rates[g // polars]
+            for i in range(SIDE):
+                heavy[g * SIDE + i] = factor * values[i]
+    for g in range(groups):
+        side = range(g * SIDE, (g + 1) * SIDE)
+        terms_ref[g] = weighted_sum([picks[i] for i in side], [heavy[i] for i in side])
+    sums_ref[...] = inner_products(
+        step, sums_in[...], cut(own), cut(delta), forms[...], across_in, beside_in
+    )
+
+
+def last_stage(
+    polars,
+    step,
+    own,
+    order_ref,
+    inverse_in,
+    across_in,
+    beside_in,
+    scale_in,
+    sums_in,
+    own_picks,
     blocks,
     edges,
     heavy,
-    *rest,
+    terms_ref,
+    sums_ref,
+    delta_ref,
 ):
-    if last:
-        terms_ref, sums_ref, field_ref = rest
-        pieces = None
-    else:
-        places, terms_ref, sums_ref, image_ref, across_ref, beside_ref, field_ref, pieces = rest
-    rows = image_in.shape[0]
-    groups = rows // 2
-    first = row_ids(rows) < groups
-    sums = sums_in[...]
-    scale = jnp.where(first, swap_halves(sums), sums)
+    rows, edge_count = own.shape
+    first = row_ids(rows) < rows // 2
+    scale = scale_in[...]
     inverse_scale = 1.0 / scale
-    rim = order_ref.shape[-1]
-    count = rim // LANES
-    order = cut(order_ref)
-    inverse = cut(inverse_ref)
-
-    def rescaled(block):
-        ratio = swap_halves(block) * inverse_scale
-        for _ in range(step):
-            block = block * ratio
-        return doubled(block)
-
     prior, above = take_rims(across_in, beside_in)
-    has_prior = jnp.where(first, swap_halves(prior[0]), prior[0])
-    has_prior = jnp.where(has_prior > 0.0, 1.0, 0.0)
-    field = joined(
-        cut(image_in),
-        [rescaled(x) for x in prior],
-        [rescaled(x) for x in above],
-        order,
-        inverse,
-    )
-    put_chunks(field_ref, field)
+    prior = [rescaled(x, inverse_scale, step) for x in prior]
+    above = [rescaled(x, inverse_scale, step) for x in above]
+    put_chunks(delta_ref, corrections(prior, above, cut(order_ref), cut(inverse_in)))
 
     def visit(g, picked):
         terms_ref[g] = weighted_sum(picked, [heavy[g * SIDE + i] for i in range(SIDE)])
 
-    forms = apply_all(field_ref, blocks, edges, polars, groups, pieces, visit)
-    fresh = put_lane(sums, 2 * step, lane_sum(squares(field, count, has_prior)))
-    fresh = put_lane(fresh, 2 * step + 1, forms)
-    sums_ref[...] = jnp.where(first, fresh, scale)
-    if not last:
-        image = scatter(pieces, edges, places, len(field))
-        put_chunks(image_ref, image)
-        put_rims(
-            across_ref,
-            beside_ref,
-            [jnp.where(first, x, scale) for x in image[:count]],
-            [jnp.where(first, x, scale) for x in image[len(image) - count :]],
-        )
-
-
-def forward_stage(polars, rates, forward, mass, live, edges, picks, heavy_ref, terms_ref):
-    dead = -live[...].astype(jnp.float32)
-    for g in range(forward.shape[0]):
-        rows = [forward[g, :, c : c + LANES] for c in range(0, forward.shape[-1], LANES)]
-        values = times_block(mass, 0, picks_of(rows, edges))
-        factor = dead * rates[g // polars]
-        values = [factor * value for value in values]
-        for i in range(SIDE):
-            heavy_ref[g * SIDE + i] = values[i]
-        terms_ref[g] = weighted_sum(values, [picks[g * SIDE + i] for i in range(SIDE)])
+    forms = apply_all(delta_ref, own_picks, blocks, edges, polars, edge_count, None, visit)
+    sums = inner_products(
+        step, sums_in[...], cut(own), cut(delta_ref), forms, across_in, beside_in
+    )
+    sums_ref[...] = jnp.where(first, sums, scale)
 
 
 def combine_stage(everyone, sums_in, terms0, terms1, terms2, out_ref):
@@ -494,7 +546,7 @@
     return pl.pallas_call(
         kernel,
         out_shape=outs,
-        in_specs=[space] * len(arguments),
+        in_specs=space if isinstance(space, list) else [space] * len(arguments),
         out_specs=jax.tree.map(lambda _: VMEM, outs),
         scratch_shapes=list(scratch),
         cost_estimate=pl.CostEstimate(flops=cost, bytes_accessed=cost, transcendentals=0),
@@ -567,8 +619,6 @@
     field_shape, rim_shape = shape(rows, edge_count), shape(rows, rim)
     sums_shape, terms_shape = shape(rows, LANES), shape(groups, tall, LANES)
     picks_shape = shape(groups * SIDE, tall, LANES)
-    field_room = pltpu.VMEM((rows, edge_count), jnp.float32)
-    piece_room = pltpu.VMEM((rows * SIDE * tall, LANES), jnp.float32)
 
     across, beside, source, order = call(
         rims_stage,
@@ -583,13 +633,14 @@
     )
     across, beside = swap(across, "dom", 1), swap(beside, "dom", 0)
     kept = [jax.ShapeDtypeStruct(x.shape, x.dtype) for x in (mass, sigma, live, edges, forward)]
-    places, blocks, scale, rates, mass, sigma, live, edges, forward = call(
+    places, blocks, scale, picks, rates, mass, sigma, live, edges, forward = call(
         table_stage,
-        pinned(angular, stiff, mass, sigma, live, edges, forward),
+        [*pinned(angular, stiff, mass, sigma, live, edges, forward), source],
         [
             shape(LANES, SIDE * slots, kind=jnp.bfloat16),
             shape(freqs * SIDE * SIDE, tall, LANES),
             sums_shape,
+            picks_shape,
             shape(freqs, tall, LANES),
             *kept,
         ],
@@ -598,45 +649,54 @@
             pltpu.VMEM(stiff.shape, stiff.dtype),
             pltpu.SemaphoreType.DMA((7,)),
         ),
-        space=HBM,
+        space=[HBM] * 7 + [VMEM],
         cost=4_000_000,
     )
-    picks, image, across, beside, inverse, sums = call(
-        functools.partial(first_stage, polars),
-        (source, order, across, beside, scale, blocks, edges, places),
-        [
-            picks_shape,
-            field_shape,
-            rim_shape,
-            rim_shape,
-            shape(rows, rim, kind=jnp.int32),
-            sums_shape,
-        ],
-        (field_room, piece_room),
-    )
-    across, beside = swap(across, "dom", 1), swap(beside, "dom", 0)
-    heavy, terms0 = call(
-        functools.partial(forward_stage, polars),
-        (rates, forward, mass, live, edges, picks),
-        [picks_shape, terms_shape],
-        cost=4_000_000,
-    )
-    terms1, sums, image, across, beside = call(
-        functools.partial(later_stage, polars, 1, False),
-        (image, order, inverse, across, beside, sums, blocks, edges, heavy, places),
-        [terms_shape, sums_shape, field_shape, rim_shape, rim_shape],
-        (field_room, piece_room),
-    )
-    across, beside = swap(across, "dom", 1), swap(beside, "dom", 0)
-    terms2, sums = call(
-        functools.partial(later_stage, polars, 2, True),
-        (image, order, inverse, across, beside, sums, blocks, edges, heavy),
+    front_shapes = [
+        shape(rows, 2 * rim),
+        picks_shape,
+        shape(rows * SIDE * tall, LANES),
+        sums_shape,
+        shape(rows, 2 * rim),
+        rim_shape,
+        rim_shape,
+    ]
+    back_shapes = [terms_shape, sums_shape, field_shape, picks_shape]
+    own, sums, terms = source, jnp.zeros((rows, LANES), jnp.float32), []
+    for step in range(2):
+        arrived = (across, beside)
+        given = (order, *arrived, scale, picks, blocks, edges, places)
+        front = functools.partial(front_stage, polars, step, edge_count)
+        if step == 0:
+            inverse, *outs = call(
+                front, given, [shape(rows, rim, kind=jnp.int32), *front_shapes]
+            )
+        else:
+            outs = call(front, (*given, inverse), front_shapes)
+        delta, picks, pieces, forms, rims, across, beside = outs
+        across, beside = swap(across, "dom", 1), swap(beside, "dom", 0)
+        given = (own, delta, forms, *arrived, sums, picks, pieces, rims, edges, places)
+        back = functools.partial(back_stage, polars, step)
+        if step == 0:
+            heavy, term, sums, own, picks = call(
+                back,
+                (*given, rates, forward, mass, live),
+                [picks_shape, *back_shapes],
+                cost=4_000_000,
+            )
+        else:
+            term, sums, own, picks = call(back, (*given, heavy), back_shapes, cost=4_000_000)
+        terms.append(term)
+    term, sums = call(
+        functools.partial(last_stage, polars, 2),
+        (own, order, inverse, across, beside, scale, sums, picks, blocks, edges, heavy),
         [terms_shape, sums_shape],
-        (field_room,),
-    )
+        (pltpu.VMEM((rows, 2 * rim), jnp.float32),),
+    )
+    terms.append(term)
     term = call(
         combine_stage,
-        (gather_all(sums, "dom"), sums, terms0, terms1, terms2),
+        (gather_all(sums, "dom"), sums, *terms),
         shape(tall, LANES),
     )
     gradient = sum_over(term, "freq").reshape(1, slots)

time: 40.1 us -> 39.8 us (level)
  Pallas kernels: 5.79 us -> 7.76 us
  waiting for transfers between devices: 4.97 us -> 3.74 us
  blocking collectives: 10.3 us -> 9.62 us
    pallas_call x7 -> x8, Pallas kernels: 5.79 us -> 7.76 us  [call(): pl.pallas_call(kernel, out_shape=outs, in_specs=space if isinstance(space...]
    ppermute x6, waiting for transfers between devices: 1.25 us -> 0.02 us  [swap(): return lax.ppermute(block, axis, route)]
    all_to_all x1, blocking collectives: 10.3 us -> 9.62 us  [gather_all(): return lax.all_to_all(copies, axis, 0, 0)]
  transfers between devices with their start and end apart: 9 -> 9, of which waited for: 4 -> 2; matrix products, arithmetic and copies ran while one was open for 0% -> 0% of each run, Pallas kernels for 5% -> 11%
where the time goes in v6:
time: 39.8 us; the launch traced here: 39.5 us
  starting transfers between devices  17 us (43%)
  blocking collectives  9.62 us (24%)
  Pallas kernels  7.76 us (19%)
  waiting for transfers between devices  3.74 us (9%)
  between operations  0.74 us (2%)
  other arithmetic  0.62 us (2%)
    ppermute x6, starting transfers between devices, swap(): return lax.ppermute(block, axis, route)  12.6 us
    all_to_all x1, blocking collectives, gather_all(): return lax.all_to_all(copies, axis, 0, 0)  9.62 us
    pallas_call x8, Pallas kernels, call(): pl.pallas_call(kernel, out_shape=outs, in_specs=space if isinstance(space...  7.76 us
    ppermute x3, starting transfers between devices, sum_over(): lax.ppermute(block, axis, [(i, i ^ step) for i in range(size)])  4.45 us
    ppermute x3, waiting for transfers between devices, sum_over(): lax.ppermute(block, axis, [(i, i ^ step) for i in range(size)])  3.72 us
  transfers between devices with their start and end apart: 9, of which 2 were waited for; matrix products, arithmetic and copies ran while one was open for 0% of the time, Pallas kernels for 11%

profile of v6, /device:TPU:0, one launch (start us, length us, event | category | flops | bytes accessed | tf_op | source)
XLA Modules:
  0.0 39.5 jit_solution(7024659011616769829)
XLA Ops:
  0.6 0.8 %shard_map.104 = (f32[8,256]{1,0:T(8,128)S(1)}, f32[8,256]{1,0:T(8,128)S(1)}, f32[8,1280]{1,0:T(8,128)S(1)}, s32[8,256]{1,0:T(8,128)S(1)}) custom-call(f32[4,1,1280]{2,1,0:T(1,128)} %bitcast.14, s32[1,256]{1,0:T(1,128)} %order_in.1), custom_call_target="tpu_custom_call" | custom-call | tf_op jit(solution)/shard_map/pallas_call | solution.py:546
  1.4 0.7 %collective-permute-start = (f32[8,256]{1,0:T(8,128)S(1)}, f32[8,256]{1,0:T(8,128)S(1)}, u32[]{:S(2)}, u32[]{:S(2)}) collective-permute-start(f32[8,256]{1,0:T(8,128)S(1)} %get-tuple-element.44), channel_id=1, source_target_pairs={{1,2},{2,1},{3,4},{4,3},{5,6},{6,5},{9,10},{10,9},{11,12},{12,11},... | collective-permute-start | bytes 24584 | tf_op jit(solution)/shard_map/ppermute | solution.py:562
  2.1 4.4 %collective-permute-start.1 = (f32[8,256]{1,0:T(8,128)S(1)}, f32[8,256]{1,0:T(8,128)S(1)}, u32[]{:S(2)}, u32[]{:S(2)}) collective-permute-start(f32[8,256]{1,0:T(8,128)S(1)} %get-tuple-element.45), channel_id=1, source_target_pairs={{0,1},{1,0},{2,3},{3,2},{4,5},{5,4},{6,7},{7,6},{8,9},{9,8},{10,11... | collective-permute-start | bytes 24584 | tf_op jit(solution)/shard_map/ppermute | solution.py:562
  6.4 1.9 %shard_map.105 = (bf16[128,6144]{1,0:T(8,128)(2,1)S(1)}, f32[72,8,128]{2,1,0:T(8,128)S(1)}, f32[8,128]{1,0:T(8,128)S(1)}, f32[24,8,128]{2,1,0:T(8,128)S(1)}, f32...) custom-call(f32[2]{0:T(128)} %angular_in.1, ...), custom_call_target="tpu_custom_call" | custom-call | flops 4000000 | bytes 4000000 | tf_op jit(solution)/shard_map/pallas_call | solution.py:546
  8.4 0.0 collective-permute-done.1.beside_in
  8.4 1.1 %shard_map.106 = (s32[8,256]{1,0:T(8,128)S(1)}, f32[8,512]{1,0:T(8,128)S(1)}, f32[24,8,128]{2,1,0:T(8,128)S(1)}, f32[384,128]{1,0:T(8,128)S(1)}, f32[8,128]{1,0:...) custom-call(s32[8,256]{1,0:T(8,128)S(1)} %get-tuple-element.43.order_ref, ...), custom_call_target="tpu_custom_call" | custom-call | tf_op jit(solution)/shard_map/pallas_call | solution.py:546
  9.5 0.7 %collective-permute-start.2 = (f32[8,256]{1,0:T(8,128)S(1)}, f32[8,256]{1,0:T(8,128)S(1)}, u32[]{:S(2)}, u32[]{:S(2)}) collective-permute-start(f32[8,256]{1,0:T(8,128)S(1)} %get-tuple-element.61), channel_id=1, source_target_pairs={{1,2},{2,1},{3,4},{4,3},{5,6},{6,5},{9,10},{10,9},{11,12},{12,11},... | collective-permute-start | bytes 24584 | tf_op jit(solution)/shard_map/ppermute | solution.py:562
  10.2 2.9 %collective-permute-start.3 = (f32[8,256]{1,0:T(8,128)S(1)}, f32[8,256]{1,0:T(8,128)S(1)}, u32[]{:S(2)}, u32[]{:S(2)}) collective-permute-start(f32[8,256]{1,0:T(8,128)S(1)} %get-tuple-element.62), channel_id=1, source_target_pairs={{0,1},{1,0},{2,3},{3,2},{4,5},{5,4},{6,7},{7,6},{8,9},{9,8},{10,11... | collective-permute-start | bytes 24584 | tf_op jit(solution)/shard_map/ppermute | solution.py:562
  13.1 1.2 %shard_map.107 = (f32[24,8,128]{2,1,0:T(8,128)S(1)}, f32[4,8,128]{2,1,0:T(8,128)S(1)}, f32[8,128]{1,0:T(8,128)S(1)}, f32[8,1280]{1,0:T(8,128)S(1)}, f32[24,8,128]{2,1,0:T(8,128)S(1)}) custom-call(f32[8,1280]{1,0:T(8,128)S(1)} %get-tuple-element.42.source.own, f32[8,512]{1,0:T(8,128)S(1)} %get-tuple-element.51.delta, f32[8,128]{1,0:T(8,128)S(1)} %get-tuple-element.52.forms, ...), custom_call_target="tpu_custom_call" | custom-call | flops 4000000 | bytes 4000000 | tf_op jit(solution)/shard_map/pallas_call | solution.py:546
  14.3 1.0 %shard_map.108 = (f32[8,512]{1,0:T(8,128)S(1)}, f32[24,8,128]{2,1,0:T(8,128)S(1)}, f32[384,128]{1,0:T(8,128)S(1)}, f32[8,128]{1,0:T(8,128)S(1)}, f32[8,512]{1,0:...) custom-call(s32[8,256]{1,0:T(8,128)S(1)} %get-tuple-element.43.order_ref, ...), custom_call_target="tpu_custom_call" | custom-call | tf_op jit(solution)/shard_map/pallas_call | solution.py:546
  15.4 0.7 %collective-permute-start.4 = (f32[8,256]{1,0:T(8,128)S(1)}, f32[8,256]{1,0:T(8,128)S(1)}, u32[]{:S(2)}, u32[]{:S(2)}) collective-permute-start(f32[8,256]{1,0:T(8,128)S(1)} %get-tuple-element.73), channel_id=1, source_target_pairs={{1,2},{2,1},{3,4},{4,3},{5,6},{6,5},{9,10},{10,9},{11,12},{12,11},... | collective-permute-start | bytes 24584 | tf_op jit(solution)/shard_map/ppermute | solution.py:562
  16.0 3.3 %collective-permute-start.5 = (f32[8,256]{1,0:T(8,128)S(1)}, f32[8,256]{1,0:T(8,128)S(1)}, u32[]{:S(2)}, u32[]{:S(2)}) collective-permute-start(f32[8,256]{1,0:T(8,128)S(1)} %get-tuple-element.74), channel_id=1, source_target_pairs={{0,1},{1,0},{2,3},{3,2},{4,5},{5,4},{6,7},{7,6},{8,9},{9,8},{10,11... | collective-permute-start | bytes 24584 | tf_op jit(solution)/shard_map/ppermute | solution.py:562
  19.3 1.1 %shard_map.109 = (f32[4,8,128]{2,1,0:T(8,128)S(1)}, f32[8,128]{1,0:T(8,128)S(1)}, f32[8,1280]{1,0:T(8,128)S(1)}, f32[24,8,128]{2,1,0:T(8,128)S(1)}) custom-call(f32[8,1280]{1,0:T(8,128)S(1)} %get-tuple-element.60.own, f32[8,512]{1,0:T(8,128)S(1)} %get-tuple-element.65.delta, f32[8,128]{1,0:T(8,128)S(1)} %get-tuple-element.66.forms, ...), custom_call_target="tpu_custom_call" | custom-call | flops 4000000 | bytes 4000000 | tf_op jit(solution)/shard_map/pallas_call | solution.py:546
  20.4 0.0 collective-permute-done.5.beside_in
  20.4 0.5 %shard_map.110 = (f32[4,8,128]{2,1,0:T(8,128)S(1)}, f32[8,128]{1,0:T(8,128)S(1)}) custom-call(f32[8,1280]{1,0:T(8,128)S(1)} %get-tuple-element.72.own, s32[8,256]{1,0:T(8,128)S(1)} %get-tuple-element.43.order_ref, s32[8,256]{1,0:T(8,128)S(1)} %get-tuple-element.64.rest_0_.inverse_in, f32[8,256]{1,0:T(8,128)S(1)} %collective-permute-done.4.across_in, ...), custom_call_target="tpu_custom_call" | custom-call | tf_op jit(solution)/shard_map/pallas_call | solution.py:546
  20.9 9.6 %all_to_all.5.everyone = f32[8,8,128]{2,1,0:T(8,128)S(1)} all-to-all(f32[8,8,128]{2,1,0:T(8,128)S(1)} %broadcast_in_dim.10), channel_id=1, replica_groups=mesh['freq'=4,'dom'=8] {'dom'}, dimensions={0} | all-to-all | bytes 65536 | tf_op jit(solution)/shard_map/all_to_all | solution.py:568
  30.6 0.1 shard_map.111
  30.7 3.7 %collective-permute-start.8 = (f32[8,128]{1,0:T(8,128)S(1)}, f32[8,128]{1,0:T(8,128)S(1)}, u32[]{:S(2)}, u32[]{:S(2)}) collective-permute-start(f32[8,128]{1,0:T(8,128)S(1)} %shard_map.111), channel_id=1, source_target_pairs={{0,24},{8,16},{16,8},{24,0},{1,25},{9,17},{17,9},{25,1},{2,26},{10... | collective-permute-start | bytes 12296 | tf_op jit(solution)/shard_map/ppermute | solution.py:578
  34.4 0.0 collective-permute-start.7
  34.4 0.8 %collective-permute-start.6 = (f32[8,128]{1,0:T(8,128)S(1)}, f32[8,128]{1,0:T(8,128)S(1)}, u32[]{:S(2)}, u32[]{:S(2)}) collective-permute-start(f32[8,128]{1,0:T(8,128)S(1)} %shard_map.111), channel_id=1, source_target_pairs={{0,8},{8,0},{16,24},{24,16},{1,9},{9,1},{17,25},{25,17},{2,10},{10... | collective-permute-start | bytes 12296 | tf_op jit(solution)/shard_map/ppermute | solution.py:578
  35.2 1.0 %collective-permute-done.8 = f32[8,128]{1,0:T(8,128)S(1)} collective-permute-done((f32[8,128]{1,0:T(8,128)S(1)}, f32[8,128]{1,0:T(8,128)S(1)}, u32[]{:S(2)}, u32[]{:S(2)}) %collective-permute-start.8) | collective-permute-done | bytes 4128 | tf_op jit(solution)/shard_map/ppermute | solution.py:578
  36.2 2.7 %collective-permute-done.7 = f32[8,128]{1,0:T(8,128)S(1)} collective-permute-done((f32[8,128]{1,0:T(8,128)S(1)}, f32[8,128]{1,0:T(8,128)S(1)}, u32[]{:S(2)}, u32[]{:S(2)}) %collective-permute-start.7) | collective-permute-done | bytes 4128 | tf_op jit(solution)/shard_map/ppermute | solution.py:578
  38.9 0.0 copy-start
  38.9 0.6 %exponential_multiply_fusion = f32[1,1024]{1,0:T(1,128)} fusion(f32[1,1024]{1,0:T(1,128)S(1)} %bitcast.9, f32[1,1024]{1,0:T(1,128)S(1)} %bitcast.15), kind=kLoop, calls=%fused_computation | loop fusion | flops 2048 | bytes 12288 | tf_op jit(solution)/shard_map/mul | solution.py:703
  (9 shorter events, 0.0 us)
Async XLA Ops:
  1.4 7.0 %collective-permute-start = (f32[8,256]{1,0:T(8,128)S(1)}, f32[8,256]{1,0:T(8,128)S(1)}, u32[]{:S(2)}, u32[]{:S(2)}) collective-permute-start(f32[8,256]{1,0:T(8,128)S(1)} %get-tuple-element.44), channel_id=1, source_target_pairs={{1,2},{2,1},{3,4},{4,3},{5,6},{6,5},{9,10},{10,9},{11,12},{12,11},... | collective-permute-start | bytes 24584 | tf_op jit(solution)/shard_map/ppermute | solution.py:562
  2.1 6.3 %collective-permute-start.1 = (f32[8,256]{1,0:T(8,128)S(1)}, f32[8,256]{1,0:T(8,128)S(1)}, u32[]{:S(2)}, u32[]{:S(2)}) collective-permute-start(f32[8,256]{1,0:T(8,128)S(1)} %get-tuple-element.45), channel_id=1, source_target_pairs={{0,1},{1,0},{2,3},{3,2},{4,5},{5,4},{6,7},{7,6},{8,9},{9,8},{10,11... | collective-permute-start | bytes 24584 | tf_op jit(solution)/shard_map/ppermute | solution.py:562
  9.5 4.8 %collective-permute-start.2 = (f32[8,256]{1,0:T(8,128)S(1)}, f32[8,256]{1,0:T(8,128)S(1)}, u32[]{:S(2)}, u32[]{:S(2)}) collective-permute-start(f32[8,256]{1,0:T(8,128)S(1)} %get-tuple-element.61), channel_id=1, source_target_pairs={{1,2},{2,1},{3,4},{4,3},{5,6},{6,5},{9,10},{10,9},{11,12},{12,11},... | collective-permute-start | bytes 24584 | tf_op jit(solution)/shard_map/ppermute | solution.py:562
  10.2 4.1 %collective-permute-start.3 = (f32[8,256]{1,0:T(8,128)S(1)}, f32[8,256]{1,0:T(8,128)S(1)}, u32[]{:S(2)}, u32[]{:S(2)}) collective-permute-start(f32[8,256]{1,0:T(8,128)S(1)} %get-tuple-element.62), channel_id=1, source_target_pairs={{0,1},{1,0},{2,3},{3,2},{4,5},{5,4},{6,7},{7,6},{8,9},{9,8},{10,11... | collective-permute-start | bytes 24584 | tf_op jit(solution)/shard_map/ppermute | solution.py:562
  15.4 5.1 %collective-permute-start.4 = (f32[8,256]{1,0:T(8,128)S(1)}, f32[8,256]{1,0:T(8,128)S(1)}, u32[]{:S(2)}, u32[]{:S(2)}) collective-permute-start(f32[8,256]{1,0:T(8,128)S(1)} %get-tuple-element.73), channel_id=1, source_target_pairs={{1,2},{2,1},{3,4},{4,3},{5,6},{6,5},{9,10},{10,9},{11,12},{12,11},... | collective-permute-start | bytes 24584 | tf_op jit(solution)/shard_map/ppermute | solution.py:562
  16.0 4.4 %collective-permute-start.5 = (f32[8,256]{1,0:T(8,128)S(1)}, f32[8,256]{1,0:T(8,128)S(1)}, u32[]{:S(2)}, u32[]{:S(2)}) collective-permute-start(f32[8,256]{1,0:T(8,128)S(1)} %get-tuple-element.74), channel_id=1, source_target_pairs={{0,1},{1,0},{2,3},{3,2},{4,5},{5,4},{6,7},{7,6},{8,9},{9,8},{10,11... | collective-permute-start | bytes 24584 | tf_op jit(solution)/shard_map/ppermute | solution.py:562
  30.7 5.5 %collective-permute-start.8 = (f32[8,128]{1,0:T(8,128)S(1)}, f32[8,128]{1,0:T(8,128)S(1)}, u32[]{:S(2)}, u32[]{:S(2)}) collective-permute-start(f32[8,128]{1,0:T(8,128)S(1)} %shard_map.111), channel_id=1, source_target_pairs={{0,24},{8,16},{16,8},{24,0},{1,25},{9,17},{17,9},{25,1},{2,26},{10... | collective-permute-start | bytes 12296 | tf_op jit(solution)/shard_map/ppermute | solution.py:578
  34.4 4.5 %collective-permute-start.7 = (f32[8,128]{1,0:T(8,128)S(1)}, f32[8,128]{1,0:T(8,128)S(1)}, u32[]{:S(2)}, u32[]{:S(2)}) collective-permute-start(f32[8,128]{1,0:T(8,128)S(1)} %shard_map.111), channel_id=1, source_target_pairs={{0,16},{8,24},{16,0},{24,8},{1,17},{9,25},{17,1},{25,9},{2,18},{10... | collective-permute-start | bytes 12296 | tf_op jit(solution)/shard_map/ppermute | solution.py:578
  34.4 4.5 %collective-permute-start.6 = (f32[8,128]{1,0:T(8,128)S(1)}, f32[8,128]{1,0:T(8,128)S(1)}, u32[]{:S(2)}, u32[]{:S(2)}) collective-permute-start(f32[8,128]{1,0:T(8,128)S(1)} %shard_map.111), channel_id=1, source_target_pairs={{0,8},{8,0},{16,24},{24,16},{1,9},{9,1},{17,25},{25,17},{2,10},{10... | collective-permute-start | bytes 12296 | tf_op jit(solution)/shard_map/ppermute | solution.py:578
  38.9 0.6 %copy-start = (f32[8,128]{1,0:T(8,128)}, f32[8,128]{1,0:T(8,128)S(1)}, u32[]{:S(2)}) copy-start(f32[8,128]{1,0:T(8,128)S(1)} %add_add_fusion) | copy-start | bytes 12292

commit v7 on v6

--- a/solution.py
+++ b/solution.py
@@ -10,6 +10,7 @@
 LANES = 128
 SUBLANES = 8
 SIDE = 6
+MOMENT_LANES = 8
 VMEM = pl.BlockSpec(memory_space=pltpu.VMEM)
 HBM = pl.BlockSpec(memory_space=pltpu.HBM)
 
@@ -145,12 +146,13 @@
             stacked = [jnp.where(high == h, both, 0.0) for h in heights]
             columns.append(jnp.concatenate(stacked, axis=0).astype(jnp.bfloat16))
         part = lax.dot_general(
+            places[:, i * slots : (i + 1) * slots],
             jnp.concatenate(columns, axis=1),
-            places[:, i * slots : (i + 1) * slots],
             (((1,), (1,)), ((), ())),
             preferred_element_type=jnp.float32,
         )
         total = part if total is None else total + part
+    total = total.T
     out = []
     for n in range(len(heights)):
         piece = total[rows * n : rows * (n + 1)]
@@ -473,7 +475,6 @@
     delta_ref,
 ):
     rows, edge_count = own.shape
-    first = row_ids(rows) < rows // 2
     scale = scale_in[...]
     inverse_scale = 1.0 / scale
     prior, above = take_rims(across_in, beside_in)
@@ -488,33 +489,31 @@
     sums = inner_products(
         step, sums_in[...], cut(own), cut(delta_ref), forms, across_in, beside_in
     )
-    sums_ref[...] = jnp.where(first, sums, scale)
-
-
-def combine_stage(everyone, sums_in, terms0, terms1, terms2, out_ref):
-    rows = sums_in.shape[0]
     groups = rows // 2
-    first = row_ids(rows) < groups
-
-    def scale_of(block):
-        return jnp.where(first, swap_halves(block), block)
-
-    parts = [everyone[q] for q in range(everyone.shape[0])]
-    scales = [scale_of(block) for block in parts]
-    top = functools.reduce(jnp.maximum, scales)
     lanes = lane_ids(rows)
-    inverse_top = 1.0 / top
-    total = None
-    for block, scale in zip(parts, scales):
-        ratio = scale * inverse_top
-        power = jnp.ones_like(ratio)
-        factor = jnp.ones_like(ratio)
-        for k in range(1, 6):
-            power = power * ratio
-            factor = jnp.where(lanes == k, power, factor)
-        term = block * factor
-        total = term if total is None else total + term
-    m = [jnp.broadcast_to(total[:, k : k + 1], (rows, LANES)) for k in range(6)]
+    half = LANES // 2
+    packed = scale
+    for g in range(groups):
+        row = pltpu.roll(spread(sums[g : g + 1], rows), MOMENT_LANES * g, 1)
+        here = (lanes >= MOMENT_LANES * g) & (lanes < MOMENT_LANES * (g + 1)) & (lanes < half)
+        packed = jnp.where(here, row, packed)
+    sums_ref[...] = packed[:1]
+
+
+def combine_stage(groups, everyone, scale_in, terms0, terms1, terms2, out_ref):
+    rows = scale_in.shape[0]
+    parts = jnp.concatenate([everyone[q] for q in range(everyone.shape[0])], axis=0)
+    scale = pltpu.roll(parts, LANES // 2, 1)
+    top = jnp.max(scale, axis=0, keepdims=True)
+    ratio = scale / top
+    kind = lane_ids(parts.shape[0]) & (MOMENT_LANES - 1)
+    power = jnp.ones_like(ratio)
+    factor = jnp.ones_like(ratio)
+    for k in range(1, 6):
+        power = power * ratio
+        factor = jnp.where(kind == k, power, factor)
+    total = spread(jnp.sum(parts * factor, axis=0, keepdims=True), rows)
+    m = [total] + [pltpu.roll(total, LANES - k, 1) for k in range(1, 6)]
     l1 = m[2] / m[1]
     l2 = m[3] / m[1]
     d2 = m[3] - l1 * m[2]
@@ -526,14 +525,16 @@
     c2 = y2 / d3
     c1 = y1 / d2 - l3 * c2
     c0 = m[0] / m[1] - l1 * c1 - l2 * c2
-    mine = scale_of(sums_in[...]) * inverse_top
-    c0 = c0 * inverse_top
-    c1 = c1 * mine * inverse_top
-    c2 = c2 * mine * mine * inverse_top
+    top = spread(top, rows)
+    mine = scale_in[...] / top
+    c0 = c0 / top
+    c1 = c1 * mine / top
+    c2 = c2 * mine * mine / top
     out = None
     for terms, c in ((terms0, c0), (terms1, c1), (terms2, c2)):
         for g in range(groups):
-            one = terms[g] * spread(c[g : g + 1], out_ref.shape[0])
+            lane = MOMENT_LANES * g
+            one = terms[g] * jnp.broadcast_to(c[:1, lane : lane + 1], out_ref.shape)
             out = one if out is None else out + one
     out_ref[...] = out
 
@@ -690,13 +691,13 @@
     term, sums = call(
         functools.partial(last_stage, polars, 2),
         (own, order, inverse, across, beside, scale, sums, picks, blocks, edges, heavy),
-        [terms_shape, sums_shape],
+        [terms_shape, shape(1, LANES)],
         (pltpu.VMEM((rows, 2 * rim), jnp.float32),),
     )
     terms.append(term)
     term = call(
-        combine_stage,
-        (gather_all(sums, "dom"), sums, *terms),
+        functools.partial(combine_stage, groups),
+        (gather_all(sums, "dom"), scale, *terms),
         shape(tall, LANES),
     )
     gradient = sum_over(term, "freq").reshape(1, slots)

time: 39.8 us -> 39.8 us (level)
  transfers between devices with their start and end apart: 9 -> 9, of which waited for: 2 -> 2; matrix products, arithmetic and copies ran while one was open for 0% -> 0% of each run, Pallas kernels for 11% -> 10%
where the time goes in v7:
time: 39.8 us; the launch traced here: 39.6 us
  starting transfers between devices  17 us (43%)
  blocking collectives  9.56 us (24%)
  Pallas kernels  7.96 us (20%)
  waiting for transfers between devices  3.74 us (9%)
  between operations  0.73 us (2%)
  other arithmetic  0.62 us (2%)
    ppermute x6, starting transfers between devices, swap(): return lax.ppermute(block, axis, route)  12.5 us
    all_to_all x1, blocking collectives, gather_all(): return lax.all_to_all(copies, axis, 0, 0)  9.56 us
    pallas_call x8, Pallas kernels, call(): pl.pallas_call(kernel, out_shape=outs, in_specs=space if isinstance(space...  7.96 us
    ppermute x3, starting transfers between devices, sum_over(): lax.ppermute(block, axis, [(i, i ^ step) for i in range(size)])  4.45 us
    ppermute x3, waiting for transfers between devices, sum_over(): lax.ppermute(block, axis, [(i, i ^ step) for i in range(size)])  3.73 us
  transfers between devices with their start and end apart: 9, of which 2 were waited for; matrix products, arithmetic and copies ran while one was open for 0% of the time, Pallas kernels for 10%

profile of v7, /device:TPU:0, one launch (start us, length us, event | category | flops | bytes accessed | tf_op | source)
XLA Modules:
  0.0 39.6 jit_solution(1811833909388153403)
XLA Ops:
  0.6 0.8 %shard_map.104 = (f32[8,256]{1,0:T(8,128)S(1)}, f32[8,256]{1,0:T(8,128)S(1)}, f32[8,1280]{1,0:T(8,128)S(1)}, s32[8,256]{1,0:T(8,128)S(1)}) custom-call(f32[4,1,1280]{2,1,0:T(1,128)} %bitcast.16, s32[1,256]{1,0:T(1,128)} %order_in.1), custom_call_target="tpu_custom_call" | custom-call | tf_op jit(solution)/shard_map/pallas_call | solution.py:547
  1.4 0.7 %collective-permute-start = (f32[8,256]{1,0:T(8,128)S(1)}, f32[8,256]{1,0:T(8,128)S(1)}, u32[]{:S(2)}, u32[]{:S(2)}) collective-permute-start(f32[8,256]{1,0:T(8,128)S(1)} %get-tuple-element.44), channel_id=1, source_target_pairs={{1,2},{2,1},{3,4},{4,3},{5,6},{6,5},{9,10},{10,9},{11,12},{12,11},... | collective-permute-start | bytes 24584 | tf_op jit(solution)/shard_map/ppermute | solution.py:563
  2.1 4.4 %collective-permute-start.1 = (f32[8,256]{1,0:T(8,128)S(1)}, f32[8,256]{1,0:T(8,128)S(1)}, u32[]{:S(2)}, u32[]{:S(2)}) collective-permute-start(f32[8,256]{1,0:T(8,128)S(1)} %get-tuple-element.45), channel_id=1, source_target_pairs={{0,1},{1,0},{2,3},{3,2},{4,5},{5,4},{6,7},{7,6},{8,9},{9,8},{10,11... | collective-permute-start | bytes 24584 | tf_op jit(solution)/shard_map/ppermute | solution.py:563
  6.4 1.9 %shard_map.105 = (bf16[128,6144]{1,0:T(8,128)(2,1)S(1)}, f32[72,8,128]{2,1,0:T(8,128)S(1)}, f32[8,128]{1,0:T(8,128)S(1)}, f32[24,8,128]{2,1,0:T(8,128)S(1)}, f32...) custom-call(f32[2]{0:T(128)} %angular_in.1, ...), custom_call_target="tpu_custom_call" | custom-call | flops 4000000 | bytes 4000000 | tf_op jit(solution)/shard_map/pallas_call | solution.py:547
  8.4 0.0 collective-permute-done.across_in
  8.4 0.0 collective-permute-done.1.beside_in
  8.4 1.1 %shard_map.106 = (s32[8,256]{1,0:T(8,128)S(1)}, f32[8,512]{1,0:T(8,128)S(1)}, f32[24,8,128]{2,1,0:T(8,128)S(1)}, f32[384,128]{1,0:T(8,128)S(1)}, f32[8,128]{1,0:...) custom-call(s32[8,256]{1,0:T(8,128)S(1)} %get-tuple-element.43.order_ref, ...), custom_call_target="tpu_custom_call" | custom-call | tf_op jit(solution)/shard_map/pallas_call | solution.py:547
  9.5 0.7 %collective-permute-start.2 = (f32[8,256]{1,0:T(8,128)S(1)}, f32[8,256]{1,0:T(8,128)S(1)}, u32[]{:S(2)}, u32[]{:S(2)}) collective-permute-start(f32[8,256]{1,0:T(8,128)S(1)} %get-tuple-element.61), channel_id=1, source_target_pairs={{1,2},{2,1},{3,4},{4,3},{5,6},{6,5},{9,10},{10,9},{11,12},{12,11},... | collective-permute-start | bytes 24584 | tf_op jit(solution)/shard_map/ppermute | solution.py:563
  10.2 2.9 %collective-permute-start.3 = (f32[8,256]{1,0:T(8,128)S(1)}, f32[8,256]{1,0:T(8,128)S(1)}, u32[]{:S(2)}, u32[]{:S(2)}) collective-permute-start(f32[8,256]{1,0:T(8,128)S(1)} %get-tuple-element.62), channel_id=1, source_target_pairs={{0,1},{1,0},{2,3},{3,2},{4,5},{5,4},{6,7},{7,6},{8,9},{9,8},{10,11... | collective-permute-start | bytes 24584 | tf_op jit(solution)/shard_map/ppermute | solution.py:563
  13.1 1.1 %shard_map.107 = (f32[24,8,128]{2,1,0:T(8,128)S(1)}, f32[4,8,128]{2,1,0:T(8,128)S(1)}, f32[8,128]{1,0:T(8,128)S(1)}, f32[8,1280]{1,0:T(8,128)S(1)}, f32[24,8,128]{2,1,0:T(8,128)S(1)}) custom-call(f32[8,1280]{1,0:T(8,128)S(1)} %get-tuple-element.42.source.own, f32[8,512]{1,0:T(8,128)S(1)} %get-tuple-element.51.delta, f32[8,128]{1,0:T(8,128)S(1)} %get-tuple-element.52.forms, ...), custom_call_target="tpu_custom_call" | custom-call | flops 4000000 | bytes 4000000 | tf_op jit(solution)/shard_map/pallas_call | solution.py:547
  14.3 0.0 collective-permute-done.2.across_in
  14.3 1.0 %shard_map.108 = (f32[8,512]{1,0:T(8,128)S(1)}, f32[24,8,128]{2,1,0:T(8,128)S(1)}, f32[384,128]{1,0:T(8,128)S(1)}, f32[8,128]{1,0:T(8,128)S(1)}, f32[8,512]{1,0:...) custom-call(s32[8,256]{1,0:T(8,128)S(1)} %get-tuple-element.43.order_ref, ...), custom_call_target="tpu_custom_call" | custom-call | tf_op jit(solution)/shard_map/pallas_call | solution.py:547
  15.3 0.7 %collective-permute-start.4 = (f32[8,256]{1,0:T(8,128)S(1)}, f32[8,256]{1,0:T(8,128)S(1)}, u32[]{:S(2)}, u32[]{:S(2)}) collective-permute-start(f32[8,256]{1,0:T(8,128)S(1)} %get-tuple-element.73), channel_id=1, source_target_pairs={{1,2},{2,1},{3,4},{4,3},{5,6},{6,5},{9,10},{10,9},{11,12},{12,11},... | collective-permute-start | bytes 24584 | tf_op jit(solution)/shard_map/ppermute | solution.py:563
  16.0 3.2 %collective-permute-start.5 = (f32[8,256]{1,0:T(8,128)S(1)}, f32[8,256]{1,0:T(8,128)S(1)}, u32[]{:S(2)}, u32[]{:S(2)}) collective-permute-start(f32[8,256]{1,0:T(8,128)S(1)} %get-tuple-element.74), channel_id=1, source_target_pairs={{0,1},{1,0},{2,3},{3,2},{4,5},{5,4},{6,7},{7,6},{8,9},{9,8},{10,11... | collective-permute-start | bytes 24584 | tf_op jit(solution)/shard_map/ppermute | solution.py:563
  19.2 1.1 %shard_map.109 = (f32[4,8,128]{2,1,0:T(8,128)S(1)}, f32[8,128]{1,0:T(8,128)S(1)}, f32[8,1280]{1,0:T(8,128)S(1)}, f32[24,8,128]{2,1,0:T(8,128)S(1)}) custom-call(f32[8,1280]{1,0:T(8,128)S(1)} %get-tuple-element.60.own, f32[8,512]{1,0:T(8,128)S(1)} %get-tuple-element.65.delta, f32[8,128]{1,0:T(8,128)S(1)} %get-tuple-element.66.forms, ...), custom_call_target="tpu_custom_call" | custom-call | flops 4000000 | bytes 4000000 | tf_op jit(solution)/shard_map/pallas_call | solution.py:547
  20.3 0.6 %shard_map.110 = (f32[4,8,128]{2,1,0:T(8,128)S(1)}, f32[1,128]{1,0:T(1,128)S(1)}) custom-call(f32[8,1280]{1,0:T(8,128)S(1)} %get-tuple-element.72.own, s32[8,256]{1,0:T(8,128)S(1)} %get-tuple-element.43.order_ref, s32[8,256]{1,0:T(8,128)S(1)} %get-tuple-element.64.rest_0_.inverse_in, f32[8,256]{1,0:T(8,128)S(1)} %collective-permute-done.4.across_in, ...), custom_call_target="tpu_custom_call" | custom-call | tf_op jit(solution)/shard_map/pallas_call | solution.py:547
  20.9 9.6 %all_to_all.5.everyone = f32[8,1,128]{2,1,0:T(1,128)S(1)} all-to-all(f32[8,1,128]{2,1,0:T(1,128)S(1)} %broadcast_in_dim.13), channel_id=1, replica_groups=mesh['freq'=4,'dom'=8] {'dom'}, dimensions={0} | all-to-all | bytes 8192 | tf_op jit(solution)/shard_map/all_to_all | solution.py:569
  30.4 0.3 shard_map.111
  30.8 3.7 %collective-permute-start.8 = (f32[8,128]{1,0:T(8,128)S(1)}, f32[8,128]{1,0:T(8,128)S(1)}, u32[]{:S(2)}, u32[]{:S(2)}) collective-permute-start(f32[8,128]{1,0:T(8,128)S(1)} %shard_map.111), channel_id=1, source_target_pairs={{0,24},{8,16},{16,8},{24,0},{1,25},{9,17},{17,9},{25,1},{2,26},{10... | collective-permute-start | bytes 12296 | tf_op jit(solution)/shard_map/ppermute | solution.py:579
  34.4 0.8 %collective-permute-start.6 = (f32[8,128]{1,0:T(8,128)S(1)}, f32[8,128]{1,0:T(8,128)S(1)}, u32[]{:S(2)}, u32[]{:S(2)}) collective-permute-start(f32[8,128]{1,0:T(8,128)S(1)} %shard_map.111), channel_id=1, source_target_pairs={{0,8},{8,0},{16,24},{24,16},{1,9},{9,1},{17,25},{25,17},{2,10},{10... | collective-permute-start | bytes 12296 | tf_op jit(solution)/shard_map/ppermute | solution.py:579
  35.2 1.0 %collective-permute-done.8 = f32[8,128]{1,0:T(8,128)S(1)} collective-permute-done((f32[8,128]{1,0:T(8,128)S(1)}, f32[8,128]{1,0:T(8,128)S(1)}, u32[]{:S(2)}, u32[]{:S(2)}) %collective-permute-start.8) | collective-permute-done | bytes 4128 | tf_op jit(solution)/shard_map/ppermute | solution.py:579
  36.2 2.7 %collective-permute-done.7 = f32[8,128]{1,0:T(8,128)S(1)} collective-permute-done((f32[8,128]{1,0:T(8,128)S(1)}, f32[8,128]{1,0:T(8,128)S(1)}, u32[]{:S(2)}, u32[]{:S(2)}) %collective-permute-start.7) | collective-permute-done | bytes 4128 | tf_op jit(solution)/shard_map/ppermute | solution.py:579
  39.0 0.0 copy-start
  39.0 0.6 %exponential_multiply_fusion = f32[1,1024]{1,0:T(1,128)} fusion(f32[1,1024]{1,0:T(1,128)S(1)} %bitcast.10, f32[1,1024]{1,0:T(1,128)S(1)} %bitcast.17), kind=kLoop, calls=%fused_computation | loop fusion | flops 2048 | bytes 12288 | tf_op jit(solution)/shard_map/mul | solution.py:704
  (9 shorter events, 0.0 us)
Async XLA Ops:
  1.4 7.0 %collective-permute-start = (f32[8,256]{1,0:T(8,128)S(1)}, f32[8,256]{1,0:T(8,128)S(1)}, u32[]{:S(2)}, u32[]{:S(2)}) collective-permute-start(f32[8,256]{1,0:T(8,128)S(1)} %get-tuple-element.44), channel_id=1, source_target_pairs={{1,2},{2,1},{3,4},{4,3},{5,6},{6,5},{9,10},{10,9},{11,12},{12,11},... | collective-permute-start | bytes 24584 | tf_op jit(solution)/shard_map/ppermute | solution.py:563
  2.1 6.3 %collective-permute-start.1 = (f32[8,256]{1,0:T(8,128)S(1)}, f32[8,256]{1,0:T(8,128)S(1)}, u32[]{:S(2)}, u32[]{:S(2)}) collective-permute-start(f32[8,256]{1,0:T(8,128)S(1)} %get-tuple-element.45), channel_id=1, source_target_pairs={{0,1},{1,0},{2,3},{3,2},{4,5},{5,4},{6,7},{7,6},{8,9},{9,8},{10,11... | collective-permute-start | bytes 24584 | tf_op jit(solution)/shard_map/ppermute | solution.py:563
  9.5 4.7 %collective-permute-start.2 = (f32[8,256]{1,0:T(8,128)S(1)}, f32[8,256]{1,0:T(8,128)S(1)}, u32[]{:S(2)}, u32[]{:S(2)}) collective-permute-start(f32[8,256]{1,0:T(8,128)S(1)} %get-tuple-element.61), channel_id=1, source_target_pairs={{1,2},{2,1},{3,4},{4,3},{5,6},{6,5},{9,10},{10,9},{11,12},{12,11},... | collective-permute-start | bytes 24584 | tf_op jit(solution)/shard_map/ppermute | solution.py:563
  10.2 4.1 %collective-permute-start.3 = (f32[8,256]{1,0:T(8,128)S(1)}, f32[8,256]{1,0:T(8,128)S(1)}, u32[]{:S(2)}, u32[]{:S(2)}) collective-permute-start(f32[8,256]{1,0:T(8,128)S(1)} %get-tuple-element.62), channel_id=1, source_target_pairs={{0,1},{1,0},{2,3},{3,2},{4,5},{5,4},{6,7},{7,6},{8,9},{9,8},{10,11... | collective-permute-start | bytes 24584 | tf_op jit(solution)/shard_map/ppermute | solution.py:563
  15.3 5.0 %collective-permute-start.4 = (f32[8,256]{1,0:T(8,128)S(1)}, f32[8,256]{1,0:T(8,128)S(1)}, u32[]{:S(2)}, u32[]{:S(2)}) collective-permute-start(f32[8,256]{1,0:T(8,128)S(1)} %get-tuple-element.73), channel_id=1, source_target_pairs={{1,2},{2,1},{3,4},{4,3},{5,6},{6,5},{9,10},{10,9},{11,12},{12,11},... | collective-permute-start | bytes 24584 | tf_op jit(solution)/shard_map/ppermute | solution.py:563
  16.0 4.3 %collective-permute-start.5 = (f32[8,256]{1,0:T(8,128)S(1)}, f32[8,256]{1,0:T(8,128)S(1)}, u32[]{:S(2)}, u32[]{:S(2)}) collective-permute-start(f32[8,256]{1,0:T(8,128)S(1)} %get-tuple-element.74), channel_id=1, source_target_pairs={{0,1},{1,0},{2,3},{3,2},{4,5},{5,4},{6,7},{7,6},{8,9},{9,8},{10,11... | collective-permute-start | bytes 24584 | tf_op jit(solution)/shard_map/ppermute | solution.py:563
  30.8 5.5 %collective-permute-start.8 = (f32[8,128]{1,0:T(8,128)S(1)}, f32[8,128]{1,0:T(8,128)S(1)}, u32[]{:S(2)}, u32[]{:S(2)}) collective-permute-start(f32[8,128]{1,0:T(8,128)S(1)} %shard_map.111), channel_id=1, source_target_pairs={{0,24},{8,16},{16,8},{24,0},{1,25},{9,17},{17,9},{25,1},{2,26},{10... | collective-permute-start | bytes 12296 | tf_op jit(solution)/shard_map/ppermute | solution.py:579
  34.4 4.5 %collective-permute-start.7 = (f32[8,128]{1,0:T(8,128)S(1)}, f32[8,128]{1,0:T(8,128)S(1)}, u32[]{:S(2)}, u32[]{:S(2)}) collective-permute-start(f32[8,128]{1,0:T(8,128)S(1)} %shard_map.111), channel_id=1, source_target_pairs={{0,16},{8,24},{16,0},{24,8},{1,17},{9,25},{17,1},{25,9},{2,18},{10... | collective-permute-start | bytes 12296 | tf_op jit(solution)/shard_map/ppermute | solution.py:579
  34.4 4.5 %collective-permute-start.6 = (f32[8,128]{1,0:T(8,128)S(1)}, f32[8,128]{1,0:T(8,128)S(1)}, u32[]{:S(2)}, u32[]{:S(2)}) collective-permute-start(f32[8,128]{1,0:T(8,128)S(1)} %shard_map.111), channel_id=1, source_target_pairs={{0,8},{8,0},{16,24},{24,16},{1,9},{9,1},{17,25},{25,17},{2,10},{10... | collective-permute-start | bytes 12296 | tf_op jit(solution)/shard_map/ppermute | solution.py:579
  39.0 0.6 %copy-start = (f32[8,128]{1,0:T(8,128)}, f32[8,128]{1,0:T(8,128)S(1)}, u32[]{:S(2)}) copy-start(f32[8,128]{1,0:T(8,128)S(1)} %add_add_fusion) | copy-start | bytes 12292

commit v8 on v6

--- a/solution.py
+++ b/solution.py
@@ -132,25 +132,24 @@
     return total
 
 
-def scatter(pieces, edges, places, heights):
+def scatter(pieces, edges, places, heights, values):
     depth = SIDE * edges.shape[1]
     rows = pieces.shape[0] // depth
-    slots = edges.shape[1] * LANES
-    total = None
     for i in range(SIDE):
-        columns = []
         for s in range(edges.shape[1]):
-            both = pieces[pl.ds(i * edges.shape[1] + s, rows, stride=depth), :]
+            at = i * edges.shape[1] + s
+            both = pieces[pl.ds(at, rows, stride=depth), :]
             high = spread(edges[i, s : s + 1, :] >> 7, rows)
             stacked = [jnp.where(high == h, both, 0.0) for h in heights]
-            columns.append(jnp.concatenate(stacked, axis=0).astype(jnp.bfloat16))
-        part = lax.dot_general(
-            jnp.concatenate(columns, axis=1),
-            places[:, i * slots : (i + 1) * slots],
-            (((1,), (1,)), ((), ())),
-            preferred_element_type=jnp.float32,
-        )
-        total = part if total is None else total + part
+            values[:, at * LANES : (at + 1) * LANES] = jnp.concatenate(stacked, axis=0).astype(
+                jnp.bfloat16
+            )
+    total = lax.dot_general(
+        values[...],
+        places[...],
+        (((1,), (1,)), ((), ())),
+        preferred_element_type=jnp.float32,
+    )
     out = []
     for n in range(len(heights)):
         piece = total[rows * n : rows * (n + 1)]
@@ -195,24 +194,23 @@
     return copies
 
 
-def rims_stage(
-    source_in, order_in, across_ref, beside_ref, stacked_ref, order_ref, source, order, arrived
-):
+def stacked_chunk(source, at):
+    piece = [source[g, :, at : at + LANES] for g in range(source.shape[0])]
+    return jnp.concatenate(piece + piece, axis=0)
+
+
+def rims_stage(source_in, order_in, across_ref, beside_ref, source, order_ref, order, arrived):
     for copy in start_copies(((source_in, source), (order_in, order)), arrived):
         copy.wait()
-    groups = source.shape[0]
-    rows = stacked_ref.shape[0]
-    first = row_ids(rows) < groups
-    chunks = []
-    for c in range(0, source.shape[-1], LANES):
-        piece = [source[g, :, c : c + LANES] for g in range(groups)]
-        chunks.append(jnp.concatenate(piece + piece, axis=0))
-    put_chunks(stacked_ref, chunks)
+    rows, rim = order_ref.shape
+    first = row_ids(rows) < rows // 2
     order_ref[...] = spread(order[...], rows)
     numbers = [x.astype(jnp.float32) for x in cut(order_ref)]
-    count = len(numbers)
-    lower = [jnp.where(first, x, o) for x, o in zip(chunks[:count], numbers)]
-    upper = [jnp.where(first, x, 1.0) for x in chunks[len(chunks) - count :]]
+    lower = [stacked_chunk(source, c) for c in range(0, rim, LANES)]
+    start = source.shape[-1] - rim
+    upper = [stacked_chunk(source, start + c) for c in range(0, rim, LANES)]
+    lower = [jnp.where(first, x, o) for x, o in zip(lower, numbers)]
+    upper = [jnp.where(first, x, 1.0) for x in upper]
     put_rims(across_ref, beside_ref, lower, upper)
 
 
@@ -229,6 +227,7 @@
     blocks_ref,
     scale_ref,
     picks_ref,
+    stacked_ref,
     rates,
     mass,
     sigma,
@@ -263,7 +262,9 @@
         return carry
 
     lax.fori_loop(0, SIDE, body, 0)
-    put_picks(picks_ref, source, edges, scale_ref.shape[0] // 2)
+    count = source.shape[-1]
+    put_chunks(stacked_ref, [stacked_chunk(source, c) for c in range(0, count, LANES)])
+    put_picks(picks_ref, stacked_ref, edges, source.shape[0])
     for copy in copies[1:]:
         copy.wait()
     for f in range(angular.shape[0]):
@@ -365,7 +366,7 @@
         inverse_ref, *rest = rest
     else:
         inverse_in, *rest = rest
-    delta_ref, picks_ref, pieces, forms_ref, rims_ref, across_ref, beside_ref = rest
+    delta_ref, picks_ref, pieces, forms_ref, rims_ref, across_ref, beside_ref, values = rest
     rows = delta_ref.shape[0]
     groups = rows // 2
     first = row_ids(rows) < groups
@@ -390,7 +391,7 @@
         delta_ref, own_picks, blocks, edges, polars, edge_count, pieces, visit
     )
     rim = len(prior)
-    chunks = scatter(pieces, edges, places, rim_heights(edge_count, rim)[0])
+    chunks = scatter(pieces, edges, places, rim_heights(edge_count, rim)[0], values)
     put_chunks(rims_ref, chunks)
     put_rims(
         across_ref,
@@ -428,14 +429,14 @@
     *rest,
 ):
     if step == 0:
-        rates, forward, mass, live, heavy, terms_ref, sums_ref, image_ref, picks_ref = rest
+        rates, forward, mass, live, heavy, terms_ref, sums_ref, image_ref, picks_ref, values = rest
     else:
-        heavy, terms_ref, sums_ref, image_ref, picks_ref = rest
+        heavy, terms_ref, sums_ref, image_ref, picks_ref, values = rest
     rows, edge_count = own.shape
     groups = rows // 2
     rim = rims.shape[-1] // LANES // 2
     outer = cut(rims)
-    inner = scatter(pieces, edges, places, rim_heights(edge_count, rim)[1])
+    inner = scatter(pieces, edges, places, rim_heights(edge_count, rim)[1], values)
     put_chunks(image_ref, outer[:rim] + inner + outer[rim:])
     put_picks(picks_ref, image_ref, edges, groups)
     if step == 0:
@@ -623,9 +624,8 @@
     across, beside, source, order = call(
         rims_stage,
         pinned(source, neighbour_map),
-        [rim_shape, rim_shape, field_shape, shape(rows, rim, kind=jnp.int32)],
+        [rim_shape, rim_shape, shape(*source.shape), shape(rows, rim, kind=jnp.int32)],
         (
-            pltpu.VMEM(source.shape, source.dtype),
             pltpu.VMEM(neighbour_map.shape, neighbour_map.dtype),
             pltpu.SemaphoreType.DMA((2,)),
         ),
@@ -633,7 +633,7 @@
     )
     across, beside = swap(across, "dom", 1), swap(beside, "dom", 0)
     kept = [jax.ShapeDtypeStruct(x.shape, x.dtype) for x in (mass, sigma, live, edges, forward)]
-    places, blocks, scale, picks, rates, mass, sigma, live, edges, forward = call(
+    places, blocks, scale, picks, own, rates, mass, sigma, live, edges, forward = call(
         table_stage,
         [*pinned(angular, stiff, mass, sigma, live, edges, forward), source],
         [
@@ -641,6 +641,7 @@
             shape(freqs * SIDE * SIDE, tall, LANES),
             sums_shape,
             picks_shape,
+            field_shape,
             shape(freqs, tall, LANES),
             *kept,
         ],
@@ -662,17 +663,20 @@
         rim_shape,
     ]
     back_shapes = [terms_shape, sums_shape, field_shape, picks_shape]
-    own, sums, terms = source, jnp.zeros((rows, LANES), jnp.float32), []
+    sums, terms = jnp.zeros((rows, LANES), jnp.float32), []
+    outer, inner = rim_heights(edge_count, rim // LANES)
+    outer = [pltpu.VMEM((rows * len(outer), SIDE * slots), jnp.bfloat16)]
+    inner = [pltpu.VMEM((rows * len(inner), SIDE * slots), jnp.bfloat16)]
     for step in range(2):
         arrived = (across, beside)
         given = (order, *arrived, scale, picks, blocks, edges, places)
         front = functools.partial(front_stage, polars, step, edge_count)
         if step == 0:
             inverse, *outs = call(
-                front, given, [shape(rows, rim, kind=jnp.int32), *front_shapes]
+                front, given, [shape(rows, rim, kind=jnp.int32), *front_shapes], outer
             )
         else:
-            outs = call(front, (*given, inverse), front_shapes)
+            outs = call(front, (*given, inverse), front_shapes, outer)
         delta, picks, pieces, forms, rims, across, beside = outs
         across, beside = swap(across, "dom", 1), swap(beside, "dom", 0)
         given = (own, delta, forms, *arrived, sums, picks, pieces, rims, edges, places)
@@ -682,10 +686,11 @@
                 back,
                 (*given, rates, forward, mass, live),
                 [picks_shape, *back_shapes],
+                inner,
                 cost=4_000_000,
             )
         else:
-            term, sums, own, picks = call(back, (*given, heavy), back_shapes, cost=4_000_000)
+            term, sums, own, picks = call(back, (*given, heavy), back_shapes, inner, cost=4_000_000)
         terms.append(term)
     term, sums = call(
         functools.partial(last_stage, polars, 2),

time: 39.8 us -> 39.8 us (level)
  no operation moved by 1% of the time
where the time goes in v8:
time: 39.8 us; the launch traced here: 39.5 us
  starting transfers between devices  17 us (43%)
  blocking collectives  9.64 us (24%)
  Pallas kernels  7.77 us (20%)
  waiting for transfers between devices  3.73 us (9%)
  between operations  0.74 us (2%)
  other arithmetic  0.62 us (2%)
    ppermute x6, starting transfers between devices, swap(): return lax.ppermute(block, axis, route)  12.5 us
    all_to_all x1, blocking collectives, gather_all(): return lax.all_to_all(copies, axis, 0, 0)  9.64 us
    pallas_call x8, Pallas kernels, call(): pl.pallas_call(kernel, out_shape=outs, in_specs=space if isinstance(space...  7.77 us
    ppermute x3, starting transfers between devices, sum_over(): lax.ppermute(block, axis, [(i, i ^ step) for i in range(size)])  4.45 us
    ppermute x3, waiting for transfers between devices, sum_over(): lax.ppermute(block, axis, [(i, i ^ step) for i in range(size)])  3.72 us
  transfers between devices with their start and end apart: 9, of which 2 were waited for; matrix products, arithmetic and copies ran while one was open for 0% of the time, Pallas kernels for 11%

profile of v8, /device:TPU:0, one launch (start us, length us, event | category | flops | bytes accessed | tf_op | source)
XLA Modules:
  0.0 39.5 jit_solution(14809039674459609391)
XLA Ops:
  0.6 0.8 %shard_map.104 = (f32[8,256]{1,0:T(8,128)S(1)}, f32[8,256]{1,0:T(8,128)S(1)}, f32[4,1,1280]{2,1,0:T(1,128)S(1)}, s32[8,256]{1,0:T(8,128)S(1)}) custom-call(f32[4,1,1280]{2,1,0:T(1,128)} %bitcast.14, s32[1,256]{1,0:T(1,128)} %order_in.1), custom_call_target="tpu_custom_call" | custom-call | tf_op jit(solution)/shard_map/pallas_call | solution.py:547
  1.4 0.7 %collective-permute-start = (f32[8,256]{1,0:T(8,128)S(1)}, f32[8,256]{1,0:T(8,128)S(1)}, u32[]{:S(2)}, u32[]{:S(2)}) collective-permute-start(f32[8,256]{1,0:T(8,128)S(1)} %get-tuple-element.46), channel_id=1, source_target_pairs={{1,2},{2,1},{3,4},{4,3},{5,6},{6,5},{9,10},{10,9},{11,12},{12,11},... | collective-permute-start | bytes 24584 | tf_op jit(solution)/shard_map/ppermute | solution.py:563
  2.1 4.4 %collective-permute-start.1 = (f32[8,256]{1,0:T(8,128)S(1)}, f32[8,256]{1,0:T(8,128)S(1)}, u32[]{:S(2)}, u32[]{:S(2)}) collective-permute-start(f32[8,256]{1,0:T(8,128)S(1)} %get-tuple-element.47), channel_id=1, source_target_pairs={{0,1},{1,0},{2,3},{3,2},{4,5},{5,4},{6,7},{7,6},{8,9},{9,8},{10,11... | collective-permute-start | bytes 24584 | tf_op jit(solution)/shard_map/ppermute | solution.py:563
  6.4 1.9 %shard_map.105 = (bf16[128,6144]{1,0:T(8,128)(2,1)S(1)}, f32[72,8,128]{2,1,0:T(8,128)S(1)}, f32[8,128]{1,0:T(8,128)S(1)}, f32[24,8,128]{2,1,0:T(8,128)S(1)}, f32...) custom-call(f32[2]{0:T(128)} %angular_in.1, ...), custom_call_target="tpu_custom_call" | custom-call | flops 4000000 | bytes 4000000 | tf_op jit(solution)/shard_map/pallas_call | solution.py:547
  8.4 1.1 %shard_map.106 = (s32[8,256]{1,0:T(8,128)S(1)}, f32[8,512]{1,0:T(8,128)S(1)}, f32[24,8,128]{2,1,0:T(8,128)S(1)}, f32[384,128]{1,0:T(8,128)S(1)}, f32[8,128]{1,0:...) custom-call(s32[8,256]{1,0:T(8,128)S(1)} %get-tuple-element.45.order_ref, ...), custom_call_target="tpu_custom_call" | custom-call | tf_op jit(solution)/shard_map/pallas_call | solution.py:547
  9.5 0.7 %collective-permute-start.2 = (f32[8,256]{1,0:T(8,128)S(1)}, f32[8,256]{1,0:T(8,128)S(1)}, u32[]{:S(2)}, u32[]{:S(2)}) collective-permute-start(f32[8,256]{1,0:T(8,128)S(1)} %get-tuple-element.63), channel_id=1, source_target_pairs={{1,2},{2,1},{3,4},{4,3},{5,6},{6,5},{9,10},{10,9},{11,12},{12,11},... | collective-permute-start | bytes 24584 | tf_op jit(solution)/shard_map/ppermute | solution.py:563
  10.2 2.9 %collective-permute-start.3 = (f32[8,256]{1,0:T(8,128)S(1)}, f32[8,256]{1,0:T(8,128)S(1)}, u32[]{:S(2)}, u32[]{:S(2)}) collective-permute-start(f32[8,256]{1,0:T(8,128)S(1)} %get-tuple-element.64), channel_id=1, source_target_pairs={{0,1},{1,0},{2,3},{3,2},{4,5},{5,4},{6,7},{7,6},{8,9},{9,8},{10,11... | collective-permute-start | bytes 24584 | tf_op jit(solution)/shard_map/ppermute | solution.py:563
  13.1 1.2 %shard_map.107 = (f32[24,8,128]{2,1,0:T(8,128)S(1)}, f32[4,8,128]{2,1,0:T(8,128)S(1)}, f32[8,128]{1,0:T(8,128)S(1)}, f32[8,1280]{1,0:T(8,128)S(1)}, f32[24,8,128]{2,1,0:T(8,128)S(1)}) custom-call(f32[8,1280]{1,0:T(8,128)S(1)} %get-tuple-element.44.own, f32[8,512]{1,0:T(8,128)S(1)} %get-tuple-element.53.delta, f32[8,128]{1,0:T(8,128)S(1)} %get-tuple-element.54.forms, ...), custom_call_target="tpu_custom_call" | custom-call | flops 4000000 | bytes 4000000 | tf_op jit(solution)/shard_map/pallas_call | solution.py:547
  14.3 0.0 collective-permute-done.2.across_in
  14.3 0.0 collective-permute-done.3.beside_in
  14.3 1.0 %shard_map.108 = (f32[8,512]{1,0:T(8,128)S(1)}, f32[24,8,128]{2,1,0:T(8,128)S(1)}, f32[384,128]{1,0:T(8,128)S(1)}, f32[8,128]{1,0:T(8,128)S(1)}, f32[8,512]{1,0:...) custom-call(s32[8,256]{1,0:T(8,128)S(1)} %get-tuple-element.45.order_ref, ...), custom_call_target="tpu_custom_call" | custom-call | tf_op jit(solution)/shard_map/pallas_call | solution.py:547
  15.4 0.7 %collective-permute-start.4 = (f32[8,256]{1,0:T(8,128)S(1)}, f32[8,256]{1,0:T(8,128)S(1)}, u32[]{:S(2)}, u32[]{:S(2)}) collective-permute-start(f32[8,256]{1,0:T(8,128)S(1)} %get-tuple-element.75), channel_id=1, source_target_pairs={{1,2},{2,1},{3,4},{4,3},{5,6},{6,5},{9,10},{10,9},{11,12},{12,11},... | collective-permute-start | bytes 24584 | tf_op jit(solution)/shard_map/ppermute | solution.py:563
  16.1 3.2 %collective-permute-start.5 = (f32[8,256]{1,0:T(8,128)S(1)}, f32[8,256]{1,0:T(8,128)S(1)}, u32[]{:S(2)}, u32[]{:S(2)}) collective-permute-start(f32[8,256]{1,0:T(8,128)S(1)} %get-tuple-element.76), channel_id=1, source_target_pairs={{0,1},{1,0},{2,3},{3,2},{4,5},{5,4},{6,7},{7,6},{8,9},{9,8},{10,11... | collective-permute-start | bytes 24584 | tf_op jit(solution)/shard_map/ppermute | solution.py:563
  19.3 1.1 %shard_map.109 = (f32[4,8,128]{2,1,0:T(8,128)S(1)}, f32[8,128]{1,0:T(8,128)S(1)}, f32[8,1280]{1,0:T(8,128)S(1)}, f32[24,8,128]{2,1,0:T(8,128)S(1)}) custom-call(f32[8,1280]{1,0:T(8,128)S(1)} %get-tuple-element.62.own, f32[8,512]{1,0:T(8,128)S(1)} %get-tuple-element.67.delta, f32[8,128]{1,0:T(8,128)S(1)} %get-tuple-element.68.forms, ...), custom_call_target="tpu_custom_call" | custom-call | flops 4000000 | bytes 4000000 | tf_op jit(solution)/shard_map/pallas_call | solution.py:547
  20.4 0.0 collective-permute-done.5.beside_in
  20.4 0.5 %shard_map.110 = (f32[4,8,128]{2,1,0:T(8,128)S(1)}, f32[8,128]{1,0:T(8,128)S(1)}) custom-call(f32[8,1280]{1,0:T(8,128)S(1)} %get-tuple-element.74.own, s32[8,256]{1,0:T(8,128)S(1)} %get-tuple-element.45.order_ref, s32[8,256]{1,0:T(8,128)S(1)} %get-tuple-element.66.rest_0_.inverse_in, f32[8,256]{1,0:T(8,128)S(1)} %collective-permute-done.4.across_in, ...), custom_call_target="tpu_custom_call" | custom-call | tf_op jit(solution)/shard_map/pallas_call | solution.py:547
  20.9 9.6 %all_to_all.5.everyone = f32[8,8,128]{2,1,0:T(8,128)S(1)} all-to-all(f32[8,8,128]{2,1,0:T(8,128)S(1)} %broadcast_in_dim.10), channel_id=1, replica_groups=mesh['freq'=4,'dom'=8] {'dom'}, dimensions={0} | all-to-all | bytes 65536 | tf_op jit(solution)/shard_map/all_to_all | solution.py:569
  30.6 0.1 shard_map.111
  30.7 3.7 %collective-permute-start.8 = (f32[8,128]{1,0:T(8,128)S(1)}, f32[8,128]{1,0:T(8,128)S(1)}, u32[]{:S(2)}, u32[]{:S(2)}) collective-permute-start(f32[8,128]{1,0:T(8,128)S(1)} %shard_map.111), channel_id=1, source_target_pairs={{0,24},{8,16},{16,8},{24,0},{1,25},{9,17},{17,9},{25,1},{2,26},{10... | collective-permute-start | bytes 12296 | tf_op jit(solution)/shard_map/ppermute | solution.py:579
  34.4 0.8 %collective-permute-start.6 = (f32[8,128]{1,0:T(8,128)S(1)}, f32[8,128]{1,0:T(8,128)S(1)}, u32[]{:S(2)}, u32[]{:S(2)}) collective-permute-start(f32[8,128]{1,0:T(8,128)S(1)} %shard_map.111), channel_id=1, source_target_pairs={{0,8},{8,0},{16,24},{24,16},{1,9},{9,1},{17,25},{25,17},{2,10},{10... | collective-permute-start | bytes 12296 | tf_op jit(solution)/shard_map/ppermute | solution.py:579
  35.2 1.0 %collective-permute-done.8 = f32[8,128]{1,0:T(8,128)S(1)} collective-permute-done((f32[8,128]{1,0:T(8,128)S(1)}, f32[8,128]{1,0:T(8,128)S(1)}, u32[]{:S(2)}, u32[]{:S(2)}) %collective-permute-start.8) | collective-permute-done | bytes 4128 | tf_op jit(solution)/shard_map/ppermute | solution.py:579
  36.2 2.7 %collective-permute-done.7 = f32[8,128]{1,0:T(8,128)S(1)} collective-permute-done((f32[8,128]{1,0:T(8,128)S(1)}, f32[8,128]{1,0:T(8,128)S(1)}, u32[]{:S(2)}, u32[]{:S(2)}) %collective-permute-start.7) | collective-permute-done | bytes 4128 | tf_op jit(solution)/shard_map/ppermute | solution.py:579
  38.9 0.0 copy-start
  38.9 0.6 %exponential_multiply_fusion = f32[1,1024]{1,0:T(1,128)} fusion(f32[1,1024]{1,0:T(1,128)S(1)} %bitcast.9, f32[1,1024]{1,0:T(1,128)S(1)} %bitcast.15), kind=kLoop, calls=%fused_computation | loop fusion | flops 2048 | bytes 12288 | tf_op jit(solution)/shard_map/mul | solution.py:708
  (9 shorter events, 0.0 us)
Async XLA Ops:
  1.4 7.0 %collective-permute-start = (f32[8,256]{1,0:T(8,128)S(1)}, f32[8,256]{1,0:T(8,128)S(1)}, u32[]{:S(2)}, u32[]{:S(2)}) collective-permute-start(f32[8,256]{1,0:T(8,128)S(1)} %get-tuple-element.46), channel_id=1, source_target_pairs={{1,2},{2,1},{3,4},{4,3},{5,6},{6,5},{9,10},{10,9},{11,12},{12,11},... | collective-permute-start | bytes 24584 | tf_op jit(solution)/shard_map/ppermute | solution.py:563
  2.1 6.3 %collective-permute-start.1 = (f32[8,256]{1,0:T(8,128)S(1)}, f32[8,256]{1,0:T(8,128)S(1)}, u32[]{:S(2)}, u32[]{:S(2)}) collective-permute-start(f32[8,256]{1,0:T(8,128)S(1)} %get-tuple-element.47), channel_id=1, source_target_pairs={{0,1},{1,0},{2,3},{3,2},{4,5},{5,4},{6,7},{7,6},{8,9},{9,8},{10,11... | collective-permute-start | bytes 24584 | tf_op jit(solution)/shard_map/ppermute | solution.py:563
  9.5 4.8 %collective-permute-start.2 = (f32[8,256]{1,0:T(8,128)S(1)}, f32[8,256]{1,0:T(8,128)S(1)}, u32[]{:S(2)}, u32[]{:S(2)}) collective-permute-start(f32[8,256]{1,0:T(8,128)S(1)} %get-tuple-element.63), channel_id=1, source_target_pairs={{1,2},{2,1},{3,4},{4,3},{5,6},{6,5},{9,10},{10,9},{11,12},{12,11},... | collective-permute-start | bytes 24584 | tf_op jit(solution)/shard_map/ppermute | solution.py:563
  10.2 4.1 %collective-permute-start.3 = (f32[8,256]{1,0:T(8,128)S(1)}, f32[8,256]{1,0:T(8,128)S(1)}, u32[]{:S(2)}, u32[]{:S(2)}) collective-permute-start(f32[8,256]{1,0:T(8,128)S(1)} %get-tuple-element.64), channel_id=1, source_target_pairs={{0,1},{1,0},{2,3},{3,2},{4,5},{5,4},{6,7},{7,6},{8,9},{9,8},{10,11... | collective-permute-start | bytes 24584 | tf_op jit(solution)/shard_map/ppermute | solution.py:563
  15.4 5.0 %collective-permute-start.4 = (f32[8,256]{1,0:T(8,128)S(1)}, f32[8,256]{1,0:T(8,128)S(1)}, u32[]{:S(2)}, u32[]{:S(2)}) collective-permute-start(f32[8,256]{1,0:T(8,128)S(1)} %get-tuple-element.75), channel_id=1, source_target_pairs={{1,2},{2,1},{3,4},{4,3},{5,6},{6,5},{9,10},{10,9},{11,12},{12,11},... | collective-permute-start | bytes 24584 | tf_op jit(solution)/shard_map/ppermute | solution.py:563
  16.1 4.4 %collective-permute-start.5 = (f32[8,256]{1,0:T(8,128)S(1)}, f32[8,256]{1,0:T(8,128)S(1)}, u32[]{:S(2)}, u32[]{:S(2)}) collective-permute-start(f32[8,256]{1,0:T(8,128)S(1)} %get-tuple-element.76), channel_id=1, source_target_pairs={{0,1},{1,0},{2,3},{3,2},{4,5},{5,4},{6,7},{7,6},{8,9},{9,8},{10,11... | collective-permute-start | bytes 24584 | tf_op jit(solution)/shard_map/ppermute | solution.py:563
  30.7 5.5 %collective-permute-start.8 = (f32[8,128]{1,0:T(8,128)S(1)}, f32[8,128]{1,0:T(8,128)S(1)}, u32[]{:S(2)}, u32[]{:S(2)}) collective-permute-start(f32[8,128]{1,0:T(8,128)S(1)} %shard_map.111), channel_id=1, source_target_pairs={{0,24},{8,16},{16,8},{24,0},{1,25},{9,17},{17,9},{25,1},{2,26},{10... | collective-permute-start | bytes 12296 | tf_op jit(solution)/shard_map/ppermute | solution.py:579
  34.4 4.5 %collective-permute-start.7 = (f32[8,128]{1,0:T(8,128)S(1)}, f32[8,128]{1,0:T(8,128)S(1)}, u32[]{:S(2)}, u32[]{:S(2)}) collective-permute-start(f32[8,128]{1,0:T(8,128)S(1)} %shard_map.111), channel_id=1, source_target_pairs={{0,16},{8,24},{16,0},{24,8},{1,17},{9,25},{17,1},{25,9},{2,18},{10... | collective-permute-start | bytes 12296 | tf_op jit(solution)/shard_map/ppermute | solution.py:579
  34.4 4.5 %collective-permute-start.6 = (f32[8,128]{1,0:T(8,128)S(1)}, f32[8,128]{1,0:T(8,128)S(1)}, u32[]{:S(2)}, u32[]{:S(2)}) collective-permute-start(f32[8,128]{1,0:T(8,128)S(1)} %shard_map.111), channel_id=1, source_target_pairs={{0,8},{8,0},{16,24},{24,16},{1,9},{9,1},{17,25},{25,17},{2,10},{10... | collective-permute-start | bytes 12296 | tf_op jit(solution)/shard_map/ppermute | solution.py:579
  38.9 0.6 %copy-start = (f32[8,128]{1,0:T(8,128)}, f32[8,128]{1,0:T(8,128)S(1)}, u32[]{:S(2)}) copy-start(f32[8,128]{1,0:T(8,128)S(1)} %add_add_fusion) | copy-start | bytes 12292

commit v9 on v8

--- a/solution.py
+++ b/solution.py
@@ -573,17 +573,10 @@
     size = lax.axis_size(axis)
     if size & (size - 1):
         return jnp.sum(gather_all(block, axis), axis=0)
-    near = min(size, 4)
-    parts = [block] + [None] * (near - 1)
-    for step in reversed(range(1, near)):
-        parts[step] = lax.ppermute(block, axis, [(i, i ^ step) for i in range(size)])
-    while len(parts) > 1:
-        parts = [a + b for a, b in zip(parts[::2], parts[1::2])]
-    block = parts[0]
-    step = near
-    while step < size:
+    step = size // 2
+    while step > 0:
         block = block + lax.ppermute(block, axis, [(i, i ^ step) for i in range(size)])
-        step *= 2
+        step //= 2
     return block
 
 

time: 39.8 us -> 39.8 us (level)
    ppermute x3 -> x2, waiting for transfers between devices: 3.72 us -> 3.95 us  [sum_over(): lax.ppermute(block, axis, [(i, i ^ step) for i in range(size)])]
    ppermute x3 -> x2, starting transfers between devices: 4.45 us -> 4.23 us  [sum_over(): lax.ppermute(block, axis, [(i, i ^ step) for i in range(size)])]
  transfers between devices with their start and end apart: 9 -> 8, of which waited for: 2 -> 2; matrix products, arithmetic and copies ran while one was open for 0% -> 0% of each run, Pallas kernels for 11% -> 11%
where the time goes in v9:
time: 39.8 us; the launch traced here: 39.5 us
  starting transfers between devices  16.8 us (42%)
  blocking collectives  9.64 us (24%)
  Pallas kernels  7.77 us (20%)
  waiting for transfers between devices  3.96 us (10%)
  between operations  0.73 us (2%)
  other arithmetic  0.62 us (2%)
    ppermute x6, starting transfers between devices, swap(): return lax.ppermute(block, axis, route)  12.5 us
    all_to_all x1, blocking collectives, gather_all(): return lax.all_to_all(copies, axis, 0, 0)  9.64 us
    pallas_call x8, Pallas kernels, call(): pl.pallas_call(kernel, out_shape=outs, in_specs=space if isinstance(space...  7.77 us
    ppermute x2, starting transfers between devices, sum_over(): lax.ppermute(block, axis, [(i, i ^ step) for i in range(size)])  4.23 us
    ppermute x2, waiting for transfers between devices, sum_over(): lax.ppermute(block, axis, [(i, i ^ step) for i in range(size)])  3.95 us
  transfers between devices with their start and end apart: 8, of which 2 were waited for; matrix products, arithmetic and copies ran while one was open for 0% of the time, Pallas kernels for 11%

profile of v9, /device:TPU:0, one launch (start us, length us, event | category | flops | bytes accessed | tf_op | source)
XLA Modules:
  0.0 39.5 jit_solution(13905909597265713562)
XLA Ops:
  0.6 0.8 %shard_map.104 = (f32[8,256]{1,0:T(8,128)S(1)}, f32[8,256]{1,0:T(8,128)S(1)}, f32[4,1,1280]{2,1,0:T(1,128)S(1)}, s32[8,256]{1,0:T(8,128)S(1)}) custom-call(f32[4,1,1280]{2,1,0:T(1,128)} %bitcast.14, s32[1,256]{1,0:T(1,128)} %order_in.1), custom_call_target="tpu_custom_call" | custom-call | tf_op jit(solution)/shard_map/pallas_call | solution.py:547
  1.4 0.7 %collective-permute-start = (f32[8,256]{1,0:T(8,128)S(1)}, f32[8,256]{1,0:T(8,128)S(1)}, u32[]{:S(2)}, u32[]{:S(2)}) collective-permute-start(f32[8,256]{1,0:T(8,128)S(1)} %get-tuple-element.46), channel_id=1, source_target_pairs={{1,2},{2,1},{3,4},{4,3},{5,6},{6,5},{9,10},{10,9},{11,12},{12,11},... | collective-permute-start | bytes 24584 | tf_op jit(solution)/shard_map/ppermute | solution.py:563
  2.1 4.4 %collective-permute-start.1 = (f32[8,256]{1,0:T(8,128)S(1)}, f32[8,256]{1,0:T(8,128)S(1)}, u32[]{:S(2)}, u32[]{:S(2)}) collective-permute-start(f32[8,256]{1,0:T(8,128)S(1)} %get-tuple-element.47), channel_id=1, source_target_pairs={{0,1},{1,0},{2,3},{3,2},{4,5},{5,4},{6,7},{7,6},{8,9},{9,8},{10,11... | collective-permute-start | bytes 24584 | tf_op jit(solution)/shard_map/ppermute | solution.py:563
  6.4 1.9 %shard_map.105 = (bf16[128,6144]{1,0:T(8,128)(2,1)S(1)}, f32[72,8,128]{2,1,0:T(8,128)S(1)}, f32[8,128]{1,0:T(8,128)S(1)}, f32[24,8,128]{2,1,0:T(8,128)S(1)}, f32...) custom-call(f32[2]{0:T(128)} %angular_in.1, ...), custom_call_target="tpu_custom_call" | custom-call | flops 4000000 | bytes 4000000 | tf_op jit(solution)/shard_map/pallas_call | solution.py:547
  8.4 0.0 collective-permute-done.across_in
  8.4 1.1 %shard_map.106 = (s32[8,256]{1,0:T(8,128)S(1)}, f32[8,512]{1,0:T(8,128)S(1)}, f32[24,8,128]{2,1,0:T(8,128)S(1)}, f32[384,128]{1,0:T(8,128)S(1)}, f32[8,128]{1,0:...) custom-call(s32[8,256]{1,0:T(8,128)S(1)} %get-tuple-element.45.order_ref, ...), custom_call_target="tpu_custom_call" | custom-call | tf_op jit(solution)/shard_map/pallas_call | solution.py:547
  9.5 0.7 %collective-permute-start.2 = (f32[8,256]{1,0:T(8,128)S(1)}, f32[8,256]{1,0:T(8,128)S(1)}, u32[]{:S(2)}, u32[]{:S(2)}) collective-permute-start(f32[8,256]{1,0:T(8,128)S(1)} %get-tuple-element.63), channel_id=1, source_target_pairs={{1,2},{2,1},{3,4},{4,3},{5,6},{6,5},{9,10},{10,9},{11,12},{12,11},... | collective-permute-start | bytes 24584 | tf_op jit(solution)/shard_map/ppermute | solution.py:563
  10.2 2.9 %collective-permute-start.3 = (f32[8,256]{1,0:T(8,128)S(1)}, f32[8,256]{1,0:T(8,128)S(1)}, u32[]{:S(2)}, u32[]{:S(2)}) collective-permute-start(f32[8,256]{1,0:T(8,128)S(1)} %get-tuple-element.64), channel_id=1, source_target_pairs={{0,1},{1,0},{2,3},{3,2},{4,5},{5,4},{6,7},{7,6},{8,9},{9,8},{10,11... | collective-permute-start | bytes 24584 | tf_op jit(solution)/shard_map/ppermute | solution.py:563
  13.1 1.2 %shard_map.107 = (f32[24,8,128]{2,1,0:T(8,128)S(1)}, f32[4,8,128]{2,1,0:T(8,128)S(1)}, f32[8,128]{1,0:T(8,128)S(1)}, f32[8,1280]{1,0:T(8,128)S(1)}, f32[24,8,128]{2,1,0:T(8,128)S(1)}) custom-call(f32[8,1280]{1,0:T(8,128)S(1)} %get-tuple-element.44.own, f32[8,512]{1,0:T(8,128)S(1)} %get-tuple-element.53.delta, f32[8,128]{1,0:T(8,128)S(1)} %get-tuple-element.54.forms, ...), custom_call_target="tpu_custom_call" | custom-call | flops 4000000 | bytes 4000000 | tf_op jit(solution)/shard_map/pallas_call | solution.py:547
  14.3 0.0 collective-permute-done.2.across_in
  14.3 0.0 collective-permute-done.3.beside_in
  14.3 1.0 %shard_map.108 = (f32[8,512]{1,0:T(8,128)S(1)}, f32[24,8,128]{2,1,0:T(8,128)S(1)}, f32[384,128]{1,0:T(8,128)S(1)}, f32[8,128]{1,0:T(8,128)S(1)}, f32[8,512]{1,0:...) custom-call(s32[8,256]{1,0:T(8,128)S(1)} %get-tuple-element.45.order_ref, ...), custom_call_target="tpu_custom_call" | custom-call | tf_op jit(solution)/shard_map/pallas_call | solution.py:547
  15.4 0.7 %collective-permute-start.4 = (f32[8,256]{1,0:T(8,128)S(1)}, f32[8,256]{1,0:T(8,128)S(1)}, u32[]{:S(2)}, u32[]{:S(2)}) collective-permute-start(f32[8,256]{1,0:T(8,128)S(1)} %get-tuple-element.75), channel_id=1, source_target_pairs={{1,2},{2,1},{3,4},{4,3},{5,6},{6,5},{9,10},{10,9},{11,12},{12,11},... | collective-permute-start | bytes 24584 | tf_op jit(solution)/shard_map/ppermute | solution.py:563
  16.1 3.2 %collective-permute-start.5 = (f32[8,256]{1,0:T(8,128)S(1)}, f32[8,256]{1,0:T(8,128)S(1)}, u32[]{:S(2)}, u32[]{:S(2)}) collective-permute-start(f32[8,256]{1,0:T(8,128)S(1)} %get-tuple-element.76), channel_id=1, source_target_pairs={{0,1},{1,0},{2,3},{3,2},{4,5},{5,4},{6,7},{7,6},{8,9},{9,8},{10,11... | collective-permute-start | bytes 24584 | tf_op jit(solution)/shard_map/ppermute | solution.py:563
  19.3 1.1 %shard_map.109 = (f32[4,8,128]{2,1,0:T(8,128)S(1)}, f32[8,128]{1,0:T(8,128)S(1)}, f32[8,1280]{1,0:T(8,128)S(1)}, f32[24,8,128]{2,1,0:T(8,128)S(1)}) custom-call(f32[8,1280]{1,0:T(8,128)S(1)} %get-tuple-element.62.own, f32[8,512]{1,0:T(8,128)S(1)} %get-tuple-element.67.delta, f32[8,128]{1,0:T(8,128)S(1)} %get-tuple-element.68.forms, ...), custom_call_target="tpu_custom_call" | custom-call | flops 4000000 | bytes 4000000 | tf_op jit(solution)/shard_map/pallas_call | solution.py:547
  20.4 0.0 collective-permute-done.5.beside_in
  20.4 0.5 %shard_map.110 = (f32[4,8,128]{2,1,0:T(8,128)S(1)}, f32[8,128]{1,0:T(8,128)S(1)}) custom-call(f32[8,1280]{1,0:T(8,128)S(1)} %get-tuple-element.74.own, s32[8,256]{1,0:T(8,128)S(1)} %get-tuple-element.45.order_ref, s32[8,256]{1,0:T(8,128)S(1)} %get-tuple-element.66.rest_0_.inverse_in, f32[8,256]{1,0:T(8,128)S(1)} %collective-permute-done.4.across_in, ...), custom_call_target="tpu_custom_call" | custom-call | tf_op jit(solution)/shard_map/pallas_call | solution.py:547
  20.9 9.6 %all_to_all.5.everyone = f32[8,8,128]{2,1,0:T(8,128)S(1)} all-to-all(f32[8,8,128]{2,1,0:T(8,128)S(1)} %broadcast_in_dim.10), channel_id=1, replica_groups=mesh['freq'=4,'dom'=8] {'dom'}, dimensions={0} | all-to-all | bytes 65536 | tf_op jit(solution)/shard_map/all_to_all | solution.py:569
  30.6 0.1 shard_map.111
  30.7 2.7 %collective-permute-start.6 = (f32[8,128]{1,0:T(8,128)S(1)}, f32[8,128]{1,0:T(8,128)S(1)}, u32[]{:S(2)}, u32[]{:S(2)}) collective-permute-start(f32[8,128]{1,0:T(8,128)S(1)} %shard_map.111), channel_id=1, source_target_pairs={{0,16},{8,24},{16,0},{24,8},{1,17},{9,25},{17,1},{25,9},{2,18},{10... | collective-permute-start | bytes 12296 | tf_op jit(solution)/shard_map/ppermute | solution.py:578
  33.4 1.9 %collective-permute-done.6 = f32[8,128]{1,0:T(8,128)S(1)} collective-permute-done((f32[8,128]{1,0:T(8,128)S(1)}, f32[8,128]{1,0:T(8,128)S(1)}, u32[]{:S(2)}, u32[]{:S(2)}) %collective-permute-start.6) | collective-permute-done | bytes 4128 | tf_op jit(solution)/shard_map/ppermute | solution.py:578
  35.3 1.6 %collective-permute-start.7 = (f32[8,128]{1,0:T(8,128)S(1)}, f32[8,128]{1,0:T(8,128)S(1)}, u32[]{:S(2)}, u32[]{:S(2)}) collective-permute-start(f32[8,128]{1,0:T(8,128)S(1)} %add.6), channel_id=1, source_target_pairs={{0,8},{8,0},{16,24},{24,16},{1,9},{9,1},{17,25},{25,17},{2,10},{10... | collective-permute-start | bytes 12296 | tf_op jit(solution)/shard_map/ppermute | solution.py:578
  36.9 2.0 %collective-permute-done.7 = f32[8,128]{1,0:T(8,128)S(1)} collective-permute-done((f32[8,128]{1,0:T(8,128)S(1)}, f32[8,128]{1,0:T(8,128)S(1)}, u32[]{:S(2)}, u32[]{:S(2)}) %collective-permute-start.7) | collective-permute-done | bytes 4128 | tf_op jit(solution)/shard_map/ppermute | solution.py:578
  38.9 0.6 %exponential_multiply_fusion = f32[1,1024]{1,0:T(1,128)} fusion(f32[1,1024]{1,0:T(1,128)S(1)} %bitcast.9, f32[1,1024]{1,0:T(1,128)S(1)} %bitcast.15), kind=kLoop, calls=%fused_computation | loop fusion | flops 2048 | bytes 12288 | tf_op jit(solution)/shard_map/mul | solution.py:701
  (8 shorter events, 0.0 us)
Async XLA Ops:
  1.4 7.0 %collective-permute-start = (f32[8,256]{1,0:T(8,128)S(1)}, f32[8,256]{1,0:T(8,128)S(1)}, u32[]{:S(2)}, u32[]{:S(2)}) collective-permute-start(f32[8,256]{1,0:T(8,128)S(1)} %get-tuple-element.46), channel_id=1, source_target_pairs={{1,2},{2,1},{3,4},{4,3},{5,6},{6,5},{9,10},{10,9},{11,12},{12,11},... | collective-permute-start | bytes 24584 | tf_op jit(solution)/shard_map/ppermute | solution.py:563
  2.1 6.3 %collective-permute-start.1 = (f32[8,256]{1,0:T(8,128)S(1)}, f32[8,256]{1,0:T(8,128)S(1)}, u32[]{:S(2)}, u32[]{:S(2)}) collective-permute-start(f32[8,256]{1,0:T(8,128)S(1)} %get-tuple-element.47), channel_id=1, source_target_pairs={{0,1},{1,0},{2,3},{3,2},{4,5},{5,4},{6,7},{7,6},{8,9},{9,8},{10,11... | collective-permute-start | bytes 24584 | tf_op jit(solution)/shard_map/ppermute | solution.py:563
  9.5 4.8 %collective-permute-start.2 = (f32[8,256]{1,0:T(8,128)S(1)}, f32[8,256]{1,0:T(8,128)S(1)}, u32[]{:S(2)}, u32[]{:S(2)}) collective-permute-start(f32[8,256]{1,0:T(8,128)S(1)} %get-tuple-element.63), channel_id=1, source_target_pairs={{1,2},{2,1},{3,4},{4,3},{5,6},{6,5},{9,10},{10,9},{11,12},{12,11},... | collective-permute-start | bytes 24584 | tf_op jit(solution)/shard_map/ppermute | solution.py:563
  10.2 4.1 %collective-permute-start.3 = (f32[8,256]{1,0:T(8,128)S(1)}, f32[8,256]{1,0:T(8,128)S(1)}, u32[]{:S(2)}, u32[]{:S(2)}) collective-permute-start(f32[8,256]{1,0:T(8,128)S(1)} %get-tuple-element.64), channel_id=1, source_target_pairs={{0,1},{1,0},{2,3},{3,2},{4,5},{5,4},{6,7},{7,6},{8,9},{9,8},{10,11... | collective-permute-start | bytes 24584 | tf_op jit(solution)/shard_map/ppermute | solution.py:563
  15.4 5.0 %collective-permute-start.4 = (f32[8,256]{1,0:T(8,128)S(1)}, f32[8,256]{1,0:T(8,128)S(1)}, u32[]{:S(2)}, u32[]{:S(2)}) collective-permute-start(f32[8,256]{1,0:T(8,128)S(1)} %get-tuple-element.75), channel_id=1, source_target_pairs={{1,2},{2,1},{3,4},{4,3},{5,6},{6,5},{9,10},{10,9},{11,12},{12,11},... | collective-permute-start | bytes 24584 | tf_op jit(solution)/shard_map/ppermute | solution.py:563
  16.1 4.4 %collective-permute-start.5 = (f32[8,256]{1,0:T(8,128)S(1)}, f32[8,256]{1,0:T(8,128)S(1)}, u32[]{:S(2)}, u32[]{:S(2)}) collective-permute-start(f32[8,256]{1,0:T(8,128)S(1)} %get-tuple-element.76), channel_id=1, source_target_pairs={{0,1},{1,0},{2,3},{3,2},{4,5},{5,4},{6,7},{7,6},{8,9},{9,8},{10,11... | collective-permute-start | bytes 24584 | tf_op jit(solution)/shard_map/ppermute | solution.py:563
  30.7 4.6 %collective-permute-start.6 = (f32[8,128]{1,0:T(8,128)S(1)}, f32[8,128]{1,0:T(8,128)S(1)}, u32[]{:S(2)}, u32[]{:S(2)}) collective-permute-start(f32[8,128]{1,0:T(8,128)S(1)} %shard_map.111), channel_id=1, source_target_pairs={{0,16},{8,24},{16,0},{24,8},{1,17},{9,25},{17,1},{25,9},{2,18},{10... | collective-permute-start | bytes 12296 | tf_op jit(solution)/shard_map/ppermute | solution.py:578
  35.3 3.6 %collective-permute-start.7 = (f32[8,128]{1,0:T(8,128)S(1)}, f32[8,128]{1,0:T(8,128)S(1)}, u32[]{:S(2)}, u32[]{:S(2)}) collective-permute-start(f32[8,128]{1,0:T(8,128)S(1)} %add.6), channel_id=1, source_target_pairs={{0,8},{8,0},{16,24},{24,16},{1,9},{9,1},{17,25},{25,17},{2,10},{10... | collective-permute-start | bytes 12296 | tf_op jit(solution)/shard_map/ppermute | solution.py:578
  38.9 0.6 %copy-start = (f32[8,128]{1,0:T(8,128)}, f32[8,128]{1,0:T(8,128)S(1)}, u32[]{:S(2)}) copy-start(f32[8,128]{1,0:T(8,128)S(1)} %add.7) | copy-start | bytes 12292

commit v10 on v9

--- a/solution.py
+++ b/solution.py
@@ -132,29 +132,42 @@
     return total
 
 
-def scatter(pieces, edges, places, heights, values):
+def scatter_side(pieces, edges, places, heights, i):
     depth = SIDE * edges.shape[1]
     rows = pieces.shape[0] // depth
-    for i in range(SIDE):
-        for s in range(edges.shape[1]):
-            at = i * edges.shape[1] + s
-            both = pieces[pl.ds(at, rows, stride=depth), :]
-            high = spread(edges[i, s : s + 1, :] >> 7, rows)
-            stacked = [jnp.where(high == h, both, 0.0) for h in heights]
-            values[:, at * LANES : (at + 1) * LANES] = jnp.concatenate(stacked, axis=0).astype(
-                jnp.bfloat16
-            )
-    total = lax.dot_general(
-        values[...],
-        places[...],
+    slots = edges.shape[1] * LANES
+    columns = []
+    for s in range(edges.shape[1]):
+        both = pieces[pl.ds(i * edges.shape[1] + s, rows, stride=depth), :]
+        high = spread(edges[i, s : s + 1, :] >> 7, rows)
+        stacked = [jnp.where(high == h, both, 0.0) for h in heights]
+        columns.append(jnp.concatenate(stacked, axis=0).astype(jnp.bfloat16))
+    return lax.dot_general(
+        jnp.concatenate(columns, axis=1),
+        places[:, i * slots : (i + 1) * slots],
         (((1,), (1,)), ((), ())),
         preferred_element_type=jnp.float32,
     )
+
+
+def add(total, part):
+    return part if total is None else total + part
+
+
+def parts_joined(total, count):
+    rows = total.shape[0] // count
     out = []
-    for n in range(len(heights)):
+    for n in range(count):
         piece = total[rows * n : rows * (n + 1)]
         out.append(piece + swap_halves(piece))
     return out
+
+
+def scatter(pieces, edges, places, heights):
+    total = None
+    for i in range(SIDE):
+        total = add(total, scatter_side(pieces, edges, places, heights, i))
+    return parts_joined(total, len(heights))
 
 
 def rim_heights(edge_count, rim):
@@ -304,29 +317,33 @@
     return lower + jnp.where(index >= start, upper, 0.0)
 
 
-def apply_all(delta_ref, own_picks, blocks, edges, polars, edge_count, pieces, visit):
-    rows = delta_ref.shape[0]
-    groups = rows // 2
-    depth = SIDE * edges.shape[1]
-    forms = jnp.zeros((rows, LANES), jnp.float32)
-    for g in range(groups):
+def corrected_picks(delta_ref, own_picks, edges, edge_count):
+    out = []
+    for g in range(delta_ref.shape[0] // 2):
         delta = group_rows(delta_ref, g)
-        picked = [
-            own_picks[g * SIDE + j] + pick_rims(delta, edges[j], edge_count)
-            for j in range(SIDE)
-        ]
-        visit(g, picked)
-        values = times_block(blocks, (g // polars) * SIDE * SIDE, picked)
-        form = jnp.sum(weighted_sum(picked, values), axis=0, keepdims=True)
-        forms = jnp.where(row_ids(rows) == g, spread(form, rows), forms)
-        if pieces is None:
-            continue
-        for i, value in enumerate(values):
-            coarse = value.astype(jnp.bfloat16).astype(jnp.float32)
-            for part, piece in enumerate((coarse, value - coarse)):
-                at = (part * groups + g) * depth + i * edges.shape[1]
-                pieces[at : at + edges.shape[1], :] = piece
-    return forms
+        out.append(
+            [
+                own_picks[g * SIDE + j] + pick_rims(delta, edges[j], edge_count)
+                for j in range(SIDE)
+            ]
+        )
+    return out
+
+
+def products(blocks, picked, polars, i):
+    out = []
+    for g, mine in enumerate(picked):
+        base = (g // polars) * SIDE * SIDE + SIDE * i
+        out.append(weighted_sum([blocks[base + j] for j in range(SIDE)], mine))
+    return out
+
+
+def rows_of_forms(forms, rows):
+    out = jnp.zeros((rows, LANES), jnp.float32)
+    for g, form in enumerate(forms):
+        row = jnp.sum(form, axis=0, keepdims=True)
+        out = jnp.where(row_ids(rows) == g, spread(row, rows), out)
+    return out
 
 
 def invert(above, groups, rows):
@@ -366,7 +383,7 @@
         inverse_ref, *rest = rest
     else:
         inverse_in, *rest = rest
-    delta_ref, picks_ref, pieces, forms_ref, rims_ref, across_ref, beside_ref, values = rest
+    delta_ref, picks_ref, pieces, forms_ref, rims_ref, across_ref, beside_ref = rest
     rows = delta_ref.shape[0]
     groups = rows // 2
     first = row_ids(rows) < groups
@@ -383,15 +400,24 @@
         above = [rescaled(x, inverse_scale, step) for x in above]
     put_chunks(delta_ref, corrections(prior, above, cut(order_ref), inverse))
 
-    def visit(g, picked):
+    picked = corrected_picks(delta_ref, own_picks, edges, edge_count)
+    for g in range(groups):
         for j in range(SIDE):
-            picks_ref[g * SIDE + j] = picked[j]
-
-    forms_ref[...] = apply_all(
-        delta_ref, own_picks, blocks, edges, polars, edge_count, pieces, visit
-    )
+            picks_ref[g * SIDE + j] = picked[g][j]
     rim = len(prior)
-    chunks = scatter(pieces, edges, places, rim_heights(edge_count, rim)[0], values)
+    heights = rim_heights(edge_count, rim)[0]
+    tall = edges.shape[1]
+    forms, total = [None] * groups, None
+    for i in range(SIDE):
+        for g, value in enumerate(products(blocks, picked, polars, i)):
+            forms[g] = add(forms[g], picked[g][i] * value)
+            coarse = value.astype(jnp.bfloat16).astype(jnp.float32)
+            for part, piece in enumerate((coarse, value - coarse)):
+                at = ((part * groups + g) * SIDE + i) * tall
+                pieces[at : at + tall, :] = piece
+        total = add(total, scatter_side(pieces, edges, places, heights, i))
+    forms_ref[...] = rows_of_forms(forms, rows)
+    chunks = parts_joined(total, len(heights))
     put_chunks(rims_ref, chunks)
     put_rims(
         across_ref,
@@ -429,14 +455,14 @@
     *rest,
 ):
     if step == 0:
-        rates, forward, mass, live, heavy, terms_ref, sums_ref, image_ref, picks_ref, values = rest
+        rates, forward, mass, live, heavy, terms_ref, sums_ref, image_ref, picks_ref = rest
     else:
-        heavy, terms_ref, sums_ref, image_ref, picks_ref, values = rest
+        heavy, terms_ref, sums_ref, image_ref, picks_ref = rest
     rows, edge_count = own.shape
     groups = rows // 2
     rim = rims.shape[-1] // LANES // 2
     outer = cut(rims)
-    inner = scatter(pieces, edges, places, rim_heights(edge_count, rim)[1], values)
+    inner = scatter(pieces, edges, places, rim_heights(edge_count, rim)[1])
     put_chunks(image_ref, outer[:rim] + inner + outer[rim:])
     put_picks(picks_ref, image_ref, edges, groups)
     if step == 0:
@@ -482,10 +508,14 @@
     above = [rescaled(x, inverse_scale, step) for x in above]
     put_chunks(delta_ref, corrections(prior, above, cut(order_ref), cut(inverse_in)))
 
-    def visit(g, picked):
-        terms_ref[g] = weighted_sum(picked, [heavy[g * SIDE + i] for i in range(SIDE)])
-
-    forms = apply_all(delta_ref, own_picks, blocks, edges, polars, edge_count, None, visit)
+    picked = corrected_picks(delta_ref, own_picks, edges, edge_count)
+    forms = [None] * len(picked)
+    for i in range(SIDE):
+        for g, value in enumerate(products(blocks, picked, polars, i)):
+            forms[g] = add(forms[g], picked[g][i] * value)
+    for g, mine in enumerate(picked):
+        terms_ref[g] = weighted_sum(mine, [heavy[g * SIDE + i] for i in range(SIDE)])
+    forms = rows_of_forms(forms, rows)
     sums = inner_products(
         step, sums_in[...], cut(own), cut(delta_ref), forms, across_in, beside_in
     )
@@ -657,19 +687,16 @@
     ]
     back_shapes = [terms_shape, sums_shape, field_shape, picks_shape]
     sums, terms = jnp.zeros((rows, LANES), jnp.float32), []
-    outer, inner = rim_heights(edge_count, rim // LANES)
-    outer = [pltpu.VMEM((rows * len(outer), SIDE * slots), jnp.bfloat16)]
-    inner = [pltpu.VMEM((rows * len(inner), SIDE * slots), jnp.bfloat16)]
     for step in range(2):
         arrived = (across, beside)
         given = (order, *arrived, scale, picks, blocks, edges, places)
         front = functools.partial(front_stage, polars, step, edge_count)
         if step == 0:
             inverse, *outs = call(
-                front, given, [shape(rows, rim, kind=jnp.int32), *front_shapes], outer
+                front, given, [shape(rows, rim, kind=jnp.int32), *front_shapes]
             )
         else:
-            outs = call(front, (*given, inverse), front_shapes, outer)
+            outs = call(front, (*given, inverse), front_shapes)
         delta, picks, pieces, forms, rims, across, beside = outs
         across, beside = swap(across, "dom", 1), swap(beside, "dom", 0)
         given = (own, delta, forms, *arrived, sums, picks, pieces, rims, edges, places)
@@ -679,11 +706,10 @@
                 back,
                 (*given, rates, forward, mass, live),
                 [picks_shape, *back_shapes],
-                inner,
                 cost=4_000_000,
             )
         else:
-            term, sums, own, picks = call(back, (*given, heavy), back_shapes, inner, cost=4_000_000)
+            term, sums, own, picks = call(back, (*given, heavy), back_shapes, cost=4_000_000)
         terms.append(term)
     term, sums = call(
         functools.partial(last_stage, polars, 2),

time: 39.8 us -> 39.7 us (level)
  no operation moved by 1% of the time
where the time goes in v10:
time: 39.7 us; the launch traced here: 39.4 us
  starting transfers between devices  16.8 us (42%)
  blocking collectives  9.67 us (24%)
  Pallas kernels  7.64 us (19%)
  waiting for transfers between devices  3.96 us (10%)
  between operations  0.73 us (2%)
  other arithmetic  0.62 us (2%)
    ppermute x6, starting transfers between devices, swap(): return lax.ppermute(block, axis, route)  12.6 us
    all_to_all x1, blocking collectives, gather_all(): return lax.all_to_all(copies, axis, 0, 0)  9.67 us
    pallas_call x8, Pallas kernels, call(): pl.pallas_call(kernel, out_shape=outs, in_specs=space if isinstance(space...  7.64 us
    ppermute x2, starting transfers between devices, sum_over(): lax.ppermute(block, axis, [(i, i ^ step) for i in range(size)])  4.23 us
    ppermute x2, waiting for transfers between devices, sum_over(): lax.ppermute(block, axis, [(i, i ^ step) for i in range(size)])  3.95 us
  transfers between devices with their start and end apart: 8, of which 2 were waited for; matrix products, arithmetic and copies ran while one was open for 0% of the time, Pallas kernels for 11%

profile of v10, /device:TPU:0, one launch (start us, length us, event | category | flops | bytes accessed | tf_op | source)
XLA Modules:
  0.0 39.4 jit_solution(15584064200447339368)
XLA Ops:
  0.6 0.8 %shard_map.104 = (f32[8,256]{1,0:T(8,128)S(1)}, f32[8,256]{1,0:T(8,128)S(1)}, f32[4,1,1280]{2,1,0:T(1,128)S(1)}, s32[8,256]{1,0:T(8,128)S(1)}) custom-call(f32[4,1,1280]{2,1,0:T(1,128)} %bitcast.14, s32[1,256]{1,0:T(1,128)} %order_in.1), custom_call_target="tpu_custom_call" | custom-call | tf_op jit(solution)/shard_map/pallas_call | solution.py:577
  1.4 0.7 %collective-permute-start = (f32[8,256]{1,0:T(8,128)S(1)}, f32[8,256]{1,0:T(8,128)S(1)}, u32[]{:S(2)}, u32[]{:S(2)}) collective-permute-start(f32[8,256]{1,0:T(8,128)S(1)} %get-tuple-element.46), channel_id=1, source_target_pairs={{1,2},{2,1},{3,4},{4,3},{5,6},{6,5},{9,10},{10,9},{11,12},{12,11},... | collective-permute-start | bytes 24584 | tf_op jit(solution)/shard_map/ppermute | solution.py:593
  2.1 4.4 %collective-permute-start.1 = (f32[8,256]{1,0:T(8,128)S(1)}, f32[8,256]{1,0:T(8,128)S(1)}, u32[]{:S(2)}, u32[]{:S(2)}) collective-permute-start(f32[8,256]{1,0:T(8,128)S(1)} %get-tuple-element.47), channel_id=1, source_target_pairs={{0,1},{1,0},{2,3},{3,2},{4,5},{5,4},{6,7},{7,6},{8,9},{9,8},{10,11... | collective-permute-start | bytes 24584 | tf_op jit(solution)/shard_map/ppermute | solution.py:593
  6.4 1.9 %shard_map.105 = (bf16[128,6144]{1,0:T(8,128)(2,1)S(1)}, f32[72,8,128]{2,1,0:T(8,128)S(1)}, f32[8,128]{1,0:T(8,128)S(1)}, f32[24,8,128]{2,1,0:T(8,128)S(1)}, f32...) custom-call(f32[2]{0:T(128)} %angular_in.1, ...), custom_call_target="tpu_custom_call" | custom-call | flops 4000000 | bytes 4000000 | tf_op jit(solution)/shard_map/pallas_call | solution.py:577
  8.4 0.0 collective-permute-done.across_in
  8.4 0.0 collective-permute-done.1.beside_in
  8.4 1.0 %shard_map.106 = (s32[8,256]{1,0:T(8,128)S(1)}, f32[8,512]{1,0:T(8,128)S(1)}, f32[24,8,128]{2,1,0:T(8,128)S(1)}, f32[384,128]{1,0:T(8,128)S(1)}, f32[8,128]{1,0:...) custom-call(s32[8,256]{1,0:T(8,128)S(1)} %get-tuple-element.45.order_ref, ...), custom_call_target="tpu_custom_call" | custom-call | tf_op jit(solution)/shard_map/pallas_call | solution.py:577
  9.4 0.7 %collective-permute-start.2 = (f32[8,256]{1,0:T(8,128)S(1)}, f32[8,256]{1,0:T(8,128)S(1)}, u32[]{:S(2)}, u32[]{:S(2)}) collective-permute-start(f32[8,256]{1,0:T(8,128)S(1)} %get-tuple-element.63), channel_id=1, source_target_pairs={{1,2},{2,1},{3,4},{4,3},{5,6},{6,5},{9,10},{10,9},{11,12},{12,11},... | collective-permute-start | bytes 24584 | tf_op jit(solution)/shard_map/ppermute | solution.py:593
  10.2 2.9 %collective-permute-start.3 = (f32[8,256]{1,0:T(8,128)S(1)}, f32[8,256]{1,0:T(8,128)S(1)}, u32[]{:S(2)}, u32[]{:S(2)}) collective-permute-start(f32[8,256]{1,0:T(8,128)S(1)} %get-tuple-element.64), channel_id=1, source_target_pairs={{0,1},{1,0},{2,3},{3,2},{4,5},{5,4},{6,7},{7,6},{8,9},{9,8},{10,11... | collective-permute-start | bytes 24584 | tf_op jit(solution)/shard_map/ppermute | solution.py:593
  13.1 1.2 %shard_map.107 = (f32[24,8,128]{2,1,0:T(8,128)S(1)}, f32[4,8,128]{2,1,0:T(8,128)S(1)}, f32[8,128]{1,0:T(8,128)S(1)}, f32[8,1280]{1,0:T(8,128)S(1)}, f32[24,8,128]{2,1,0:T(8,128)S(1)}) custom-call(f32[8,1280]{1,0:T(8,128)S(1)} %get-tuple-element.44.own, f32[8,512]{1,0:T(8,128)S(1)} %get-tuple-element.53.delta, f32[8,128]{1,0:T(8,128)S(1)} %get-tuple-element.54.forms, ...), custom_call_target="tpu_custom_call" | custom-call | flops 4000000 | bytes 4000000 | tf_op jit(solution)/shard_map/pallas_call | solution.py:577
  14.3 0.0 collective-permute-done.3.beside_in
  14.3 1.0 %shard_map.108 = (f32[8,512]{1,0:T(8,128)S(1)}, f32[24,8,128]{2,1,0:T(8,128)S(1)}, f32[384,128]{1,0:T(8,128)S(1)}, f32[8,128]{1,0:T(8,128)S(1)}, f32[8,512]{1,0:...) custom-call(s32[8,256]{1,0:T(8,128)S(1)} %get-tuple-element.45.order_ref, ...), custom_call_target="tpu_custom_call" | custom-call | tf_op jit(solution)/shard_map/pallas_call | solution.py:577
  15.3 0.7 %collective-permute-start.4 = (f32[8,256]{1,0:T(8,128)S(1)}, f32[8,256]{1,0:T(8,128)S(1)}, u32[]{:S(2)}, u32[]{:S(2)}) collective-permute-start(f32[8,256]{1,0:T(8,128)S(1)} %get-tuple-element.75), channel_id=1, source_target_pairs={{1,2},{2,1},{3,4},{4,3},{5,6},{6,5},{9,10},{10,9},{11,12},{12,11},... | collective-permute-start | bytes 24584 | tf_op jit(solution)/shard_map/ppermute | solution.py:593
  15.9 3.2 %collective-permute-start.5 = (f32[8,256]{1,0:T(8,128)S(1)}, f32[8,256]{1,0:T(8,128)S(1)}, u32[]{:S(2)}, u32[]{:S(2)}) collective-permute-start(f32[8,256]{1,0:T(8,128)S(1)} %get-tuple-element.76), channel_id=1, source_target_pairs={{0,1},{1,0},{2,3},{3,2},{4,5},{5,4},{6,7},{7,6},{8,9},{9,8},{10,11... | collective-permute-start | bytes 24584 | tf_op jit(solution)/shard_map/ppermute | solution.py:593
  19.2 1.1 %shard_map.109 = (f32[4,8,128]{2,1,0:T(8,128)S(1)}, f32[8,128]{1,0:T(8,128)S(1)}, f32[8,1280]{1,0:T(8,128)S(1)}, f32[24,8,128]{2,1,0:T(8,128)S(1)}) custom-call(f32[8,1280]{1,0:T(8,128)S(1)} %get-tuple-element.62.own, f32[8,512]{1,0:T(8,128)S(1)} %get-tuple-element.67.delta, f32[8,128]{1,0:T(8,128)S(1)} %get-tuple-element.68.forms, ...), custom_call_target="tpu_custom_call" | custom-call | flops 4000000 | bytes 4000000 | tf_op jit(solution)/shard_map/pallas_call | solution.py:577
  20.3 0.0 collective-permute-done.5.beside_in
  20.3 0.5 %shard_map.110 = (f32[4,8,128]{2,1,0:T(8,128)S(1)}, f32[8,128]{1,0:T(8,128)S(1)}) custom-call(f32[8,1280]{1,0:T(8,128)S(1)} %get-tuple-element.74.own, s32[8,256]{1,0:T(8,128)S(1)} %get-tuple-element.45.order_ref, s32[8,256]{1,0:T(8,128)S(1)} %get-tuple-element.66.rest_0_.inverse_in, f32[8,256]{1,0:T(8,128)S(1)} %collective-permute-done.4.across_in, ...), custom_call_target="tpu_custom_call" | custom-call | tf_op jit(solution)/shard_map/pallas_call | solution.py:577
  20.8 9.7 %all_to_all.5.everyone = f32[8,8,128]{2,1,0:T(8,128)S(1)} all-to-all(f32[8,8,128]{2,1,0:T(8,128)S(1)} %broadcast_in_dim.10), channel_id=1, replica_groups=mesh['freq'=4,'dom'=8] {'dom'}, dimensions={0} | all-to-all | bytes 65536 | tf_op jit(solution)/shard_map/all_to_all | solution.py:599
  30.5 0.1 shard_map.111
  30.6 2.7 %collective-permute-start.6 = (f32[8,128]{1,0:T(8,128)S(1)}, f32[8,128]{1,0:T(8,128)S(1)}, u32[]{:S(2)}, u32[]{:S(2)}) collective-permute-start(f32[8,128]{1,0:T(8,128)S(1)} %shard_map.111), channel_id=1, source_target_pairs={{0,16},{8,24},{16,0},{24,8},{1,17},{9,25},{17,1},{25,9},{2,18},{10... | collective-permute-start | bytes 12296 | tf_op jit(solution)/shard_map/ppermute | solution.py:608
  33.3 1.9 %collective-permute-done.6 = f32[8,128]{1,0:T(8,128)S(1)} collective-permute-done((f32[8,128]{1,0:T(8,128)S(1)}, f32[8,128]{1,0:T(8,128)S(1)}, u32[]{:S(2)}, u32[]{:S(2)}) %collective-permute-start.6) | collective-permute-done | bytes 4128 | tf_op jit(solution)/shard_map/ppermute | solution.py:608
  35.2 1.6 %collective-permute-start.7 = (f32[8,128]{1,0:T(8,128)S(1)}, f32[8,128]{1,0:T(8,128)S(1)}, u32[]{:S(2)}, u32[]{:S(2)}) collective-permute-start(f32[8,128]{1,0:T(8,128)S(1)} %add.6), channel_id=1, source_target_pairs={{0,8},{8,0},{16,24},{24,16},{1,9},{9,1},{17,25},{25,17},{2,10},{10... | collective-permute-start | bytes 12296 | tf_op jit(solution)/shard_map/ppermute | solution.py:608
  36.8 2.0 %collective-permute-done.7 = f32[8,128]{1,0:T(8,128)S(1)} collective-permute-done((f32[8,128]{1,0:T(8,128)S(1)}, f32[8,128]{1,0:T(8,128)S(1)}, u32[]{:S(2)}, u32[]{:S(2)}) %collective-permute-start.7) | collective-permute-done | bytes 4128 | tf_op jit(solution)/shard_map/ppermute | solution.py:608
  38.8 0.6 %exponential_multiply_fusion = f32[1,1024]{1,0:T(1,128)} fusion(f32[1,1024]{1,0:T(1,128)S(1)} %bitcast.9, f32[1,1024]{1,0:T(1,128)S(1)} %bitcast.15), kind=kLoop, calls=%fused_computation | loop fusion | flops 2048 | bytes 12288 | tf_op jit(solution)/shard_map/mul | solution.py:727
  (8 shorter events, 0.0 us)
Async XLA Ops:
  1.4 7.0 %collective-permute-start = (f32[8,256]{1,0:T(8,128)S(1)}, f32[8,256]{1,0:T(8,128)S(1)}, u32[]{:S(2)}, u32[]{:S(2)}) collective-permute-start(f32[8,256]{1,0:T(8,128)S(1)} %get-tuple-element.46), channel_id=1, source_target_pairs={{1,2},{2,1},{3,4},{4,3},{5,6},{6,5},{9,10},{10,9},{11,12},{12,11},... | collective-permute-start | bytes 24584 | tf_op jit(solution)/shard_map/ppermute | solution.py:593
  2.1 6.3 %collective-permute-start.1 = (f32[8,256]{1,0:T(8,128)S(1)}, f32[8,256]{1,0:T(8,128)S(1)}, u32[]{:S(2)}, u32[]{:S(2)}) collective-permute-start(f32[8,256]{1,0:T(8,128)S(1)} %get-tuple-element.47), channel_id=1, source_target_pairs={{0,1},{1,0},{2,3},{3,2},{4,5},{5,4},{6,7},{7,6},{8,9},{9,8},{10,11... | collective-permute-start | bytes 24584 | tf_op jit(solution)/shard_map/ppermute | solution.py:593
  9.4 4.8 %collective-permute-start.2 = (f32[8,256]{1,0:T(8,128)S(1)}, f32[8,256]{1,0:T(8,128)S(1)}, u32[]{:S(2)}, u32[]{:S(2)}) collective-permute-start(f32[8,256]{1,0:T(8,128)S(1)} %get-tuple-element.63), channel_id=1, source_target_pairs={{1,2},{2,1},{3,4},{4,3},{5,6},{6,5},{9,10},{10,9},{11,12},{12,11},... | collective-permute-start | bytes 24584 | tf_op jit(solution)/shard_map/ppermute | solution.py:593
  10.2 4.1 %collective-permute-start.3 = (f32[8,256]{1,0:T(8,128)S(1)}, f32[8,256]{1,0:T(8,128)S(1)}, u32[]{:S(2)}, u32[]{:S(2)}) collective-permute-start(f32[8,256]{1,0:T(8,128)S(1)} %get-tuple-element.64), channel_id=1, source_target_pairs={{0,1},{1,0},{2,3},{3,2},{4,5},{5,4},{6,7},{7,6},{8,9},{9,8},{10,11... | collective-permute-start | bytes 24584 | tf_op jit(solution)/shard_map/ppermute | solution.py:593
  15.3 5.0 %collective-permute-start.4 = (f32[8,256]{1,0:T(8,128)S(1)}, f32[8,256]{1,0:T(8,128)S(1)}, u32[]{:S(2)}, u32[]{:S(2)}) collective-permute-start(f32[8,256]{1,0:T(8,128)S(1)} %get-tuple-element.75), channel_id=1, source_target_pairs={{1,2},{2,1},{3,4},{4,3},{5,6},{6,5},{9,10},{10,9},{11,12},{12,11},... | collective-permute-start | bytes 24584 | tf_op jit(solution)/shard_map/ppermute | solution.py:593
  15.9 4.3 %collective-permute-start.5 = (f32[8,256]{1,0:T(8,128)S(1)}, f32[8,256]{1,0:T(8,128)S(1)}, u32[]{:S(2)}, u32[]{:S(2)}) collective-permute-start(f32[8,256]{1,0:T(8,128)S(1)} %get-tuple-element.76), channel_id=1, source_target_pairs={{0,1},{1,0},{2,3},{3,2},{4,5},{5,4},{6,7},{7,6},{8,9},{9,8},{10,11... | collective-permute-start | bytes 24584 | tf_op jit(solution)/shard_map/ppermute | solution.py:593
  30.6 4.6 %collective-permute-start.6 = (f32[8,128]{1,0:T(8,128)S(1)}, f32[8,128]{1,0:T(8,128)S(1)}, u32[]{:S(2)}, u32[]{:S(2)}) collective-permute-start(f32[8,128]{1,0:T(8,128)S(1)} %shard_map.111), channel_id=1, source_target_pairs={{0,16},{8,24},{16,0},{24,8},{1,17},{9,25},{17,1},{25,9},{2,18},{10... | collective-permute-start | bytes 12296 | tf_op jit(solution)/shard_map/ppermute | solution.py:608
  35.2 3.6 %collective-permute-start.7 = (f32[8,128]{1,0:T(8,128)S(1)}, f32[8,128]{1,0:T(8,128)S(1)}, u32[]{:S(2)}, u32[]{:S(2)}) collective-permute-start(f32[8,128]{1,0:T(8,128)S(1)} %add.6), channel_id=1, source_target_pairs={{0,8},{8,0},{16,24},{24,16},{1,9},{9,1},{17,25},{25,17},{2,10},{10... | collective-permute-start | bytes 12296 | tf_op jit(solution)/shard_map/ppermute | solution.py:608
  38.8 0.6 %copy-start = (f32[8,128]{1,0:T(8,128)}, f32[8,128]{1,0:T(8,128)S(1)}, u32[]{:S(2)}) copy-start(f32[8,128]{1,0:T(8,128)S(1)} %add.7) | copy-start | bytes 12292

commit v11 on v10

--- a/solution.py
+++ b/solution.py
@@ -495,11 +495,17 @@
     blocks,
     edges,
     heavy,
+    terms0,
+    terms1,
     terms_ref,
     sums_ref,
     delta_ref,
 ):
     rows, edge_count = own.shape
+    groups = rows // 2
+    terms_ref[:groups] = terms0[...]
+    terms_ref[groups : 2 * groups] = terms1[...]
+    terms_ref[3 * groups] = jnp.broadcast_to(scale_in[:1, :1], terms_ref.shape[1:])
     first = row_ids(rows) < rows // 2
     scale = scale_in[...]
     inverse_scale = 1.0 / scale
@@ -514,7 +520,9 @@
         for g, value in enumerate(products(blocks, picked, polars, i)):
             forms[g] = add(forms[g], picked[g][i] * value)
     for g, mine in enumerate(picked):
-        terms_ref[g] = weighted_sum(mine, [heavy[g * SIDE + i] for i in range(SIDE)])
+        terms_ref[2 * groups + g] = weighted_sum(
+            mine, [heavy[g * SIDE + i] for i in range(SIDE)]
+        )
     forms = rows_of_forms(forms, rows)
     sums = inner_products(
         step, sums_in[...], cut(own), cut(delta_ref), forms, across_in, beside_in
@@ -522,8 +530,8 @@
     sums_ref[...] = jnp.where(first, sums, scale)
 
 
-def combine_stage(everyone, sums_in, terms0, terms1, terms2, out_ref):
-    rows = sums_in.shape[0]
+def combine_stage(everyone, own, other, out_ref):
+    rows = everyone.shape[1]
     groups = rows // 2
     first = row_ids(rows) < groups
 
@@ -557,16 +565,18 @@
     c2 = y2 / d3
     c1 = y1 / d2 - l3 * c2
     c0 = m[0] / m[1] - l1 * c1 - l2 * c2
-    mine = scale_of(sums_in[...]) * inverse_top
-    c0 = c0 * inverse_top
-    c1 = c1 * mine * inverse_top
-    c2 = c2 * mine * mine * inverse_top
-    out = None
-    for terms, c in ((terms0, c0), (terms1, c1), (terms2, c2)):
-        for g in range(groups):
-            one = terms[g] * spread(c[g : g + 1], out_ref.shape[0])
-            out = one if out is None else out + one
-    out_ref[...] = out
+    tall = out_ref.shape[1]
+    for n, terms in enumerate((own, other)):
+        mine = terms[3 * groups] * inverse_top[:1]
+        weight = spread(inverse_top[:1], tall)
+        out = None
+        for place, c in enumerate((c0, c1, c2)):
+            part = None
+            for g in range(groups):
+                part = add(part, terms[place * groups + g] * spread(c[g : g + 1], tall))
+            out = add(out, part * weight)
+            weight = weight * mine
+        out_ref[n] = out
 
 
 def pinned(*arguments):
@@ -599,13 +609,13 @@
     return lax.all_to_all(copies, axis, 0, 0)
 
 
-def sum_over(block, axis):
-    size = lax.axis_size(axis)
-    if size & (size - 1):
-        return jnp.sum(gather_all(block, axis), axis=0)
+def sum_over_freq(block):
+    size, width = lax.axis_size("freq"), lax.axis_size("dom")
+    places = range(1, width, 2)
     step = size // 2
     while step > 0:
-        block = block + lax.ppermute(block, axis, [(i, i ^ step) for i in range(size)])
+        route = [(f * width + p, (f ^ step) * width + p) for f in range(size) for p in places]
+        block = block + lax.ppermute(block, ("freq", "dom"), route)
         step //= 2
     return block
 
@@ -711,19 +721,21 @@
         else:
             term, sums, own, picks = call(back, (*given, heavy), back_shapes, cost=4_000_000)
         terms.append(term)
-    term, sums = call(
+    terms, sums = call(
         functools.partial(last_stage, polars, 2),
-        (own, order, inverse, across, beside, scale, sums, picks, blocks, edges, heavy),
-        [terms_shape, sums_shape],
+        (own, order, inverse, across, beside, scale, sums, picks, blocks, edges, heavy, *terms),
+        [shape(3 * groups + 1, tall, LANES), sums_shape],
         (pltpu.VMEM((rows, 2 * rim), jnp.float32),),
     )
-    terms.append(term)
-    term = call(
+    both = call(
         combine_stage,
-        (gather_all(sums, "dom"), sums, *terms),
-        shape(tall, LANES),
-    )
-    gradient = sum_over(term, "freq").reshape(1, slots)
+        (gather_all(sums, "dom"), terms, swap(terms, "dom", 0)),
+        shape(2, tall, LANES),
+    )
+    both = sum_over_freq(both)
+    returned = swap(both[1], "dom", 0)
+    odd = lax.rem(lax.axis_index("dom"), 2) == 1
+    gradient = jnp.where(odd, both[0], returned).reshape(1, slots)
     updated = sigma.reshape(1, slots) * jnp.exp(-0.5 * jnp.tanh(gradient))
     return gradient, updated
 

time: 39.7 us -> 41.9 us (1.055)
  starting transfers between devices: 16.8 us -> 22.1 us
  waiting for transfers between devices: 3.96 us -> 0.85 us
    ppermute x6 -> x8, starting transfers between devices: 12.6 us -> 20.7 us  [swap(): return lax.ppermute(block, axis, route)]
    ppermute x2, waiting for transfers between devices: 3.95 us -> 0.01 us  [sum_over_freq(): block = block + lax.ppermute(block, ('freq', 'dom'), route)]
    ppermute x2, starting transfers between devices: 4.23 us -> 1.32 us  [sum_over_freq(): block = block + lax.ppermute(block, ('freq', 'dom'), route)]
    ppermute x6 -> x8, waiting for transfers between devices: 0.02 us -> 0.84 us  [swap(): return lax.ppermute(block, axis, route)]
  transfers between devices with their start and end apart: 8 -> 10, of which waited for: 2 -> 1; matrix products, arithmetic and copies ran while one was open for 0% -> 0% of each run, Pallas kernels for 11% -> 10%
where the time goes in v11:
time: 41.9 us; the launch traced here: 41.6 us
  starting transfers between devices  22.1 us (53%)
  blocking collectives  9.63 us (23%)
  Pallas kernels  7.64 us (18%)
  waiting for transfers between devices  0.85 us (2%)
  between operations  0.78 us (2%)
  other arithmetic  0.63 us (2%)
    ppermute x8, starting transfers between devices, swap(): return lax.ppermute(block, axis, route)  20.7 us
    all_to_all x1, blocking collectives, gather_all(): return lax.all_to_all(copies, axis, 0, 0)  9.63 us
    pallas_call x8, Pallas kernels, call(): pl.pallas_call(kernel, out_shape=outs, in_specs=space if isinstance(space...  7.64 us
    ppermute x2, starting transfers between devices, sum_over_freq(): block = block + lax.ppermute(block, ('freq', 'dom'), route)  1.32 us
    ppermute x8, waiting for transfers between devices, swap(): return lax.ppermute(block, axis, route)  0.84 us
  transfers between devices with their start and end apart: 10, of which 1 were waited for; matrix products, arithmetic and copies ran while one was open for 0% of the time, Pallas kernels for 10%

profile of v11, /device:TPU:0, one launch (start us, length us, event | category | flops | bytes accessed | tf_op | source)
XLA Modules:
  0.0 41.6 jit_solution(7063135489244836380)
XLA Ops:
  0.6 0.8 %shard_map.104 = (f32[8,256]{1,0:T(8,128)S(1)}, f32[8,256]{1,0:T(8,128)S(1)}, f32[4,1,1280]{2,1,0:T(1,128)S(1)}, s32[8,256]{1,0:T(8,128)S(1)}) custom-call(f32[4,1,1280]{2,1,0:T(1,128)} %bitcast.20, s32[1,256]{1,0:T(1,128)} %order_in.1), custom_call_target="tpu_custom_call" | custom-call | tf_op jit(solution)/shard_map/pallas_call | solution.py:587
  1.4 0.7 %collective-permute-start = (f32[8,256]{1,0:T(8,128)S(1)}, f32[8,256]{1,0:T(8,128)S(1)}, u32[]{:S(2)}, u32[]{:S(2)}) collective-permute-start(f32[8,256]{1,0:T(8,128)S(1)} %get-tuple-element.46), channel_id=1, source_target_pairs={{1,2},{2,1},{3,4},{4,3},{5,6},{6,5},{9,10},{10,9},{11,12},{12,11},... | collective-permute-start | bytes 24584 | tf_op jit(solution)/shard_map/ppermute | solution.py:603
  2.1 4.4 %collective-permute-start.1 = (f32[8,256]{1,0:T(8,128)S(1)}, f32[8,256]{1,0:T(8,128)S(1)}, u32[]{:S(2)}, u32[]{:S(2)}) collective-permute-start(f32[8,256]{1,0:T(8,128)S(1)} %get-tuple-element.47), channel_id=1, source_target_pairs={{0,1},{1,0},{2,3},{3,2},{4,5},{5,4},{6,7},{7,6},{8,9},{9,8},{10,11... | collective-permute-start | bytes 24584 | tf_op jit(solution)/shard_map/ppermute | solution.py:603
  6.4 1.9 %shard_map.105 = (bf16[128,6144]{1,0:T(8,128)(2,1)S(1)}, f32[72,8,128]{2,1,0:T(8,128)S(1)}, f32[8,128]{1,0:T(8,128)S(1)}, f32[24,8,128]{2,1,0:T(8,128)S(1)}, f32...) custom-call(f32[2]{0:T(128)} %angular_in.1, ...), custom_call_target="tpu_custom_call" | custom-call | flops 4000000 | bytes 4000000 | tf_op jit(solution)/shard_map/pallas_call | solution.py:587
  8.4 0.0 collective-permute-done.1.beside_in
  8.4 1.0 %shard_map.106 = (s32[8,256]{1,0:T(8,128)S(1)}, f32[8,512]{1,0:T(8,128)S(1)}, f32[24,8,128]{2,1,0:T(8,128)S(1)}, f32[384,128]{1,0:T(8,128)S(1)}, f32[8,128]{1,0:...) custom-call(s32[8,256]{1,0:T(8,128)S(1)} %get-tuple-element.45.order_ref, ...), custom_call_target="tpu_custom_call" | custom-call | tf_op jit(solution)/shard_map/pallas_call | solution.py:587
  9.4 0.7 %collective-permute-start.2 = (f32[8,256]{1,0:T(8,128)S(1)}, f32[8,256]{1,0:T(8,128)S(1)}, u32[]{:S(2)}, u32[]{:S(2)}) collective-permute-start(f32[8,256]{1,0:T(8,128)S(1)} %get-tuple-element.63), channel_id=1, source_target_pairs={{1,2},{2,1},{3,4},{4,3},{5,6},{6,5},{9,10},{10,9},{11,12},{12,11},... | collective-permute-start | bytes 24584 | tf_op jit(solution)/shard_map/ppermute | solution.py:603
  10.2 2.9 %collective-permute-start.3 = (f32[8,256]{1,0:T(8,128)S(1)}, f32[8,256]{1,0:T(8,128)S(1)}, u32[]{:S(2)}, u32[]{:S(2)}) collective-permute-start(f32[8,256]{1,0:T(8,128)S(1)} %get-tuple-element.64), channel_id=1, source_target_pairs={{0,1},{1,0},{2,3},{3,2},{4,5},{5,4},{6,7},{7,6},{8,9},{9,8},{10,11... | collective-permute-start | bytes 24584 | tf_op jit(solution)/shard_map/ppermute | solution.py:603
  13.1 1.2 %shard_map.107 = (f32[24,8,128]{2,1,0:T(8,128)S(1)}, f32[4,8,128]{2,1,0:T(8,128)S(1)}, f32[8,128]{1,0:T(8,128)S(1)}, f32[8,1280]{1,0:T(8,128)S(1)}, f32[24,8,128]{2,1,0:T(8,128)S(1)}) custom-call(f32[8,1280]{1,0:T(8,128)S(1)} %get-tuple-element.44.own, f32[8,512]{1,0:T(8,128)S(1)} %get-tuple-element.53.delta, f32[8,128]{1,0:T(8,128)S(1)} %get-tuple-element.54.forms, ...), custom_call_target="tpu_custom_call" | custom-call | flops 4000000 | bytes 4000000 | tf_op jit(solution)/shard_map/pallas_call | solution.py:587
  14.3 0.0 collective-permute-done.3.beside_in
  14.3 1.0 %shard_map.108 = (f32[8,512]{1,0:T(8,128)S(1)}, f32[24,8,128]{2,1,0:T(8,128)S(1)}, f32[384,128]{1,0:T(8,128)S(1)}, f32[8,128]{1,0:T(8,128)S(1)}, f32[8,512]{1,0:...) custom-call(s32[8,256]{1,0:T(8,128)S(1)} %get-tuple-element.45.order_ref, ...), custom_call_target="tpu_custom_call" | custom-call | tf_op jit(solution)/shard_map/pallas_call | solution.py:587
  15.3 0.7 %collective-permute-start.4 = (f32[8,256]{1,0:T(8,128)S(1)}, f32[8,256]{1,0:T(8,128)S(1)}, u32[]{:S(2)}, u32[]{:S(2)}) collective-permute-start(f32[8,256]{1,0:T(8,128)S(1)} %get-tuple-element.75), channel_id=1, source_target_pairs={{1,2},{2,1},{3,4},{4,3},{5,6},{6,5},{9,10},{10,9},{11,12},{12,11},... | collective-permute-start | bytes 24584 | tf_op jit(solution)/shard_map/ppermute | solution.py:603
  15.9 3.2 %collective-permute-start.5 = (f32[8,256]{1,0:T(8,128)S(1)}, f32[8,256]{1,0:T(8,128)S(1)}, u32[]{:S(2)}, u32[]{:S(2)}) collective-permute-start(f32[8,256]{1,0:T(8,128)S(1)} %get-tuple-element.76), channel_id=1, source_target_pairs={{0,1},{1,0},{2,3},{3,2},{4,5},{5,4},{6,7},{7,6},{8,9},{9,8},{10,11... | collective-permute-start | bytes 24584 | tf_op jit(solution)/shard_map/ppermute | solution.py:603
  19.2 1.1 %shard_map.109 = (f32[4,8,128]{2,1,0:T(8,128)S(1)}, f32[8,128]{1,0:T(8,128)S(1)}, f32[8,1280]{1,0:T(8,128)S(1)}, f32[24,8,128]{2,1,0:T(8,128)S(1)}) custom-call(f32[8,1280]{1,0:T(8,128)S(1)} %get-tuple-element.62.own, f32[8,512]{1,0:T(8,128)S(1)} %get-tuple-element.67.delta, f32[8,128]{1,0:T(8,128)S(1)} %get-tuple-element.68.forms, ...), custom_call_target="tpu_custom_call" | custom-call | flops 4000000 | bytes 4000000 | tf_op jit(solution)/shard_map/pallas_call | solution.py:587
  20.3 0.0 collective-permute-done.4.across_in
  20.3 0.5 %shard_map.110 = (f32[13,8,128]{2,1,0:T(8,128)S(1)}, f32[8,128]{1,0:T(8,128)S(1)}) custom-call(f32[8,1280]{1,0:T(8,128)S(1)} %get-tuple-element.74.own, s32[8,256]{1,0:T(8,128)S(1)} %get-tuple-element.45.order_ref, s32[8,256]{1,0:T(8,128)S(1)} %get-tuple-element.66.rest_0_.inverse_in, f32[8,256]{1,0:T(8,128)S(1)} %collective-permute-done.4.across_in, ...), custom_call_target="tpu_custom_call" | custom-call | tf_op jit(solution)/shard_map/pallas_call | solution.py:587
  20.8 0.2 collective-permute-start.6
  21.0 9.6 %all_to_all.5.everyone = f32[8,8,128]{2,1,0:T(8,128)S(1)} all-to-all(f32[8,8,128]{2,1,0:T(8,128)S(1)} %broadcast_in_dim.10), channel_id=1, replica_groups=mesh['freq'=4,'dom'=8] {'dom'}, dimensions={0} | all-to-all | bytes 65536 | tf_op jit(solution)/shard_map/all_to_all | solution.py:609
  30.6 0.1 shard_map.111
  30.7 0.7 %collective-permute-start.7 = (f32[2,8,128]{2,1,0:T(8,128)S(1)}, f32[2,8,128]{2,1,0:T(8,128)S(1)}, u32[]{:S(2)}, u32[]{:S(2)}) collective-permute-start(f32[2,8,128]{2,1,0:T(8,128)S(1)} %shard_map.111), channel_id=1, source_target_pairs={{1,17},{3,19},{5,21},{7,23},{9,25},{11,27},{13,29},{15,31},{17,1},... | collective-permute-start | bytes 24584 | tf_op jit(solution)/shard_map/ppermute | solution.py:618
  31.4 0.7 %collective-permute-start.8 = (f32[2,8,128]{2,1,0:T(8,128)S(1)}, f32[2,8,128]{2,1,0:T(8,128)S(1)}, u32[]{:S(2)}, u32[]{:S(2)}) collective-permute-start(f32[2,8,128]{2,1,0:T(8,128)S(1)} %add.6), channel_id=1, source_target_pairs={{1,9},{3,11},{5,13},{7,15},{9,1},{11,3},{13,5},{15,7},{17,25},{19,... | collective-permute-start | bytes 24584 | tf_op jit(solution)/shard_map/ppermute | solution.py:618
  32.1 8.0 %collective-permute-start.9 = (f32[8,128]{1,0:T(8,128)S(1)}, f32[8,128]{1,0:T(8,128)S(1)}, u32[]{:S(2)}, u32[]{:S(2)}) collective-permute-start(f32[8,128]{1,0:T(8,128)S(1)} %slice_bitcast_fusion), channel_id=1, source_target_pairs={{0,1},{1,0},{2,3},{3,2},{4,5},{5,4},{6,7},{7,6},{8,9},{9,8},{10,11... | collective-permute-start | bytes 12296 | tf_op jit(solution)/shard_map/ppermute | solution.py:603
  40.2 0.8 %collective-permute-done.9 = f32[8,128]{1,0:T(8,128)S(1)} collective-permute-done((f32[8,128]{1,0:T(8,128)S(1)}, f32[8,128]{1,0:T(8,128)S(1)}, u32[]{:S(2)}, u32[]{:S(2)}) %collective-permute-start.9) | collective-permute-done | bytes 4128 | tf_op jit(solution)/shard_map/ppermute | solution.py:603
  41.0 0.6 %exponential_multiply_fusion = f32[1,1024]{1,0:T(1,128)} fusion(f32[1,1024]{1,0:T(1,128)S(1)} %bitcast.15, f32[1,1024]{1,0:T(1,128)S(1)} %bitcast.21), kind=kLoop, calls=%fused_computation.3 | loop fusion | flops 2048 | bytes 12288 | tf_op jit(solution)/shard_map/mul | solution.py:739
  (14 shorter events, 0.0 us)
Async XLA Ops:
  1.4 7.0 %collective-permute-start = (f32[8,256]{1,0:T(8,128)S(1)}, f32[8,256]{1,0:T(8,128)S(1)}, u32[]{:S(2)}, u32[]{:S(2)}) collective-permute-start(f32[8,256]{1,0:T(8,128)S(1)} %get-tuple-element.46), channel_id=1, source_target_pairs={{1,2},{2,1},{3,4},{4,3},{5,6},{6,5},{9,10},{10,9},{11,12},{12,11},... | collective-permute-start | bytes 24584 | tf_op jit(solution)/shard_map/ppermute | solution.py:603
  2.1 6.3 %collective-permute-start.1 = (f32[8,256]{1,0:T(8,128)S(1)}, f32[8,256]{1,0:T(8,128)S(1)}, u32[]{:S(2)}, u32[]{:S(2)}) collective-permute-start(f32[8,256]{1,0:T(8,128)S(1)} %get-tuple-element.47), channel_id=1, source_target_pairs={{0,1},{1,0},{2,3},{3,2},{4,5},{5,4},{6,7},{7,6},{8,9},{9,8},{10,11... | collective-permute-start | bytes 24584 | tf_op jit(solution)/shard_map/ppermute | solution.py:603
  9.4 4.8 %collective-permute-start.2 = (f32[8,256]{1,0:T(8,128)S(1)}, f32[8,256]{1,0:T(8,128)S(1)}, u32[]{:S(2)}, u32[]{:S(2)}) collective-permute-start(f32[8,256]{1,0:T(8,128)S(1)} %get-tuple-element.63), channel_id=1, source_target_pairs={{1,2},{2,1},{3,4},{4,3},{5,6},{6,5},{9,10},{10,9},{11,12},{12,11},... | collective-permute-start | bytes 24584 | tf_op jit(solution)/shard_map/ppermute | solution.py:603
  10.2 4.1 %collective-permute-start.3 = (f32[8,256]{1,0:T(8,128)S(1)}, f32[8,256]{1,0:T(8,128)S(1)}, u32[]{:S(2)}, u32[]{:S(2)}) collective-permute-start(f32[8,256]{1,0:T(8,128)S(1)} %get-tuple-element.64), channel_id=1, source_target_pairs={{0,1},{1,0},{2,3},{3,2},{4,5},{5,4},{6,7},{7,6},{8,9},{9,8},{10,11... | collective-permute-start | bytes 24584 | tf_op jit(solution)/shard_map/ppermute | solution.py:603
  15.3 5.0 %collective-permute-start.4 = (f32[8,256]{1,0:T(8,128)S(1)}, f32[8,256]{1,0:T(8,128)S(1)}, u32[]{:S(2)}, u32[]{:S(2)}) collective-permute-start(f32[8,256]{1,0:T(8,128)S(1)} %get-tuple-element.75), channel_id=1, source_target_pairs={{1,2},{2,1},{3,4},{4,3},{5,6},{6,5},{9,10},{10,9},{11,12},{12,11},... | collective-permute-start | bytes 24584 | tf_op jit(solution)/shard_map/ppermute | solution.py:603
  15.9 4.3 %collective-permute-start.5 = (f32[8,256]{1,0:T(8,128)S(1)}, f32[8,256]{1,0:T(8,128)S(1)}, u32[]{:S(2)}, u32[]{:S(2)}) collective-permute-start(f32[8,256]{1,0:T(8,128)S(1)} %get-tuple-element.76), channel_id=1, source_target_pairs={{0,1},{1,0},{2,3},{3,2},{4,5},{5,4},{6,7},{7,6},{8,9},{9,8},{10,11... | collective-permute-start | bytes 24584 | tf_op jit(solution)/shard_map/ppermute | solution.py:603
  20.8 9.8 %collective-permute-start.6 = (f32[13,8,128]{2,1,0:T(8,128)S(1)}, f32[13,8,128]{2,1,0:T(8,128)S(1)}, u32[]{:S(2)}, u32[]{:S(2)}) collective-permute-start(f32[13,8,128]{2,1,0:T(8,128)S(1)} %get-tuple-element.82.own), channel_id=1, source_target_pairs={{0,1},{1,0},{2,3},{3,2},{4,5},{5,4},{6,7},{7,6},{8,9},{9,8},{10,11... | collective-permute-start | bytes 159752 | tf_op jit(solution)/shard_map/ppermute | solution.py:603
  30.7 0.7 %collective-permute-start.7 = (f32[2,8,128]{2,1,0:T(8,128)S(1)}, f32[2,8,128]{2,1,0:T(8,128)S(1)}, u32[]{:S(2)}, u32[]{:S(2)}) collective-permute-start(f32[2,8,128]{2,1,0:T(8,128)S(1)} %shard_map.111), channel_id=1, source_target_pairs={{1,17},{3,19},{5,21},{7,23},{9,25},{11,27},{13,29},{15,31},{17,1},... | collective-permute-start | bytes 24584 | tf_op jit(solution)/shard_map/ppermute | solution.py:618
  31.4 0.7 %collective-permute-start.8 = (f32[2,8,128]{2,1,0:T(8,128)S(1)}, f32[2,8,128]{2,1,0:T(8,128)S(1)}, u32[]{:S(2)}, u32[]{:S(2)}) collective-permute-start(f32[2,8,128]{2,1,0:T(8,128)S(1)} %add.6), channel_id=1, source_target_pairs={{1,9},{3,11},{5,13},{7,15},{9,1},{11,3},{13,5},{15,7},{17,25},{19,... | collective-permute-start | bytes 24584 | tf_op jit(solution)/shard_map/ppermute | solution.py:618
  32.1 8.9 %collective-permute-start.9 = (f32[8,128]{1,0:T(8,128)S(1)}, f32[8,128]{1,0:T(8,128)S(1)}, u32[]{:S(2)}, u32[]{:S(2)}) collective-permute-start(f32[8,128]{1,0:T(8,128)S(1)} %slice_bitcast_fusion), channel_id=1, source_target_pairs={{0,1},{1,0},{2,3},{3,2},{4,5},{5,4},{6,7},{7,6},{8,9},{9,8},{10,11... | collective-permute-start | bytes 12296 | tf_op jit(solution)/shard_map/ppermute | solution.py:603
  41.0 0.6 %copy-start = (f32[8,128]{1,0:T(8,128)}, f32[8,128]{1,0:T(8,128)S(1)}, u32[]{:S(2)}) copy-start(f32[8,128]{1,0:T(8,128)S(1)} %fusion) | copy-start | bytes 12292

commit v12 on v10

--- a/solution.py
+++ b/solution.py
@@ -99,7 +99,11 @@
 
 def take_rims(across_ref, beside_ref):
     even = is_even()
-    pairs = list(zip(cut(across_ref), cut(beside_ref)))
+    device = lax.axis_index("dom")
+    outermost = (device == 0) | (device == lax.axis_size("dom") - 1)
+    pairs = [
+        (jnp.where(outermost, 0.0, a), b) for a, b in zip(cut(across_ref), cut(beside_ref))
+    ]
     prior = [jnp.where(even, a, b) for a, b in pairs]
     above = [jnp.where(even, b, a) for a, b in pairs]
     return prior, above
@@ -585,12 +589,17 @@
     )(*arguments)
 
 
-def swap(block, axis, offset):
-    size = lax.axis_size(axis)
+def swap_across(block):
+    size = lax.axis_size("dom")
     route = []
-    for low in range(offset, size - 1, 2):
-        route += [(low, low + 1), (low + 1, low)]
-    return lax.ppermute(block, axis, route)
+    for low in range(1, size, 2):
+        high = (low + 1) % size
+        route += [(low, high), (high, low)]
+    return lax.ppermute(block, "dom", route)
+
+
+def swap_beside(block):
+    return lax.ppermute(block, "dom", [(i, i ^ 1) for i in range(lax.axis_size("dom"))])
 
 
 def gather_all(block, axis):
@@ -654,7 +663,7 @@
         ),
         space=HBM,
     )
-    across, beside = swap(across, "dom", 1), swap(beside, "dom", 0)
+    across, beside = swap_across(across), swap_beside(beside)
     kept = [jax.ShapeDtypeStruct(x.shape, x.dtype) for x in (mass, sigma, live, edges, forward)]
     places, blocks, scale, picks, own, rates, mass, sigma, live, edges, forward = call(
         table_stage,
@@ -698,7 +707,7 @@
         else:
             outs = call(front, (*given, inverse), front_shapes)
         delta, picks, pieces, forms, rims, across, beside = outs
-        across, beside = swap(across, "dom", 1), swap(beside, "dom", 0)
+        across, beside = swap_across(across), swap_beside(beside)
         given = (own, delta, forms, *arrived, sums, picks, pieces, rims, edges, places)
         back = functools.partial(back_stage, polars, step)
         if step == 0:

time: 39.7 us -> 34.5 us (0.87)
  starting transfers between devices: 16.8 us -> 11.7 us
  blocking collectives: 9.67 us -> 7.86 us
  waiting for transfers between devices: 3.96 us -> 5.7 us
    ppermute x6, starting transfers between devices: 12.6 us -> 7.5 us  [the longest x3 7.49 us: swap_across(): return lax.ppermute(block, 'dom', route)]
    all_to_all x1, blocking collectives: 9.67 us -> 7.86 us  [gather_all(): return lax.all_to_all(copies, axis, 0, 0)]
    ppermute x6, waiting for transfers between devices: 0.02 us -> 1.76 us  [the longest x3 1.75 us: swap_across(): return lax.ppermute(block, 'dom', route)]
  transfers between devices with their start and end apart: 8 -> 8, of which waited for: 2 -> 4; matrix products, arithmetic and copies ran while one was open for 0% -> 0% of each run, Pallas kernels for 11% -> 12%
where the time goes in v12:
time: 34.5 us; the launch traced here: 34.2 us
  starting transfers between devices  11.7 us (34%)
  blocking collectives  7.86 us (23%)
  Pallas kernels  7.63 us (22%)
  waiting for transfers between devices  5.7 us (17%)
  between operations  0.69 us (2%)
  other arithmetic  0.62 us (2%)
    all_to_all x1, blocking collectives, gather_all(): return lax.all_to_all(copies, axis, 0, 0)  7.86 us
    pallas_call x8, Pallas kernels, call(): pl.pallas_call(kernel, out_shape=outs, in_specs=space if isinstance(space...  7.63 us
    ppermute x3, starting transfers between devices, swap_across(): return lax.ppermute(block, 'dom', route)  7.49 us
    ppermute x2, starting transfers between devices, sum_over(): lax.ppermute(block, axis, [(i, i ^ step) for i in range(size)])  4.23 us
    ppermute x2, waiting for transfers between devices, sum_over(): lax.ppermute(block, axis, [(i, i ^ step) for i in range(size)])  3.94 us
    ppermute x3, waiting for transfers between devices, swap_across(): return lax.ppermute(block, 'dom', route)  1.75 us
  transfers between devices with their start and end apart: 8, of which 4 were waited for; matrix products, arithmetic and copies ran while one was open for 0% of the time, Pallas kernels for 12%

profile of v12, /device:TPU:0, one launch (start us, length us, event | category | flops | bytes accessed | tf_op | source)
XLA Modules:
  0.0 34.2 jit_solution(9920407109221080493)
XLA Ops:
  0.6 0.8 %shard_map.104 = (f32[8,256]{1,0:T(8,128)S(1)}, f32[8,256]{1,0:T(8,128)S(1)}, f32[4,1,1280]{2,1,0:T(1,128)S(1)}, s32[8,256]{1,0:T(8,128)S(1)}) custom-call(f32[4,1,1280]{2,1,0:T(1,128)} %bitcast.14, s32[1,256]{1,0:T(1,128)} %order_in.1), custom_call_target="tpu_custom_call" | custom-call | tf_op jit(solution)/shard_map/pallas_call | solution.py:581
  1.4 3.4 %collective-permute-start = (f32[8,256]{1,0:T(8,128)S(1)}, f32[8,256]{1,0:T(8,128)S(1)}, u32[]{:S(2)}, u32[]{:S(2)}) collective-permute-start(f32[8,256]{1,0:T(8,128)S(1)} %get-tuple-element.46), channel_id=1, source_target_pairs={{1,2},{2,1},{3,4},{4,3},{5,6},{6,5},{7,0},{0,7},{9,10},{10,9},{11,... | collective-permute-start | bytes 24584 | tf_op jit(solution)/shard_map/ppermute | solution.py:598
  4.8 0.0 collective-permute-start.1
  4.8 1.9 %shard_map.105 = (bf16[128,6144]{1,0:T(8,128)(2,1)S(1)}, f32[72,8,128]{2,1,0:T(8,128)S(1)}, f32[8,128]{1,0:T(8,128)S(1)}, f32[24,8,128]{2,1,0:T(8,128)S(1)}, f32...) custom-call(f32[2]{0:T(128)} %angular_in.1, ...), custom_call_target="tpu_custom_call" | custom-call | flops 4000000 | bytes 4000000 | tf_op jit(solution)/shard_map/pallas_call | solution.py:581
  6.7 0.0 collective-permute-done.across_in
  6.8 0.0 collective-permute-done.1.beside_in
  6.8 1.0 %shard_map.106 = (s32[8,256]{1,0:T(8,128)S(1)}, f32[8,512]{1,0:T(8,128)S(1)}, f32[24,8,128]{2,1,0:T(8,128)S(1)}, f32[384,128]{1,0:T(8,128)S(1)}, f32[8,128]{1,0:...) custom-call(s32[8,256]{1,0:T(8,128)S(1)} %get-tuple-element.45.order_ref, ...), custom_call_target="tpu_custom_call" | custom-call | tf_op jit(solution)/shard_map/pallas_call | solution.py:581
  7.8 2.1 %collective-permute-start.2 = (f32[8,256]{1,0:T(8,128)S(1)}, f32[8,256]{1,0:T(8,128)S(1)}, u32[]{:S(2)}, u32[]{:S(2)}) collective-permute-start(f32[8,256]{1,0:T(8,128)S(1)} %get-tuple-element.63), channel_id=1, source_target_pairs={{1,2},{2,1},{3,4},{4,3},{5,6},{6,5},{7,0},{0,7},{9,10},{10,9},{11,... | collective-permute-start | bytes 24584 | tf_op jit(solution)/shard_map/ppermute | solution.py:598
  9.9 0.0 collective-permute-start.3
  9.9 1.2 %shard_map.107 = (f32[24,8,128]{2,1,0:T(8,128)S(1)}, f32[4,8,128]{2,1,0:T(8,128)S(1)}, f32[8,128]{1,0:T(8,128)S(1)}, f32[8,1280]{1,0:T(8,128)S(1)}, f32[24,8,128]{2,1,0:T(8,128)S(1)}) custom-call(f32[8,1280]{1,0:T(8,128)S(1)} %get-tuple-element.44.own, f32[8,512]{1,0:T(8,128)S(1)} %get-tuple-element.53.delta, f32[8,128]{1,0:T(8,128)S(1)} %get-tuple-element.54.forms, ...), custom_call_target="tpu_custom_call" | custom-call | flops 4000000 | bytes 4000000 | tf_op jit(solution)/shard_map/pallas_call | solution.py:581
  11.1 0.8 %collective-permute-done.2.across_in = f32[8,256]{1,0:T(8,128)S(1)} collective-permute-done((f32[8,256]{1,0:T(8,128)S(1)}, f32[8,256]{1,0:T(8,128)S(1)}, u32[]{:S(2)}, u32[]{:S(2)}) %collective-permute-start.2) | collective-permute-done | bytes 8224 | tf_op jit(solution)/shard_map/ppermute | solution.py:598
  11.9 0.0 collective-permute-done.3.beside_in
  11.9 1.0 %shard_map.108 = (f32[8,512]{1,0:T(8,128)S(1)}, f32[24,8,128]{2,1,0:T(8,128)S(1)}, f32[384,128]{1,0:T(8,128)S(1)}, f32[8,128]{1,0:T(8,128)S(1)}, f32[8,512]{1,0:...) custom-call(s32[8,256]{1,0:T(8,128)S(1)} %get-tuple-element.45.order_ref, ...), custom_call_target="tpu_custom_call" | custom-call | tf_op jit(solution)/shard_map/pallas_call | solution.py:581
  12.9 2.0 %collective-permute-start.4 = (f32[8,256]{1,0:T(8,128)S(1)}, f32[8,256]{1,0:T(8,128)S(1)}, u32[]{:S(2)}, u32[]{:S(2)}) collective-permute-start(f32[8,256]{1,0:T(8,128)S(1)} %get-tuple-element.75), channel_id=1, source_target_pairs={{1,2},{2,1},{3,4},{4,3},{5,6},{6,5},{7,0},{0,7},{9,10},{10,9},{11,... | collective-permute-start | bytes 24584 | tf_op jit(solution)/shard_map/ppermute | solution.py:598
  14.9 1.1 %shard_map.109 = (f32[4,8,128]{2,1,0:T(8,128)S(1)}, f32[8,128]{1,0:T(8,128)S(1)}, f32[8,1280]{1,0:T(8,128)S(1)}, f32[24,8,128]{2,1,0:T(8,128)S(1)}) custom-call(f32[8,1280]{1,0:T(8,128)S(1)} %get-tuple-element.62.own, f32[8,512]{1,0:T(8,128)S(1)} %get-tuple-element.67.delta, f32[8,128]{1,0:T(8,128)S(1)} %get-tuple-element.68.forms, ...), custom_call_target="tpu_custom_call" | custom-call | flops 4000000 | bytes 4000000 | tf_op jit(solution)/shard_map/pallas_call | solution.py:581
  16.0 0.9 %collective-permute-done.4.across_in = f32[8,256]{1,0:T(8,128)S(1)} collective-permute-done((f32[8,256]{1,0:T(8,128)S(1)}, f32[8,256]{1,0:T(8,128)S(1)}, u32[]{:S(2)}, u32[]{:S(2)}) %collective-permute-start.4) | collective-permute-done | bytes 8224 | tf_op jit(solution)/shard_map/ppermute | solution.py:598
  16.9 0.5 %shard_map.110 = (f32[4,8,128]{2,1,0:T(8,128)S(1)}, f32[8,128]{1,0:T(8,128)S(1)}) custom-call(f32[8,1280]{1,0:T(8,128)S(1)} %get-tuple-element.74.own, s32[8,256]{1,0:T(8,128)S(1)} %get-tuple-element.45.order_ref, s32[8,256]{1,0:T(8,128)S(1)} %get-tuple-element.66.rest_0_.inverse_in, f32[8,256]{1,0:T(8,128)S(1)} %collective-permute-done.4.across_in, ...), custom_call_target="tpu_custom_call" | custom-call | tf_op jit(solution)/shard_map/pallas_call | solution.py:581
  17.4 7.9 %all_to_all.5.everyone = f32[8,8,128]{2,1,0:T(8,128)S(1)} all-to-all(f32[8,8,128]{2,1,0:T(8,128)S(1)} %broadcast_in_dim.10), channel_id=1, replica_groups=mesh['freq'=4,'dom'=8] {'dom'}, dimensions={0} | all-to-all | bytes 65536 | tf_op jit(solution)/shard_map/all_to_all | solution.py:608
  25.3 0.1 shard_map.111
  25.4 2.7 %collective-permute-start.6 = (f32[8,128]{1,0:T(8,128)S(1)}, f32[8,128]{1,0:T(8,128)S(1)}, u32[]{:S(2)}, u32[]{:S(2)}) collective-permute-start(f32[8,128]{1,0:T(8,128)S(1)} %shard_map.111), channel_id=1, source_target_pairs={{0,16},{8,24},{16,0},{24,8},{1,17},{9,25},{17,1},{25,9},{2,18},{10... | collective-permute-start | bytes 12296 | tf_op jit(solution)/shard_map/ppermute | solution.py:617
  28.1 1.9 %collective-permute-done.6 = f32[8,128]{1,0:T(8,128)S(1)} collective-permute-done((f32[8,128]{1,0:T(8,128)S(1)}, f32[8,128]{1,0:T(8,128)S(1)}, u32[]{:S(2)}, u32[]{:S(2)}) %collective-permute-start.6) | collective-permute-done | bytes 4128 | tf_op jit(solution)/shard_map/ppermute | solution.py:617
  30.0 1.6 %collective-permute-start.7 = (f32[8,128]{1,0:T(8,128)S(1)}, f32[8,128]{1,0:T(8,128)S(1)}, u32[]{:S(2)}, u32[]{:S(2)}) collective-permute-start(f32[8,128]{1,0:T(8,128)S(1)} %add.6), channel_id=1, source_target_pairs={{0,8},{8,0},{16,24},{24,16},{1,9},{9,1},{17,25},{25,17},{2,10},{10... | collective-permute-start | bytes 12296 | tf_op jit(solution)/shard_map/ppermute | solution.py:617
  31.6 2.0 %collective-permute-done.7 = f32[8,128]{1,0:T(8,128)S(1)} collective-permute-done((f32[8,128]{1,0:T(8,128)S(1)}, f32[8,128]{1,0:T(8,128)S(1)}, u32[]{:S(2)}, u32[]{:S(2)}) %collective-permute-start.7) | collective-permute-done | bytes 4128 | tf_op jit(solution)/shard_map/ppermute | solution.py:617
  33.6 0.6 %exponential_multiply_fusion = f32[1,1024]{1,0:T(1,128)} fusion(f32[1,1024]{1,0:T(1,128)S(1)} %bitcast.9, f32[1,1024]{1,0:T(1,128)S(1)} %bitcast.15), kind=kLoop, calls=%fused_computation | loop fusion | flops 2048 | bytes 12288 | tf_op jit(solution)/shard_map/mul | solution.py:736
  (8 shorter events, 0.0 us)
Async XLA Ops:
  1.4 5.4 %collective-permute-start = (f32[8,256]{1,0:T(8,128)S(1)}, f32[8,256]{1,0:T(8,128)S(1)}, u32[]{:S(2)}, u32[]{:S(2)}) collective-permute-start(f32[8,256]{1,0:T(8,128)S(1)} %get-tuple-element.46), channel_id=1, source_target_pairs={{1,2},{2,1},{3,4},{4,3},{5,6},{6,5},{7,0},{0,7},{9,10},{10,9},{11,... | collective-permute-start | bytes 24584 | tf_op jit(solution)/shard_map/ppermute | solution.py:598
  4.8 2.0 %collective-permute-start.1 = (f32[8,256]{1,0:T(8,128)S(1)}, f32[8,256]{1,0:T(8,128)S(1)}, u32[]{:S(2)}, u32[]{:S(2)}) collective-permute-start(f32[8,256]{1,0:T(8,128)S(1)} %get-tuple-element.47), channel_id=1, source_target_pairs={{0,1},{1,0},{2,3},{3,2},{4,5},{5,4},{6,7},{7,6},{8,9},{9,8},{10,11... | collective-permute-start | bytes 24584 | tf_op jit(solution)/shard_map/ppermute | solution.py:602
  7.8 4.1 %collective-permute-start.2 = (f32[8,256]{1,0:T(8,128)S(1)}, f32[8,256]{1,0:T(8,128)S(1)}, u32[]{:S(2)}, u32[]{:S(2)}) collective-permute-start(f32[8,256]{1,0:T(8,128)S(1)} %get-tuple-element.63), channel_id=1, source_target_pairs={{1,2},{2,1},{3,4},{4,3},{5,6},{6,5},{7,0},{0,7},{9,10},{10,9},{11,... | collective-permute-start | bytes 24584 | tf_op jit(solution)/shard_map/ppermute | solution.py:598
  9.9 2.0 %collective-permute-start.3 = (f32[8,256]{1,0:T(8,128)S(1)}, f32[8,256]{1,0:T(8,128)S(1)}, u32[]{:S(2)}, u32[]{:S(2)}) collective-permute-start(f32[8,256]{1,0:T(8,128)S(1)} %get-tuple-element.64), channel_id=1, source_target_pairs={{0,1},{1,0},{2,3},{3,2},{4,5},{5,4},{6,7},{7,6},{8,9},{9,8},{10,11... | collective-permute-start | bytes 24584 | tf_op jit(solution)/shard_map/ppermute | solution.py:602
  12.9 4.0 %collective-permute-start.4 = (f32[8,256]{1,0:T(8,128)S(1)}, f32[8,256]{1,0:T(8,128)S(1)}, u32[]{:S(2)}, u32[]{:S(2)}) collective-permute-start(f32[8,256]{1,0:T(8,128)S(1)} %get-tuple-element.75), channel_id=1, source_target_pairs={{1,2},{2,1},{3,4},{4,3},{5,6},{6,5},{7,0},{0,7},{9,10},{10,9},{11,... | collective-permute-start | bytes 24584 | tf_op jit(solution)/shard_map/ppermute | solution.py:598
  14.9 2.0 %collective-permute-start.5 = (f32[8,256]{1,0:T(8,128)S(1)}, f32[8,256]{1,0:T(8,128)S(1)}, u32[]{:S(2)}, u32[]{:S(2)}) collective-permute-start(f32[8,256]{1,0:T(8,128)S(1)} %get-tuple-element.76), channel_id=1, source_target_pairs={{0,1},{1,0},{2,3},{3,2},{4,5},{5,4},{6,7},{7,6},{8,9},{9,8},{10,11... | collective-permute-start | bytes 24584 | tf_op jit(solution)/shard_map/ppermute | solution.py:602
  25.4 4.6 %collective-permute-start.6 = (f32[8,128]{1,0:T(8,128)S(1)}, f32[8,128]{1,0:T(8,128)S(1)}, u32[]{:S(2)}, u32[]{:S(2)}) collective-permute-start(f32[8,128]{1,0:T(8,128)S(1)} %shard_map.111), channel_id=1, source_target_pairs={{0,16},{8,24},{16,0},{24,8},{1,17},{9,25},{17,1},{25,9},{2,18},{10... | collective-permute-start | bytes 12296 | tf_op jit(solution)/shard_map/ppermute | solution.py:617
  30.0 3.6 %collective-permute-start.7 = (f32[8,128]{1,0:T(8,128)S(1)}, f32[8,128]{1,0:T(8,128)S(1)}, u32[]{:S(2)}, u32[]{:S(2)}) collective-permute-start(f32[8,128]{1,0:T(8,128)S(1)} %add.6), channel_id=1, source_target_pairs={{0,8},{8,0},{16,24},{24,16},{1,9},{9,1},{17,25},{25,17},{2,10},{10... | collective-permute-start | bytes 12296 | tf_op jit(solution)/shard_map/ppermute | solution.py:617
  33.6 0.6 %copy-start = (f32[8,128]{1,0:T(8,128)}, f32[8,128]{1,0:T(8,128)S(1)}, u32[]{:S(2)}) copy-start(f32[8,128]{1,0:T(8,128)S(1)} %add.7) | copy-start | bytes 12292

commit v13 on v12

--- a/solution.py
+++ b/solution.py
@@ -526,7 +526,8 @@
     sums_ref[...] = jnp.where(first, sums, scale)
 
 
-def combine_stage(everyone, sums_in, terms0, terms1, terms2, out_ref):
+def combine_stage(count, *refs):
+    everyone, (sums_in, terms0, terms1, terms2, out_ref) = refs[:count], refs[count:]
     rows = sums_in.shape[0]
     groups = rows // 2
     first = row_ids(rows) < groups
@@ -534,7 +535,9 @@
     def scale_of(block):
         return jnp.where(first, swap_halves(block), block)
 
-    parts = [everyone[q] for q in range(everyone.shape[0])]
+    parts = [
+        ref[at : at + rows, :] for ref in everyone for at in range(0, ref.shape[0], rows)
+    ]
     scales = [scale_of(block) for block in parts]
     top = functools.reduce(jnp.maximum, scales)
     lanes = lane_ids(rows)
@@ -591,10 +594,9 @@
 
 def swap_across(block):
     size = lax.axis_size("dom")
-    route = []
-    for low in range(1, size, 2):
-        high = (low + 1) % size
-        route += [(low, high), (high, low)]
+    route = [(0, 0), (size - 1, size - 1)]
+    for low in range(1, size - 1, 2):
+        route += [(low, low + 1), (low + 1, low)]
     return lax.ppermute(block, "dom", route)
 
 
@@ -606,6 +608,17 @@
     size = lax.axis_size(axis)
     copies = jnp.broadcast_to(block[None], (size, *block.shape))
     return lax.all_to_all(copies, axis, 0, 0)
+
+
+def gather_sums(block):
+    size = lax.axis_size("dom")
+    if size > 8:
+        return [gather_all(block, "dom").reshape(-1, block.shape[1])]
+    pair = jnp.concatenate([block, swap_beside(block)], axis=0)
+    return [pair] + [
+        lax.ppermute(pair, "dom", [(i, i ^ step) for i in range(size)])
+        for step in range(size - 2, 0, -2)
+    ]
 
 
 def sum_over(block, axis):
@@ -727,9 +740,10 @@
         (pltpu.VMEM((rows, 2 * rim), jnp.float32),),
     )
     terms.append(term)
+    everyone = gather_sums(sums)
     term = call(
-        combine_stage,
-        (gather_all(sums, "dom"), sums, *terms),
+        functools.partial(combine_stage, len(everyone)),
+        (*everyone, sums, *terms),
         shape(tall, LANES),
     )
     gradient = sum_over(term, "freq").reshape(1, slots)

time: 34.5 us -> 39.5 us (1.14)
  starting transfers between devices: 11.7 us -> 22.2 us
  blocking collectives: 7.86 us -> 0 us
  waiting for transfers between devices: 5.7 us -> 8.05 us
    ppermute x3 -> x4, starting transfers between devices: 0.01 us -> 10.7 us  [swap_beside(): lax.ppermute(block, 'dom', [(i, i ^ 1) for i in range(lax.axis_size('dom'...]
    all_to_all x1 -> x0, blocking collectives: 7.86 us -> none  [gather_all(): return lax.all_to_all(copies, axis, 0, 0)]
    ppermute x3, starting transfers between devices: 7.49 us -> 2.05 us  [swap_across(): return lax.ppermute(block, 'dom', route)]
    ppermute x0 -> x3, starting transfers between devices: none -> 5.22 us  [gather_sums(): lax.ppermute(pair, 'dom', [(i, i ^ step) for i in range(size)])]
    ppermute x0 -> x3, waiting for transfers between devices: none -> 3.09 us  [gather_sums(): lax.ppermute(pair, 'dom', [(i, i ^ step) for i in range(size)])]
    ppermute x3, waiting for transfers between devices: 1.75 us -> 0.01 us  [swap_across(): return lax.ppermute(block, 'dom', route)]
    ppermute x3 -> x4, waiting for transfers between devices: 0.01 us -> 1.01 us  [swap_beside(): lax.ppermute(block, 'dom', [(i, i ^ 1) for i in range(lax.axis_size('dom'...]
  transfers between devices with their start and end apart: 8 -> 12, of which waited for: 4 -> 5; matrix products, arithmetic and copies ran while one was open for 0% -> 0% of each run, Pallas kernels for 12% -> 11%
where the time goes in v13:
time: 39.5 us; the launch traced here: 39.2 us
  starting transfers between devices  22.2 us (56%)
  waiting for transfers between devices  8.05 us (20%)
  Pallas kernels  7.65 us (19%)
  between operations  0.73 us (2%)
  other arithmetic  0.62 us (2%)
    ppermute x4, starting transfers between devices, swap_beside(): lax.ppermute(block, 'dom', [(i, i ^ 1) for i in range(lax.axis_size('dom'...  10.7 us
    pallas_call x8, Pallas kernels, call(): pl.pallas_call(kernel, out_shape=outs, in_specs=space if isinstance(space...  7.65 us
    ppermute x3, starting transfers between devices, gather_sums(): lax.ppermute(pair, 'dom', [(i, i ^ step) for i in range(size)])  5.22 us
    ppermute x2, starting transfers between devices, sum_over(): lax.ppermute(block, axis, [(i, i ^ step) for i in range(size)])  4.23 us
    ppermute x2, waiting for transfers between devices, sum_over(): lax.ppermute(block, axis, [(i, i ^ step) for i in range(size)])  3.94 us
    ppermute x3, waiting for transfers between devices, gather_sums(): lax.ppermute(pair, 'dom', [(i, i ^ step) for i in range(size)])  3.09 us
    ppermute x3, starting transfers between devices, swap_across(): return lax.ppermute(block, 'dom', route)  2.05 us
    ppermute x4, waiting for transfers between devices, swap_beside(): lax.ppermute(block, 'dom', [(i, i ^ 1) for i in range(lax.axis_size('dom'...  1.01 us
  transfers between devices with their start and end apart: 12, of which 5 were waited for; matrix products, arithmetic and copies ran while one was open for 0% of the time, Pallas kernels for 11%

profile of v13, /device:TPU:0, one launch (start us, length us, event | category | flops | bytes accessed | tf_op | source)
XLA Modules:
  0.0 39.2 jit_solution(7315417678105750777)
XLA Ops:
  0.6 0.8 %shard_map.104 = (f32[8,256]{1,0:T(8,128)S(1)}, f32[8,256]{1,0:T(8,128)S(1)}, f32[4,1,1280]{2,1,0:T(1,128)S(1)}, s32[8,256]{1,0:T(8,128)S(1)}) custom-call(f32[4,1,1280]{2,1,0:T(1,128)} %bitcast.14, s32[1,256]{1,0:T(1,128)} %order_in.1), custom_call_target="tpu_custom_call" | custom-call | tf_op jit(solution)/shard_map/pallas_call | solution.py:584
  1.4 0.7 %collective-permute-start = (f32[8,256]{1,0:T(8,128)S(1)}, f32[8,256]{1,0:T(8,128)S(1)}, u32[]{:S(2)}, u32[]{:S(2)}) collective-permute-start(f32[8,256]{1,0:T(8,128)S(1)} %get-tuple-element.46), channel_id=1, source_target_pairs={{0,0},{7,7},{1,2},{2,1},{3,4},{4,3},{5,6},{6,5},{8,8},{15,15},{9,1... | collective-permute-start | bytes 24584 | tf_op jit(solution)/shard_map/ppermute | solution.py:600
  2.1 4.4 %collective-permute-start.1 = (f32[8,256]{1,0:T(8,128)S(1)}, f32[8,256]{1,0:T(8,128)S(1)}, u32[]{:S(2)}, u32[]{:S(2)}) collective-permute-start(f32[8,256]{1,0:T(8,128)S(1)} %get-tuple-element.47), channel_id=1, source_target_pairs={{0,1},{1,0},{2,3},{3,2},{4,5},{5,4},{6,7},{7,6},{8,9},{9,8},{10,11... | collective-permute-start | bytes 24584 | tf_op jit(solution)/shard_map/ppermute | solution.py:604
  6.4 1.9 %shard_map.105 = (bf16[128,6144]{1,0:T(8,128)(2,1)S(1)}, f32[72,8,128]{2,1,0:T(8,128)S(1)}, f32[8,128]{1,0:T(8,128)S(1)}, f32[24,8,128]{2,1,0:T(8,128)S(1)}, f32...) custom-call(f32[2]{0:T(128)} %angular_in.1, ...), custom_call_target="tpu_custom_call" | custom-call | flops 4000000 | bytes 4000000 | tf_op jit(solution)/shard_map/pallas_call | solution.py:584
  8.4 1.0 %shard_map.106 = (s32[8,256]{1,0:T(8,128)S(1)}, f32[8,512]{1,0:T(8,128)S(1)}, f32[24,8,128]{2,1,0:T(8,128)S(1)}, f32[384,128]{1,0:T(8,128)S(1)}, f32[8,128]{1,0:...) custom-call(s32[8,256]{1,0:T(8,128)S(1)} %get-tuple-element.45.order_ref, ...), custom_call_target="tpu_custom_call" | custom-call | tf_op jit(solution)/shard_map/pallas_call | solution.py:584
  9.4 0.7 %collective-permute-start.2 = (f32[8,256]{1,0:T(8,128)S(1)}, f32[8,256]{1,0:T(8,128)S(1)}, u32[]{:S(2)}, u32[]{:S(2)}) collective-permute-start(f32[8,256]{1,0:T(8,128)S(1)} %get-tuple-element.63), channel_id=1, source_target_pairs={{0,0},{7,7},{1,2},{2,1},{3,4},{4,3},{5,6},{6,5},{8,8},{15,15},{9,1... | collective-permute-start | bytes 24584 | tf_op jit(solution)/shard_map/ppermute | solution.py:600
  10.2 2.9 %collective-permute-start.3 = (f32[8,256]{1,0:T(8,128)S(1)}, f32[8,256]{1,0:T(8,128)S(1)}, u32[]{:S(2)}, u32[]{:S(2)}) collective-permute-start(f32[8,256]{1,0:T(8,128)S(1)} %get-tuple-element.64), channel_id=1, source_target_pairs={{0,1},{1,0},{2,3},{3,2},{4,5},{5,4},{6,7},{7,6},{8,9},{9,8},{10,11... | collective-permute-start | bytes 24584 | tf_op jit(solution)/shard_map/ppermute | solution.py:604
  13.1 1.2 %shard_map.107 = (f32[24,8,128]{2,1,0:T(8,128)S(1)}, f32[4,8,128]{2,1,0:T(8,128)S(1)}, f32[8,128]{1,0:T(8,128)S(1)}, f32[8,1280]{1,0:T(8,128)S(1)}, f32[24,8,128]{2,1,0:T(8,128)S(1)}) custom-call(f32[8,1280]{1,0:T(8,128)S(1)} %get-tuple-element.44.own, f32[8,512]{1,0:T(8,128)S(1)} %get-tuple-element.53.delta, f32[8,128]{1,0:T(8,128)S(1)} %get-tuple-element.54.forms, ...), custom_call_target="tpu_custom_call" | custom-call | flops 4000000 | bytes 4000000 | tf_op jit(solution)/shard_map/pallas_call | solution.py:584
  14.3 1.0 %shard_map.108 = (f32[8,512]{1,0:T(8,128)S(1)}, f32[24,8,128]{2,1,0:T(8,128)S(1)}, f32[384,128]{1,0:T(8,128)S(1)}, f32[8,128]{1,0:T(8,128)S(1)}, f32[8,512]{1,0:...) custom-call(s32[8,256]{1,0:T(8,128)S(1)} %get-tuple-element.45.order_ref, ...), custom_call_target="tpu_custom_call" | custom-call | tf_op jit(solution)/shard_map/pallas_call | solution.py:584
  15.3 0.7 %collective-permute-start.4 = (f32[8,256]{1,0:T(8,128)S(1)}, f32[8,256]{1,0:T(8,128)S(1)}, u32[]{:S(2)}, u32[]{:S(2)}) collective-permute-start(f32[8,256]{1,0:T(8,128)S(1)} %get-tuple-element.75), channel_id=1, source_target_pairs={{0,0},{7,7},{1,2},{2,1},{3,4},{4,3},{5,6},{6,5},{8,8},{15,15},{9,1... | collective-permute-start | bytes 24584 | tf_op jit(solution)/shard_map/ppermute | solution.py:600
  15.9 3.2 %collective-permute-start.5 = (f32[8,256]{1,0:T(8,128)S(1)}, f32[8,256]{1,0:T(8,128)S(1)}, u32[]{:S(2)}, u32[]{:S(2)}) collective-permute-start(f32[8,256]{1,0:T(8,128)S(1)} %get-tuple-element.76), channel_id=1, source_target_pairs={{0,1},{1,0},{2,3},{3,2},{4,5},{5,4},{6,7},{7,6},{8,9},{9,8},{10,11... | collective-permute-start | bytes 24584 | tf_op jit(solution)/shard_map/ppermute | solution.py:604
  19.2 1.1 %shard_map.109 = (f32[4,8,128]{2,1,0:T(8,128)S(1)}, f32[8,128]{1,0:T(8,128)S(1)}, f32[8,1280]{1,0:T(8,128)S(1)}, f32[24,8,128]{2,1,0:T(8,128)S(1)}) custom-call(f32[8,1280]{1,0:T(8,128)S(1)} %get-tuple-element.62.own, f32[8,512]{1,0:T(8,128)S(1)} %get-tuple-element.67.delta, f32[8,128]{1,0:T(8,128)S(1)} %get-tuple-element.68.forms, ...), custom_call_target="tpu_custom_call" | custom-call | flops 4000000 | bytes 4000000 | tf_op jit(solution)/shard_map/pallas_call | solution.py:584
  20.3 0.5 %shard_map.110 = (f32[4,8,128]{2,1,0:T(8,128)S(1)}, f32[8,128]{1,0:T(8,128)S(1)}) custom-call(f32[8,1280]{1,0:T(8,128)S(1)} %get-tuple-element.74.own, s32[8,256]{1,0:T(8,128)S(1)} %get-tuple-element.45.order_ref, s32[8,256]{1,0:T(8,128)S(1)} %get-tuple-element.66.rest_0_.inverse_in, f32[8,256]{1,0:T(8,128)S(1)} %collective-permute-done.4.across_in, ...), custom_call_target="tpu_custom_call" | custom-call | tf_op jit(solution)/shard_map/pallas_call | solution.py:584
  21.0 1.0 %collective-permute-done.6 = f32[8,128]{1,0:T(8,128)S(1)} collective-permute-done((f32[8,128]{1,0:T(8,128)S(1)}, f32[8,128]{1,0:T(8,128)S(1)}, u32[]{:S(2)}, u32[]{:S(2)}) %collective-permute-start.6) | collective-permute-done | bytes 4128 | tf_op jit(solution)/shard_map/ppermute | solution.py:604
  22.0 3.3 %collective-permute-start.9 = (f32[16,128]{1,0:T(8,128)S(1)}, f32[16,128]{1,0:T(8,128)S(1)}, u32[]{:S(2)}, u32[]{:S(2)}) collective-permute-start(f32[16,128]{1,0:T(8,128)S(1)} %constant_dynamic-update-slice_fusion.refs_0_), channel_id=1, source_target_pairs={{0,2},{1,3},{2,0},{3,1},{4,6},{5,7},{6,4},{7,5},{8,10},{9,11},{10,... | collective-permute-start | bytes 24584 | tf_op jit(solution)/shard_map/ppermute | solution.py:619
  25.2 0.5 %collective-permute-start.8 = (f32[16,128]{1,0:T(8,128)S(1)}, f32[16,128]{1,0:T(8,128)S(1)}, u32[]{:S(2)}, u32[]{:S(2)}) collective-permute-start(f32[16,128]{1,0:T(8,128)S(1)} %constant_dynamic-update-slice_fusion.refs_0_), channel_id=1, source_target_pairs={{0,4},{1,5},{2,6},{3,7},{4,0},{5,1},{6,2},{7,3},{8,12},{9,13},{10,... | collective-permute-start | bytes 24584 | tf_op jit(solution)/shard_map/ppermute | solution.py:619
  25.7 1.5 %collective-permute-start.7 = (f32[16,128]{1,0:T(8,128)S(1)}, f32[16,128]{1,0:T(8,128)S(1)}, u32[]{:S(2)}, u32[]{:S(2)}) collective-permute-start(f32[16,128]{1,0:T(8,128)S(1)} %constant_dynamic-update-slice_fusion.refs_0_), channel_id=1, source_target_pairs={{0,6},{1,7},{2,4},{3,5},{4,2},{5,3},{6,0},{7,1},{8,14},{9,15},{10,... | collective-permute-start | bytes 24584 | tf_op jit(solution)/shard_map/ppermute | solution.py:619
  27.2 1.7 %collective-permute-done.8.refs_2_ = f32[16,128]{1,0:T(8,128)S(1)} collective-permute-done((f32[16,128]{1,0:T(8,128)S(1)}, f32[16,128]{1,0:T(8,128)S(1)}, u32[]{:S(2)}, u32[]{:S(2)}) %collective-permute-start.8) | collective-permute-done | bytes 8224 | tf_op jit(solution)/shard_map/ppermute | solution.py:619
  28.9 1.4 %collective-permute-done.7.refs_1_ = f32[16,128]{1,0:T(8,128)S(1)} collective-permute-done((f32[16,128]{1,0:T(8,128)S(1)}, f32[16,128]{1,0:T(8,128)S(1)}, u32[]{:S(2)}, u32[]{:S(2)}) %collective-permute-start.7) | collective-permute-done | bytes 8224 | tf_op jit(solution)/shard_map/ppermute | solution.py:619
  30.4 2.7 %collective-permute-start.10 = (f32[8,128]{1,0:T(8,128)S(1)}, f32[8,128]{1,0:T(8,128)S(1)}, u32[]{:S(2)}, u32[]{:S(2)}) collective-permute-start(f32[8,128]{1,0:T(8,128)S(1)} %shard_map.111), channel_id=1, source_target_pairs={{0,16},{8,24},{16,0},{24,8},{1,17},{9,25},{17,1},{25,9},{2,18},{10... | collective-permute-start | bytes 12296 | tf_op jit(solution)/shard_map/ppermute | solution.py:630
  33.1 1.9 %collective-permute-done.10 = f32[8,128]{1,0:T(8,128)S(1)} collective-permute-done((f32[8,128]{1,0:T(8,128)S(1)}, f32[8,128]{1,0:T(8,128)S(1)}, u32[]{:S(2)}, u32[]{:S(2)}) %collective-permute-start.10) | collective-permute-done | bytes 4128 | tf_op jit(solution)/shard_map/ppermute | solution.py:630
  35.0 1.6 %collective-permute-start.11 = (f32[8,128]{1,0:T(8,128)S(1)}, f32[8,128]{1,0:T(8,128)S(1)}, u32[]{:S(2)}, u32[]{:S(2)}) collective-permute-start(f32[8,128]{1,0:T(8,128)S(1)} %add.6), channel_id=1, source_target_pairs={{0,8},{8,0},{16,24},{24,16},{1,9},{9,1},{17,25},{25,17},{2,10},{10... | collective-permute-start | bytes 12296 | tf_op jit(solution)/shard_map/ppermute | solution.py:630
  36.6 2.0 %collective-permute-done.11 = f32[8,128]{1,0:T(8,128)S(1)} collective-permute-done((f32[8,128]{1,0:T(8,128)S(1)}, f32[8,128]{1,0:T(8,128)S(1)}, u32[]{:S(2)}, u32[]{:S(2)}) %collective-permute-start.11) | collective-permute-done | bytes 4128 | tf_op jit(solution)/shard_map/ppermute | solution.py:630
  38.6 0.6 %exponential_multiply_fusion = f32[1,1024]{1,0:T(1,128)} fusion(f32[1,1024]{1,0:T(1,128)S(1)} %bitcast.9, f32[1,1024]{1,0:T(1,128)S(1)} %bitcast.15), kind=kLoop, calls=%fused_computation.2 | loop fusion | flops 2048 | bytes 12288 | tf_op jit(solution)/shard_map/mul | solution.py:750
  (16 shorter events, 0.3 us)
Async XLA Ops:
  1.4 7.0 %collective-permute-start = (f32[8,256]{1,0:T(8,128)S(1)}, f32[8,256]{1,0:T(8,128)S(1)}, u32[]{:S(2)}, u32[]{:S(2)}) collective-permute-start(f32[8,256]{1,0:T(8,128)S(1)} %get-tuple-element.46), channel_id=1, source_target_pairs={{0,0},{7,7},{1,2},{2,1},{3,4},{4,3},{5,6},{6,5},{8,8},{15,15},{9,1... | collective-permute-start | bytes 24584 | tf_op jit(solution)/shard_map/ppermute | solution.py:600
  2.1 6.3 %collective-permute-start.1 = (f32[8,256]{1,0:T(8,128)S(1)}, f32[8,256]{1,0:T(8,128)S(1)}, u32[]{:S(2)}, u32[]{:S(2)}) collective-permute-start(f32[8,256]{1,0:T(8,128)S(1)} %get-tuple-element.47), channel_id=1, source_target_pairs={{0,1},{1,0},{2,3},{3,2},{4,5},{5,4},{6,7},{7,6},{8,9},{9,8},{10,11... | collective-permute-start | bytes 24584 | tf_op jit(solution)/shard_map/ppermute | solution.py:604
  9.4 4.8 %collective-permute-start.2 = (f32[8,256]{1,0:T(8,128)S(1)}, f32[8,256]{1,0:T(8,128)S(1)}, u32[]{:S(2)}, u32[]{:S(2)}) collective-permute-start(f32[8,256]{1,0:T(8,128)S(1)} %get-tuple-element.63), channel_id=1, source_target_pairs={{0,0},{7,7},{1,2},{2,1},{3,4},{4,3},{5,6},{6,5},{8,8},{15,15},{9,1... | collective-permute-start | bytes 24584 | tf_op jit(solution)/shard_map/ppermute | solution.py:600
  10.2 4.1 %collective-permute-start.3 = (f32[8,256]{1,0:T(8,128)S(1)}, f32[8,256]{1,0:T(8,128)S(1)}, u32[]{:S(2)}, u32[]{:S(2)}) collective-permute-start(f32[8,256]{1,0:T(8,128)S(1)} %get-tuple-element.64), channel_id=1, source_target_pairs={{0,1},{1,0},{2,3},{3,2},{4,5},{5,4},{6,7},{7,6},{8,9},{9,8},{10,11... | collective-permute-start | bytes 24584 | tf_op jit(solution)/shard_map/ppermute | solution.py:604
  15.3 5.0 %collective-permute-start.4 = (f32[8,256]{1,0:T(8,128)S(1)}, f32[8,256]{1,0:T(8,128)S(1)}, u32[]{:S(2)}, u32[]{:S(2)}) collective-permute-start(f32[8,256]{1,0:T(8,128)S(1)} %get-tuple-element.75), channel_id=1, source_target_pairs={{0,0},{7,7},{1,2},{2,1},{3,4},{4,3},{5,6},{6,5},{8,8},{15,15},{9,1... | collective-permute-start | bytes 24584 | tf_op jit(solution)/shard_map/ppermute | solution.py:600
  15.9 4.3 %collective-permute-start.5 = (f32[8,256]{1,0:T(8,128)S(1)}, f32[8,256]{1,0:T(8,128)S(1)}, u32[]{:S(2)}, u32[]{:S(2)}) collective-permute-start(f32[8,256]{1,0:T(8,128)S(1)} %get-tuple-element.76), channel_id=1, source_target_pairs={{0,1},{1,0},{2,3},{3,2},{4,5},{5,4},{6,7},{7,6},{8,9},{9,8},{10,11... | collective-permute-start | bytes 24584 | tf_op jit(solution)/shard_map/ppermute | solution.py:604
  20.8 1.2 %collective-permute-start.6 = (f32[8,128]{1,0:T(8,128)S(1)}, f32[8,128]{1,0:T(8,128)S(1)}, u32[]{:S(2)}, u32[]{:S(2)}) collective-permute-start(f32[8,128]{1,0:T(8,128)S(1)} %get-tuple-element.79.refs_4_), channel_id=1, source_target_pairs={{0,1},{1,0},{2,3},{3,2},{4,5},{5,4},{6,7},{7,6},{8,9},{9,8},{10,11... | collective-permute-start | bytes 12296 | tf_op jit(solution)/shard_map/ppermute | solution.py:604
  22.0 5.2 %collective-permute-start.9 = (f32[16,128]{1,0:T(8,128)S(1)}, f32[16,128]{1,0:T(8,128)S(1)}, u32[]{:S(2)}, u32[]{:S(2)}) collective-permute-start(f32[16,128]{1,0:T(8,128)S(1)} %constant_dynamic-update-slice_fusion.refs_0_), channel_id=1, source_target_pairs={{0,2},{1,3},{2,0},{3,1},{4,6},{5,7},{6,4},{7,5},{8,10},{9,11},{10,... | collective-permute-start | bytes 24584 | tf_op jit(solution)/shard_map/ppermute | solution.py:619
  25.2 3.7 %collective-permute-start.8 = (f32[16,128]{1,0:T(8,128)S(1)}, f32[16,128]{1,0:T(8,128)S(1)}, u32[]{:S(2)}, u32[]{:S(2)}) collective-permute-start(f32[16,128]{1,0:T(8,128)S(1)} %constant_dynamic-update-slice_fusion.refs_0_), channel_id=1, source_target_pairs={{0,4},{1,5},{2,6},{3,7},{4,0},{5,1},{6,2},{7,3},{8,12},{9,13},{10,... | collective-permute-start | bytes 24584 | tf_op jit(solution)/shard_map/ppermute | solution.py:619
  25.7 4.5 %collective-permute-start.7 = (f32[16,128]{1,0:T(8,128)S(1)}, f32[16,128]{1,0:T(8,128)S(1)}, u32[]{:S(2)}, u32[]{:S(2)}) collective-permute-start(f32[16,128]{1,0:T(8,128)S(1)} %constant_dynamic-update-slice_fusion.refs_0_), channel_id=1, source_target_pairs={{0,6},{1,7},{2,4},{3,5},{4,2},{5,3},{6,0},{7,1},{8,14},{9,15},{10,... | collective-permute-start | bytes 24584 | tf_op jit(solution)/shard_map/ppermute | solution.py:619
  30.4 4.6 %collective-permute-start.10 = (f32[8,128]{1,0:T(8,128)S(1)}, f32[8,128]{1,0:T(8,128)S(1)}, u32[]{:S(2)}, u32[]{:S(2)}) collective-permute-start(f32[8,128]{1,0:T(8,128)S(1)} %shard_map.111), channel_id=1, source_target_pairs={{0,16},{8,24},{16,0},{24,8},{1,17},{9,25},{17,1},{25,9},{2,18},{10... | collective-permute-start | bytes 12296 | tf_op jit(solution)/shard_map/ppermute | solution.py:630
  35.0 3.6 %collective-permute-start.11 = (f32[8,128]{1,0:T(8,128)S(1)}, f32[8,128]{1,0:T(8,128)S(1)}, u32[]{:S(2)}, u32[]{:S(2)}) collective-permute-start(f32[8,128]{1,0:T(8,128)S(1)} %add.6), channel_id=1, source_target_pairs={{0,8},{8,0},{16,24},{24,16},{1,9},{9,1},{17,25},{25,17},{2,10},{10... | collective-permute-start | bytes 12296 | tf_op jit(solution)/shard_map/ppermute | solution.py:630
  38.6 0.6 %copy-start = (f32[8,128]{1,0:T(8,128)}, f32[8,128]{1,0:T(8,128)S(1)}, u32[]{:S(2)}) copy-start(f32[8,128]{1,0:T(8,128)S(1)} %add.7) | copy-start | bytes 12292

commit v14 on v11

--- a/solution.py
+++ b/solution.py
@@ -99,7 +99,11 @@
 
 def take_rims(across_ref, beside_ref):
     even = is_even()
-    pairs = list(zip(cut(across_ref), cut(beside_ref)))
+    device = lax.axis_index("dom")
+    outermost = (device == 0) | (device == lax.axis_size("dom") - 1)
+    pairs = [
+        (jnp.where(outermost, 0.0, a), b) for a, b in zip(cut(across_ref), cut(beside_ref))
+    ]
     prior = [jnp.where(even, a, b) for a, b in pairs]
     above = [jnp.where(even, b, a) for a, b in pairs]
     return prior, above
@@ -595,12 +599,17 @@
     )(*arguments)
 
 
-def swap(block, axis, offset):
-    size = lax.axis_size(axis)
+def swap_across(block):
+    size = lax.axis_size("dom")
     route = []
-    for low in range(offset, size - 1, 2):
-        route += [(low, low + 1), (low + 1, low)]
-    return lax.ppermute(block, axis, route)
+    for low in range(1, size, 2):
+        high = (low + 1) % size
+        route += [(low, high), (high, low)]
+    return lax.ppermute(block, "dom", route)
+
+
+def swap_beside(block):
+    return lax.ppermute(block, "dom", [(i, i ^ 1) for i in range(lax.axis_size("dom"))])
 
 
 def gather_all(block, axis):
@@ -611,10 +620,13 @@
 
 def sum_over_freq(block):
     size, width = lax.axis_size("freq"), lax.axis_size("dom")
-    places = range(1, width, 2)
     step = size // 2
     while step > 0:
-        route = [(f * width + p, (f ^ step) * width + p) for f in range(size) for p in places]
+        route = []
+        for f in range(size):
+            for p in range(width):
+                there = (f ^ step) * width + p if p % 2 else f * width + (p ^ 2)
+                route.append((f * width + p, there))
         block = block + lax.ppermute(block, ("freq", "dom"), route)
         step //= 2
     return block
@@ -664,7 +676,7 @@
         ),
         space=HBM,
     )
-    across, beside = swap(across, "dom", 1), swap(beside, "dom", 0)
+    across, beside = swap_across(across), swap_beside(beside)
     kept = [jax.ShapeDtypeStruct(x.shape, x.dtype) for x in (mass, sigma, live, edges, forward)]
     places, blocks, scale, picks, own, rates, mass, sigma, live, edges, forward = call(
         table_stage,
@@ -708,7 +720,7 @@
         else:
             outs = call(front, (*given, inverse), front_shapes)
         delta, picks, pieces, forms, rims, across, beside = outs
-        across, beside = swap(across, "dom", 1), swap(beside, "dom", 0)
+        across, beside = swap_across(across), swap_beside(beside)
         given = (own, delta, forms, *arrived, sums, picks, pieces, rims, edges, places)
         back = functools.partial(back_stage, polars, step)
         if step == 0:
@@ -729,11 +741,11 @@
     )
     both = call(
         combine_stage,
-        (gather_all(sums, "dom"), terms, swap(terms, "dom", 0)),
+        (gather_all(sums, "dom"), terms, swap_beside(terms)),
         shape(2, tall, LANES),
     )
     both = sum_over_freq(both)
-    returned = swap(both[1], "dom", 0)
+    returned = swap_beside(both[1])
     odd = lax.rem(lax.axis_index("dom"), 2) == 1
     gradient = jnp.where(odd, both[0], returned).reshape(1, slots)
     updated = sigma.reshape(1, slots) * jnp.exp(-0.5 * jnp.tanh(gradient))

time: 41.9 us -> 35.2 us (0.84)
  starting transfers between devices: 22.1 us -> 8.69 us
  waiting for transfers between devices: 0.85 us -> 9.1 us
  blocking collectives: 9.63 us -> 8.24 us
    ppermute x8, starting transfers between devices: 20.7 us -> 7.5 us  [the longest x3 7.49 us: swap_across(): return lax.ppermute(block, 'dom', route)]
    ppermute x2, waiting for transfers between devices: 0.01 us -> 6.18 us  [sum_over_freq(): block = block + lax.ppermute(block, ('freq', 'dom'), route)]
    ppermute x8, waiting for transfers between devices: 0.84 us -> 2.92 us  [the longest x3 1.75 us: swap_across(): return lax.ppermute(block, 'dom', route)]
    all_to_all x1, blocking collectives: 9.63 us -> 8.24 us  [gather_all(): return lax.all_to_all(copies, axis, 0, 0)]
  transfers between devices with their start and end apart: 10 -> 10, of which waited for: 1 -> 5; matrix products, arithmetic and copies ran while one was open for 0% -> 0% of each run, Pallas kernels for 10% -> 12%
where the time goes in v14:
time: 35.2 us; the launch traced here: 35 us
  waiting for transfers between devices  9.1 us (26%)
  starting transfers between devices  8.69 us (25%)
  blocking collectives  8.24 us (23%)
  Pallas kernels  7.64 us (22%)
  between operations  0.71 us (2%)
  other arithmetic  0.62 us (2%)
    all_to_all x1, blocking collectives, gather_all(): return lax.all_to_all(copies, axis, 0, 0)  8.24 us
    pallas_call x8, Pallas kernels, call(): pl.pallas_call(kernel, out_shape=outs, in_specs=space if isinstance(space...  7.64 us
    ppermute x3, starting transfers between devices, swap_across(): return lax.ppermute(block, 'dom', route)  7.49 us
    ppermute x2, waiting for transfers between devices, sum_over_freq(): block = block + lax.ppermute(block, ('freq', 'dom'), route)  6.18 us
    ppermute x3, waiting for transfers between devices, swap_across(): return lax.ppermute(block, 'dom', route)  1.75 us
    ppermute x2, starting transfers between devices, sum_over_freq(): block = block + lax.ppermute(block, ('freq', 'dom'), route)  1.19 us
    ppermute x5, waiting for transfers between devices, swap_beside(): lax.ppermute(block, 'dom', [(i, i ^ 1) for i in range(lax.axis_size('dom'...  1.17 us
  transfers between devices with their start and end apart: 10, of which 5 were waited for; matrix products, arithmetic and copies ran while one was open for 0% of the time, Pallas kernels for 12%

profile of v14, /device:TPU:0, one launch (start us, length us, event | category | flops | bytes accessed | tf_op | source)
XLA Modules:
  0.0 35.0 jit_solution(16276396924943025680)
XLA Ops:
  0.6 0.8 %shard_map.104 = (f32[8,256]{1,0:T(8,128)S(1)}, f32[8,256]{1,0:T(8,128)S(1)}, f32[4,1,1280]{2,1,0:T(1,128)S(1)}, s32[8,256]{1,0:T(8,128)S(1)}) custom-call(f32[4,1,1280]{2,1,0:T(1,128)} %bitcast.20, s32[1,256]{1,0:T(1,128)} %order_in.1), custom_call_target="tpu_custom_call" | custom-call | tf_op jit(solution)/shard_map/pallas_call | solution.py:591
  1.4 3.4 %collective-permute-start = (f32[8,256]{1,0:T(8,128)S(1)}, f32[8,256]{1,0:T(8,128)S(1)}, u32[]{:S(2)}, u32[]{:S(2)}) collective-permute-start(f32[8,256]{1,0:T(8,128)S(1)} %get-tuple-element.46), channel_id=1, source_target_pairs={{1,2},{2,1},{3,4},{4,3},{5,6},{6,5},{7,0},{0,7},{9,10},{10,9},{11,... | collective-permute-start | bytes 24584 | tf_op jit(solution)/shard_map/ppermute | solution.py:608
  4.8 0.0 collective-permute-start.1
  4.8 1.9 %shard_map.105 = (bf16[128,6144]{1,0:T(8,128)(2,1)S(1)}, f32[72,8,128]{2,1,0:T(8,128)S(1)}, f32[8,128]{1,0:T(8,128)S(1)}, f32[24,8,128]{2,1,0:T(8,128)S(1)}, f32...) custom-call(f32[2]{0:T(128)} %angular_in.1, ...), custom_call_target="tpu_custom_call" | custom-call | flops 4000000 | bytes 4000000 | tf_op jit(solution)/shard_map/pallas_call | solution.py:591
  6.7 0.0 collective-permute-done.across_in
  6.8 1.0 %shard_map.106 = (s32[8,256]{1,0:T(8,128)S(1)}, f32[8,512]{1,0:T(8,128)S(1)}, f32[24,8,128]{2,1,0:T(8,128)S(1)}, f32[384,128]{1,0:T(8,128)S(1)}, f32[8,128]{1,0:...) custom-call(s32[8,256]{1,0:T(8,128)S(1)} %get-tuple-element.45.order_ref, ...), custom_call_target="tpu_custom_call" | custom-call | tf_op jit(solution)/shard_map/pallas_call | solution.py:591
  7.8 2.1 %collective-permute-start.2 = (f32[8,256]{1,0:T(8,128)S(1)}, f32[8,256]{1,0:T(8,128)S(1)}, u32[]{:S(2)}, u32[]{:S(2)}) collective-permute-start(f32[8,256]{1,0:T(8,128)S(1)} %get-tuple-element.63), channel_id=1, source_target_pairs={{1,2},{2,1},{3,4},{4,3},{5,6},{6,5},{7,0},{0,7},{9,10},{10,9},{11,... | collective-permute-start | bytes 24584 | tf_op jit(solution)/shard_map/ppermute | solution.py:608
  9.9 0.0 collective-permute-start.3
  9.9 1.2 %shard_map.107 = (f32[24,8,128]{2,1,0:T(8,128)S(1)}, f32[4,8,128]{2,1,0:T(8,128)S(1)}, f32[8,128]{1,0:T(8,128)S(1)}, f32[8,1280]{1,0:T(8,128)S(1)}, f32[24,8,128]{2,1,0:T(8,128)S(1)}) custom-call(f32[8,1280]{1,0:T(8,128)S(1)} %get-tuple-element.44.own, f32[8,512]{1,0:T(8,128)S(1)} %get-tuple-element.53.delta, f32[8,128]{1,0:T(8,128)S(1)} %get-tuple-element.54.forms, ...), custom_call_target="tpu_custom_call" | custom-call | flops 4000000 | bytes 4000000 | tf_op jit(solution)/shard_map/pallas_call | solution.py:591
  11.1 0.8 %collective-permute-done.2.across_in = f32[8,256]{1,0:T(8,128)S(1)} collective-permute-done((f32[8,256]{1,0:T(8,128)S(1)}, f32[8,256]{1,0:T(8,128)S(1)}, u32[]{:S(2)}, u32[]{:S(2)}) %collective-permute-start.2) | collective-permute-done | bytes 8224 | tf_op jit(solution)/shard_map/ppermute | solution.py:608
  11.9 1.0 %shard_map.108 = (f32[8,512]{1,0:T(8,128)S(1)}, f32[24,8,128]{2,1,0:T(8,128)S(1)}, f32[384,128]{1,0:T(8,128)S(1)}, f32[8,128]{1,0:T(8,128)S(1)}, f32[8,512]{1,0:...) custom-call(s32[8,256]{1,0:T(8,128)S(1)} %get-tuple-element.45.order_ref, ...), custom_call_target="tpu_custom_call" | custom-call | tf_op jit(solution)/shard_map/pallas_call | solution.py:591
  12.9 2.0 %collective-permute-start.4 = (f32[8,256]{1,0:T(8,128)S(1)}, f32[8,256]{1,0:T(8,128)S(1)}, u32[]{:S(2)}, u32[]{:S(2)}) collective-permute-start(f32[8,256]{1,0:T(8,128)S(1)} %get-tuple-element.75), channel_id=1, source_target_pairs={{1,2},{2,1},{3,4},{4,3},{5,6},{6,5},{7,0},{0,7},{9,10},{10,9},{11,... | collective-permute-start | bytes 24584 | tf_op jit(solution)/shard_map/ppermute | solution.py:608
  14.9 1.1 %shard_map.109 = (f32[4,8,128]{2,1,0:T(8,128)S(1)}, f32[8,128]{1,0:T(8,128)S(1)}, f32[8,1280]{1,0:T(8,128)S(1)}, f32[24,8,128]{2,1,0:T(8,128)S(1)}) custom-call(f32[8,1280]{1,0:T(8,128)S(1)} %get-tuple-element.62.own, f32[8,512]{1,0:T(8,128)S(1)} %get-tuple-element.67.delta, f32[8,128]{1,0:T(8,128)S(1)} %get-tuple-element.68.forms, ...), custom_call_target="tpu_custom_call" | custom-call | flops 4000000 | bytes 4000000 | tf_op jit(solution)/shard_map/pallas_call | solution.py:591
  16.0 0.9 %collective-permute-done.4.across_in = f32[8,256]{1,0:T(8,128)S(1)} collective-permute-done((f32[8,256]{1,0:T(8,128)S(1)}, f32[8,256]{1,0:T(8,128)S(1)}, u32[]{:S(2)}, u32[]{:S(2)}) %collective-permute-start.4) | collective-permute-done | bytes 8224 | tf_op jit(solution)/shard_map/ppermute | solution.py:608
  16.9 0.5 %shard_map.110 = (f32[13,8,128]{2,1,0:T(8,128)S(1)}, f32[8,128]{1,0:T(8,128)S(1)}) custom-call(f32[8,1280]{1,0:T(8,128)S(1)} %get-tuple-element.74.own, s32[8,256]{1,0:T(8,128)S(1)} %get-tuple-element.45.order_ref, s32[8,256]{1,0:T(8,128)S(1)} %get-tuple-element.66.rest_0_.inverse_in, f32[8,256]{1,0:T(8,128)S(1)} %collective-permute-done.4.across_in, ...), custom_call_target="tpu_custom_call" | custom-call | tf_op jit(solution)/shard_map/pallas_call | solution.py:591
  17.4 0.0 collective-permute-start.6
  17.5 8.2 %all_to_all.5.everyone = f32[8,8,128]{2,1,0:T(8,128)S(1)} all-to-all(f32[8,8,128]{2,1,0:T(8,128)S(1)} %broadcast_in_dim.10), channel_id=1, replica_groups=mesh['freq'=4,'dom'=8] {'dom'}, dimensions={0} | all-to-all | bytes 65536 | tf_op jit(solution)/shard_map/all_to_all | solution.py:618
  25.7 0.1 shard_map.111
  25.8 0.6 %collective-permute-start.7 = (f32[2,8,128]{2,1,0:T(8,128)S(1)}, f32[2,8,128]{2,1,0:T(8,128)S(1)}, u32[]{:S(2)}, u32[]{:S(2)}) collective-permute-start(f32[2,8,128]{2,1,0:T(8,128)S(1)} %shard_map.111), channel_id=1, source_target_pairs={{0,2},{1,17},{2,0},{3,19},{4,6},{5,21},{6,4},{7,23},{8,10},{9,25},... | collective-permute-start | bytes 24584 | tf_op jit(solution)/shard_map/ppermute | solution.py:630
  26.5 3.1 %collective-permute-done.7 = f32[2,8,128]{2,1,0:T(8,128)S(1)} collective-permute-done((f32[2,8,128]{2,1,0:T(8,128)S(1)}, f32[2,8,128]{2,1,0:T(8,128)S(1)}, u32[]{:S(2)}, u32[]{:S(2)}) %collective-permute-start.7) | collective-permute-done | bytes 8224 | tf_op jit(solution)/shard_map/ppermute | solution.py:630
  29.6 0.6 %collective-permute-start.8 = (f32[2,8,128]{2,1,0:T(8,128)S(1)}, f32[2,8,128]{2,1,0:T(8,128)S(1)}, u32[]{:S(2)}, u32[]{:S(2)}) collective-permute-start(f32[2,8,128]{2,1,0:T(8,128)S(1)} %add.6), channel_id=1, source_target_pairs={{0,2},{1,9},{2,0},{3,11},{4,6},{5,13},{6,4},{7,15},{8,10},{9,1},{1... | collective-permute-start | bytes 24584 | tf_op jit(solution)/shard_map/ppermute | solution.py:630
  30.1 3.1 %collective-permute-done.8 = f32[2,8,128]{2,1,0:T(8,128)S(1)} collective-permute-done((f32[2,8,128]{2,1,0:T(8,128)S(1)}, f32[2,8,128]{2,1,0:T(8,128)S(1)}, u32[]{:S(2)}, u32[]{:S(2)}) %collective-permute-start.8) | collective-permute-done | bytes 8224 | tf_op jit(solution)/shard_map/ppermute | solution.py:630
  33.2 1.2 %collective-permute-done.9 = f32[8,128]{1,0:T(8,128)S(1)} collective-permute-done((f32[8,128]{1,0:T(8,128)S(1)}, f32[8,128]{1,0:T(8,128)S(1)}, u32[]{:S(2)}, u32[]{:S(2)}) %collective-permute-start.9) | collective-permute-done | bytes 4128 | tf_op jit(solution)/shard_map/ppermute | solution.py:612
  34.4 0.6 %exponential_multiply_fusion = f32[1,1024]{1,0:T(1,128)} fusion(f32[1,1024]{1,0:T(1,128)S(1)} %bitcast.15, f32[1,1024]{1,0:T(1,128)S(1)} %bitcast.21), kind=kLoop, calls=%fused_computation.3 | loop fusion | flops 2048 | bytes 12288 | tf_op jit(solution)/shard_map/mul | solution.py:751
  (14 shorter events, 0.0 us)
Async XLA Ops:
  1.4 5.4 %collective-permute-start = (f32[8,256]{1,0:T(8,128)S(1)}, f32[8,256]{1,0:T(8,128)S(1)}, u32[]{:S(2)}, u32[]{:S(2)}) collective-permute-start(f32[8,256]{1,0:T(8,128)S(1)} %get-tuple-element.46), channel_id=1, source_target_pairs={{1,2},{2,1},{3,4},{4,3},{5,6},{6,5},{7,0},{0,7},{9,10},{10,9},{11,... | collective-permute-start | bytes 24584 | tf_op jit(solution)/shard_map/ppermute | solution.py:608
  4.8 2.0 %collective-permute-start.1 = (f32[8,256]{1,0:T(8,128)S(1)}, f32[8,256]{1,0:T(8,128)S(1)}, u32[]{:S(2)}, u32[]{:S(2)}) collective-permute-start(f32[8,256]{1,0:T(8,128)S(1)} %get-tuple-element.47), channel_id=1, source_target_pairs={{0,1},{1,0},{2,3},{3,2},{4,5},{5,4},{6,7},{7,6},{8,9},{9,8},{10,11... | collective-permute-start | bytes 24584 | tf_op jit(solution)/shard_map/ppermute | solution.py:612
  7.8 4.1 %collective-permute-start.2 = (f32[8,256]{1,0:T(8,128)S(1)}, f32[8,256]{1,0:T(8,128)S(1)}, u32[]{:S(2)}, u32[]{:S(2)}) collective-permute-start(f32[8,256]{1,0:T(8,128)S(1)} %get-tuple-element.63), channel_id=1, source_target_pairs={{1,2},{2,1},{3,4},{4,3},{5,6},{6,5},{7,0},{0,7},{9,10},{10,9},{11,... | collective-permute-start | bytes 24584 | tf_op jit(solution)/shard_map/ppermute | solution.py:608
  9.9 2.0 %collective-permute-start.3 = (f32[8,256]{1,0:T(8,128)S(1)}, f32[8,256]{1,0:T(8,128)S(1)}, u32[]{:S(2)}, u32[]{:S(2)}) collective-permute-start(f32[8,256]{1,0:T(8,128)S(1)} %get-tuple-element.64), channel_id=1, source_target_pairs={{0,1},{1,0},{2,3},{3,2},{4,5},{5,4},{6,7},{7,6},{8,9},{9,8},{10,11... | collective-permute-start | bytes 24584 | tf_op jit(solution)/shard_map/ppermute | solution.py:612
  12.9 4.0 %collective-permute-start.4 = (f32[8,256]{1,0:T(8,128)S(1)}, f32[8,256]{1,0:T(8,128)S(1)}, u32[]{:S(2)}, u32[]{:S(2)}) collective-permute-start(f32[8,256]{1,0:T(8,128)S(1)} %get-tuple-element.75), channel_id=1, source_target_pairs={{1,2},{2,1},{3,4},{4,3},{5,6},{6,5},{7,0},{0,7},{9,10},{10,9},{11,... | collective-permute-start | bytes 24584 | tf_op jit(solution)/shard_map/ppermute | solution.py:608
  14.9 2.0 %collective-permute-start.5 = (f32[8,256]{1,0:T(8,128)S(1)}, f32[8,256]{1,0:T(8,128)S(1)}, u32[]{:S(2)}, u32[]{:S(2)}) collective-permute-start(f32[8,256]{1,0:T(8,128)S(1)} %get-tuple-element.76), channel_id=1, source_target_pairs={{0,1},{1,0},{2,3},{3,2},{4,5},{5,4},{6,7},{7,6},{8,9},{9,8},{10,11... | collective-permute-start | bytes 24584 | tf_op jit(solution)/shard_map/ppermute | solution.py:612
  17.4 8.3 %collective-permute-start.6 = (f32[13,8,128]{2,1,0:T(8,128)S(1)}, f32[13,8,128]{2,1,0:T(8,128)S(1)}, u32[]{:S(2)}, u32[]{:S(2)}) collective-permute-start(f32[13,8,128]{2,1,0:T(8,128)S(1)} %get-tuple-element.82.own), channel_id=1, source_target_pairs={{0,1},{1,0},{2,3},{3,2},{4,5},{5,4},{6,7},{7,6},{8,9},{9,8},{10,11... | collective-permute-start | bytes 159752 | tf_op jit(solution)/shard_map/ppermute | solution.py:612
  25.8 3.7 %collective-permute-start.7 = (f32[2,8,128]{2,1,0:T(8,128)S(1)}, f32[2,8,128]{2,1,0:T(8,128)S(1)}, u32[]{:S(2)}, u32[]{:S(2)}) collective-permute-start(f32[2,8,128]{2,1,0:T(8,128)S(1)} %shard_map.111), channel_id=1, source_target_pairs={{0,2},{1,17},{2,0},{3,19},{4,6},{5,21},{6,4},{7,23},{8,10},{9,25},... | collective-permute-start | bytes 24584 | tf_op jit(solution)/shard_map/ppermute | solution.py:630
  29.6 3.7 %collective-permute-start.8 = (f32[2,8,128]{2,1,0:T(8,128)S(1)}, f32[2,8,128]{2,1,0:T(8,128)S(1)}, u32[]{:S(2)}, u32[]{:S(2)}) collective-permute-start(f32[2,8,128]{2,1,0:T(8,128)S(1)} %add.6), channel_id=1, source_target_pairs={{0,2},{1,9},{2,0},{3,11},{4,6},{5,13},{6,4},{7,15},{8,10},{9,1},{1... | collective-permute-start | bytes 24584 | tf_op jit(solution)/shard_map/ppermute | solution.py:630
  33.2 1.2 %collective-permute-start.9 = (f32[8,128]{1,0:T(8,128)S(1)}, f32[8,128]{1,0:T(8,128)S(1)}, u32[]{:S(2)}, u32[]{:S(2)}) collective-permute-start(f32[8,128]{1,0:T(8,128)S(1)} %slice_bitcast_fusion), channel_id=1, source_target_pairs={{0,1},{1,0},{2,3},{3,2},{4,5},{5,4},{6,7},{7,6},{8,9},{9,8},{10,11... | collective-permute-start | bytes 12296 | tf_op jit(solution)/shard_map/ppermute | solution.py:612
  34.4 0.6 %copy-start = (f32[8,128]{1,0:T(8,128)}, f32[8,128]{1,0:T(8,128)S(1)}, u32[]{:S(2)}) copy-start(f32[8,128]{1,0:T(8,128)S(1)} %fusion) | copy-start | bytes 12292

commit v15 on v12

--- a/solution.py
+++ b/solution.py
@@ -590,12 +590,18 @@
 
 
 def swap_across(block):
-    size = lax.axis_size("dom")
+    size, planes = lax.axis_size("dom"), lax.axis_size("freq")
     route = []
-    for low in range(1, size, 2):
-        high = (low + 1) % size
-        route += [(low, high), (high, low)]
-    return lax.ppermute(block, "dom", route)
+    for f in range(planes):
+        for p in range(size):
+            if p in (0, size - 1) and planes % 2 == 0:
+                there = (f ^ 1) * size + p
+            elif p % 2:
+                there = f * size + (p + 1) % size
+            else:
+                there = f * size + (p - 1) % size
+            route.append((f * size + p, there))
+    return lax.ppermute(block, ("freq", "dom"), route)
 
 
 def swap_beside(block):

time: 34.5 us -> 34.1 us (0.988)
  starting transfers between devices: 11.7 us -> 10.8 us
  blocking collectives: 7.86 us -> 8.47 us
    ppermute x3, starting transfers between devices: 7.49 us -> 6.52 us  [swap_across(): return lax.ppermute(block, ('freq', 'dom'), route)]
    all_to_all x1, blocking collectives: 7.86 us -> 8.47 us  [gather_all(): return lax.all_to_all(copies, axis, 0, 0)]
where the time goes in v15:
time: 34.1 us; the launch traced here: 33.9 us
  starting transfers between devices  10.8 us (32%)
  blocking collectives  8.47 us (25%)
  Pallas kernels  7.64 us (22%)
  waiting for transfers between devices  5.67 us (17%)
  between operations  0.69 us (2%)
  other arithmetic  0.62 us (2%)
    all_to_all x1, blocking collectives, gather_all(): return lax.all_to_all(copies, axis, 0, 0)  8.47 us
    pallas_call x8, Pallas kernels, call(): pl.pallas_call(kernel, out_shape=outs, in_specs=space if isinstance(space...  7.64 us
    ppermute x3, starting transfers between devices, swap_across(): return lax.ppermute(block, ('freq', 'dom'), route)  6.52 us
    ppermute x2, starting transfers between devices, sum_over(): lax.ppermute(block, axis, [(i, i ^ step) for i in range(size)])  4.23 us
    ppermute x2, waiting for transfers between devices, sum_over(): lax.ppermute(block, axis, [(i, i ^ step) for i in range(size)])  3.94 us
    ppermute x3, waiting for transfers between devices, swap_across(): return lax.ppermute(block, ('freq', 'dom'), route)  1.71 us
  transfers between devices with their start and end apart: 8, of which 4 were waited for; matrix products, arithmetic and copies ran while one was open for 0% of the time, Pallas kernels for 12%

profile of v15, /device:TPU:0, one launch (start us, length us, event | category | flops | bytes accessed | tf_op | source)
XLA Modules:
  0.0 33.9 jit_solution(9327625512030825311)
XLA Ops:
  0.6 0.8 %shard_map.104 = (f32[8,256]{1,0:T(8,128)S(1)}, f32[8,256]{1,0:T(8,128)S(1)}, f32[4,1,1280]{2,1,0:T(1,128)S(1)}, s32[8,256]{1,0:T(8,128)S(1)}) custom-call(f32[4,1,1280]{2,1,0:T(1,128)} %bitcast.14, s32[1,256]{1,0:T(1,128)} %order_in.1), custom_call_target="tpu_custom_call" | custom-call | tf_op jit(solution)/shard_map/pallas_call | solution.py:581
  1.4 3.1 %collective-permute-start = (f32[8,256]{1,0:T(8,128)S(1)}, f32[8,256]{1,0:T(8,128)S(1)}, u32[]{:S(2)}, u32[]{:S(2)}) collective-permute-start(f32[8,256]{1,0:T(8,128)S(1)} %get-tuple-element.46), channel_id=1, source_target_pairs={{0,8},{1,2},{2,1},{3,4},{4,3},{5,6},{6,5},{7,15},{8,0},{9,10},{10,... | collective-permute-start | bytes 24584 | tf_op jit(solution)/shard_map/ppermute | solution.py:604
  4.5 0.0 collective-permute-start.1
  4.5 1.9 %shard_map.105 = (bf16[128,6144]{1,0:T(8,128)(2,1)S(1)}, f32[72,8,128]{2,1,0:T(8,128)S(1)}, f32[8,128]{1,0:T(8,128)S(1)}, f32[24,8,128]{2,1,0:T(8,128)S(1)}, f32...) custom-call(f32[2]{0:T(128)} %angular_in.1, ...), custom_call_target="tpu_custom_call" | custom-call | flops 4000000 | bytes 4000000 | tf_op jit(solution)/shard_map/pallas_call | solution.py:581
  6.5 0.0 collective-permute-done.across_in
  6.5 1.0 %shard_map.106 = (s32[8,256]{1,0:T(8,128)S(1)}, f32[8,512]{1,0:T(8,128)S(1)}, f32[24,8,128]{2,1,0:T(8,128)S(1)}, f32[384,128]{1,0:T(8,128)S(1)}, f32[8,128]{1,0:...) custom-call(s32[8,256]{1,0:T(8,128)S(1)} %get-tuple-element.45.order_ref, ...), custom_call_target="tpu_custom_call" | custom-call | tf_op jit(solution)/shard_map/pallas_call | solution.py:581
  7.5 1.7 %collective-permute-start.2 = (f32[8,256]{1,0:T(8,128)S(1)}, f32[8,256]{1,0:T(8,128)S(1)}, u32[]{:S(2)}, u32[]{:S(2)}) collective-permute-start(f32[8,256]{1,0:T(8,128)S(1)} %get-tuple-element.63), channel_id=1, source_target_pairs={{0,8},{1,2},{2,1},{3,4},{4,3},{5,6},{6,5},{7,15},{8,0},{9,10},{10,... | collective-permute-start | bytes 24584 | tf_op jit(solution)/shard_map/ppermute | solution.py:604
  9.3 0.0 collective-permute-start.3
  9.3 1.2 %shard_map.107 = (f32[24,8,128]{2,1,0:T(8,128)S(1)}, f32[4,8,128]{2,1,0:T(8,128)S(1)}, f32[8,128]{1,0:T(8,128)S(1)}, f32[8,1280]{1,0:T(8,128)S(1)}, f32[24,8,128]{2,1,0:T(8,128)S(1)}) custom-call(f32[8,1280]{1,0:T(8,128)S(1)} %get-tuple-element.44.own, f32[8,512]{1,0:T(8,128)S(1)} %get-tuple-element.53.delta, f32[8,128]{1,0:T(8,128)S(1)} %get-tuple-element.54.forms, ...), custom_call_target="tpu_custom_call" | custom-call | flops 4000000 | bytes 4000000 | tf_op jit(solution)/shard_map/pallas_call | solution.py:581
  10.4 0.8 %collective-permute-done.2.across_in = f32[8,256]{1,0:T(8,128)S(1)} collective-permute-done((f32[8,256]{1,0:T(8,128)S(1)}, f32[8,256]{1,0:T(8,128)S(1)}, u32[]{:S(2)}, u32[]{:S(2)}) %collective-permute-start.2) | collective-permute-done | bytes 8224 | tf_op jit(solution)/shard_map/ppermute | solution.py:604
  11.3 1.0 %shard_map.108 = (f32[8,512]{1,0:T(8,128)S(1)}, f32[24,8,128]{2,1,0:T(8,128)S(1)}, f32[384,128]{1,0:T(8,128)S(1)}, f32[8,128]{1,0:T(8,128)S(1)}, f32[8,512]{1,0:...) custom-call(s32[8,256]{1,0:T(8,128)S(1)} %get-tuple-element.45.order_ref, ...), custom_call_target="tpu_custom_call" | custom-call | tf_op jit(solution)/shard_map/pallas_call | solution.py:581
  12.3 1.7 %collective-permute-start.4 = (f32[8,256]{1,0:T(8,128)S(1)}, f32[8,256]{1,0:T(8,128)S(1)}, u32[]{:S(2)}, u32[]{:S(2)}) collective-permute-start(f32[8,256]{1,0:T(8,128)S(1)} %get-tuple-element.75), channel_id=1, source_target_pairs={{0,8},{1,2},{2,1},{3,4},{4,3},{5,6},{6,5},{7,15},{8,0},{9,10},{10,... | collective-permute-start | bytes 24584 | tf_op jit(solution)/shard_map/ppermute | solution.py:604
  14.0 0.0 collective-permute-start.5
  14.0 1.1 %shard_map.109 = (f32[4,8,128]{2,1,0:T(8,128)S(1)}, f32[8,128]{1,0:T(8,128)S(1)}, f32[8,1280]{1,0:T(8,128)S(1)}, f32[24,8,128]{2,1,0:T(8,128)S(1)}) custom-call(f32[8,1280]{1,0:T(8,128)S(1)} %get-tuple-element.62.own, f32[8,512]{1,0:T(8,128)S(1)} %get-tuple-element.67.delta, f32[8,128]{1,0:T(8,128)S(1)} %get-tuple-element.68.forms, ...), custom_call_target="tpu_custom_call" | custom-call | flops 4000000 | bytes 4000000 | tf_op jit(solution)/shard_map/pallas_call | solution.py:581
  15.1 0.9 %collective-permute-done.4.across_in = f32[8,256]{1,0:T(8,128)S(1)} collective-permute-done((f32[8,256]{1,0:T(8,128)S(1)}, f32[8,256]{1,0:T(8,128)S(1)}, u32[]{:S(2)}, u32[]{:S(2)}) %collective-permute-start.4) | collective-permute-done | bytes 8224 | tf_op jit(solution)/shard_map/ppermute | solution.py:604
  16.0 0.0 collective-permute-done.5.beside_in
  16.0 0.5 %shard_map.110 = (f32[4,8,128]{2,1,0:T(8,128)S(1)}, f32[8,128]{1,0:T(8,128)S(1)}) custom-call(f32[8,1280]{1,0:T(8,128)S(1)} %get-tuple-element.74.own, s32[8,256]{1,0:T(8,128)S(1)} %get-tuple-element.45.order_ref, s32[8,256]{1,0:T(8,128)S(1)} %get-tuple-element.66.rest_0_.inverse_in, f32[8,256]{1,0:T(8,128)S(1)} %collective-permute-done.4.across_in, ...), custom_call_target="tpu_custom_call" | custom-call | tf_op jit(solution)/shard_map/pallas_call | solution.py:581
  16.5 8.5 %all_to_all.5.everyone = f32[8,8,128]{2,1,0:T(8,128)S(1)} all-to-all(f32[8,8,128]{2,1,0:T(8,128)S(1)} %broadcast_in_dim.10), channel_id=1, replica_groups=mesh['freq'=4,'dom'=8] {'dom'}, dimensions={0} | all-to-all | bytes 65536 | tf_op jit(solution)/shard_map/all_to_all | solution.py:614
  24.9 0.1 shard_map.111
  25.1 2.7 %collective-permute-start.6 = (f32[8,128]{1,0:T(8,128)S(1)}, f32[8,128]{1,0:T(8,128)S(1)}, u32[]{:S(2)}, u32[]{:S(2)}) collective-permute-start(f32[8,128]{1,0:T(8,128)S(1)} %shard_map.111), channel_id=1, source_target_pairs={{0,16},{8,24},{16,0},{24,8},{1,17},{9,25},{17,1},{25,9},{2,18},{10... | collective-permute-start | bytes 12296 | tf_op jit(solution)/shard_map/ppermute | solution.py:623
  27.7 1.9 %collective-permute-done.6 = f32[8,128]{1,0:T(8,128)S(1)} collective-permute-done((f32[8,128]{1,0:T(8,128)S(1)}, f32[8,128]{1,0:T(8,128)S(1)}, u32[]{:S(2)}, u32[]{:S(2)}) %collective-permute-start.6) | collective-permute-done | bytes 4128 | tf_op jit(solution)/shard_map/ppermute | solution.py:623
  29.7 1.6 %collective-permute-start.7 = (f32[8,128]{1,0:T(8,128)S(1)}, f32[8,128]{1,0:T(8,128)S(1)}, u32[]{:S(2)}, u32[]{:S(2)}) collective-permute-start(f32[8,128]{1,0:T(8,128)S(1)} %add.6), channel_id=1, source_target_pairs={{0,8},{8,0},{16,24},{24,16},{1,9},{9,1},{17,25},{25,17},{2,10},{10... | collective-permute-start | bytes 12296 | tf_op jit(solution)/shard_map/ppermute | solution.py:623
  31.2 2.0 %collective-permute-done.7 = f32[8,128]{1,0:T(8,128)S(1)} collective-permute-done((f32[8,128]{1,0:T(8,128)S(1)}, f32[8,128]{1,0:T(8,128)S(1)}, u32[]{:S(2)}, u32[]{:S(2)}) %collective-permute-start.7) | collective-permute-done | bytes 4128 | tf_op jit(solution)/shard_map/ppermute | solution.py:623
  33.3 0.6 %exponential_multiply_fusion = f32[1,1024]{1,0:T(1,128)} fusion(f32[1,1024]{1,0:T(1,128)S(1)} %bitcast.9, f32[1,1024]{1,0:T(1,128)S(1)} %bitcast.15), kind=kLoop, calls=%fused_computation | loop fusion | flops 2048 | bytes 12288 | tf_op jit(solution)/shard_map/mul | solution.py:742
  (8 shorter events, 0.0 us)
Async XLA Ops:
  1.4 5.1 %collective-permute-start = (f32[8,256]{1,0:T(8,128)S(1)}, f32[8,256]{1,0:T(8,128)S(1)}, u32[]{:S(2)}, u32[]{:S(2)}) collective-permute-start(f32[8,256]{1,0:T(8,128)S(1)} %get-tuple-element.46), channel_id=1, source_target_pairs={{0,8},{1,2},{2,1},{3,4},{4,3},{5,6},{6,5},{7,15},{8,0},{9,10},{10,... | collective-permute-start | bytes 24584 | tf_op jit(solution)/shard_map/ppermute | solution.py:604
  4.5 2.0 %collective-permute-start.1 = (f32[8,256]{1,0:T(8,128)S(1)}, f32[8,256]{1,0:T(8,128)S(1)}, u32[]{:S(2)}, u32[]{:S(2)}) collective-permute-start(f32[8,256]{1,0:T(8,128)S(1)} %get-tuple-element.47), channel_id=1, source_target_pairs={{0,1},{1,0},{2,3},{3,2},{4,5},{5,4},{6,7},{7,6},{8,9},{9,8},{10,11... | collective-permute-start | bytes 24584 | tf_op jit(solution)/shard_map/ppermute | solution.py:608
  7.5 3.7 %collective-permute-start.2 = (f32[8,256]{1,0:T(8,128)S(1)}, f32[8,256]{1,0:T(8,128)S(1)}, u32[]{:S(2)}, u32[]{:S(2)}) collective-permute-start(f32[8,256]{1,0:T(8,128)S(1)} %get-tuple-element.63), channel_id=1, source_target_pairs={{0,8},{1,2},{2,1},{3,4},{4,3},{5,6},{6,5},{7,15},{8,0},{9,10},{10,... | collective-permute-start | bytes 24584 | tf_op jit(solution)/shard_map/ppermute | solution.py:604
  9.3 2.0 %collective-permute-start.3 = (f32[8,256]{1,0:T(8,128)S(1)}, f32[8,256]{1,0:T(8,128)S(1)}, u32[]{:S(2)}, u32[]{:S(2)}) collective-permute-start(f32[8,256]{1,0:T(8,128)S(1)} %get-tuple-element.64), channel_id=1, source_target_pairs={{0,1},{1,0},{2,3},{3,2},{4,5},{5,4},{6,7},{7,6},{8,9},{9,8},{10,11... | collective-permute-start | bytes 24584 | tf_op jit(solution)/shard_map/ppermute | solution.py:608
  12.3 3.7 %collective-permute-start.4 = (f32[8,256]{1,0:T(8,128)S(1)}, f32[8,256]{1,0:T(8,128)S(1)}, u32[]{:S(2)}, u32[]{:S(2)}) collective-permute-start(f32[8,256]{1,0:T(8,128)S(1)} %get-tuple-element.75), channel_id=1, source_target_pairs={{0,8},{1,2},{2,1},{3,4},{4,3},{5,6},{6,5},{7,15},{8,0},{9,10},{10,... | collective-permute-start | bytes 24584 | tf_op jit(solution)/shard_map/ppermute | solution.py:604
  14.0 2.0 %collective-permute-start.5 = (f32[8,256]{1,0:T(8,128)S(1)}, f32[8,256]{1,0:T(8,128)S(1)}, u32[]{:S(2)}, u32[]{:S(2)}) collective-permute-start(f32[8,256]{1,0:T(8,128)S(1)} %get-tuple-element.76), channel_id=1, source_target_pairs={{0,1},{1,0},{2,3},{3,2},{4,5},{5,4},{6,7},{7,6},{8,9},{9,8},{10,11... | collective-permute-start | bytes 24584 | tf_op jit(solution)/shard_map/ppermute | solution.py:608
  25.1 4.6 %collective-permute-start.6 = (f32[8,128]{1,0:T(8,128)S(1)}, f32[8,128]{1,0:T(8,128)S(1)}, u32[]{:S(2)}, u32[]{:S(2)}) collective-permute-start(f32[8,128]{1,0:T(8,128)S(1)} %shard_map.111), channel_id=1, source_target_pairs={{0,16},{8,24},{16,0},{24,8},{1,17},{9,25},{17,1},{25,9},{2,18},{10... | collective-permute-start | bytes 12296 | tf_op jit(solution)/shard_map/ppermute | solution.py:623
  29.7 3.6 %collective-permute-start.7 = (f32[8,128]{1,0:T(8,128)S(1)}, f32[8,128]{1,0:T(8,128)S(1)}, u32[]{:S(2)}, u32[]{:S(2)}) collective-permute-start(f32[8,128]{1,0:T(8,128)S(1)} %add.6), channel_id=1, source_target_pairs={{0,8},{8,0},{16,24},{24,16},{1,9},{9,1},{17,25},{25,17},{2,10},{10... | collective-permute-start | bytes 12296 | tf_op jit(solution)/shard_map/ppermute | solution.py:623
  33.3 0.6 %copy-start = (f32[8,128]{1,0:T(8,128)}, f32[8,128]{1,0:T(8,128)S(1)}, u32[]{:S(2)}) copy-start(f32[8,128]{1,0:T(8,128)S(1)} %add.7) | copy-start | bytes 12292

commit v16 on v15

--- a/solution.py
+++ b/solution.py
@@ -369,6 +369,16 @@
     return doubled(block)
 
 
+def unpacked(blocks, with_scale, inverse_scale, step):
+    ratio = doubled(swap_halves(with_scale)) * inverse_scale
+    out = []
+    for block in blocks:
+        for _ in range(step):
+            block = block * ratio
+        out += [doubled(block), doubled(swap_halves(block))]
+    return out
+
+
 def front_stage(
     polars,
     step,
@@ -423,12 +433,14 @@
     forms_ref[...] = rows_of_forms(forms, rows)
     chunks = parts_joined(total, len(heights))
     put_chunks(rims_ref, chunks)
-    put_rims(
-        across_ref,
-        beside_ref,
-        [jnp.where(first, x, scale) for x in chunks[:rim]],
-        [jnp.where(first, x, scale) for x in chunks[rim:]],
-    )
+    lower, upper = chunks[:rim], chunks[rim:]
+    if step == 0:
+        lower = [jnp.where(first, x, scale) for x in lower]
+        upper = [jnp.where(first, x, scale) for x in upper]
+    else:
+        lower = [jnp.where(first, a, b) for a, b in zip(lower[::2], lower[1::2])]
+        upper = [jnp.where(first, a, b) for a, b in zip(upper[::2], upper[1::2])]
+    put_rims(across_ref, beside_ref, lower, upper)
 
 
 def inner_products(step, sums, own, delta, forms, across_in, beside_in):
@@ -493,6 +505,8 @@
     inverse_in,
     across_in,
     beside_in,
+    across_before,
+    beside_before,
     scale_in,
     sums_in,
     own_picks,
@@ -507,9 +521,12 @@
     first = row_ids(rows) < rows // 2
     scale = scale_in[...]
     inverse_scale = 1.0 / scale
-    prior, above = take_rims(across_in, beside_in)
-    prior = [rescaled(x, inverse_scale, step) for x in prior]
-    above = [rescaled(x, inverse_scale, step) for x in above]
+    prior, above = (
+        unpacked(now, before[0], inverse_scale, step)
+        for now, before in zip(
+            take_rims(across_in, beside_in), take_rims(across_before, beside_before)
+        )
+    )
     put_chunks(delta_ref, corrections(prior, above, cut(order_ref), cut(inverse_in)))
 
     picked = corrected_picks(delta_ref, own_picks, edges, edge_count)
@@ -521,7 +538,7 @@
         terms_ref[g] = weighted_sum(mine, [heavy[g * SIDE + i] for i in range(SIDE)])
     forms = rows_of_forms(forms, rows)
     sums = inner_products(
-        step, sums_in[...], cut(own), cut(delta_ref), forms, across_in, beside_in
+        step, sums_in[...], cut(own), cut(delta_ref), forms, across_before, beside_before
     )
     sums_ref[...] = jnp.where(first, sums, scale)
 
@@ -711,7 +728,9 @@
                 front, given, [shape(rows, rim, kind=jnp.int32), *front_shapes]
             )
         else:
-            outs = call(front, (*given, inverse), front_shapes)
+            outs = call(
+                front, (*given, inverse), [*front_shapes[:-2], *[shape(rows, rim // 2)] * 2]
+            )
         delta, picks, pieces, forms, rims, across, beside = outs
         across, beside = swap_across(across), swap_beside(beside)
         given = (own, delta, forms, *arrived, sums, picks, pieces, rims, edges, places)
@@ -728,7 +747,20 @@
         terms.append(term)
     term, sums = call(
         functools.partial(last_stage, polars, 2),
-        (own, order, inverse, across, beside, scale, sums, picks, blocks, edges, heavy),
+        (
+            own,
+            order,
+            inverse,
+            across,
+            beside,
+            *arrived,
+            scale,
+            sums,
+            picks,
+            blocks,
+            edges,
+            heavy,
+        ),
         [terms_shape, sums_shape],
         (pltpu.VMEM((rows, 2 * rim), jnp.float32),),
     )

time: 34.1 us -> 34 us (level)
  no operation moved by 1% of the time
where the time goes in v16:
time: 34 us; the launch traced here: 33.8 us
  starting transfers between devices  10.8 us (32%)
  blocking collectives  8.47 us (25%)
  Pallas kernels  7.65 us (22%)
  waiting for transfers between devices  5.63 us (17%)
  between operations  0.69 us (2%)
  other arithmetic  0.62 us (2%)
    all_to_all x1, blocking collectives, gather_all(): return lax.all_to_all(copies, axis, 0, 0)  8.47 us
    pallas_call x8, Pallas kernels, call(): pl.pallas_call(kernel, out_shape=outs, in_specs=space if isinstance(space...  7.65 us
    ppermute x3, starting transfers between devices, swap_across(): return lax.ppermute(block, ('freq', 'dom'), route)  6.49 us
    ppermute x2, starting transfers between devices, sum_over(): lax.ppermute(block, axis, [(i, i ^ step) for i in range(size)])  4.23 us
    ppermute x2, waiting for transfers between devices, sum_over(): lax.ppermute(block, axis, [(i, i ^ step) for i in range(size)])  3.94 us
    ppermute x3, waiting for transfers between devices, swap_across(): return lax.ppermute(block, ('freq', 'dom'), route)  1.67 us
  transfers between devices with their start and end apart: 8, of which 4 were waited for; matrix products, arithmetic and copies ran while one was open for 0% of the time, Pallas kernels for 12%

profile of v16, /device:TPU:0, one launch (start us, length us, event | category | flops | bytes accessed | tf_op | source)
XLA Modules:
  0.0 33.8 jit_solution(2184457636783618914)
XLA Ops:
  0.6 0.8 %shard_map.104 = (f32[8,256]{1,0:T(8,128)S(1)}, f32[8,256]{1,0:T(8,128)S(1)}, f32[4,1,1280]{2,1,0:T(1,128)S(1)}, s32[8,256]{1,0:T(8,128)S(1)}) custom-call(f32[4,1,1280]{2,1,0:T(1,128)} %bitcast.14, s32[1,256]{1,0:T(1,128)} %order_in.1), custom_call_target="tpu_custom_call" | custom-call | tf_op jit(solution)/shard_map/pallas_call | solution.py:598
  1.4 3.1 %collective-permute-start = (f32[8,256]{1,0:T(8,128)S(1)}, f32[8,256]{1,0:T(8,128)S(1)}, u32[]{:S(2)}, u32[]{:S(2)}) collective-permute-start(f32[8,256]{1,0:T(8,128)S(1)} %get-tuple-element.46), channel_id=1, source_target_pairs={{0,8},{1,2},{2,1},{3,4},{4,3},{5,6},{6,5},{7,15},{8,0},{9,10},{10,... | collective-permute-start | bytes 24584 | tf_op jit(solution)/shard_map/ppermute | solution.py:621
  4.5 0.0 collective-permute-start.1
  4.5 1.9 %shard_map.105 = (bf16[128,6144]{1,0:T(8,128)(2,1)S(1)}, f32[72,8,128]{2,1,0:T(8,128)S(1)}, f32[8,128]{1,0:T(8,128)S(1)}, f32[24,8,128]{2,1,0:T(8,128)S(1)}, f32...) custom-call(f32[2]{0:T(128)} %angular_in.1, ...), custom_call_target="tpu_custom_call" | custom-call | flops 4000000 | bytes 4000000 | tf_op jit(solution)/shard_map/pallas_call | solution.py:598
  6.5 0.0 collective-permute-done.across_in
  6.5 0.0 collective-permute-done.1.beside_in
  6.5 1.0 %shard_map.106 = (s32[8,256]{1,0:T(8,128)S(1)}, f32[8,512]{1,0:T(8,128)S(1)}, f32[24,8,128]{2,1,0:T(8,128)S(1)}, f32[384,128]{1,0:T(8,128)S(1)}, f32[8,128]{1,0:...) custom-call(s32[8,256]{1,0:T(8,128)S(1)} %get-tuple-element.45.order_ref, ...), custom_call_target="tpu_custom_call" | custom-call | tf_op jit(solution)/shard_map/pallas_call | solution.py:598
  7.5 1.7 %collective-permute-start.2 = (f32[8,256]{1,0:T(8,128)S(1)}, f32[8,256]{1,0:T(8,128)S(1)}, u32[]{:S(2)}, u32[]{:S(2)}) collective-permute-start(f32[8,256]{1,0:T(8,128)S(1)} %get-tuple-element.63), channel_id=1, source_target_pairs={{0,8},{1,2},{2,1},{3,4},{4,3},{5,6},{6,5},{7,15},{8,0},{9,10},{10,... | collective-permute-start | bytes 24584 | tf_op jit(solution)/shard_map/ppermute | solution.py:621
  9.3 1.2 %shard_map.107 = (f32[24,8,128]{2,1,0:T(8,128)S(1)}, f32[4,8,128]{2,1,0:T(8,128)S(1)}, f32[8,128]{1,0:T(8,128)S(1)}, f32[8,1280]{1,0:T(8,128)S(1)}, f32[24,8,128]{2,1,0:T(8,128)S(1)}) custom-call(f32[8,1280]{1,0:T(8,128)S(1)} %get-tuple-element.44.own, f32[8,512]{1,0:T(8,128)S(1)} %get-tuple-element.53.delta, f32[8,128]{1,0:T(8,128)S(1)} %get-tuple-element.54.forms, ...), custom_call_target="tpu_custom_call" | custom-call | flops 4000000 | bytes 4000000 | tf_op jit(solution)/shard_map/pallas_call | solution.py:598
  10.4 0.8 %collective-permute-done.2.across_in.across_before = f32[8,256]{1,0:T(8,128)S(1)} collective-permute-done((f32[8,256]{1,0:T(8,128)S(1)}, f32[8,256]{1,0:T(8,128)S(1)}, u32[]{:S(2)}, u32[]{:S(2)}) %collective-permute-start.2) | collective-permute-done | bytes 8224 | tf_op jit(solution)/shard_map/ppermute | solution.py:621
  11.3 0.0 collective-permute-done.3.beside_in.beside_before
  11.3 1.0 %shard_map.108 = (f32[8,512]{1,0:T(8,128)S(1)}, f32[24,8,128]{2,1,0:T(8,128)S(1)}, f32[384,128]{1,0:T(8,128)S(1)}, f32[8,128]{1,0:T(8,128)S(1)}, f32[8,512]{1,0:...) custom-call(s32[8,256]{1,0:T(8,128)S(1)} %get-tuple-element.45.order_ref, ...), custom_call_target="tpu_custom_call" | custom-call | tf_op jit(solution)/shard_map/pallas_call | solution.py:598
  12.3 1.7 %collective-permute-start.4 = (f32[8,128]{1,0:T(8,128)S(1)}, f32[8,128]{1,0:T(8,128)S(1)}, u32[]{:S(2)}, u32[]{:S(2)}) collective-permute-start(f32[8,128]{1,0:T(8,128)S(1)} %get-tuple-element.75), channel_id=1, source_target_pairs={{0,8},{1,2},{2,1},{3,4},{4,3},{5,6},{6,5},{7,15},{8,0},{9,10},{10,... | collective-permute-start | bytes 12296 | tf_op jit(solution)/shard_map/ppermute | solution.py:621
  13.9 0.0 collective-permute-start.5
  13.9 1.1 %shard_map.109 = (f32[4,8,128]{2,1,0:T(8,128)S(1)}, f32[8,128]{1,0:T(8,128)S(1)}, f32[8,1280]{1,0:T(8,128)S(1)}, f32[24,8,128]{2,1,0:T(8,128)S(1)}) custom-call(f32[8,1280]{1,0:T(8,128)S(1)} %get-tuple-element.62.own, f32[8,512]{1,0:T(8,128)S(1)} %get-tuple-element.67.delta, f32[8,128]{1,0:T(8,128)S(1)} %get-tuple-element.68.forms, ...), custom_call_target="tpu_custom_call" | custom-call | flops 4000000 | bytes 4000000 | tf_op jit(solution)/shard_map/pallas_call | solution.py:598
  15.0 0.9 %collective-permute-done.4.across_in = f32[8,128]{1,0:T(8,128)S(1)} collective-permute-done((f32[8,128]{1,0:T(8,128)S(1)}, f32[8,128]{1,0:T(8,128)S(1)}, u32[]{:S(2)}, u32[]{:S(2)}) %collective-permute-start.4) | collective-permute-done | bytes 4128 | tf_op jit(solution)/shard_map/ppermute | solution.py:621
  15.9 0.5 %shard_map.110 = (f32[4,8,128]{2,1,0:T(8,128)S(1)}, f32[8,128]{1,0:T(8,128)S(1)}) custom-call(f32[8,1280]{1,0:T(8,128)S(1)} %get-tuple-element.74.own, s32[8,256]{1,0:T(8,128)S(1)} %get-tuple-element.45.order_ref, s32[8,256]{1,0:T(8,128)S(1)} %get-tuple-element.66.rest_0_.inverse_in, f32[8,128]{1,0:T(8,128)S(1)} %collective-permute-done.4.across_in, ...), custom_call_target="tpu_custom_call" | custom-call | tf_op jit(solution)/shard_map/pallas_call | solution.py:598
  16.4 8.5 %all_to_all.5.everyone = f32[8,8,128]{2,1,0:T(8,128)S(1)} all-to-all(f32[8,8,128]{2,1,0:T(8,128)S(1)} %broadcast_in_dim.10), channel_id=1, replica_groups=mesh['freq'=4,'dom'=8] {'dom'}, dimensions={0} | all-to-all | bytes 65536 | tf_op jit(solution)/shard_map/all_to_all | solution.py:631
  24.9 0.1 shard_map.111
  25.0 2.7 %collective-permute-start.6 = (f32[8,128]{1,0:T(8,128)S(1)}, f32[8,128]{1,0:T(8,128)S(1)}, u32[]{:S(2)}, u32[]{:S(2)}) collective-permute-start(f32[8,128]{1,0:T(8,128)S(1)} %shard_map.111), channel_id=1, source_target_pairs={{0,16},{8,24},{16,0},{24,8},{1,17},{9,25},{17,1},{25,9},{2,18},{10... | collective-permute-start | bytes 12296 | tf_op jit(solution)/shard_map/ppermute | solution.py:640
  27.7 1.9 %collective-permute-done.6 = f32[8,128]{1,0:T(8,128)S(1)} collective-permute-done((f32[8,128]{1,0:T(8,128)S(1)}, f32[8,128]{1,0:T(8,128)S(1)}, u32[]{:S(2)}, u32[]{:S(2)}) %collective-permute-start.6) | collective-permute-done | bytes 4128 | tf_op jit(solution)/shard_map/ppermute | solution.py:640
  29.6 1.6 %collective-permute-start.7 = (f32[8,128]{1,0:T(8,128)S(1)}, f32[8,128]{1,0:T(8,128)S(1)}, u32[]{:S(2)}, u32[]{:S(2)}) collective-permute-start(f32[8,128]{1,0:T(8,128)S(1)} %add.6), channel_id=1, source_target_pairs={{0,8},{8,0},{16,24},{24,16},{1,9},{9,1},{17,25},{25,17},{2,10},{10... | collective-permute-start | bytes 12296 | tf_op jit(solution)/shard_map/ppermute | solution.py:640
  31.2 2.0 %collective-permute-done.7 = f32[8,128]{1,0:T(8,128)S(1)} collective-permute-done((f32[8,128]{1,0:T(8,128)S(1)}, f32[8,128]{1,0:T(8,128)S(1)}, u32[]{:S(2)}, u32[]{:S(2)}) %collective-permute-start.7) | collective-permute-done | bytes 4128 | tf_op jit(solution)/shard_map/ppermute | solution.py:640
  33.2 0.6 %exponential_multiply_fusion = f32[1,1024]{1,0:T(1,128)} fusion(f32[1,1024]{1,0:T(1,128)S(1)} %bitcast.9, f32[1,1024]{1,0:T(1,128)S(1)} %bitcast.15), kind=kLoop, calls=%fused_computation | loop fusion | flops 2048 | bytes 12288 | tf_op jit(solution)/shard_map/mul | solution.py:774
  (8 shorter events, 0.0 us)
Async XLA Ops:
  1.4 5.1 %collective-permute-start = (f32[8,256]{1,0:T(8,128)S(1)}, f32[8,256]{1,0:T(8,128)S(1)}, u32[]{:S(2)}, u32[]{:S(2)}) collective-permute-start(f32[8,256]{1,0:T(8,128)S(1)} %get-tuple-element.46), channel_id=1, source_target_pairs={{0,8},{1,2},{2,1},{3,4},{4,3},{5,6},{6,5},{7,15},{8,0},{9,10},{10,... | collective-permute-start | bytes 24584 | tf_op jit(solution)/shard_map/ppermute | solution.py:621
  4.5 2.0 %collective-permute-start.1 = (f32[8,256]{1,0:T(8,128)S(1)}, f32[8,256]{1,0:T(8,128)S(1)}, u32[]{:S(2)}, u32[]{:S(2)}) collective-permute-start(f32[8,256]{1,0:T(8,128)S(1)} %get-tuple-element.47), channel_id=1, source_target_pairs={{0,1},{1,0},{2,3},{3,2},{4,5},{5,4},{6,7},{7,6},{8,9},{9,8},{10,11... | collective-permute-start | bytes 24584 | tf_op jit(solution)/shard_map/ppermute | solution.py:625
  7.5 3.7 %collective-permute-start.2 = (f32[8,256]{1,0:T(8,128)S(1)}, f32[8,256]{1,0:T(8,128)S(1)}, u32[]{:S(2)}, u32[]{:S(2)}) collective-permute-start(f32[8,256]{1,0:T(8,128)S(1)} %get-tuple-element.63), channel_id=1, source_target_pairs={{0,8},{1,2},{2,1},{3,4},{4,3},{5,6},{6,5},{7,15},{8,0},{9,10},{10,... | collective-permute-start | bytes 24584 | tf_op jit(solution)/shard_map/ppermute | solution.py:621
  9.3 2.0 %collective-permute-start.3 = (f32[8,256]{1,0:T(8,128)S(1)}, f32[8,256]{1,0:T(8,128)S(1)}, u32[]{:S(2)}, u32[]{:S(2)}) collective-permute-start(f32[8,256]{1,0:T(8,128)S(1)} %get-tuple-element.64), channel_id=1, source_target_pairs={{0,1},{1,0},{2,3},{3,2},{4,5},{5,4},{6,7},{7,6},{8,9},{9,8},{10,11... | collective-permute-start | bytes 24584 | tf_op jit(solution)/shard_map/ppermute | solution.py:625
  12.3 3.6 %collective-permute-start.4 = (f32[8,128]{1,0:T(8,128)S(1)}, f32[8,128]{1,0:T(8,128)S(1)}, u32[]{:S(2)}, u32[]{:S(2)}) collective-permute-start(f32[8,128]{1,0:T(8,128)S(1)} %get-tuple-element.75), channel_id=1, source_target_pairs={{0,8},{1,2},{2,1},{3,4},{4,3},{5,6},{6,5},{7,15},{8,0},{9,10},{10,... | collective-permute-start | bytes 12296 | tf_op jit(solution)/shard_map/ppermute | solution.py:621
  13.9 2.0 %collective-permute-start.5 = (f32[8,128]{1,0:T(8,128)S(1)}, f32[8,128]{1,0:T(8,128)S(1)}, u32[]{:S(2)}, u32[]{:S(2)}) collective-permute-start(f32[8,128]{1,0:T(8,128)S(1)} %get-tuple-element.76), channel_id=1, source_target_pairs={{0,1},{1,0},{2,3},{3,2},{4,5},{5,4},{6,7},{7,6},{8,9},{9,8},{10,11... | collective-permute-start | bytes 12296 | tf_op jit(solution)/shard_map/ppermute | solution.py:625
  25.0 4.6 %collective-permute-start.6 = (f32[8,128]{1,0:T(8,128)S(1)}, f32[8,128]{1,0:T(8,128)S(1)}, u32[]{:S(2)}, u32[]{:S(2)}) collective-permute-start(f32[8,128]{1,0:T(8,128)S(1)} %shard_map.111), channel_id=1, source_target_pairs={{0,16},{8,24},{16,0},{24,8},{1,17},{9,25},{17,1},{25,9},{2,18},{10... | collective-permute-start | bytes 12296 | tf_op jit(solution)/shard_map/ppermute | solution.py:640
  29.6 3.6 %collective-permute-start.7 = (f32[8,128]{1,0:T(8,128)S(1)}, f32[8,128]{1,0:T(8,128)S(1)}, u32[]{:S(2)}, u32[]{:S(2)}) collective-permute-start(f32[8,128]{1,0:T(8,128)S(1)} %add.6), channel_id=1, source_target_pairs={{0,8},{8,0},{16,24},{24,16},{1,9},{9,1},{17,25},{25,17},{2,10},{10... | collective-permute-start | bytes 12296 | tf_op jit(solution)/shard_map/ppermute | solution.py:640
  33.2 0.6 %copy-start = (f32[8,128]{1,0:T(8,128)}, f32[8,128]{1,0:T(8,128)S(1)}, u32[]{:S(2)}) copy-start(f32[8,128]{1,0:T(8,128)S(1)} %add.7) | copy-start | bytes 12292

commit v17 on v16

--- a/solution.py
+++ b/solution.py
@@ -635,10 +635,17 @@
     size = lax.axis_size(axis)
     if size & (size - 1):
         return jnp.sum(gather_all(block, axis), axis=0)
-    step = size // 2
-    while step > 0:
+    near = min(size, 4)
+    parts = [block] + [None] * (near - 1)
+    for step in [*range(near // 2, near), *range(1, near // 2)]:
+        parts[step] = lax.ppermute(block, axis, [(i, i ^ step) for i in range(size)])
+    while len(parts) > 1:
+        parts = [a + b for a, b in zip(parts[::2], parts[1::2])]
+    block = parts[0]
+    step = near
+    while step < size:
         block = block + lax.ppermute(block, axis, [(i, i ^ step) for i in range(size)])
-        step //= 2
+        step *= 2
     return block
 
 

time: 34 us -> 34.1 us (level)
    ppermute x2 -> x3, waiting for transfers between devices: 3.94 us -> 3.72 us  [sum_over(): lax.ppermute(block, axis, [(i, i ^ step) for i in range(size)])]
    ppermute x2 -> x3, starting transfers between devices: 4.23 us -> 4.45 us  [sum_over(): lax.ppermute(block, axis, [(i, i ^ step) for i in range(size)])]
  transfers between devices with their start and end apart: 8 -> 9, of which waited for: 4 -> 4; matrix products, arithmetic and copies ran while one was open for 0% -> 0% of each run, Pallas kernels for 12% -> 12%
where the time goes in v17:
time: 34.1 us; the launch traced here: 33.8 us
  starting transfers between devices  11 us (32%)
  blocking collectives  8.47 us (25%)
  Pallas kernels  7.65 us (22%)
  waiting for transfers between devices  5.41 us (16%)
  between operations  0.69 us (2%)
  other arithmetic  0.62 us (2%)
    all_to_all x1, blocking collectives, gather_all(): return lax.all_to_all(copies, axis, 0, 0)  8.47 us
    pallas_call x8, Pallas kernels, call(): pl.pallas_call(kernel, out_shape=outs, in_specs=space if isinstance(space...  7.65 us
    ppermute x3, starting transfers between devices, swap_across(): return lax.ppermute(block, ('freq', 'dom'), route)  6.49 us
    ppermute x3, starting transfers between devices, sum_over(): lax.ppermute(block, axis, [(i, i ^ step) for i in range(size)])  4.45 us
    ppermute x3, waiting for transfers between devices, sum_over(): lax.ppermute(block, axis, [(i, i ^ step) for i in range(size)])  3.72 us
    ppermute x3, waiting for transfers between devices, swap_across(): return lax.ppermute(block, ('freq', 'dom'), route)  1.67 us
  transfers between devices with their start and end apart: 9, of which 4 were waited for; matrix products, arithmetic and copies ran while one was open for 0% of the time, Pallas kernels for 12%

profile of v17, /device:TPU:0, one launch (start us, length us, event | category | flops | bytes accessed | tf_op | source)
XLA Modules:
  0.0 33.8 jit_solution(2239442544406821762)
XLA Ops:
  0.6 0.8 %shard_map.104 = (f32[8,256]{1,0:T(8,128)S(1)}, f32[8,256]{1,0:T(8,128)S(1)}, f32[4,1,1280]{2,1,0:T(1,128)S(1)}, s32[8,256]{1,0:T(8,128)S(1)}) custom-call(f32[4,1,1280]{2,1,0:T(1,128)} %bitcast.14, s32[1,256]{1,0:T(1,128)} %order_in.1), custom_call_target="tpu_custom_call" | custom-call | tf_op jit(solution)/shard_map/pallas_call | solution.py:598
  1.4 3.1 %collective-permute-start = (f32[8,256]{1,0:T(8,128)S(1)}, f32[8,256]{1,0:T(8,128)S(1)}, u32[]{:S(2)}, u32[]{:S(2)}) collective-permute-start(f32[8,256]{1,0:T(8,128)S(1)} %get-tuple-element.46), channel_id=1, source_target_pairs={{0,8},{1,2},{2,1},{3,4},{4,3},{5,6},{6,5},{7,15},{8,0},{9,10},{10,... | collective-permute-start | bytes 24584 | tf_op jit(solution)/shard_map/ppermute | solution.py:621
  4.5 0.0 collective-permute-start.1
  4.5 1.9 %shard_map.105 = (bf16[128,6144]{1,0:T(8,128)(2,1)S(1)}, f32[72,8,128]{2,1,0:T(8,128)S(1)}, f32[8,128]{1,0:T(8,128)S(1)}, f32[24,8,128]{2,1,0:T(8,128)S(1)}, f32...) custom-call(f32[2]{0:T(128)} %angular_in.1, ...), custom_call_target="tpu_custom_call" | custom-call | flops 4000000 | bytes 4000000 | tf_op jit(solution)/shard_map/pallas_call | solution.py:598
  6.5 0.0 collective-permute-done.1.beside_in
  6.5 1.0 %shard_map.106 = (s32[8,256]{1,0:T(8,128)S(1)}, f32[8,512]{1,0:T(8,128)S(1)}, f32[24,8,128]{2,1,0:T(8,128)S(1)}, f32[384,128]{1,0:T(8,128)S(1)}, f32[8,128]{1,0:...) custom-call(s32[8,256]{1,0:T(8,128)S(1)} %get-tuple-element.45.order_ref, ...), custom_call_target="tpu_custom_call" | custom-call | tf_op jit(solution)/shard_map/pallas_call | solution.py:598
  7.5 1.7 %collective-permute-start.2 = (f32[8,256]{1,0:T(8,128)S(1)}, f32[8,256]{1,0:T(8,128)S(1)}, u32[]{:S(2)}, u32[]{:S(2)}) collective-permute-start(f32[8,256]{1,0:T(8,128)S(1)} %get-tuple-element.63), channel_id=1, source_target_pairs={{0,8},{1,2},{2,1},{3,4},{4,3},{5,6},{6,5},{7,15},{8,0},{9,10},{10,... | collective-permute-start | bytes 24584 | tf_op jit(solution)/shard_map/ppermute | solution.py:621
  9.3 0.0 collective-permute-start.3
  9.3 1.2 %shard_map.107 = (f32[24,8,128]{2,1,0:T(8,128)S(1)}, f32[4,8,128]{2,1,0:T(8,128)S(1)}, f32[8,128]{1,0:T(8,128)S(1)}, f32[8,1280]{1,0:T(8,128)S(1)}, f32[24,8,128]{2,1,0:T(8,128)S(1)}) custom-call(f32[8,1280]{1,0:T(8,128)S(1)} %get-tuple-element.44.own, f32[8,512]{1,0:T(8,128)S(1)} %get-tuple-element.53.delta, f32[8,128]{1,0:T(8,128)S(1)} %get-tuple-element.54.forms, ...), custom_call_target="tpu_custom_call" | custom-call | flops 4000000 | bytes 4000000 | tf_op jit(solution)/shard_map/pallas_call | solution.py:598
  10.4 0.8 %collective-permute-done.2.across_in.across_before = f32[8,256]{1,0:T(8,128)S(1)} collective-permute-done((f32[8,256]{1,0:T(8,128)S(1)}, f32[8,256]{1,0:T(8,128)S(1)}, u32[]{:S(2)}, u32[]{:S(2)}) %collective-permute-start.2) | collective-permute-done | bytes 8224 | tf_op jit(solution)/shard_map/ppermute | solution.py:621
  11.3 1.0 %shard_map.108 = (f32[8,512]{1,0:T(8,128)S(1)}, f32[24,8,128]{2,1,0:T(8,128)S(1)}, f32[384,128]{1,0:T(8,128)S(1)}, f32[8,128]{1,0:T(8,128)S(1)}, f32[8,512]{1,0:...) custom-call(s32[8,256]{1,0:T(8,128)S(1)} %get-tuple-element.45.order_ref, ...), custom_call_target="tpu_custom_call" | custom-call | tf_op jit(solution)/shard_map/pallas_call | solution.py:598
  12.3 1.7 %collective-permute-start.4 = (f32[8,128]{1,0:T(8,128)S(1)}, f32[8,128]{1,0:T(8,128)S(1)}, u32[]{:S(2)}, u32[]{:S(2)}) collective-permute-start(f32[8,128]{1,0:T(8,128)S(1)} %get-tuple-element.75), channel_id=1, source_target_pairs={{0,8},{1,2},{2,1},{3,4},{4,3},{5,6},{6,5},{7,15},{8,0},{9,10},{10,... | collective-permute-start | bytes 12296 | tf_op jit(solution)/shard_map/ppermute | solution.py:621
  13.9 0.0 collective-permute-start.5
  13.9 1.1 %shard_map.109 = (f32[4,8,128]{2,1,0:T(8,128)S(1)}, f32[8,128]{1,0:T(8,128)S(1)}, f32[8,1280]{1,0:T(8,128)S(1)}, f32[24,8,128]{2,1,0:T(8,128)S(1)}) custom-call(f32[8,1280]{1,0:T(8,128)S(1)} %get-tuple-element.62.own, f32[8,512]{1,0:T(8,128)S(1)} %get-tuple-element.67.delta, f32[8,128]{1,0:T(8,128)S(1)} %get-tuple-element.68.forms, ...), custom_call_target="tpu_custom_call" | custom-call | flops 4000000 | bytes 4000000 | tf_op jit(solution)/shard_map/pallas_call | solution.py:598
  15.0 0.9 %collective-permute-done.4.across_in = f32[8,128]{1,0:T(8,128)S(1)} collective-permute-done((f32[8,128]{1,0:T(8,128)S(1)}, f32[8,128]{1,0:T(8,128)S(1)}, u32[]{:S(2)}, u32[]{:S(2)}) %collective-permute-start.4) | collective-permute-done | bytes 4128 | tf_op jit(solution)/shard_map/ppermute | solution.py:621
  15.9 0.5 %shard_map.110 = (f32[4,8,128]{2,1,0:T(8,128)S(1)}, f32[8,128]{1,0:T(8,128)S(1)}) custom-call(f32[8,1280]{1,0:T(8,128)S(1)} %get-tuple-element.74.own, s32[8,256]{1,0:T(8,128)S(1)} %get-tuple-element.45.order_ref, s32[8,256]{1,0:T(8,128)S(1)} %get-tuple-element.66.rest_0_.inverse_in, f32[8,128]{1,0:T(8,128)S(1)} %collective-permute-done.4.across_in, ...), custom_call_target="tpu_custom_call" | custom-call | tf_op jit(solution)/shard_map/pallas_call | solution.py:598
  16.4 8.5 %all_to_all.5.everyone = f32[8,8,128]{2,1,0:T(8,128)S(1)} all-to-all(f32[8,8,128]{2,1,0:T(8,128)S(1)} %broadcast_in_dim.10), channel_id=1, replica_groups=mesh['freq'=4,'dom'=8] {'dom'}, dimensions={0} | all-to-all | bytes 65536 | tf_op jit(solution)/shard_map/all_to_all | solution.py:631
  24.9 0.1 shard_map.111
  25.0 3.7 %collective-permute-start.8 = (f32[8,128]{1,0:T(8,128)S(1)}, f32[8,128]{1,0:T(8,128)S(1)}, u32[]{:S(2)}, u32[]{:S(2)}) collective-permute-start(f32[8,128]{1,0:T(8,128)S(1)} %shard_map.111), channel_id=1, source_target_pairs={{0,24},{8,16},{16,8},{24,0},{1,25},{9,17},{17,9},{25,1},{2,26},{10... | collective-permute-start | bytes 12296 | tf_op jit(solution)/shard_map/ppermute | solution.py:641
  28.7 0.8 %collective-permute-start.6 = (f32[8,128]{1,0:T(8,128)S(1)}, f32[8,128]{1,0:T(8,128)S(1)}, u32[]{:S(2)}, u32[]{:S(2)}) collective-permute-start(f32[8,128]{1,0:T(8,128)S(1)} %shard_map.111), channel_id=1, source_target_pairs={{0,8},{8,0},{16,24},{24,16},{1,9},{9,1},{17,25},{25,17},{2,10},{10... | collective-permute-start | bytes 12296 | tf_op jit(solution)/shard_map/ppermute | solution.py:641
  29.5 1.0 %collective-permute-done.8 = f32[8,128]{1,0:T(8,128)S(1)} collective-permute-done((f32[8,128]{1,0:T(8,128)S(1)}, f32[8,128]{1,0:T(8,128)S(1)}, u32[]{:S(2)}, u32[]{:S(2)}) %collective-permute-start.8) | collective-permute-done | bytes 4128 | tf_op jit(solution)/shard_map/ppermute | solution.py:641
  30.5 2.7 %collective-permute-done.7 = f32[8,128]{1,0:T(8,128)S(1)} collective-permute-done((f32[8,128]{1,0:T(8,128)S(1)}, f32[8,128]{1,0:T(8,128)S(1)}, u32[]{:S(2)}, u32[]{:S(2)}) %collective-permute-start.7) | collective-permute-done | bytes 4128 | tf_op jit(solution)/shard_map/ppermute | solution.py:641
  33.2 0.0 copy-start
  33.2 0.6 %exponential_multiply_fusion = f32[1,1024]{1,0:T(1,128)} fusion(f32[1,1024]{1,0:T(1,128)S(1)} %bitcast.9, f32[1,1024]{1,0:T(1,128)S(1)} %bitcast.15), kind=kLoop, calls=%fused_computation | loop fusion | flops 2048 | bytes 12288 | tf_op jit(solution)/shard_map/mul | solution.py:781
  (9 shorter events, 0.0 us)
Async XLA Ops:
  1.4 5.1 %collective-permute-start = (f32[8,256]{1,0:T(8,128)S(1)}, f32[8,256]{1,0:T(8,128)S(1)}, u32[]{:S(2)}, u32[]{:S(2)}) collective-permute-start(f32[8,256]{1,0:T(8,128)S(1)} %get-tuple-element.46), channel_id=1, source_target_pairs={{0,8},{1,2},{2,1},{3,4},{4,3},{5,6},{6,5},{7,15},{8,0},{9,10},{10,... | collective-permute-start | bytes 24584 | tf_op jit(solution)/shard_map/ppermute | solution.py:621
  4.5 2.0 %collective-permute-start.1 = (f32[8,256]{1,0:T(8,128)S(1)}, f32[8,256]{1,0:T(8,128)S(1)}, u32[]{:S(2)}, u32[]{:S(2)}) collective-permute-start(f32[8,256]{1,0:T(8,128)S(1)} %get-tuple-element.47), channel_id=1, source_target_pairs={{0,1},{1,0},{2,3},{3,2},{4,5},{5,4},{6,7},{7,6},{8,9},{9,8},{10,11... | collective-permute-start | bytes 24584 | tf_op jit(solution)/shard_map/ppermute | solution.py:625
  7.5 3.7 %collective-permute-start.2 = (f32[8,256]{1,0:T(8,128)S(1)}, f32[8,256]{1,0:T(8,128)S(1)}, u32[]{:S(2)}, u32[]{:S(2)}) collective-permute-start(f32[8,256]{1,0:T(8,128)S(1)} %get-tuple-element.63), channel_id=1, source_target_pairs={{0,8},{1,2},{2,1},{3,4},{4,3},{5,6},{6,5},{7,15},{8,0},{9,10},{10,... | collective-permute-start | bytes 24584 | tf_op jit(solution)/shard_map/ppermute | solution.py:621
  9.3 2.0 %collective-permute-start.3 = (f32[8,256]{1,0:T(8,128)S(1)}, f32[8,256]{1,0:T(8,128)S(1)}, u32[]{:S(2)}, u32[]{:S(2)}) collective-permute-start(f32[8,256]{1,0:T(8,128)S(1)} %get-tuple-element.64), channel_id=1, source_target_pairs={{0,1},{1,0},{2,3},{3,2},{4,5},{5,4},{6,7},{7,6},{8,9},{9,8},{10,11... | collective-permute-start | bytes 24584 | tf_op jit(solution)/shard_map/ppermute | solution.py:625
  12.3 3.6 %collective-permute-start.4 = (f32[8,128]{1,0:T(8,128)S(1)}, f32[8,128]{1,0:T(8,128)S(1)}, u32[]{:S(2)}, u32[]{:S(2)}) collective-permute-start(f32[8,128]{1,0:T(8,128)S(1)} %get-tuple-element.75), channel_id=1, source_target_pairs={{0,8},{1,2},{2,1},{3,4},{4,3},{5,6},{6,5},{7,15},{8,0},{9,10},{10,... | collective-permute-start | bytes 12296 | tf_op jit(solution)/shard_map/ppermute | solution.py:621
  13.9 2.0 %collective-permute-start.5 = (f32[8,128]{1,0:T(8,128)S(1)}, f32[8,128]{1,0:T(8,128)S(1)}, u32[]{:S(2)}, u32[]{:S(2)}) collective-permute-start(f32[8,128]{1,0:T(8,128)S(1)} %get-tuple-element.76), channel_id=1, source_target_pairs={{0,1},{1,0},{2,3},{3,2},{4,5},{5,4},{6,7},{7,6},{8,9},{9,8},{10,11... | collective-permute-start | bytes 12296 | tf_op jit(solution)/shard_map/ppermute | solution.py:625
  25.0 5.5 %collective-permute-start.8 = (f32[8,128]{1,0:T(8,128)S(1)}, f32[8,128]{1,0:T(8,128)S(1)}, u32[]{:S(2)}, u32[]{:S(2)}) collective-permute-start(f32[8,128]{1,0:T(8,128)S(1)} %shard_map.111), channel_id=1, source_target_pairs={{0,24},{8,16},{16,8},{24,0},{1,25},{9,17},{17,9},{25,1},{2,26},{10... | collective-permute-start | bytes 12296 | tf_op jit(solution)/shard_map/ppermute | solution.py:641
  28.7 4.5 %collective-permute-start.7 = (f32[8,128]{1,0:T(8,128)S(1)}, f32[8,128]{1,0:T(8,128)S(1)}, u32[]{:S(2)}, u32[]{:S(2)}) collective-permute-start(f32[8,128]{1,0:T(8,128)S(1)} %shard_map.111), channel_id=1, source_target_pairs={{0,16},{8,24},{16,0},{24,8},{1,17},{9,25},{17,1},{25,9},{2,18},{10... | collective-permute-start | bytes 12296 | tf_op jit(solution)/shard_map/ppermute | solution.py:641
  28.7 4.5 %collective-permute-start.6 = (f32[8,128]{1,0:T(8,128)S(1)}, f32[8,128]{1,0:T(8,128)S(1)}, u32[]{:S(2)}, u32[]{:S(2)}) collective-permute-start(f32[8,128]{1,0:T(8,128)S(1)} %shard_map.111), channel_id=1, source_target_pairs={{0,8},{8,0},{16,24},{24,16},{1,9},{9,1},{17,25},{25,17},{2,10},{10... | collective-permute-start | bytes 12296 | tf_op jit(solution)/shard_map/ppermute | solution.py:641
  33.2 0.6 %copy-start = (f32[8,128]{1,0:T(8,128)}, f32[8,128]{1,0:T(8,128)S(1)}, u32[]{:S(2)}) copy-start(f32[8,128]{1,0:T(8,128)S(1)} %add_add_fusion) | copy-start | bytes 12292

commit v18 on v17

--- a/solution.py
+++ b/solution.py
@@ -639,9 +639,10 @@
     parts = [block] + [None] * (near - 1)
     for step in [*range(near // 2, near), *range(1, near // 2)]:
         parts[step] = lax.ppermute(block, axis, [(i, i ^ step) for i in range(size)])
-    while len(parts) > 1:
-        parts = [a + b for a, b in zip(parts[::2], parts[1::2])]
-    block = parts[0]
+    if near == 4:
+        block = (parts[0] + parts[1]) + (parts[3] + parts[2])
+    else:
+        block = sum(parts[1:], parts[0])
     step = near
     while step < size:
         block = block + lax.ppermute(block, axis, [(i, i ^ step) for i in range(size)])

time: 34.1 us -> 33.9 us (level)
  transfers between devices with their start and end apart: 9 -> 9, of which waited for: 4 -> 4; matrix products, arithmetic and copies ran while one was open for 0% -> 0% of each run, Pallas kernels for 12% -> 13%
where the time goes in v18:
time: 33.9 us; the launch traced here: 33.7 us
  starting transfers between devices  10.8 us (32%)
  blocking collectives  8.47 us (25%)
  Pallas kernels  7.65 us (23%)
  waiting for transfers between devices  5.51 us (16%)
  between operations  0.69 us (2%)
  other arithmetic  0.62 us (2%)
    all_to_all x1, blocking collectives, gather_all(): return lax.all_to_all(copies, axis, 0, 0)  8.47 us
    pallas_call x8, Pallas kernels, call(): pl.pallas_call(kernel, out_shape=outs, in_specs=space if isinstance(space...  7.65 us
    ppermute x3, starting transfers between devices, swap_across(): return lax.ppermute(block, ('freq', 'dom'), route)  6.49 us
    ppermute x3, starting transfers between devices, sum_over(): lax.ppermute(block, axis, [(i, i ^ step) for i in range(size)])  4.24 us
    ppermute x3, waiting for transfers between devices, sum_over(): lax.ppermute(block, axis, [(i, i ^ step) for i in range(size)])  3.83 us
    ppermute x3, waiting for transfers between devices, swap_across(): return lax.ppermute(block, ('freq', 'dom'), route)  1.67 us
  transfers between devices with their start and end apart: 9, of which 4 were waited for; matrix products, arithmetic and copies ran while one was open for 0% of the time, Pallas kernels for 13%

profile of v18, /device:TPU:0, one launch (start us, length us, event | category | flops | bytes accessed | tf_op | source)
XLA Modules:
  0.0 33.7 jit_solution(16572805074190186130)
XLA Ops:
  0.6 0.8 %shard_map.104 = (f32[8,256]{1,0:T(8,128)S(1)}, f32[8,256]{1,0:T(8,128)S(1)}, f32[4,1,1280]{2,1,0:T(1,128)S(1)}, s32[8,256]{1,0:T(8,128)S(1)}) custom-call(f32[4,1,1280]{2,1,0:T(1,128)} %bitcast.14, s32[1,256]{1,0:T(1,128)} %order_in.1), custom_call_target="tpu_custom_call" | custom-call | tf_op jit(solution)/shard_map/pallas_call | solution.py:598
  1.4 3.1 %collective-permute-start = (f32[8,256]{1,0:T(8,128)S(1)}, f32[8,256]{1,0:T(8,128)S(1)}, u32[]{:S(2)}, u32[]{:S(2)}) collective-permute-start(f32[8,256]{1,0:T(8,128)S(1)} %get-tuple-element.46), channel_id=1, source_target_pairs={{0,8},{1,2},{2,1},{3,4},{4,3},{5,6},{6,5},{7,15},{8,0},{9,10},{10,... | collective-permute-start | bytes 24584 | tf_op jit(solution)/shard_map/ppermute | solution.py:621
  4.5 0.0 collective-permute-start.1
  4.5 1.9 %shard_map.105 = (bf16[128,6144]{1,0:T(8,128)(2,1)S(1)}, f32[72,8,128]{2,1,0:T(8,128)S(1)}, f32[8,128]{1,0:T(8,128)S(1)}, f32[24,8,128]{2,1,0:T(8,128)S(1)}, f32...) custom-call(f32[2]{0:T(128)} %angular_in.1, ...), custom_call_target="tpu_custom_call" | custom-call | flops 4000000 | bytes 4000000 | tf_op jit(solution)/shard_map/pallas_call | solution.py:598
  6.5 0.0 collective-permute-done.across_in
  6.5 0.0 collective-permute-done.1.beside_in
  6.5 1.0 %shard_map.106 = (s32[8,256]{1,0:T(8,128)S(1)}, f32[8,512]{1,0:T(8,128)S(1)}, f32[24,8,128]{2,1,0:T(8,128)S(1)}, f32[384,128]{1,0:T(8,128)S(1)}, f32[8,128]{1,0:...) custom-call(s32[8,256]{1,0:T(8,128)S(1)} %get-tuple-element.45.order_ref, ...), custom_call_target="tpu_custom_call" | custom-call | tf_op jit(solution)/shard_map/pallas_call | solution.py:598
  7.5 1.7 %collective-permute-start.2 = (f32[8,256]{1,0:T(8,128)S(1)}, f32[8,256]{1,0:T(8,128)S(1)}, u32[]{:S(2)}, u32[]{:S(2)}) collective-permute-start(f32[8,256]{1,0:T(8,128)S(1)} %get-tuple-element.63), channel_id=1, source_target_pairs={{0,8},{1,2},{2,1},{3,4},{4,3},{5,6},{6,5},{7,15},{8,0},{9,10},{10,... | collective-permute-start | bytes 24584 | tf_op jit(solution)/shard_map/ppermute | solution.py:621
  9.3 1.2 %shard_map.107 = (f32[24,8,128]{2,1,0:T(8,128)S(1)}, f32[4,8,128]{2,1,0:T(8,128)S(1)}, f32[8,128]{1,0:T(8,128)S(1)}, f32[8,1280]{1,0:T(8,128)S(1)}, f32[24,8,128]{2,1,0:T(8,128)S(1)}) custom-call(f32[8,1280]{1,0:T(8,128)S(1)} %get-tuple-element.44.own, f32[8,512]{1,0:T(8,128)S(1)} %get-tuple-element.53.delta, f32[8,128]{1,0:T(8,128)S(1)} %get-tuple-element.54.forms, ...), custom_call_target="tpu_custom_call" | custom-call | flops 4000000 | bytes 4000000 | tf_op jit(solution)/shard_map/pallas_call | solution.py:598
  10.4 0.8 %collective-permute-done.2.across_in.across_before = f32[8,256]{1,0:T(8,128)S(1)} collective-permute-done((f32[8,256]{1,0:T(8,128)S(1)}, f32[8,256]{1,0:T(8,128)S(1)}, u32[]{:S(2)}, u32[]{:S(2)}) %collective-permute-start.2) | collective-permute-done | bytes 8224 | tf_op jit(solution)/shard_map/ppermute | solution.py:621
  11.3 1.0 %shard_map.108 = (f32[8,512]{1,0:T(8,128)S(1)}, f32[24,8,128]{2,1,0:T(8,128)S(1)}, f32[384,128]{1,0:T(8,128)S(1)}, f32[8,128]{1,0:T(8,128)S(1)}, f32[8,512]{1,0:...) custom-call(s32[8,256]{1,0:T(8,128)S(1)} %get-tuple-element.45.order_ref, ...), custom_call_target="tpu_custom_call" | custom-call | tf_op jit(solution)/shard_map/pallas_call | solution.py:598
  12.3 1.7 %collective-permute-start.4 = (f32[8,128]{1,0:T(8,128)S(1)}, f32[8,128]{1,0:T(8,128)S(1)}, u32[]{:S(2)}, u32[]{:S(2)}) collective-permute-start(f32[8,128]{1,0:T(8,128)S(1)} %get-tuple-element.75), channel_id=1, source_target_pairs={{0,8},{1,2},{2,1},{3,4},{4,3},{5,6},{6,5},{7,15},{8,0},{9,10},{10,... | collective-permute-start | bytes 12296 | tf_op jit(solution)/shard_map/ppermute | solution.py:621
  13.9 1.1 %shard_map.109 = (f32[4,8,128]{2,1,0:T(8,128)S(1)}, f32[8,128]{1,0:T(8,128)S(1)}, f32[8,1280]{1,0:T(8,128)S(1)}, f32[24,8,128]{2,1,0:T(8,128)S(1)}) custom-call(f32[8,1280]{1,0:T(8,128)S(1)} %get-tuple-element.62.own, f32[8,512]{1,0:T(8,128)S(1)} %get-tuple-element.67.delta, f32[8,128]{1,0:T(8,128)S(1)} %get-tuple-element.68.forms, ...), custom_call_target="tpu_custom_call" | custom-call | flops 4000000 | bytes 4000000 | tf_op jit(solution)/shard_map/pallas_call | solution.py:598
  15.0 0.9 %collective-permute-done.4.across_in = f32[8,128]{1,0:T(8,128)S(1)} collective-permute-done((f32[8,128]{1,0:T(8,128)S(1)}, f32[8,128]{1,0:T(8,128)S(1)}, u32[]{:S(2)}, u32[]{:S(2)}) %collective-permute-start.4) | collective-permute-done | bytes 4128 | tf_op jit(solution)/shard_map/ppermute | solution.py:621
  15.9 0.5 %shard_map.110 = (f32[4,8,128]{2,1,0:T(8,128)S(1)}, f32[8,128]{1,0:T(8,128)S(1)}) custom-call(f32[8,1280]{1,0:T(8,128)S(1)} %get-tuple-element.74.own, s32[8,256]{1,0:T(8,128)S(1)} %get-tuple-element.45.order_ref, s32[8,256]{1,0:T(8,128)S(1)} %get-tuple-element.66.rest_0_.inverse_in, f32[8,128]{1,0:T(8,128)S(1)} %collective-permute-done.4.across_in, ...), custom_call_target="tpu_custom_call" | custom-call | tf_op jit(solution)/shard_map/pallas_call | solution.py:598
  16.4 8.5 %all_to_all.5.everyone = f32[8,8,128]{2,1,0:T(8,128)S(1)} all-to-all(f32[8,8,128]{2,1,0:T(8,128)S(1)} %broadcast_in_dim.10), channel_id=1, replica_groups=mesh['freq'=4,'dom'=8] {'dom'}, dimensions={0} | all-to-all | bytes 65536 | tf_op jit(solution)/shard_map/all_to_all | solution.py:631
  24.9 0.1 shard_map.111
  25.0 2.7 %collective-permute-start.8 = (f32[8,128]{1,0:T(8,128)S(1)}, f32[8,128]{1,0:T(8,128)S(1)}, u32[]{:S(2)}, u32[]{:S(2)}) collective-permute-start(f32[8,128]{1,0:T(8,128)S(1)} %shard_map.111), channel_id=1, source_target_pairs={{0,16},{8,24},{16,0},{24,8},{1,17},{9,25},{17,1},{25,9},{2,18},{10... | collective-permute-start | bytes 12296 | tf_op jit(solution)/shard_map/ppermute | solution.py:641
  27.7 1.3 %collective-permute-start.7 = (f32[8,128]{1,0:T(8,128)S(1)}, f32[8,128]{1,0:T(8,128)S(1)}, u32[]{:S(2)}, u32[]{:S(2)}) collective-permute-start(f32[8,128]{1,0:T(8,128)S(1)} %shard_map.111), channel_id=1, source_target_pairs={{0,24},{8,16},{16,8},{24,0},{1,25},{9,17},{17,9},{25,1},{2,26},{10... | collective-permute-start | bytes 12296 | tf_op jit(solution)/shard_map/ppermute | solution.py:641
  29.0 0.2 collective-permute-start.6
  29.3 0.3 collective-permute-done.8
  29.6 3.5 %collective-permute-done.7 = f32[8,128]{1,0:T(8,128)S(1)} collective-permute-done((f32[8,128]{1,0:T(8,128)S(1)}, f32[8,128]{1,0:T(8,128)S(1)}, u32[]{:S(2)}, u32[]{:S(2)}) %collective-permute-start.7) | collective-permute-done | bytes 4128 | tf_op jit(solution)/shard_map/ppermute | solution.py:641
  33.1 0.0 copy-start
  33.1 0.6 %exponential_multiply_fusion = f32[1,1024]{1,0:T(1,128)} fusion(f32[1,1024]{1,0:T(1,128)S(1)} %bitcast.9, f32[1,1024]{1,0:T(1,128)S(1)} %bitcast.15), kind=kLoop, calls=%fused_computation | loop fusion | flops 2048 | bytes 12288 | tf_op jit(solution)/shard_map/mul | solution.py:782
  (9 shorter events, 0.0 us)
Async XLA Ops:
  1.4 5.1 %collective-permute-start = (f32[8,256]{1,0:T(8,128)S(1)}, f32[8,256]{1,0:T(8,128)S(1)}, u32[]{:S(2)}, u32[]{:S(2)}) collective-permute-start(f32[8,256]{1,0:T(8,128)S(1)} %get-tuple-element.46), channel_id=1, source_target_pairs={{0,8},{1,2},{2,1},{3,4},{4,3},{5,6},{6,5},{7,15},{8,0},{9,10},{10,... | collective-permute-start | bytes 24584 | tf_op jit(solution)/shard_map/ppermute | solution.py:621
  4.5 2.0 %collective-permute-start.1 = (f32[8,256]{1,0:T(8,128)S(1)}, f32[8,256]{1,0:T(8,128)S(1)}, u32[]{:S(2)}, u32[]{:S(2)}) collective-permute-start(f32[8,256]{1,0:T(8,128)S(1)} %get-tuple-element.47), channel_id=1, source_target_pairs={{0,1},{1,0},{2,3},{3,2},{4,5},{5,4},{6,7},{7,6},{8,9},{9,8},{10,11... | collective-permute-start | bytes 24584 | tf_op jit(solution)/shard_map/ppermute | solution.py:625
  7.5 3.7 %collective-permute-start.2 = (f32[8,256]{1,0:T(8,128)S(1)}, f32[8,256]{1,0:T(8,128)S(1)}, u32[]{:S(2)}, u32[]{:S(2)}) collective-permute-start(f32[8,256]{1,0:T(8,128)S(1)} %get-tuple-element.63), channel_id=1, source_target_pairs={{0,8},{1,2},{2,1},{3,4},{4,3},{5,6},{6,5},{7,15},{8,0},{9,10},{10,... | collective-permute-start | bytes 24584 | tf_op jit(solution)/shard_map/ppermute | solution.py:621
  9.3 2.0 %collective-permute-start.3 = (f32[8,256]{1,0:T(8,128)S(1)}, f32[8,256]{1,0:T(8,128)S(1)}, u32[]{:S(2)}, u32[]{:S(2)}) collective-permute-start(f32[8,256]{1,0:T(8,128)S(1)} %get-tuple-element.64), channel_id=1, source_target_pairs={{0,1},{1,0},{2,3},{3,2},{4,5},{5,4},{6,7},{7,6},{8,9},{9,8},{10,11... | collective-permute-start | bytes 24584 | tf_op jit(solution)/shard_map/ppermute | solution.py:625
  12.3 3.6 %collective-permute-start.4 = (f32[8,128]{1,0:T(8,128)S(1)}, f32[8,128]{1,0:T(8,128)S(1)}, u32[]{:S(2)}, u32[]{:S(2)}) collective-permute-start(f32[8,128]{1,0:T(8,128)S(1)} %get-tuple-element.75), channel_id=1, source_target_pairs={{0,8},{1,2},{2,1},{3,4},{4,3},{5,6},{6,5},{7,15},{8,0},{9,10},{10,... | collective-permute-start | bytes 12296 | tf_op jit(solution)/shard_map/ppermute | solution.py:621
  13.9 2.0 %collective-permute-start.5 = (f32[8,128]{1,0:T(8,128)S(1)}, f32[8,128]{1,0:T(8,128)S(1)}, u32[]{:S(2)}, u32[]{:S(2)}) collective-permute-start(f32[8,128]{1,0:T(8,128)S(1)} %get-tuple-element.76), channel_id=1, source_target_pairs={{0,1},{1,0},{2,3},{3,2},{4,5},{5,4},{6,7},{7,6},{8,9},{9,8},{10,11... | collective-permute-start | bytes 12296 | tf_op jit(solution)/shard_map/ppermute | solution.py:625
  25.0 4.6 %collective-permute-start.8 = (f32[8,128]{1,0:T(8,128)S(1)}, f32[8,128]{1,0:T(8,128)S(1)}, u32[]{:S(2)}, u32[]{:S(2)}) collective-permute-start(f32[8,128]{1,0:T(8,128)S(1)} %shard_map.111), channel_id=1, source_target_pairs={{0,16},{8,24},{16,0},{24,8},{1,17},{9,25},{17,1},{25,9},{2,18},{10... | collective-permute-start | bytes 12296 | tf_op jit(solution)/shard_map/ppermute | solution.py:641
  27.7 5.4 %collective-permute-start.7 = (f32[8,128]{1,0:T(8,128)S(1)}, f32[8,128]{1,0:T(8,128)S(1)}, u32[]{:S(2)}, u32[]{:S(2)}) collective-permute-start(f32[8,128]{1,0:T(8,128)S(1)} %shard_map.111), channel_id=1, source_target_pairs={{0,24},{8,16},{16,8},{24,0},{1,25},{9,17},{17,9},{25,1},{2,26},{10... | collective-permute-start | bytes 12296 | tf_op jit(solution)/shard_map/ppermute | solution.py:641
  29.0 4.1 %collective-permute-start.6 = (f32[8,128]{1,0:T(8,128)S(1)}, f32[8,128]{1,0:T(8,128)S(1)}, u32[]{:S(2)}, u32[]{:S(2)}) collective-permute-start(f32[8,128]{1,0:T(8,128)S(1)} %shard_map.111), channel_id=1, source_target_pairs={{0,8},{8,0},{16,24},{24,16},{1,9},{9,1},{17,25},{25,17},{2,10},{10... | collective-permute-start | bytes 12296 | tf_op jit(solution)/shard_map/ppermute | solution.py:641
  33.1 0.6 %copy-start = (f32[8,128]{1,0:T(8,128)}, f32[8,128]{1,0:T(8,128)S(1)}, u32[]{:S(2)}) copy-start(f32[8,128]{1,0:T(8,128)S(1)} %add_add_fusion) | copy-start | bytes 12292
